TPU v7x, 256 devices: a whole 4x4x8 slice. The times are simulated.
256 devices in a mesh: prow: 8 (over z), pcol: 32 (over x, y, core).
Axes of the slice: x: 4, y: 4, z: 8, core: 2. Of those that a mesh axis runs over, the one named last changes fastest.
Arguments:
- trailing: bfloat16 [196608, 4096], P('prow', 'pcol'), may hold values from -6 to 6
- panel_t: bfloat16 [256, 196608], P('pcol', 'prow'), may hold values from -0.25 to 0.25
- pivots: int32 [256], replicated, may hold values from 256 to 196607, as said below
Outputs:
- updated: bfloat16 [196608, 4096], P('prow', 'pcol')
Inputs may be any that keep to these rules, and one draw needn't show every extreme that they name: The 256 pivots are distinct, and each is 256 or more; pivots[0] is 196607 and pivots[1] is 256.
All inputs are finite; a program needn't handle non-finite values.
Results may differ from a plain program's by a relative error of at most 0.0035.
Values may be sent and summed in bfloat16 or wider, within the bound.
No kernel may reach another device: no remote copies, remote signals or barrier semaphores. Data moves between devices by JAX's collectives and lax.ppermute only.
A program may use at most 64 MiB of HBM per device.

v0:
```python
import jax
import jax.numpy as jnp
from jax import lax
from jax.sharding import PartitionSpec as P


def spread(block, axis, owner):
    block = jnp.where(lax.axis_index(axis) == owner, block, jnp.zeros_like(block))
    return lax.psum(block, axis)


def body(trailing, panel_t, pivots):
    rows_here = trailing.shape[0]
    width = panel_t.shape[0] * lax.axis_size("pcol")
    me = lax.axis_index("prow")
    first_row = me * rows_here
    top_index = jnp.arange(width, dtype=jnp.int32)
    places = jnp.concatenate([top_index, pivots])
    sources = jnp.concatenate([pivots, top_index])
    owned = (sources >= first_row) & (sources < first_row + rows_here)
    local_src = jnp.clip(sources - first_row, 0, rows_here - 1)
    picked = jnp.where(owned[:, None], trailing[local_src].astype(jnp.float32), 0.0)
    moved = lax.psum(picked.astype(jnp.bfloat16), "prow")
    mine = (places >= first_row) & (places < first_row + rows_here)
    dest = jnp.where(mine, places - first_row, rows_here)
    swapped = trailing.at[dest].set(moved, mode="drop")
    top_rows = moved[:width].astype(jnp.float32)
    diag_cols = lax.all_gather(panel_t[:, :width], "pcol", axis=0, tiled=True)
    shared_block = spread(diag_cols, "prow", 0)
    lower_block = shared_block.astype(jnp.float32).T
    unit = jnp.tril(lower_block, -1) + jnp.eye(width, dtype=jnp.float32)
    urows = lax.linalg.triangular_solve(
        unit, top_rows, left_side=True, lower=True, unit_diagonal=True
    ).astype(jnp.bfloat16)
    full_panel = lax.all_gather(panel_t, "pcol", axis=0, tiled=True)
    product = lax.dot_general(
        full_panel, urows, (((0,), (0,)), ((), ())), preferred_element_type=jnp.float32
    )
    result = (swapped.astype(jnp.float32) - product).astype(jnp.bfloat16)
    head = jnp.where(me == 0, urows, result[:width])
    return lax.dynamic_update_slice(result, head, (0, 0))


def solution(mesh):
    return jax.shard_map(
        body,
        mesh=mesh,
        in_specs=(P("prow", "pcol"), P("pcol", "prow"), P()),
        out_specs=P("prow", "pcol"),
        check_vma=False,
    )
```

profile of v0, /device:TPU:1, one launch (start us, length us, event | category | flops | bytes accessed | tf_op | source)
XLA Modules:
  0.0 172.5 jit_solution(7199933855212409870)
XLA Ops:
  7.4 0.0 copy-start
  7.4 0.0 all-reduce.3.cloned.1.call-start
  7.4 6.4 %copy.27 = bf16[24576,128]{1,0:T(8,128)(2,1)} copy(bf16[24576,128]{1,0:T(8,128)(2,1)} %param.3) | data formatting | bytes 12582912
  13.8 0.0 copy-done
  13.9 0.7 slice.20
  14.6 26.2 %all_gather.6 = bf16[256,256]{1,0:T(8,128)(2,1)S(1)} all-gather(bf16[8,256]{1,0:T(8,128)(2,1)S(1)} %slice.20), channel_id=1, replica_groups=mesh['prow'=8,'pcol'=32] {'pcol'}, dimensions={0}, use_global_device_ids=true | all-gather | bytes 135168 | tf_op jit(solution)/shard_map/all_gather | solution.py:28
  40.8 4.6 %gather_fusion = bf16[512,128]{1,0:T(8,128)(2,1)S(1)} fusion(bf16[24576,128]{1,0:T(8,128)(2,1)} %copy.27, s32[1024]{0:T(1024)S(1)} %pad_clamp_fusion), kind=kCustom, calls=%fused_computation | custom fusion | bytes 264192 | tf_op jit(solution)/shard_map/gather | solution.py:22
  45.4 0.8 select_convert_fusion
  46.2 0.7 select_bitcast_fusion
  46.9 0.0 all-reduce.3.cloned.1.call-update
  46.9 0.0 all-gather.2.cloned.1.call-start
  47.0 0.5 all-gather.2.cloned.1.call-update
  47.5 68.9 %all-reduce.3.cloned.1.call-done = (bf16[512,128]{1,0:T(8,128)(2,1)}, bf16[256,256]{0,1:T(8,128)(2,1)}) async-done(((bf16[512,128]{1,0:T(8,128)(2,1)}, bf16[256,256]{0,1:T(8,128)(2,1)}), (bf16[512,128]{1,0:T(8,128)(2,1)}, bf16[256,256]{0,1:T(8,128)(2,1)})) %all-reduce.3.cloned.1.call-update) | async-done | bytes 262160 | tf_op jit(solution)/shard_map/psum | solution.py:23
  116.4 1.0 convert_add_fusion
  117.5 0.1 triangular_solve.90
  117.5 4.4 %while.1 = (s32[]{:T(128)}, f32[256,256]{0,1:T(8,128)S(1)}, s32[2,2]{1,0:T(2,128)S(1)}, f32[2,128,128]{2,1,0:T(8,128)S(1)}, s32[]{:T(128)}) while((s32[]{:T(128)}, f32[256,256]{0,1:T(8,128)S(1)}, s32[2,2]{1,0:T(2,128)S(1)}, f32[2,128,128]{2,1,0:T(8,128)S(1)}, s32[]{:T(128)}) %tuple.22), condition=%wide.while_cond, body=%wide.while_body.sunk | while | flops 2 | bytes 393321 | solution.py:32
  117.5 0.6 fusion.14
  118.2 1.4 dynamic-slice.7
  119.6 0.1 copy.13
  119.8 0.6 fusion.14
  120.4 1.4 dynamic-slice.7
  121.8 0.1 copy.13
  121.9 19.7 %custom-call.3 = f32[2,128,128]{1,2,0:T(8,128)S(1)} custom-call(f32[2,128,128]{2,1,0:T(8,128)S(1)} %get-tuple-element.12), custom_call_target="InvertDiagBlocksLowerTriangular" | custom-call | tf_op jit(solution)/shard_map/triangular_solve | solution.py:32
  141.6 8.9 %scatter_fusion = bf16[24576,128]{1,0:T(8,128)(2,1)} fusion(bf16[24576,128]{1,0:T(8,128)(2,1)} %copy.27, s32[512]{0:T(512)S(1)} %bitcast.32, bf16[512,128]{1,0:T(8,128)(2,1)} %get-tuple-element.25), kind=kCustom, calls=%fused_computation.1 | custom fusion | bytes 395264 | tf_op jit(solution)/shard_map/scatter | solution.py:26
  150.5 1.0 fusion.9
  151.6 1.0 convolution_subtract_fusion
  152.6 0.3 convolution_convert_fusion
  152.9 0.0 all-gather.2.cloned.1.call-done
  152.9 10.7 %fusion.1 = bf16[24576,128]{1,0:T(8,128)(2,1)} fusion(bf16[256,24576]{1,0:T(8,128)(2,1)} %all-gather.2.cloned.1.call-done, bf16[24576,128]{1,0:T(8,128)(2,1)} %scatter_fusion, bf16[128,128]{1,0:T(8,128)(2,1)S(1)} %convolution_convert_fusion, bf16[128,128]{1,0:T(8,128)(2,1)S(1)} %get-tuple-element.31), kind=kOutput, calls=%fused_computation.6 | convolution fusion | flops 1620180992 | bytes 25231360 | tf_op jit(solution)/shard_map/dot_general | solution.py:36
  163.6 1.5 fusion.2
  (13 shorter events, 0.1 us)
Async XLA Ops:
  7.4 6.4 %copy-start = (s32[256]{0:T(256)S(1)}, s32[256]{0:T(256)}, u32[]{:S(2)}) copy-start(s32[256]{0:T(256)} %param.5) | copy-start | bytes 3076
  7.4 109.1 %all-reduce.3.cloned.1.call-start = ((), (), s32[]{:S(2)}) async-start(), calls=%async_computation.1 | async-start | bytes 524288 | tf_op jit(solution)/shard_map/psum | solution.py:23
  46.9 106.0 %all-gather.2.cloned.1.call-start = ((), (), s32[]{:S(2)}) async-start(), calls=%async_computation | async-start | bytes 12976128 | tf_op jit(solution)/shard_map/all_gather | solution.py:35
Sparse Core Ops, SparseCore 0:
  47.0 69.3 all-reduce.2
Sparse Core Ops, SparseCore 1:
  50.0 68.4 all-gather.1
where the time goes:
time: 176 us; the launch traced here: 173 us
  waiting for transfers between devices  69.5 us (39%)
  blocking collectives  26.2 us (15%)
  local copies, waits for them, and re-layouts  25.1 us (14%)
  other arithmetic  23.7 us (13%)
  between operations  15 us (9%)
  matrix products  13 us (7%)
    psum x1, waiting for transfers between devices, body(): moved = lax.psum(picked.astype(jnp.bfloat16), 'prow')  68.9 us
    all_gather x1, blocking collectives, body(): diag_cols = lax.all_gather(panel_t[:, :width], 'pcol', axis=0, tiled=True)  26.2 us
    another operation x4, other arithmetic, body(): lax.linalg.triangular_solve(unit, top_rows, left_side=True, lower=True, u...  20.7 us
    dot_general x1, matrix products, body(): lax.dot_general(full_panel, urows, (((0,), (0,)), ((), ())), preferred_el...  10.7 us
    scatter x1, local copies, waits for them, and re-layouts, body(): swapped = trailing.at[dest].set(moved, mode='drop')  8.93 us
    unnamed x3, local copies, waits for them, and re-layouts  6.43 us
    gather x1, local copies, waits for them, and re-layouts, body(): trailing[local_src].astype(jnp.float32)  4.65 us
    another operation x10, local copies, waits for them, and re-layouts  4.33 us
  transfers between devices with their start and end apart: 2, of which 1 were waited for; matrix products, arithmetic and copies ran while one was open for 21% of the time, Pallas kernels for 0%

commit v1 on v0

v1 whole, which is shorter than its diff:
```python
import functools

import jax
import jax.numpy as jnp
from jax import lax
from jax.experimental import pallas as pl
from jax.experimental.pallas import tpu as pltpu
from jax.sharding import PartitionSpec as P

NX = 4
NY = 4
OFFSETS = (0, -1, 1, 2)
HIGHEST = lax.Precision.HIGHEST


def place(x, y, c):
    return ((x % NX) * NY + (y % NY)) * 2 + c


def hop(dx, dy, turn):
    pairs = []
    for x in range(NX):
        for y in range(NY):
            for c in range(2):
                a, b = (dy, dx) if turn and c == 1 else (dx, dy)
                pairs.append((place(x, y, c), place(x + a, y + b, c)))
    return pairs


CORES = [(p, p ^ 1) for p in range(NX * NY * 2)]


def send(block, pairs):
    return lax.ppermute(block, "pcol", pairs)


def pick_kernel(blk, piv_ref, first_ref, trailing_ref, top_ref, out_ref, cnt_ref, lst_ref, rows_ref):
    width = piv_ref.shape[0]
    rows = trailing_ref.shape[0]
    first = first_ref[0]
    for b in range(cnt_ref.shape[0]):
        cnt_ref[b] = 0
    rows_ref[...] = jnp.zeros_like(rows_ref)
    sub = lax.broadcasted_iota(jnp.int32, (16, 128), 0)

    def step(i, carry):
        loc = piv_ref[i] - first

        @pl.when((loc >= 0) & (loc < rows))
        def _():
            b = lax.div(loc, blk)
            k = cnt_ref[b]
            lst_ref[b * width + k] = i
            cnt_ref[b] = k + 1
            base = pl.multiple_of(loc & ~15, 16)
            tile = trailing_ref[pl.ds(base, 16), :].astype(jnp.float32)
            row = jnp.sum(jnp.where(sub == (loc & 15), tile, 0.0), axis=0, keepdims=True)
            rows_ref[pl.ds(i, 1), :] = row

        return carry

    lax.fori_loop(0, width, step, 0)
    out_ref[:width, :] = rows_ref[...].astype(jnp.bfloat16)
    keep = (first == 0).astype(jnp.float32)
    head = trailing_ref[:width, :].astype(jnp.float32)
    out_ref[width : 2 * width, :] = (head * keep).astype(jnp.bfloat16)
    top = top_ref[...].astype(jnp.float32) * keep
    both = jnp.concatenate([top[:, :128], top[:, 128:]], axis=0)
    out_ref[2 * width :, :] = both.astype(jnp.bfloat16)


def pick(trailing, panel_t, pivots, first, blk):
    rows, cols = trailing.shape
    width = pivots.shape[0]
    nblk = rows // blk
    return pl.pallas_call(
        functools.partial(pick_kernel, blk),
        grid=(1,),
        in_specs=[
            pl.BlockSpec(memory_space=pltpu.SMEM),
            pl.BlockSpec(memory_space=pltpu.SMEM),
            pl.BlockSpec((rows, cols), lambda i: (0, 0), pipeline_mode=pl.Buffered(1)),
            pl.BlockSpec((8, width), lambda i: (0, 0)),
        ],
        out_specs=[
            pl.BlockSpec((2 * width + 16, cols), lambda i: (0, 0)),
            pl.BlockSpec(memory_space=pltpu.SMEM),
            pl.BlockSpec(memory_space=pltpu.SMEM),
        ],
        out_shape=[
            jax.ShapeDtypeStruct((2 * width + 16, cols), jnp.bfloat16),
            jax.ShapeDtypeStruct((nblk,), jnp.int32),
            jax.ShapeDtypeStruct((nblk * width,), jnp.int32),
        ],
        scratch_shapes=[pltpu.VMEM((width, cols), jnp.float32)],
        compiler_params=pltpu.CompilerParams(vmem_limit_bytes=24 << 20),
        name="pick",
    )(pivots, first, trailing, panel_t)


def dot(a, b):
    return lax.dot_general(
        a, b, (((1,), (0,)), ((), ())), precision=HIGHEST, preferred_element_type=jnp.float32
    )


def solve_kernel(from_ref, to_ref, own_ref, other_ref, top_ref, nat_ref, perm_ref, a_ref, u_ref):
    n = nat_ref.shape[0]
    half = n // 16
    for b in range(n // 8):
        src = own_ref if b < half else other_ref
        k = (b % half) * 16
        piece = src[k : k + 16, :].astype(jnp.float32)
        at = pl.ds(pl.multiple_of(from_ref[b] * 8, 8), 8)
        a_ref[at, :128] = piece[:8]
        a_ref[at, 128:] = piece[8:]
    r = lax.broadcasted_iota(jnp.int32, (n, n), 0)
    c = lax.broadcasted_iota(jnp.int32, (n, n), 1)
    strict = jnp.where(r > c, a_ref[...].T, 0.0)
    d = jnp.where((r >> 4) == (c >> 4), strict, 0.0)
    x = jnp.where(r == c, 1.0, 0.0) - d
    for _ in range(3):
        d = dot(d, d)
        x = x + dot(x, d)
    for lg in (4, 5, 6, 7):
        inside = ((r >> (lg + 1)) == (c >> (lg + 1))) & ((r >> lg) != (c >> lg))
        x = x - dot(x, dot(jnp.where(inside, strict, 0.0), x))
    u = dot(x, top_ref[...].astype(jnp.float32))
    u = u.astype(jnp.bfloat16).astype(jnp.float32)
    u_ref[...] = u
    nat_ref[...] = u.astype(jnp.bfloat16)
    for b in range(n // 8):
        a_ref[8 * b : 8 * b + 8, :128] = u_ref[pl.ds(pl.multiple_of(to_ref[b] * 8, 8), 8), :]
    perm_ref[...] = a_ref[:, :128].astype(jnp.bfloat16)


def solve(order_l, order_u, own, other, top):
    n, cols = top.shape
    smem = pl.BlockSpec(memory_space=pltpu.SMEM)
    vmem = pl.BlockSpec(memory_space=pltpu.VMEM)
    return pl.pallas_call(
        solve_kernel,
        in_specs=[smem, smem, vmem, vmem, vmem],
        out_specs=[vmem, vmem],
        out_shape=[jax.ShapeDtypeStruct((n, cols), jnp.bfloat16)] * 2,
        scratch_shapes=[pltpu.VMEM((n, n), jnp.float32), pltpu.VMEM((n, cols), jnp.float32)],
        compiler_params=pltpu.CompilerParams(vmem_limit_bytes=24 << 20),
        name="solve",
    )(order_l, order_u, own, other, top)


def update_kernel(nblk, cnt_ref, lst_ref, piv_ref, first_ref, *refs):
    tr_ref, u_ref, nat_ref, disp_ref = refs[:4]
    parts = refs[4:14]
    out_ref, acc_ref, drow_ref = refs[14:]
    blk = tr_ref.shape[0]
    width = nat_ref.shape[0]
    b = pl.program_id(0)
    first = first_ref[0]

    @pl.when(b == 0)
    def _():
        drow_ref[...] = disp_ref[...].astype(jnp.float32)

    early = b < nblk // 2
    pieces = []
    for s in (parts[:5], parts[5:]):
        pieces += [s[0][...], s[1][...], s[2][...], jnp.where(early, s[3][...], s[4][...])]
    panel = jnp.concatenate(pieces, axis=0)
    acc_ref[...] = lax.dot_general(
        panel, u_ref[...], (((0,), (0,)), ((), ())), preferred_element_type=jnp.float32
    )
    out_ref[...] = (tr_ref[...].astype(jnp.float32) - acc_ref[...]).astype(jnp.bfloat16)
    sub = lax.broadcasted_iota(jnp.int32, (16, 128), 0)

    def fix(k, carry):
        i = lst_ref[b * width + k]
        loc = piv_ref[i] - first - b * blk
        at = pl.ds(pl.multiple_of(loc & ~15, 16), 16)
        new = drow_ref[pl.ds(i, 1), :] - acc_ref[at, :]
        old = out_ref[at, :].astype(jnp.float32)
        out_ref[at, :] = jnp.where(sub == (loc & 15), new, old).astype(jnp.bfloat16)
        return carry

    lax.fori_loop(0, cnt_ref[b], fix, 0)

    @pl.when((b == 0) & (first == 0))
    def _():
        out_ref[:width, :] = nat_ref[...]


def update(cnt, lst, pivots, first, trailing, u, nat, disp, own, other, blk):
    rows, cols = trailing.shape
    width = nat.shape[0]
    nblk = rows // blk
    hb = nblk // 2

    def whole(shape):
        return pl.BlockSpec(shape, lambda b, *_: (0, 0))

    tall = pl.BlockSpec((blk, cols), lambda b, *_: (b, 0))
    wide = pl.BlockSpec((32, blk), lambda b, *_: (0, b))
    low = pl.BlockSpec((32, blk), lambda b, *_: (0, jnp.minimum(b, hb - 1)))
    high = pl.BlockSpec((32, blk), lambda b, *_: (0, jnp.maximum(b - hb, 0)))
    group = [wide, wide, wide, low, high]
    return pl.pallas_call(
        functools.partial(update_kernel, nblk),
        grid_spec=pltpu.PrefetchScalarGridSpec(
            num_scalar_prefetch=4,
            grid=(nblk,),
            in_specs=[tall, whole((width, cols)), whole((width, cols)), whole((width, cols))]
            + group
            + group,
            out_specs=tall,
            scratch_shapes=[
                pltpu.VMEM((blk, cols), jnp.float32),
                pltpu.VMEM((width, cols), jnp.float32),
            ],
        ),
        out_shape=jax.ShapeDtypeStruct((rows, cols), jnp.bfloat16),
        compiler_params=pltpu.CompilerParams(vmem_limit_bytes=32 << 20),
        name="update",
    )(cnt, lst, pivots, first, trailing, u, nat, disp, *own, *other)


def around(block, hops):
    return jnp.concatenate([block] + [send(block, h) for h in hops], axis=0)


def body(trailing, panel_t, pivots):
    rows = trailing.shape[0]
    width = pivots.shape[0]
    blk = rows // 12
    first = (lax.axis_index("prow") * rows).astype(jnp.int32).reshape(1)
    me = lax.axis_index("pcol")
    mx, my, mc = me // (NY * 2), (me // 2) % NY, me % 2

    block = around(panel_t, [hop(1, 0, True), hop(-1, 0, True), hop(2, 0, True)])
    up, down = hop(0, 1, True), hop(0, -1, True)
    half = rows // 2
    near, far = send(block, up), send(block, down)
    own = [block, near, far, send(near[:, :half], up), send(far[:, half:], down)]
    other = [send(t, CORES) for t in own]

    load, cnt, lst = pick(trailing, panel_t, pivots, first, blk)
    nz = lax.axis_size("prow")
    for d in (1, 2, 4):
        load = load + lax.ppermute(load, "prow", [(i, i ^ d) for i in range(nz)])
    top, disp, diag = load[:width], load[width : 2 * width], load[2 * width :]
    diag = around(diag, [hop(1, 0, False), hop(-1, 0, False), hop(2, 0, False)])
    diag = around(diag, [hop(0, 1, False), hop(0, -1, False), hop(0, 2, False)])
    diag_other = send(diag, CORES)

    offs = jnp.array(OFFSETS, jnp.int32)
    outer = jnp.repeat(offs, 4)
    inner = jnp.tile(offs, 4)
    order_l = jnp.concatenate([place(mx + inner, my + outer, mc), place(mx + inner, my + outer, 1 - mc)])
    cross = [place(mx + inner, my + outer, 0), place(mx + outer, my + inner, 1)]
    order_u = jnp.concatenate(
        [jnp.where(mc == 0, cross[0], cross[1]), jnp.where(mc == 0, cross[1], cross[0])]
    )
    nat, perm = solve(order_l.astype(jnp.int32), order_u.astype(jnp.int32), diag, diag_other, top)
    return update(cnt, lst, pivots, first, trailing, perm, nat, disp, own, other, blk)


def solution(mesh):
    return jax.shard_map(
        body,
        mesh=mesh,
        in_specs=(P("prow", "pcol"), P("pcol", "prow"), P()),
        out_specs=P("prow", "pcol"),
        check_vma=False,
    )
```

time: 176 us -> 115 us (0.65); the launches traced: 173 us -> 114 us
  starting transfers between devices: 0.05 us -> 39.8 us
  waiting for transfers between devices: 69.5 us -> 34.4 us
  Pallas kernels: 0 us -> 26.8 us
  blocking collectives: 26.2 us -> 0 us
  other arithmetic: 23.7 us -> 0.22 us
  between operations: 15 us -> 0.19 us
  matrix products: 13 us -> 0 us
  local copies, waits for them, and re-layouts: 25.1 us -> 12.9 us
    psum x1 -> x0, waiting for transfers between devices: 68.9 us -> none  [body(): moved = lax.psum(picked.astype(jnp.bfloat16), 'prow')]
    ppermute x0 -> x22, starting transfers between devices: none -> 39.8 us  [the longest x19 28.9 us: send(): return lax.ppermute(block, 'pcol', pairs)]
    ppermute x0 -> x22, waiting for transfers between devices: none -> 34.4 us  [the longest x19 25.1 us: send(): return lax.ppermute(block, 'pcol', pairs)]
    pallas_call x0 -> x3, Pallas kernels: none -> 26.8 us  [the longest x1 13.7 us: update(): pl.pallas_call(functools.partial(update_kernel, nblk), grid_spec=pltpu.Pr...]
    all_gather x1 -> x0, blocking collectives: 26.2 us -> none  [body(): diag_cols = lax.all_gather(panel_t[:, :width], 'pcol', axis=0, tiled=True)]
    another operation x4 -> x0, other arithmetic: 20.7 us -> none  [body(): lax.linalg.triangular_solve(unit, top_rows, left_side=True, lower=True, u...]
    dot_general x1 -> x0, matrix products: 10.7 us -> none  [body(): lax.dot_general(full_panel, urows, (((0,), (0,)), ((), ())), preferred_el...]
    scatter x1 -> x0, local copies, waits for them, and re-layouts: 8.93 us -> none  [body(): swapped = trailing.at[dest].set(moved, mode='drop')]
  transfers between devices with their start and end apart: 2 -> 22, of which waited for: 1 -> 9; matrix products, arithmetic and copies ran while one was open for 21% -> 5% of each run, Pallas kernels for 0% -> 11%
where the time goes in v1:
time: 115 us; the launch traced here: 114 us
  starting transfers between devices  39.8 us (35%)
  waiting for transfers between devices  34.4 us (30%)
  Pallas kernels  26.8 us (23%)
  local copies, waits for them, and re-layouts  12.9 us (11%)
    ppermute x19, starting transfers between devices, send(): return lax.ppermute(block, 'pcol', pairs)  28.9 us
    ppermute x19, waiting for transfers between devices, send(): return lax.ppermute(block, 'pcol', pairs)  25.1 us
    pallas_call x1, Pallas kernels, update(): pl.pallas_call(functools.partial(update_kernel, nblk), grid_spec=pltpu.Pr...  13.7 us
    ppermute x3, starting transfers between devices, body(): load = load + lax.ppermute(load, 'prow', [(i, i ^ d) for i in range(nz)])  10.9 us
    unnamed x26, local copies, waits for them, and re-layouts  9.69 us
    ppermute x3, waiting for transfers between devices, body(): load = load + lax.ppermute(load, 'prow', [(i, i ^ d) for i in range(nz)])  9.25 us
    pallas_call x1, Pallas kernels, solve(): pl.pallas_call(solve_kernel, in_specs=[smem, smem, vmem, vmem, vmem], out...  7.56 us
    pallas_call x1, Pallas kernels, pick(): pl.pallas_call(functools.partial(pick_kernel, blk), grid=(1,), in_specs=[...  5.53 us
  transfers between devices with their start and end apart: 22, of which 9 were waited for; matrix products, arithmetic and copies ran while one was open for 5% of the time, Pallas kernels for 11%

profile of v1, /device:TPU:1, one launch (start us, length us, event | category | flops | bytes accessed | tf_op | source)
XLA Modules:
  0.0 114.3 jit_solution(6826287812902735396)
XLA Ops:
  0.0 3.6 %collective-permute-start.11 = (bf16[8,24576]{1,0:T(8,128)(2,1)}, bf16[8,24576]{1,0:T(8,128)(2,1)S(1)}, u32[]{:S(2)}, u32[]{:S(2)}) collective-permute-start(bf16[8,24576]{1,0:T(8,128)(2,1)} %top_ref.1), channel_id=1, source_target_pairs={{0,24},{1,7},{2,26},{3,1},{4,28},{5,3},{6,30},{7,5},{8,0},{9,15},{... | collective-permute-start | bytes 1179656 | tf_op jit(solution)/shard_map/ppermute | solution.py:34
  3.6 1.6 %collective-permute-start.12 = (bf16[8,24576]{1,0:T(8,128)(2,1)}, bf16[8,24576]{1,0:T(8,128)(2,1)S(1)}, u32[]{:S(2)}, u32[]{:S(2)}) collective-permute-start(bf16[8,24576]{1,0:T(8,128)(2,1)} %top_ref.1), channel_id=1, source_target_pairs={{0,16},{1,5},{2,18},{3,7},{4,20},{5,1},{6,22},{7,3},{8,24},{9,13},... | collective-permute-start | bytes 1179656 | tf_op jit(solution)/shard_map/ppermute | solution.py:34
  5.2 1.8 %constant_dynamic-update-slice_fusion.10 = bf16[32,24576]{1,0:T(8,128)(2,1)} fusion(bf16[8,24576]{1,0:T(8,128)(2,1)} %top_ref.1), kind=kLoop, calls=%fused_computation.10 | loop fusion | bytes 786432
  7.0 9.1 %collective-permute-done.10 = bf16[8,24576]{1,0:T(8,128)(2,1)S(1)} collective-permute-done((bf16[8,24576]{1,0:T(8,128)(2,1)}, bf16[8,24576]{1,0:T(8,128)(2,1)S(1)}, u32[]{:S(2)}, u32[]{:S(2)}) %collective-permute-start.10) | collective-permute-done | bytes 393248 | tf_op jit(solution)/shard_map/ppermute | solution.py:34
  16.1 0.8 constant_dynamic-update-slice_fusion.9
  16.9 0.8 constant_dynamic-update-slice_fusion.8
  17.7 0.8 constant_dynamic-update-slice_fusion.7.refs_4_
  18.5 2.2 %collective-permute-start.14 = (bf16[32,24576]{1,0:T(8,128)(2,1)}, bf16[32,24576]{1,0:T(8,128)(2,1)S(1)}, u32[]{:S(2)}, u32[]{:S(2)}) collective-permute-start(bf16[32,24576]{1,0:T(8,128)(2,1)} %constant_dynamic-update-slice_fusion.7.refs_4_), channel_id=1, source_target_pairs={{0,6},{1,25},{2,0},{3,27},{4,2},{5,29},{6,4},{7,31},{8,14},{9,1},{... | collective-permute-start | bytes 4718600 | tf_op jit(solution)/shard_map/ppermute | solution.py:34
  20.7 0.0 copy-start
  20.7 2.8 %copy-done = bf16[24576,128]{1,0:T(8,128)(2,1)S(1)} copy-done((bf16[24576,128]{1,0:T(8,128)(2,1)S(1)}, bf16[24576,128]{1,0:T(8,128)(2,1)}, u32[]{:S(2)}) %copy-start) | copy-done | bytes 6291480
  23.5 5.5 %pick.1 = (bf16[528,128]{1,0:T(8,128)(2,1)S(1)}, s32[12]{0:T(128)S(1)}, s32[3072]{0:T(1024)S(1)}) custom-call(s32[256]{0:T(256)S(1)} %copy-done.3, s32[1]{0:T(128)} %bitcast.first_ref, bf16[24576,128]{1,0:T(8,128)(2,1)S(1)} %copy-done, bf16[8,24576]{1,0:T(8,128)(2,1)S(1)} %copy-done.2), custom_call_target="tpu_custom_call" | custom-call | tf_op jit(solution)/shard_map/pick/pallas_call | solution.py:76
  29.0 1.7 %collective-permute-start = (bf16[528,128]{1,0:T(8,128)(2,1)S(1)}, bf16[528,128]{1,0:T(8,128)(2,1)S(1)}, u32[]{:S(2)}, u32[]{:S(2)}) collective-permute-start(bf16[528,128]{1,0:T(8,128)(2,1)S(1)} %get-tuple-element.12), channel_id=1, source_target_pairs={{0,32},{32,0},{64,96},{96,64},{128,160},{160,128},{192,224},{224,1... | collective-permute-start | bytes 405512 | tf_op jit(solution)/shard_map/ppermute | solution.py:248
  30.7 2.7 %collective-permute-done = bf16[528,128]{1,0:T(8,128)(2,1)S(1)} collective-permute-done((bf16[528,128]{1,0:T(8,128)(2,1)S(1)}, bf16[528,128]{1,0:T(8,128)(2,1)S(1)}, u32[]{:S(2)}, u32[]{:S(2)}) %collective-permute-start) | collective-permute-done | bytes 135200 | tf_op jit(solution)/shard_map/ppermute | solution.py:248
  33.5 3.1 %collective-permute-start.1 = (bf16[528,128]{1,0:T(8,128)(2,1)S(1)}, bf16[528,128]{1,0:T(8,128)(2,1)S(1)}, u32[]{:S(2)}, u32[]{:S(2)}) collective-permute-start(bf16[528,128]{1,0:T(8,128)(2,1)S(1)} %add.128), channel_id=1, source_target_pairs={{0,64},{32,96},{64,0},{96,32},{128,192},{160,224},{192,128},{224,1... | collective-permute-start | bytes 405512 | tf_op jit(solution)/shard_map/ppermute | solution.py:248
  36.6 4.1 %collective-permute-done.1 = bf16[528,128]{1,0:T(8,128)(2,1)S(1)} collective-permute-done((bf16[528,128]{1,0:T(8,128)(2,1)S(1)}, bf16[528,128]{1,0:T(8,128)(2,1)S(1)}, u32[]{:S(2)}, u32[]{:S(2)}) %collective-permute-start.1) | collective-permute-done | bytes 135200 | tf_op jit(solution)/shard_map/ppermute | solution.py:248
  40.8 6.1 %collective-permute-start.2 = (bf16[528,128]{1,0:T(8,128)(2,1)S(1)}, bf16[528,128]{1,0:T(8,128)(2,1)S(1)}, u32[]{:S(2)}, u32[]{:S(2)}) collective-permute-start(bf16[528,128]{1,0:T(8,128)(2,1)S(1)} %add.129), channel_id=1, source_target_pairs={{0,128},{32,160},{64,192},{96,224},{128,0},{160,32},{192,64},{224,... | collective-permute-start | bytes 405512 | tf_op jit(solution)/shard_map/ppermute | solution.py:248
  46.9 2.4 %collective-permute-done.2 = bf16[528,128]{1,0:T(8,128)(2,1)S(1)} collective-permute-done((bf16[528,128]{1,0:T(8,128)(2,1)S(1)}, bf16[528,128]{1,0:T(8,128)(2,1)S(1)}, u32[]{:S(2)}, u32[]{:S(2)}) %collective-permute-start.2) | collective-permute-done | bytes 135200 | tf_op jit(solution)/shard_map/ppermute | solution.py:248
  49.4 6.0 %collective-permute-start.5 = (bf16[16,128]{1,0:T(8,128)(2,1)S(1)}, bf16[16,128]{1,0:T(8,128)(2,1)S(1)}, u32[]{:S(2)}, u32[]{:S(2)}) collective-permute-start(bf16[16,128]{1,0:T(8,128)(2,1)S(1)} %get-tuple-element.20), channel_id=1, source_target_pairs={{0,16},{1,17},{2,18},{3,19},{4,20},{5,21},{6,22},{7,23},{8,24},{9,... | collective-permute-start | bytes 12296 | tf_op jit(solution)/shard_map/ppermute | solution.py:34
  55.4 1.1 %collective-permute-start.4 = (bf16[16,128]{1,0:T(8,128)(2,1)S(1)}, bf16[16,128]{1,0:T(8,128)(2,1)S(1)}, u32[]{:S(2)}, u32[]{:S(2)}) collective-permute-start(bf16[16,128]{1,0:T(8,128)(2,1)S(1)} %get-tuple-element.20), channel_id=1, source_target_pairs={{0,24},{1,25},{2,26},{3,27},{4,28},{5,29},{6,30},{7,31},{8,0},{9,1... | collective-permute-start | bytes 12296 | tf_op jit(solution)/shard_map/ppermute | solution.py:34
  56.6 0.4 collective-permute-start.3
  56.9 1.0 collective-permute-done.4
  58.0 2.3 %collective-permute-done.3 = bf16[16,128]{1,0:T(8,128)(2,1)S(1)} collective-permute-done((bf16[16,128]{1,0:T(8,128)(2,1)S(1)}, bf16[16,128]{1,0:T(8,128)(2,1)S(1)}, u32[]{:S(2)}, u32[]{:S(2)}) %collective-permute-start.3) | collective-permute-done | bytes 4128 | tf_op jit(solution)/shard_map/ppermute | solution.py:34
  60.2 1.5 %collective-permute-start.6 = (bf16[64,128]{1,0:T(8,128)(2,1)S(1)}, bf16[64,128]{1,0:T(8,128)(2,1)S(1)}, u32[]{:S(2)}, u32[]{:S(2)}) collective-permute-start(bf16[64,128]{1,0:T(8,128)(2,1)S(1)} %pad_maximum_fusion), channel_id=1, source_target_pairs={{0,2},{1,3},{2,4},{3,5},{4,6},{5,7},{6,0},{7,1},{8,10},{9,11},{10,... | collective-permute-start | bytes 49160 | tf_op jit(solution)/shard_map/ppermute | solution.py:34
  61.7 2.9 %collective-permute-done.6 = bf16[64,128]{1,0:T(8,128)(2,1)S(1)} collective-permute-done((bf16[64,128]{1,0:T(8,128)(2,1)S(1)}, bf16[64,128]{1,0:T(8,128)(2,1)S(1)}, u32[]{:S(2)}, u32[]{:S(2)}) %collective-permute-start.6) | collective-permute-done | bytes 16416 | tf_op jit(solution)/shard_map/ppermute | solution.py:34
  64.7 0.0 copy-start.8
  64.7 7.2 %collective-permute-start.9 = (bf16[256,128]{1,0:T(8,128)(2,1)S(1)}, bf16[256,128]{1,0:T(8,128)(2,1)S(1)}, u32[]{:S(2)}, u32[]{:S(2)}) collective-permute-start(bf16[256,128]{1,0:T(8,128)(2,1)S(1)} %constant_dynamic-update-slice_fusion.own_ref), channel_id=1, source_target_pairs={{0,1},{1,0},{2,3},{3,2},{4,5},{5,4},{6,7},{7,6},{8,9},{9,8},{10,11... | collective-permute-start | bytes 196616 | tf_op jit(solution)/shard_map/ppermute | solution.py:34
  71.9 1.0 slice.24
  72.9 1.1 collective-permute-start.16
  74.0 0.9 slice.23
  74.9 0.4 collective-permute-start.15
  75.3 0.6 collective-permute-start.17
  75.9 0.1 collective-permute-start.19
  76.0 0.4 collective-permute-start.18
  76.4 0.1 broadcast_in_dim.6
  76.5 0.1 add.122
  76.6 0.1 add.109
  76.7 0.1 add.124
  76.7 0.1 broadcast_in_dim.5
  76.8 0.1 add.114
  76.9 7.4 %collective-permute-done.16.refs_8_ = bf16[32,12288]{1,0:T(8,128)(2,1)} collective-permute-done((bf16[32,12288]{1,0:T(8,128)(2,1)}, bf16[32,12288]{1,0:T(8,128)(2,1)}, u32[]{:S(2)}, u32[]{:S(2)}) %collective-permute-start.16) | collective-permute-done | bytes 786464 | tf_op jit(solution)/shard_map/ppermute | solution.py:34
  84.3 0.9 collective-permute-start.21
  85.2 2.4 %collective-permute-done.15.refs_7_ = bf16[32,12288]{1,0:T(8,128)(2,1)} collective-permute-done((bf16[32,12288]{1,0:T(8,128)(2,1)}, bf16[32,12288]{1,0:T(8,128)(2,1)}, u32[]{:S(2)}, u32[]{:S(2)}) %collective-permute-start.15) | collective-permute-done | bytes 786464 | tf_op jit(solution)/shard_map/ppermute | solution.py:34
  87.6 1.8 %collective-permute-start.20 = (bf16[32,12288]{1,0:T(8,128)(2,1)}, bf16[32,12288]{1,0:T(8,128)(2,1)S(1)}, u32[]{:S(2)}, u32[]{:S(2)}) collective-permute-start(bf16[32,12288]{1,0:T(8,128)(2,1)} %collective-permute-done.15.refs_7_), channel_id=1, source_target_pairs={{0,1},{1,0},{2,3},{3,2},{4,5},{5,4},{6,7},{7,6},{8,9},{9,8},{10,11... | collective-permute-start | bytes 2359304 | tf_op jit(solution)/shard_map/ppermute | solution.py:34
  89.4 0.1 pad_add_fusion
  89.5 7.6 %solve.1 = (bf16[256,128]{1,0:T(8,128)(2,1)S(1)}, bf16[256,128]{1,0:T(8,128)(2,1)S(1)}) custom-call(s32[32]{0:T(128)S(1)} %get-tuple-element.27.from_ref, s32[32]{0:T(128)S(1)} %get-tuple-element.28.to_ref, bf16[256,128]{1,0:T(8,128)(2,1)S(1)} %constant_dynamic-update-slice_fusion.own_ref, bf16[256,128]{1,0:T(8,128)(2,1)S(1)} %collective-permute-done.9.other_ref, ...), custom_call_target="tpu_custom_call" | custom-call | tf_op jit(solution)/shard_map/solve/pallas_call | solution.py:141
  97.2 2.8 %copy-done.1 = bf16[24576,128]{1,0:T(8,128)(2,1)S(1)} copy-done((bf16[24576,128]{1,0:T(8,128)(2,1)S(1)}, bf16[24576,128]{1,0:T(8,128)(2,1)}, u32[]{:S(2)}) %copy-start.1) | copy-done | bytes 6291480
  99.9 0.7 copy-done.5
  100.6 13.7 %update.1 = bf16[24576,128]{1,0:T(8,128)(2,1)} custom-call(s32[12]{0:T(128)S(1)} %copy-done.5, s32[3072]{0:T(1024)S(1)} %get-tuple-element.11.lst_ref, s32[256]{0:T(256)S(1)} %copy-done.3, s32[1]{0:T(128)} %bitcast.first_ref, bf16[24576,128]{1,0:T(8,128)(2,1)S(1)} %copy-done.1, bf16[256,128]{1,0:T(8,128)(2,1)S(1)} %get-tuple-element.13.refs_1_, ...), custom_call_target="tpu_custom_call" | custom-call | tf_op jit(solution)/shard_map/update/pallas_call | solution.py:206
  (47 shorter events, 0.3 us)
Async XLA Ops:
  0.0 20.7 %copy-start.2 = (bf16[8,24576]{1,0:T(8,128)(2,1)S(1)}, bf16[8,24576]{1,0:T(8,128)(2,1)}, u32[]{:S(2)}) copy-start(bf16[8,24576]{1,0:T(8,128)(2,1)} %top_ref.1) | copy-start | bytes 1179652
  0.0 20.7 %copy-start.3 = (s32[256]{0:T(256)S(1)}, s32[256]{0:T(256)}, u32[]{:S(2)}) copy-start(s32[256]{0:T(256)} %piv_ref.3) | copy-start | bytes 3076
  0.0 16.9 %collective-permute-start.11 = (bf16[8,24576]{1,0:T(8,128)(2,1)}, bf16[8,24576]{1,0:T(8,128)(2,1)S(1)}, u32[]{:S(2)}, u32[]{:S(2)}) collective-permute-start(bf16[8,24576]{1,0:T(8,128)(2,1)} %top_ref.1), channel_id=1, source_target_pairs={{0,24},{1,7},{2,26},{3,1},{4,28},{5,3},{6,30},{7,5},{8,0},{9,15},{... | collective-permute-start | bytes 1179656 | tf_op jit(solution)/shard_map/ppermute | solution.py:34
  3.6 12.6 %collective-permute-start.10 = (bf16[8,24576]{1,0:T(8,128)(2,1)}, bf16[8,24576]{1,0:T(8,128)(2,1)S(1)}, u32[]{:S(2)}, u32[]{:S(2)}) collective-permute-start(bf16[8,24576]{1,0:T(8,128)(2,1)} %top_ref.1), channel_id=1, source_target_pairs={{0,8},{1,3},{2,10},{3,5},{4,12},{5,7},{6,14},{7,1},{8,16},{9,11},{... | collective-permute-start | bytes 1179656 | tf_op jit(solution)/shard_map/ppermute | solution.py:34
  3.6 14.1 %collective-permute-start.12 = (bf16[8,24576]{1,0:T(8,128)(2,1)}, bf16[8,24576]{1,0:T(8,128)(2,1)S(1)}, u32[]{:S(2)}, u32[]{:S(2)}) collective-permute-start(bf16[8,24576]{1,0:T(8,128)(2,1)} %top_ref.1), channel_id=1, source_target_pairs={{0,16},{1,5},{2,18},{3,7},{4,20},{5,1},{6,22},{7,3},{8,24},{9,13},... | collective-permute-start | bytes 1179656 | tf_op jit(solution)/shard_map/ppermute | solution.py:34
  18.5 53.4 %collective-permute-start.14 = (bf16[32,24576]{1,0:T(8,128)(2,1)}, bf16[32,24576]{1,0:T(8,128)(2,1)S(1)}, u32[]{:S(2)}, u32[]{:S(2)}) collective-permute-start(bf16[32,24576]{1,0:T(8,128)(2,1)} %constant_dynamic-update-slice_fusion.7.refs_4_), channel_id=1, source_target_pairs={{0,6},{1,25},{2,0},{3,27},{4,2},{5,29},{6,4},{7,31},{8,14},{9,1},{... | collective-permute-start | bytes 4718600 | tf_op jit(solution)/shard_map/ppermute | solution.py:34
  20.7 53.3 %collective-permute-start.13 = (bf16[32,24576]{1,0:T(8,128)(2,1)}, bf16[32,24576]{1,0:T(8,128)(2,1)S(1)}, u32[]{:S(2)}, u32[]{:S(2)}) collective-permute-start(bf16[32,24576]{1,0:T(8,128)(2,1)} %constant_dynamic-update-slice_fusion.7.refs_4_), channel_id=1, source_target_pairs={{0,2},{1,9},{2,4},{3,11},{4,6},{5,13},{6,0},{7,15},{8,10},{9,17},{... | collective-permute-start | bytes 4718600 | tf_op jit(solution)/shard_map/ppermute | solution.py:34
  20.7 2.8 %copy-start = (bf16[24576,128]{1,0:T(8,128)(2,1)S(1)}, bf16[24576,128]{1,0:T(8,128)(2,1)}, u32[]{:S(2)}) copy-start(bf16[24576,128]{1,0:T(8,128)(2,1)} %refs_0_.1) | copy-start | bytes 18874372
  29.0 45.9 %copy-start.4 = (s32[12]{0:T(128)}, s32[12]{0:T(128)S(1)}, u32[]{:S(2)}) copy-start(s32[12]{0:T(128)S(1)} %get-tuple-element.10.cnt_ref) | copy-start | bytes 148
  29.0 4.4 %collective-permute-start = (bf16[528,128]{1,0:T(8,128)(2,1)S(1)}, bf16[528,128]{1,0:T(8,128)(2,1)S(1)}, u32[]{:S(2)}, u32[]{:S(2)}) collective-permute-start(bf16[528,128]{1,0:T(8,128)(2,1)S(1)} %get-tuple-element.12), channel_id=1, source_target_pairs={{0,32},{32,0},{64,96},{96,64},{128,160},{160,128},{192,224},{224,1... | collective-permute-start | bytes 405512 | tf_op jit(solution)/shard_map/ppermute | solution.py:248
  33.5 7.2 %collective-permute-start.1 = (bf16[528,128]{1,0:T(8,128)(2,1)S(1)}, bf16[528,128]{1,0:T(8,128)(2,1)S(1)}, u32[]{:S(2)}, u32[]{:S(2)}) collective-permute-start(bf16[528,128]{1,0:T(8,128)(2,1)S(1)} %add.128), channel_id=1, source_target_pairs={{0,64},{32,96},{64,0},{96,32},{128,192},{160,224},{192,128},{224,1... | collective-permute-start | bytes 405512 | tf_op jit(solution)/shard_map/ppermute | solution.py:248
  40.8 8.5 %collective-permute-start.2 = (bf16[528,128]{1,0:T(8,128)(2,1)S(1)}, bf16[528,128]{1,0:T(8,128)(2,1)S(1)}, u32[]{:S(2)}, u32[]{:S(2)}) collective-permute-start(bf16[528,128]{1,0:T(8,128)(2,1)S(1)} %add.129), channel_id=1, source_target_pairs={{0,128},{32,160},{64,192},{96,224},{128,0},{160,32},{192,64},{224,... | collective-permute-start | bytes 405512 | tf_op jit(solution)/shard_map/ppermute | solution.py:248
  49.3 15.3 %copy-start.6 = (bf16[528,128]{1,0:T(8,128)(2,1)}, bf16[528,128]{1,0:T(8,128)(2,1)S(1)}, u32[]{:S(2)}) copy-start(bf16[528,128]{1,0:T(8,128)(2,1)S(1)} %add.130) | copy-start | bytes 405508
  49.4 7.6 %collective-permute-start.5 = (bf16[16,128]{1,0:T(8,128)(2,1)S(1)}, bf16[16,128]{1,0:T(8,128)(2,1)S(1)}, u32[]{:S(2)}, u32[]{:S(2)}) collective-permute-start(bf16[16,128]{1,0:T(8,128)(2,1)S(1)} %get-tuple-element.20), channel_id=1, source_target_pairs={{0,16},{1,17},{2,18},{3,19},{4,20},{5,21},{6,22},{7,23},{8,24},{9,... | collective-permute-start | bytes 12296 | tf_op jit(solution)/shard_map/ppermute | solution.py:34
  55.4 2.5 %collective-permute-start.4 = (bf16[16,128]{1,0:T(8,128)(2,1)S(1)}, bf16[16,128]{1,0:T(8,128)(2,1)S(1)}, u32[]{:S(2)}, u32[]{:S(2)}) collective-permute-start(bf16[16,128]{1,0:T(8,128)(2,1)S(1)} %get-tuple-element.20), channel_id=1, source_target_pairs={{0,24},{1,25},{2,26},{3,27},{4,28},{5,29},{6,30},{7,31},{8,0},{9,1... | collective-permute-start | bytes 12296 | tf_op jit(solution)/shard_map/ppermute | solution.py:34
  56.6 3.7 %collective-permute-start.3 = (bf16[16,128]{1,0:T(8,128)(2,1)S(1)}, bf16[16,128]{1,0:T(8,128)(2,1)S(1)}, u32[]{:S(2)}, u32[]{:S(2)}) collective-permute-start(bf16[16,128]{1,0:T(8,128)(2,1)S(1)} %get-tuple-element.20), channel_id=1, source_target_pairs={{0,8},{1,9},{2,10},{3,11},{4,12},{5,13},{6,14},{7,15},{8,16},{9,17... | collective-permute-start | bytes 12296 | tf_op jit(solution)/shard_map/ppermute | solution.py:34
  60.2 4.4 %collective-permute-start.8 = (bf16[64,128]{1,0:T(8,128)(2,1)S(1)}, bf16[64,128]{1,0:T(8,128)(2,1)S(1)}, u32[]{:S(2)}, u32[]{:S(2)}) collective-permute-start(bf16[64,128]{1,0:T(8,128)(2,1)S(1)} %pad_maximum_fusion), channel_id=1, source_target_pairs={{0,4},{1,5},{2,6},{3,7},{4,0},{5,1},{6,2},{7,3},{8,12},{9,13},{10,... | collective-permute-start | bytes 49160 | tf_op jit(solution)/shard_map/ppermute | solution.py:34
  60.2 4.4 %collective-permute-start.7 = (bf16[64,128]{1,0:T(8,128)(2,1)S(1)}, bf16[64,128]{1,0:T(8,128)(2,1)S(1)}, u32[]{:S(2)}, u32[]{:S(2)}) collective-permute-start(bf16[64,128]{1,0:T(8,128)(2,1)S(1)} %pad_maximum_fusion), channel_id=1, source_target_pairs={{0,6},{1,7},{2,0},{3,1},{4,2},{5,3},{6,4},{7,5},{8,14},{9,15},{10,... | collective-permute-start | bytes 49160 | tf_op jit(solution)/shard_map/ppermute | solution.py:34
  60.2 4.4 %collective-permute-start.6 = (bf16[64,128]{1,0:T(8,128)(2,1)S(1)}, bf16[64,128]{1,0:T(8,128)(2,1)S(1)}, u32[]{:S(2)}, u32[]{:S(2)}) collective-permute-start(bf16[64,128]{1,0:T(8,128)(2,1)S(1)} %pad_maximum_fusion), channel_id=1, source_target_pairs={{0,2},{1,3},{2,4},{3,5},{4,6},{5,7},{6,0},{7,1},{8,10},{9,11},{10,... | collective-permute-start | bytes 49160 | tf_op jit(solution)/shard_map/ppermute | solution.py:34
  64.7 11.7 %copy-start.8 = (s32[4]{0:T(128)S(1)}, s32[4]{0:T(128)}, u32[]{:S(2)}) copy-start(s32[4]{0:T(128)} %constant.97.clone) | copy-start | bytes 52
  64.7 11.3 %collective-permute-start.9 = (bf16[256,128]{1,0:T(8,128)(2,1)S(1)}, bf16[256,128]{1,0:T(8,128)(2,1)S(1)}, u32[]{:S(2)}, u32[]{:S(2)}) collective-permute-start(bf16[256,128]{1,0:T(8,128)(2,1)S(1)} %constant_dynamic-update-slice_fusion.own_ref), channel_id=1, source_target_pairs={{0,1},{1,0},{2,3},{3,2},{4,5},{5,4},{6,7},{7,6},{8,9},{9,8},{10,11... | collective-permute-start | bytes 196616 | tf_op jit(solution)/shard_map/ppermute | solution.py:34
  71.9 17.6 %copy-start.7 = (bf16[528,128]{1,0:T(8,128)(2,1)S(1)}, bf16[528,128]{1,0:T(8,128)(2,1)}, u32[]{:S(2)}) copy-start(bf16[528,128]{1,0:T(8,128)(2,1)} %copy-done.6) | copy-start | bytes 405508
  72.9 11.5 %collective-permute-start.16 = (bf16[32,12288]{1,0:T(8,128)(2,1)}, bf16[32,12288]{1,0:T(8,128)(2,1)}, u32[]{:S(2)}, u32[]{:S(2)}) collective-permute-start(bf16[32,12288]{1,0:T(8,128)(2,1)} %slice.24), channel_id=1, source_target_pairs={{0,6},{1,25},{2,0},{3,27},{4,2},{5,29},{6,4},{7,31},{8,14},{9,1},{... | collective-permute-start | bytes 2359304 | tf_op jit(solution)/shard_map/ppermute | solution.py:34
  74.9 12.7 %collective-permute-start.15 = (bf16[32,12288]{1,0:T(8,128)(2,1)}, bf16[32,12288]{1,0:T(8,128)(2,1)}, u32[]{:S(2)}, u32[]{:S(2)}) collective-permute-start(bf16[32,12288]{1,0:T(8,128)(2,1)} %slice.23), channel_id=1, source_target_pairs={{0,2},{1,9},{2,4},{3,11},{4,6},{5,13},{6,0},{7,15},{8,10},{9,17},{... | collective-permute-start | bytes 2359304 | tf_op jit(solution)/shard_map/ppermute | solution.py:34
  75.3 21.8 %collective-permute-start.17 = (bf16[32,24576]{1,0:T(8,128)(2,1)}, bf16[32,24576]{1,0:T(8,128)(2,1)}, u32[]{:S(2)}, u32[]{:S(2)}) collective-permute-start(bf16[32,24576]{1,0:T(8,128)(2,1)} %constant_dynamic-update-slice_fusion.7.refs_4_), channel_id=1, source_target_pairs={{0,1},{1,0},{2,3},{3,2},{4,5},{5,4},{6,7},{7,6},{8,9},{9,8},{10,11... | collective-permute-start | bytes 4718600 | tf_op jit(solution)/shard_map/ppermute | solution.py:34
  75.9 21.2 %collective-permute-start.19 = (bf16[32,24576]{1,0:T(8,128)(2,1)S(1)}, bf16[32,24576]{1,0:T(8,128)(2,1)}, u32[]{:S(2)}, u32[]{:S(2)}) collective-permute-start(bf16[32,24576]{1,0:T(8,128)(2,1)S(1)} %collective-permute-done.14.refs_6_), channel_id=1, source_target_pairs={{0,1},{1,0},{2,3},{3,2},{4,5},{5,4},{6,7},{7,6},{8,9},{9,8},{10,11... | collective-permute-start | bytes 4718600 | tf_op jit(solution)/shard_map/ppermute | solution.py:34
  76.0 21.2 %collective-permute-start.18 = (bf16[32,24576]{1,0:T(8,128)(2,1)S(1)}, bf16[32,24576]{1,0:T(8,128)(2,1)}, u32[]{:S(2)}, u32[]{:S(2)}) collective-permute-start(bf16[32,24576]{1,0:T(8,128)(2,1)S(1)} %collective-permute-done.13.refs_5_), channel_id=1, source_target_pairs={{0,1},{1,0},{2,3},{3,2},{4,5},{5,4},{6,7},{7,6},{8,9},{9,8},{10,11... | collective-permute-start | bytes 4718600 | tf_op jit(solution)/shard_map/ppermute | solution.py:34
  84.3 12.8 %collective-permute-start.21 = (bf16[32,12288]{1,0:T(8,128)(2,1)}, bf16[32,12288]{1,0:T(8,128)(2,1)S(1)}, u32[]{:S(2)}, u32[]{:S(2)}) collective-permute-start(bf16[32,12288]{1,0:T(8,128)(2,1)} %collective-permute-done.16.refs_8_), channel_id=1, source_target_pairs={{0,1},{1,0},{2,3},{3,2},{4,5},{5,4},{6,7},{7,6},{8,9},{9,8},{10,11... | collective-permute-start | bytes 2359304 | tf_op jit(solution)/shard_map/ppermute | solution.py:34
  87.6 9.5 %collective-permute-start.20 = (bf16[32,12288]{1,0:T(8,128)(2,1)}, bf16[32,12288]{1,0:T(8,128)(2,1)S(1)}, u32[]{:S(2)}, u32[]{:S(2)}) collective-permute-start(bf16[32,12288]{1,0:T(8,128)(2,1)} %collective-permute-done.15.refs_7_), channel_id=1, source_target_pairs={{0,1},{1,0},{2,3},{3,2},{4,5},{5,4},{6,7},{7,6},{8,9},{9,8},{10,11... | collective-permute-start | bytes 2359304 | tf_op jit(solution)/shard_map/ppermute | solution.py:34
  97.1 2.8 %copy-start.1 = (bf16[24576,128]{1,0:T(8,128)(2,1)S(1)}, bf16[24576,128]{1,0:T(8,128)(2,1)}, u32[]{:S(2)}) copy-start(bf16[24576,128]{1,0:T(8,128)(2,1)} %refs_0_.1) | copy-start | bytes 18874372
  99.9 0.7 copy-start.5

commit v2 on v0

v2 whole, which is shorter than its diff:
```python
import functools

import jax
import jax.numpy as jnp
from jax import lax
from jax.experimental import pallas as pl
from jax.experimental.pallas import tpu as pltpu
from jax.sharding import PartitionSpec as P

NX = 4
NY = 4
OFFSETS = (0, -1, 1, 2)
NBLK = 12
UPD_LIMIT = 16 << 20
SMEM = pl.BlockSpec(memory_space=pltpu.SMEM)
VMEM = pl.BlockSpec(memory_space=pltpu.VMEM)
HIGHEST = lax.Precision.HIGHEST


def place(x, y, c):
    return ((x % NX) * NY + (y % NY)) * 2 + c


def hop(dx, dy, turn):
    pairs = []
    for x in range(NX):
        for y in range(NY):
            for c in range(2):
                a, b = (dy, dx) if turn and c == 1 else (dx, dy)
                pairs.append((place(x, y, c), place(x + a, y + b, c)))
    return pairs


CORES = [(p, p ^ 1) for p in range(NX * NY * 2)]


def send(block, pairs):
    return lax.ppermute(block, "pcol", pairs)


def pick_kernel(blk, piv_ref, first_ref, trailing_ref, out_ref, copy_ref, cnt_ref, lst_ref, own_ref, rows_ref, sem):
    width = piv_ref.shape[0]
    rows = trailing_ref.shape[0]
    first = first_ref[0]
    copy = pltpu.make_async_copy(trailing_ref, copy_ref, sem)
    copy.start()
    for b in range(cnt_ref.shape[0]):
        cnt_ref[b] = 0

    def filt(i, n):
        loc = piv_ref[i] - first
        own_ref[n] = i
        return n + ((loc >= 0) & (loc < rows)).astype(jnp.int32)

    n = lax.fori_loop(0, width, filt, 0, unroll=8)

    def bucket(k, carry):
        i = own_ref[k]
        b = lax.div(piv_ref[i] - first, blk)
        m = cnt_ref[b]
        lst_ref[b * width + m] = i
        cnt_ref[b] = m + 1
        return carry

    lax.fori_loop(0, n, bucket, 0)
    rows_ref[...] = jnp.zeros_like(rows_ref)
    sub = lax.broadcasted_iota(jnp.int32, (16, 128), 0)
    copy.wait()

    def extract(k, carry):
        i = own_ref[k]
        loc = piv_ref[i] - first
        base = pl.multiple_of(loc & ~15, 16)
        tile = copy_ref[pl.ds(base, 16), :].astype(jnp.float32)
        row = jnp.sum(jnp.where(sub == (loc & 15), tile, 0.0), axis=0, keepdims=True)
        rows_ref[pl.ds(i, 1), :] = row
        return carry

    lax.fori_loop(0, n, extract, 0)
    out_ref[:width, :] = rows_ref[...].astype(jnp.bfloat16)
    keep = jnp.where(first == 0, 1.0, 0.0)
    out_ref[width:, :] = (copy_ref[:width, :].astype(jnp.float32) * keep).astype(jnp.bfloat16)


def pick(trailing, pivots, first, blk):
    rows, cols = trailing.shape
    width = pivots.shape[0]
    nblk = rows // blk
    return pl.pallas_call(
        functools.partial(pick_kernel, blk),
        in_specs=[SMEM, SMEM, pl.BlockSpec(memory_space=pltpu.HBM)],
        out_specs=[VMEM, VMEM, SMEM, SMEM],
        out_shape=[
            jax.ShapeDtypeStruct((2 * width, cols), jnp.bfloat16),
            jax.ShapeDtypeStruct((rows, cols), jnp.bfloat16),
            jax.ShapeDtypeStruct((nblk,), jnp.int32),
            jax.ShapeDtypeStruct((nblk * width,), jnp.int32),
        ],
        scratch_shapes=[
            pltpu.SMEM((width + 8,), jnp.int32),
            pltpu.VMEM((width, cols), jnp.float32),
            pltpu.SemaphoreType.DMA,
        ],
        compiler_params=pltpu.CompilerParams(vmem_limit_bytes=12 << 20),
        name="pick",
    )(pivots, first, pltpu.with_memory_space_constraint(trailing, pltpu.HBM))


def dot(a, b):
    return lax.dot_general(
        a, b, (((1,), (0,)), ((), ())), precision=HIGHEST, preferred_element_type=jnp.float32
    )


def dot_exact(a, b):
    n = b.shape[1]
    hi = b.astype(jnp.bfloat16)
    rest = b - hi.astype(jnp.float32)
    mid = rest.astype(jnp.bfloat16)
    low = (rest - mid.astype(jnp.float32)).astype(jnp.bfloat16)
    r = lax.dot_general(
        a, jnp.concatenate([hi, mid, low], axis=1), (((1,), (0,)), ((), ())),
        preferred_element_type=jnp.float32,
    )
    return r[:, 2 * n :] + r[:, n : 2 * n] + r[:, :n]


def unit_inverse(strict):
    n = strict.shape[0]
    r = lax.broadcasted_iota(jnp.int32, (n, n), 0)
    c = lax.broadcasted_iota(jnp.int32, (n, n), 1)
    d = jnp.where((r >> 4) == (c >> 4), strict, 0.0)
    x = jnp.where(r == c, 1.0, 0.0) - d
    for step in range(3):
        d = dot_exact(d.astype(jnp.bfloat16), d) if step == 0 else dot(d, d)
        x = x + dot(x, d)
    for lg in (4, 5, 6):
        inside = ((r >> (lg + 1)) == (c >> (lg + 1))) & ((r >> lg) != (c >> lg))
        part = jnp.where(inside, strict, 0.0).astype(jnp.bfloat16)
        x = x - dot(x, dot_exact(part, x))
    return x


def solve_kernel(me_ref, own_ref, other_ref, top_ref, nat_ref, perm_ref, a_ref, u_ref):
    n = nat_ref.shape[0]
    h = n // 2
    me = me_ref[0]
    mx, my, mc = me >> 3, (me >> 1) & 3, me & 1

    def at(x, y, c):
        p = (((x & 3) << 2) + (y & 3)) * 2 + c
        return pl.ds(pl.multiple_of(p * 8, 8), 8)

    blocks = [(k, outer, inner) for k in range(2) for outer in OFFSETS for inner in OFFSETS]
    for b, (k, outer, inner) in enumerate(blocks):
        src = other_ref if k else own_ref
        t = (b % 16) * 16
        piece = src[t : t + 16, :].astype(jnp.float32)
        to = at(mx + inner, my + outer, mc ^ k)
        a_ref[to, :h] = piece[:8]
        a_ref[to, h:] = piece[8:]
    r = lax.broadcasted_iota(jnp.int32, (h, h), 0)
    c = lax.broadcasted_iota(jnp.int32, (h, h), 1)
    s11 = jnp.where(r > c, a_ref[:h, :h].T, 0.0)
    s22 = jnp.where(r > c, a_ref[h:, h:].T, 0.0)
    s21 = a_ref[:h, h:].T
    x1 = unit_inverse(s11)
    x2 = unit_inverse(s22)
    u1 = dot(x1, top_ref[:h, :].astype(jnp.float32))
    u2 = dot(x2, top_ref[h:, :].astype(jnp.float32) - dot_exact(s21.astype(jnp.bfloat16), u1))
    u = jnp.concatenate([u1, u2], axis=0).astype(jnp.bfloat16)
    nat_ref[...] = u
    u_ref[...] = u.astype(jnp.float32)
    for b, (k, outer, inner) in enumerate(blocks):
        core = mc ^ k
        dx = jnp.where(core == 0, inner, outer)
        dy = jnp.where(core == 0, outer, inner)
        a_ref[8 * b : 8 * b + 8, :h] = u_ref[at(mx + dx, my + dy, core), :]
    perm_ref[...] = a_ref[:, :h].astype(jnp.bfloat16)


def solve(me, own, other, top):
    n, cols = top.shape
    return pl.pallas_call(
        solve_kernel,
        in_specs=[SMEM, VMEM, VMEM, VMEM],
        out_specs=[VMEM, VMEM],
        out_shape=[jax.ShapeDtypeStruct((n, cols), jnp.bfloat16)] * 2,
        scratch_shapes=[pltpu.VMEM((n, n), jnp.float32), pltpu.VMEM((n, cols), jnp.float32)],
        compiler_params=pltpu.CompilerParams(vmem_limit_bytes=12 << 20),
        name="solve",
    )(me, own, other, top)


def update_kernel(nblk, cnt_ref, lst_ref, piv_ref, first_ref, tr_ref, u_ref, nat_ref, disp_ref, *refs):
    parts = refs[:10]
    out_ref, acc_ref, drow_ref = refs[10:]
    blk = out_ref.shape[0]
    width = nat_ref.shape[0]
    b = pl.program_id(0)
    first = first_ref[0]

    @pl.when(b == 0)
    def _():
        drow_ref[...] = disp_ref[...].astype(jnp.float32)

    def cols(start):
        return pl.ds(pl.multiple_of(start, 128), blk)

    def compute(s, late):
        here = cols(b * blk)
        there = cols(b * blk - (nblk // 2) * blk) if late else here
        pieces = []
        for s in (parts[:5], parts[5:]):
            pieces += [s[0][:, here], s[1][:, here], s[2][:, here], s[3 + late][:, there]]
        acc_ref[...] = lax.dot_general(
            jnp.concatenate(pieces, axis=0), u_ref[...], (((0,), (0,)), ((), ())),
            preferred_element_type=jnp.float32,
        )

    @pl.when(b < nblk // 2)
    def _():
        compute(parts, 0)

    @pl.when(b >= nblk // 2)
    def _():
        compute(parts, 1)

    tr = tr_ref[pl.ds(pl.multiple_of(b * blk, 16), blk), :].astype(jnp.float32)
    out_ref[...] = (tr - acc_ref[...]).astype(jnp.bfloat16)
    sub = lax.broadcasted_iota(jnp.int32, (16, 128), 0)

    def fix(k, carry):
        i = lst_ref[b * width + k]
        loc = piv_ref[i] - first - b * blk
        at = pl.ds(pl.multiple_of(loc & ~15, 16), 16)
        new = drow_ref[pl.ds(i, 1), :] - acc_ref[at, :]
        old = out_ref[at, :].astype(jnp.float32)
        out_ref[at, :] = jnp.where(sub == (loc & 15), new, old).astype(jnp.bfloat16)
        return carry

    lax.fori_loop(0, cnt_ref[b], fix, 0)

    @pl.when((b == 0) & (first == 0))
    def _():
        out_ref[:width, :] = nat_ref[...]


def update(cnt, lst, pivots, first, trailing, u, nat, disp, own, other, blk):
    rows, cols = trailing.shape
    width = nat.shape[0]
    nblk = rows // blk
    return pl.pallas_call(
        functools.partial(update_kernel, nblk),
        grid=(nblk,),
        in_specs=[SMEM] * 4 + [VMEM] * 14,
        out_specs=pl.BlockSpec((blk, cols), lambda b: (b, 0)),
        scratch_shapes=[
            pltpu.VMEM((blk, cols), jnp.float32),
            pltpu.VMEM((width, cols), jnp.float32),
        ],
        out_shape=jax.ShapeDtypeStruct((rows, cols), jnp.bfloat16),
        compiler_params=pltpu.CompilerParams(vmem_limit_bytes=UPD_LIMIT),
        name="update",
    )(cnt, lst, pivots, first, trailing, u, nat, disp, *own, *other)


def after(x, *deps):
    return lax.optimization_barrier((x,) + deps)[0]


def body(trailing, panel_t, pivots):
    rows = trailing.shape[0]
    width = pivots.shape[0]
    blk = rows // NBLK
    half = rows // 2
    nz = lax.axis_size("prow")
    zi = lax.axis_index("prow")
    first = (zi * rows).astype(jnp.int32).reshape(1)
    me = lax.axis_index("pcol")

    def around(x, hops):
        return jnp.concatenate([x] + [send(x, h) for h in hops], axis=0)

    def zsend(x, pairs):
        return lax.ppermute(x, "prow", pairs)

    def shift(k):
        return [(i, (i + k) % nz) for i in range(nz)]

    hops = [hop(1, 0, True), hop(-1, 0, True), hop(2, 0, True)]
    first_hops = [send(panel_t, h) for h in hops]

    diag = panel_t[:, :width]
    diag = jnp.concatenate([diag[:, :128], diag[:, 128:]], axis=0)
    diag = jnp.where(zi == 0, diag, jnp.zeros_like(diag))

    def spread(x, d):
        return x + zsend(x, [(i, i + d) for i in range(0, nz, 2 * d)])

    diag = spread(diag, 4)
    load, copy, cnt, lst = pick(trailing, pivots, first, blk)
    diag = spread(diag, 2)

    diag, load, p, m, q = lax.optimization_barrier((diag, load, *first_hops))
    block = jnp.concatenate([panel_t, p, m, q], axis=0)
    up, down = hop(0, 1, True), hop(0, -1, True)
    near, far = send(block, up), send(block, down)

    diag, load = lax.optimization_barrier((diag, load, block))[:2]
    diag = spread(diag, 1)
    a, b = zsend(load, shift(1)), zsend(load, shift(-1))
    diag = around(diag, [hop(1, 0, False), hop(-1, 0, False), hop(2, 0, False)])
    load = jnp.where(load != 0, load, jnp.where(a != 0, a, b))
    load = after(load, diag)
    a, b = zsend(load, shift(3)), zsend(load, shift(-3))
    diag = around(diag, [hop(0, 1, False), hop(0, -1, False), hop(0, 2, False)])
    diag, near, far = lax.optimization_barrier((diag, near, far))
    own = [block, near, far, send(near[:, :half], up), send(far[:, half:], down)]
    diag_other = send(diag, CORES)
    load = jnp.where(load != 0, load, jnp.where(a != 0, a, b))
    top, disp = load[:width], load[width:]
    other = [send(t, CORES) for t in own]
    nat, perm = solve(me.astype(jnp.int32).reshape(1), diag, diag_other, top)
    return update(cnt, lst, pivots, first, copy, perm, nat, disp, own, other, blk)


def solution(mesh):
    return jax.shard_map(
        body,
        mesh=mesh,
        in_specs=(P("prow", "pcol"), P("pcol", "prow"), P()),
        out_specs=P("prow", "pcol"),
        check_vma=False,
    )
```

time: 176 us -> 106 us (0.60); the launches traced: 173 us -> 105 us
  starting transfers between devices: 0.05 us -> 33.2 us
  waiting for transfers between devices: 69.5 us -> 37.8 us
  blocking collectives: 26.2 us -> 0 us
  other arithmetic: 23.7 us -> 1.04 us
  Pallas kernels: 0 us -> 22 us
  between operations: 15 us -> 0.19 us
  local copies, waits for them, and re-layouts: 25.1 us -> 11.2 us
  matrix products: 13 us -> 0 us
    psum x1 -> x0, waiting for transfers between devices: 68.9 us -> none  [body(): moved = lax.psum(picked.astype(jnp.bfloat16), 'prow')]
    ppermute x0 -> x26, waiting for transfers between devices: none -> 37.8 us  [the longest x19 29.3 us: send(): return lax.ppermute(block, 'pcol', pairs)]
    ppermute x0 -> x26, starting transfers between devices: none -> 33.2 us  [the longest x7 17 us: zsend(): return lax.ppermute(x, 'prow', pairs)]
    all_gather x1 -> x0, blocking collectives: 26.2 us -> none  [body(): diag_cols = lax.all_gather(panel_t[:, :width], 'pcol', axis=0, tiled=True)]
    pallas_call x0 -> x3, Pallas kernels: none -> 22 us  [the longest x1 13.1 us: update(): pl.pallas_call(functools.partial(update_kernel, nblk), grid=(nblk,), in_s...]
    another operation x4 -> x0, other arithmetic: 20.7 us -> none  [body(): lax.linalg.triangular_solve(unit, top_rows, left_side=True, lower=True, u...]
    dot_general x1 -> x0, matrix products: 10.7 us -> none  [body(): lax.dot_general(full_panel, urows, (((0,), (0,)), ((), ())), preferred_el...]
    scatter x1 -> x0, local copies, waits for them, and re-layouts: 8.93 us -> none  [body(): swapped = trailing.at[dest].set(moved, mode='drop')]
  transfers between devices with their start and end apart: 2 -> 26, of which waited for: 1 -> 9; matrix products, arithmetic and copies ran while one was open for 21% -> 3% of each run, Pallas kernels for 0% -> 8%
where the time goes in v2:
time: 106 us; the launch traced here: 105 us
  waiting for transfers between devices  37.8 us (36%)
  starting transfers between devices  33.2 us (31%)
  Pallas kernels  22 us (21%)
  local copies, waits for them, and re-layouts  11.2 us (11%)
    ppermute x19, waiting for transfers between devices, send(): return lax.ppermute(block, 'pcol', pairs)  29.3 us
    ppermute x7, starting transfers between devices, zsend(): return lax.ppermute(x, 'prow', pairs)  17 us
    ppermute x19, starting transfers between devices, send(): return lax.ppermute(block, 'pcol', pairs)  16.2 us
    pallas_call x1, Pallas kernels, update(): pl.pallas_call(functools.partial(update_kernel, nblk), grid=(nblk,), in_s...  13.1 us
    unnamed x20, local copies, waits for them, and re-layouts  9.55 us
    ppermute x7, waiting for transfers between devices, zsend(): return lax.ppermute(x, 'prow', pairs)  8.58 us
    pallas_call x1, Pallas kernels, pick(): pl.pallas_call(functools.partial(pick_kernel, blk), in_specs=[SMEM, SMEM,...  4.67 us
    pallas_call x1, Pallas kernels, solve(): pl.pallas_call(solve_kernel, in_specs=[SMEM, VMEM, VMEM, VMEM], out_specs...  4.25 us
  transfers between devices with their start and end apart: 26, of which 9 were waited for; matrix products, arithmetic and copies ran while one was open for 3% of the time, Pallas kernels for 8%

profile of v2, /device:TPU:1, one launch (start us, length us, event | category | flops | bytes accessed | tf_op | source)
XLA Modules:
  0.0 105.5 jit_solution(10922914774801727503)
XLA Ops:
  0.0 0.7 fusion
  0.7 9.6 %collective-permute-start = (bf16[16,128]{1,0:T(8,128)(2,1)S(1)}, bf16[16,128]{1,0:T(8,128)(2,1)S(1)}, u32[]{:S(2)}, u32[]{:S(2)}) collective-permute-start(bf16[16,128]{1,0:T(8,128)(2,1)S(1)} %maximum_select_fusion), channel_id=1, source_target_pairs={{0,128},{1,129},{2,130},{3,131},{4,132},{5,133},{6,134},{7,135},{8... | collective-permute-start | bytes 12296 | tf_op jit(solution)/shard_map/ppermute | solution.py:286
  10.3 1.4 %collective-permute-start.2 = (bf16[8,24576]{1,0:T(8,128)(2,1)}, bf16[8,24576]{1,0:T(8,128)(2,1)S(1)}, u32[]{:S(2)}, u32[]{:S(2)}) collective-permute-start(bf16[8,24576]{1,0:T(8,128)(2,1)} %param.4), channel_id=1, source_target_pairs={{0,8},{1,3},{2,10},{3,5},{4,12},{5,7},{6,14},{7,1},{8,16},{9,11},{... | collective-permute-start | bytes 1179656 | tf_op jit(solution)/shard_map/ppermute | solution.py:38
  11.7 1.5 %collective-permute-start.3 = (bf16[8,24576]{1,0:T(8,128)(2,1)}, bf16[8,24576]{1,0:T(8,128)(2,1)S(1)}, u32[]{:S(2)}, u32[]{:S(2)}) collective-permute-start(bf16[8,24576]{1,0:T(8,128)(2,1)} %param.4), channel_id=1, source_target_pairs={{0,24},{1,7},{2,26},{3,1},{4,28},{5,3},{6,30},{7,5},{8,0},{9,15},{... | collective-permute-start | bytes 1179656 | tf_op jit(solution)/shard_map/ppermute | solution.py:38
  13.3 1.6 %collective-permute-start.4 = (bf16[8,24576]{1,0:T(8,128)(2,1)}, bf16[8,24576]{1,0:T(8,128)(2,1)S(1)}, u32[]{:S(2)}, u32[]{:S(2)}) collective-permute-start(bf16[8,24576]{1,0:T(8,128)(2,1)} %param.4), channel_id=1, source_target_pairs={{0,16},{1,5},{2,18},{3,7},{4,20},{5,1},{6,22},{7,3},{8,24},{9,13},... | collective-permute-start | bytes 1179656 | tf_op jit(solution)/shard_map/ppermute | solution.py:38
  14.8 1.3 %collective-permute-start.1 = (bf16[16,128]{1,0:T(8,128)(2,1)S(1)}, bf16[16,128]{1,0:T(8,128)(2,1)S(1)}, u32[]{:S(2)}, u32[]{:S(2)}) collective-permute-start(bf16[16,128]{1,0:T(8,128)(2,1)S(1)} %add.9), channel_id=1, source_target_pairs={{0,64},{128,192},{1,65},{129,193},{2,66},{130,194},{3,67},{131,195... | collective-permute-start | bytes 12296 | tf_op jit(solution)/shard_map/ppermute | solution.py:286
  16.1 1.8 %constant_dynamic-update-slice_fusion.3 = bf16[32,24576]{1,0:T(8,128)(2,1)} fusion(bf16[8,24576]{1,0:T(8,128)(2,1)} %param.4), kind=kLoop, calls=%fused_computation.7 | loop fusion | bytes 786432
  17.9 0.7 copy-done.2
  18.6 4.7 %pick.1 = (bf16[512,128]{1,0:T(8,128)(2,1)S(1)}, bf16[24576,128]{1,0:T(8,128)(2,1)S(1)}, s32[12]{0:T(128)S(1)}, s32[3072]{0:T(1024)S(1)}) custom-call(s32[256]{0:T(256)S(1)} %copy-done.2, s32[1]{0:T(128)} %bitcast.first_ref, bf16[24576,128]{1,0:T(8,128)(2,1)} %trailing_ref.1), custom_call_target="tpu_custom_call" | custom-call | tf_op jit(solution)/shard_map/pick/pallas_call | solution.py:89
  23.3 0.0 copy-start
  23.3 2.7 %copy-done = bf16[24576,128]{1,0:T(8,128)(2,1)} copy-done((bf16[24576,128]{1,0:T(8,128)(2,1)}, bf16[24576,128]{1,0:T(8,128)(2,1)S(1)}, u32[]{:S(2)}) %copy-start) | copy-done | bytes 6291480
  26.0 0.8 constant_dynamic-update-slice_fusion.2
  26.8 0.8 constant_dynamic-update-slice_fusion.1
  27.6 0.8 constant_dynamic-update-slice_fusion.refs_0_
  28.3 2.5 %collective-permute-start.13 = (bf16[32,24576]{1,0:T(8,128)(2,1)}, bf16[32,24576]{1,0:T(8,128)(2,1)S(1)}, u32[]{:S(2)}, u32[]{:S(2)}) collective-permute-start(bf16[32,24576]{1,0:T(8,128)(2,1)} %constant_dynamic-update-slice_fusion.refs_0_), channel_id=1, source_target_pairs={{0,6},{1,25},{2,0},{3,27},{4,2},{5,29},{6,4},{7,31},{8,14},{9,1},{... | collective-permute-start | bytes 4718600 | tf_op jit(solution)/shard_map/ppermute | solution.py:38
  30.8 1.3 %collective-permute-start.5 = (bf16[16,128]{1,0:T(8,128)(2,1)S(1)}, bf16[16,128]{1,0:T(8,128)(2,1)S(1)}, u32[]{:S(2)}, u32[]{:S(2)}) collective-permute-start(bf16[16,128]{1,0:T(8,128)(2,1)S(1)} %add.10), channel_id=1, source_target_pairs={{0,32},{64,96},{128,160},{192,224},{1,33},{65,97},{129,161},{193,2... | collective-permute-start | bytes 12296 | tf_op jit(solution)/shard_map/ppermute | solution.py:286
  32.1 0.7 collective-permute-done.5
  32.9 1.7 %collective-permute-start.8 = (bf16[16,128]{1,0:T(8,128)(2,1)S(1)}, bf16[16,128]{1,0:T(8,128)(2,1)S(1)}, u32[]{:S(2)}, u32[]{:S(2)}) collective-permute-start(bf16[16,128]{1,0:T(8,128)(2,1)S(1)} %get-tuple-element.40), channel_id=1, source_target_pairs={{0,16},{1,17},{2,18},{3,19},{4,20},{5,21},{6,22},{7,23},{8,24},{9,... | collective-permute-start | bytes 12296 | tf_op jit(solution)/shard_map/ppermute | solution.py:38
  34.6 1.0 collective-permute-start.7
  35.6 0.5 collective-permute-start.6
  36.1 14.7 %collective-permute-done.8 = bf16[16,128]{1,0:T(8,128)(2,1)S(1)} collective-permute-done((bf16[16,128]{1,0:T(8,128)(2,1)S(1)}, bf16[16,128]{1,0:T(8,128)(2,1)S(1)}, u32[]{:S(2)}, u32[]{:S(2)}) %collective-permute-start.8) | collective-permute-done | bytes 4128 | tf_op jit(solution)/shard_map/ppermute | solution.py:38
  50.8 1.5 %collective-permute-start.15 = (bf16[512,128]{1,0:T(8,128)(2,1)S(1)}, bf16[512,128]{1,0:T(8,128)(2,1)S(1)}, u32[]{:S(2)}, u32[]{:S(2)}) collective-permute-start(bf16[512,128]{1,0:T(8,128)(2,1)S(1)} %get-tuple-element.33), channel_id=1, source_target_pairs={{0,32},{32,64},{64,96},{96,128},{128,160},{160,192},{192,224},{224... | collective-permute-start | bytes 393224 | tf_op jit(solution)/shard_map/ppermute | solution.py:286
  52.3 0.4 collective-permute-start.9
  52.7 3.4 %collective-permute-done.9 = bf16[64,128]{1,0:T(8,128)(2,1)S(1)} collective-permute-done((bf16[64,128]{1,0:T(8,128)(2,1)S(1)}, bf16[64,128]{1,0:T(8,128)(2,1)S(1)}, u32[]{:S(2)}, u32[]{:S(2)}) %collective-permute-start.9) | collective-permute-done | bytes 16416 | tf_op jit(solution)/shard_map/ppermute | solution.py:38
  56.1 2.6 %collective-permute-done.10 = bf16[64,128]{1,0:T(8,128)(2,1)S(1)} collective-permute-done((bf16[64,128]{1,0:T(8,128)(2,1)S(1)}, bf16[64,128]{1,0:T(8,128)(2,1)S(1)}, u32[]{:S(2)}, u32[]{:S(2)}) %collective-permute-start.10) | collective-permute-done | bytes 16416 | tf_op jit(solution)/shard_map/ppermute | solution.py:38
  58.7 0.2 collective-permute-start.11
  58.9 2.4 %collective-permute-start.18 = (bf16[512,128]{1,0:T(8,128)(2,1)S(1)}, bf16[512,128]{1,0:T(8,128)(2,1)S(1)}, u32[]{:S(2)}, u32[]{:S(2)}) collective-permute-start(bf16[512,128]{1,0:T(8,128)(2,1)S(1)} %compare_select_fusion.3), channel_id=1, source_target_pairs={{0,160},{32,192},{64,224},{96,0},{128,32},{160,64},{192,96},{224,1... | collective-permute-start | bytes 393224 | tf_op jit(solution)/shard_map/ppermute | solution.py:286
  61.3 0.9 collective-permute-start.17
  62.3 0.5 collective-permute-done.11
  62.8 1.3 %collective-permute-start.14 = (bf16[256,128]{1,0:T(8,128)(2,1)S(1)}, bf16[256,128]{1,0:T(8,128)(2,1)S(1)}, u32[]{:S(2)}, u32[]{:S(2)}) collective-permute-start(bf16[256,128]{1,0:T(8,128)(2,1)S(1)} %constant_dynamic-update-slice_fusion.4.own_ref), channel_id=1, source_target_pairs={{0,1},{1,0},{2,3},{3,2},{4,5},{5,4},{6,7},{7,6},{8,9},{9,8},{10,11... | collective-permute-start | bytes 196616 | tf_op jit(solution)/shard_map/ppermute | solution.py:38
  64.1 0.3 collective-permute-start.21
  64.4 0.1 slice.25
  64.4 0.0 copy-start.3
  64.4 0.1 slice.26
  64.5 0.9 collective-permute-start.20
  65.4 5.1 %collective-permute-done.18 = bf16[512,128]{1,0:T(8,128)(2,1)S(1)} collective-permute-done((bf16[512,128]{1,0:T(8,128)(2,1)S(1)}, bf16[512,128]{1,0:T(8,128)(2,1)S(1)}, u32[]{:S(2)}, u32[]{:S(2)}) %collective-permute-start.18) | collective-permute-done | bytes 131104 | tf_op jit(solution)/shard_map/ppermute | solution.py:286
  70.5 2.8 %collective-permute-done.17 = bf16[512,128]{1,0:T(8,128)(2,1)S(1)} collective-permute-done((bf16[512,128]{1,0:T(8,128)(2,1)S(1)}, bf16[512,128]{1,0:T(8,128)(2,1)S(1)}, u32[]{:S(2)}, u32[]{:S(2)}) %collective-permute-start.17) | collective-permute-done | bytes 131104 | tf_op jit(solution)/shard_map/ppermute | solution.py:286
  73.3 0.1 collective-permute-start.22
  73.4 0.4 collective-permute-start.23
  73.8 2.0 %collective-permute-done.20.refs_4_ = bf16[32,12288]{1,0:T(8,128)(2,1)} collective-permute-done((bf16[32,12288]{1,0:T(8,128)(2,1)S(1)}, bf16[32,12288]{1,0:T(8,128)(2,1)}, u32[]{:S(2)}, u32[]{:S(2)}) %collective-permute-start.20) | collective-permute-done | bytes 786464 | tf_op jit(solution)/shard_map/ppermute | solution.py:38
  75.8 1.1 %collective-permute-start.25 = (bf16[32,12288]{1,0:T(8,128)(2,1)}, bf16[32,12288]{1,0:T(8,128)(2,1)}, u32[]{:S(2)}, u32[]{:S(2)}) collective-permute-start(bf16[32,12288]{1,0:T(8,128)(2,1)} %collective-permute-done.20.refs_4_), channel_id=1, source_target_pairs={{0,1},{1,0},{2,3},{3,2},{4,5},{5,4},{6,7},{7,6},{8,9},{9,8},{10,11... | collective-permute-start | bytes 2359304 | tf_op jit(solution)/shard_map/ppermute | solution.py:38
  76.9 6.1 %collective-permute-done.19.refs_3_ = bf16[32,12288]{1,0:T(8,128)(2,1)} collective-permute-done((bf16[32,12288]{1,0:T(8,128)(2,1)S(1)}, bf16[32,12288]{1,0:T(8,128)(2,1)}, u32[]{:S(2)}, u32[]{:S(2)}) %collective-permute-start.19) | collective-permute-done | bytes 786464 | tf_op jit(solution)/shard_map/ppermute | solution.py:38
  82.9 1.3 %collective-permute-start.24 = (bf16[32,12288]{1,0:T(8,128)(2,1)}, bf16[32,12288]{1,0:T(8,128)(2,1)}, u32[]{:S(2)}, u32[]{:S(2)}) collective-permute-start(bf16[32,12288]{1,0:T(8,128)(2,1)} %collective-permute-done.19.refs_3_), channel_id=1, source_target_pairs={{0,1},{1,0},{2,3},{3,2},{4,5},{5,4},{6,7},{7,6},{8,9},{9,8},{10,11... | collective-permute-start | bytes 2359304 | tf_op jit(solution)/shard_map/ppermute | solution.py:38
  84.2 1.0 compare_select_fusion.1
  85.2 4.2 %solve.1 = (bf16[256,128]{1,0:T(8,128)(2,1)S(1)}, bf16[256,128]{1,0:T(8,128)(2,1)S(1)}) custom-call(s32[1]{0:T(128)} %bitcast.1.me_ref, bf16[256,128]{1,0:T(8,128)(2,1)S(1)} %constant_dynamic-update-slice_fusion.4.own_ref, bf16[256,128]{1,0:T(8,128)(2,1)S(1)} %collective-permute-done.14.other_ref, bf16[256,128]{1,0:T(8,128)(2,1)S(1)} %get-tuple-element.44.top_ref), custom_call_target="tpu_custom_call" | custom-call | tf_op jit(solution)/shard_map/solve/pallas_call | solution.py:184
  89.6 0.0 copy-start.1
  89.6 2.8 %copy-done.1 = bf16[24576,128]{1,0:T(8,128)(2,1)S(1)} copy-done((bf16[24576,128]{1,0:T(8,128)(2,1)S(1)}, bf16[24576,128]{1,0:T(8,128)(2,1)}, u32[]{:S(2)}) %copy-start.1) | copy-done | bytes 6291480
  92.3 13.1 %update.1 = bf16[24576,128]{1,0:T(8,128)(2,1)} custom-call(s32[12]{0:T(128)S(1)} %get-tuple-element.22.cnt_ref, s32[3072]{0:T(1024)S(1)} %get-tuple-element.23.lst_ref, s32[256]{0:T(256)S(1)} %copy-done.3, s32[1]{0:T(128)} %bitcast.first_ref, bf16[24576,128]{1,0:T(8,128)(2,1)S(1)} %copy-done.1, bf16[256,128]{1,0:T(8,128)(2,1)S(1)} %get-tuple-element.35.u_ref, ...), custom_call_target="tpu_custom_call" | custom-call | tf_op jit(solution)/shard_map/update/pallas_call | solution.py:253
  (40 shorter events, 0.2 us)
Async XLA Ops:
  0.7 14.1 %collective-permute-start = (bf16[16,128]{1,0:T(8,128)(2,1)S(1)}, bf16[16,128]{1,0:T(8,128)(2,1)S(1)}, u32[]{:S(2)}, u32[]{:S(2)}) collective-permute-start(bf16[16,128]{1,0:T(8,128)(2,1)S(1)} %maximum_select_fusion), channel_id=1, source_target_pairs={{0,128},{1,129},{2,130},{3,131},{4,132},{5,133},{6,134},{7,135},{8... | collective-permute-start | bytes 12296 | tf_op jit(solution)/shard_map/ppermute | solution.py:286
  10.3 15.6 %collective-permute-start.2 = (bf16[8,24576]{1,0:T(8,128)(2,1)}, bf16[8,24576]{1,0:T(8,128)(2,1)S(1)}, u32[]{:S(2)}, u32[]{:S(2)}) collective-permute-start(bf16[8,24576]{1,0:T(8,128)(2,1)} %param.4), channel_id=1, source_target_pairs={{0,8},{1,3},{2,10},{3,5},{4,12},{5,7},{6,14},{7,1},{8,16},{9,11},{... | collective-permute-start | bytes 1179656 | tf_op jit(solution)/shard_map/ppermute | solution.py:38
  11.7 14.3 %collective-permute-start.3 = (bf16[8,24576]{1,0:T(8,128)(2,1)}, bf16[8,24576]{1,0:T(8,128)(2,1)S(1)}, u32[]{:S(2)}, u32[]{:S(2)}) collective-permute-start(bf16[8,24576]{1,0:T(8,128)(2,1)} %param.4), channel_id=1, source_target_pairs={{0,24},{1,7},{2,26},{3,1},{4,28},{5,3},{6,30},{7,5},{8,0},{9,15},{... | collective-permute-start | bytes 1179656 | tf_op jit(solution)/shard_map/ppermute | solution.py:38
  13.3 12.7 %collective-permute-start.4 = (bf16[8,24576]{1,0:T(8,128)(2,1)}, bf16[8,24576]{1,0:T(8,128)(2,1)S(1)}, u32[]{:S(2)}, u32[]{:S(2)}) collective-permute-start(bf16[8,24576]{1,0:T(8,128)(2,1)} %param.4), channel_id=1, source_target_pairs={{0,16},{1,5},{2,18},{3,7},{4,20},{5,1},{6,22},{7,3},{8,24},{9,13},... | collective-permute-start | bytes 1179656 | tf_op jit(solution)/shard_map/ppermute | solution.py:38
  14.8 11.1 %collective-permute-start.1 = (bf16[16,128]{1,0:T(8,128)(2,1)S(1)}, bf16[16,128]{1,0:T(8,128)(2,1)S(1)}, u32[]{:S(2)}, u32[]{:S(2)}) collective-permute-start(bf16[16,128]{1,0:T(8,128)(2,1)S(1)} %add.9), channel_id=1, source_target_pairs={{0,64},{128,192},{1,65},{129,193},{2,66},{130,194},{3,67},{131,195... | collective-permute-start | bytes 12296 | tf_op jit(solution)/shard_map/ppermute | solution.py:286
  17.9 0.7 copy-start.2
  23.3 2.7 %copy-start = (bf16[24576,128]{1,0:T(8,128)(2,1)}, bf16[24576,128]{1,0:T(8,128)(2,1)S(1)}, u32[]{:S(2)}) copy-start(bf16[24576,128]{1,0:T(8,128)(2,1)S(1)} %get-tuple-element.24.tr_ref) | copy-start | bytes 18874372
  28.3 34.4 %collective-permute-start.13 = (bf16[32,24576]{1,0:T(8,128)(2,1)}, bf16[32,24576]{1,0:T(8,128)(2,1)S(1)}, u32[]{:S(2)}, u32[]{:S(2)}) collective-permute-start(bf16[32,24576]{1,0:T(8,128)(2,1)} %constant_dynamic-update-slice_fusion.refs_0_), channel_id=1, source_target_pairs={{0,6},{1,25},{2,0},{3,27},{4,2},{5,29},{6,4},{7,31},{8,14},{9,1},{... | collective-permute-start | bytes 4718600 | tf_op jit(solution)/shard_map/ppermute | solution.py:38
  30.8 32.0 %collective-permute-start.12 = (bf16[32,24576]{1,0:T(8,128)(2,1)}, bf16[32,24576]{1,0:T(8,128)(2,1)S(1)}, u32[]{:S(2)}, u32[]{:S(2)}) collective-permute-start(bf16[32,24576]{1,0:T(8,128)(2,1)} %constant_dynamic-update-slice_fusion.refs_0_), channel_id=1, source_target_pairs={{0,2},{1,9},{2,4},{3,11},{4,6},{5,13},{6,0},{7,15},{8,10},{9,17},{... | collective-permute-start | bytes 4718600 | tf_op jit(solution)/shard_map/ppermute | solution.py:38
  30.8 2.0 %collective-permute-start.5 = (bf16[16,128]{1,0:T(8,128)(2,1)S(1)}, bf16[16,128]{1,0:T(8,128)(2,1)S(1)}, u32[]{:S(2)}, u32[]{:S(2)}) collective-permute-start(bf16[16,128]{1,0:T(8,128)(2,1)S(1)} %add.10), channel_id=1, source_target_pairs={{0,32},{64,96},{128,160},{192,224},{1,33},{65,97},{129,161},{193,2... | collective-permute-start | bytes 12296 | tf_op jit(solution)/shard_map/ppermute | solution.py:286
  32.9 17.9 %collective-permute-start.8 = (bf16[16,128]{1,0:T(8,128)(2,1)S(1)}, bf16[16,128]{1,0:T(8,128)(2,1)S(1)}, u32[]{:S(2)}, u32[]{:S(2)}) collective-permute-start(bf16[16,128]{1,0:T(8,128)(2,1)S(1)} %get-tuple-element.40), channel_id=1, source_target_pairs={{0,16},{1,17},{2,18},{3,19},{4,20},{5,21},{6,22},{7,23},{8,24},{9,... | collective-permute-start | bytes 12296 | tf_op jit(solution)/shard_map/ppermute | solution.py:38
  34.6 16.2 %collective-permute-start.7 = (bf16[16,128]{1,0:T(8,128)(2,1)S(1)}, bf16[16,128]{1,0:T(8,128)(2,1)S(1)}, u32[]{:S(2)}, u32[]{:S(2)}) collective-permute-start(bf16[16,128]{1,0:T(8,128)(2,1)S(1)} %get-tuple-element.40), channel_id=1, source_target_pairs={{0,24},{1,25},{2,26},{3,27},{4,28},{5,29},{6,30},{7,31},{8,0},{9,1... | collective-permute-start | bytes 12296 | tf_op jit(solution)/shard_map/ppermute | solution.py:38
  35.6 16.7 %collective-permute-start.6 = (bf16[16,128]{1,0:T(8,128)(2,1)S(1)}, bf16[16,128]{1,0:T(8,128)(2,1)S(1)}, u32[]{:S(2)}, u32[]{:S(2)}) collective-permute-start(bf16[16,128]{1,0:T(8,128)(2,1)S(1)} %get-tuple-element.40), channel_id=1, source_target_pairs={{0,8},{1,9},{2,10},{3,11},{4,12},{5,13},{6,14},{7,15},{8,16},{9,17... | collective-permute-start | bytes 12296 | tf_op jit(solution)/shard_map/ppermute | solution.py:38
  50.8 8.1 %collective-permute-start.16 = (bf16[512,128]{1,0:T(8,128)(2,1)S(1)}, bf16[512,128]{1,0:T(8,128)(2,1)S(1)}, u32[]{:S(2)}, u32[]{:S(2)}) collective-permute-start(bf16[512,128]{1,0:T(8,128)(2,1)S(1)} %get-tuple-element.33), channel_id=1, source_target_pairs={{0,224},{32,0},{64,32},{96,64},{128,96},{160,128},{192,160},{224,1... | collective-permute-start | bytes 393224 | tf_op jit(solution)/shard_map/ppermute | solution.py:286
  50.8 8.1 %collective-permute-start.15 = (bf16[512,128]{1,0:T(8,128)(2,1)S(1)}, bf16[512,128]{1,0:T(8,128)(2,1)S(1)}, u32[]{:S(2)}, u32[]{:S(2)}) collective-permute-start(bf16[512,128]{1,0:T(8,128)(2,1)S(1)} %get-tuple-element.33), channel_id=1, source_target_pairs={{0,32},{32,64},{64,96},{96,128},{128,160},{160,192},{192,224},{224... | collective-permute-start | bytes 393224 | tf_op jit(solution)/shard_map/ppermute | solution.py:286
  52.3 3.8 %collective-permute-start.9 = (bf16[64,128]{1,0:T(8,128)(2,1)S(1)}, bf16[64,128]{1,0:T(8,128)(2,1)S(1)}, u32[]{:S(2)}, u32[]{:S(2)}) collective-permute-start(bf16[64,128]{1,0:T(8,128)(2,1)S(1)} %pad_maximum_fusion), channel_id=1, source_target_pairs={{0,2},{1,3},{2,4},{3,5},{4,6},{5,7},{6,0},{7,1},{8,10},{9,11},{10,... | collective-permute-start | bytes 49160 | tf_op jit(solution)/shard_map/ppermute | solution.py:38
  56.1 2.6 %collective-permute-start.10 = (bf16[64,128]{1,0:T(8,128)(2,1)S(1)}, bf16[64,128]{1,0:T(8,128)(2,1)S(1)}, u32[]{:S(2)}, u32[]{:S(2)}) collective-permute-start(bf16[64,128]{1,0:T(8,128)(2,1)S(1)} %pad_maximum_fusion), channel_id=1, source_target_pairs={{0,6},{1,7},{2,0},{3,1},{4,2},{5,3},{6,4},{7,5},{8,14},{9,15},{10,... | collective-permute-start | bytes 49160 | tf_op jit(solution)/shard_map/ppermute | solution.py:38
  58.7 4.1 %collective-permute-start.11 = (bf16[64,128]{1,0:T(8,128)(2,1)S(1)}, bf16[64,128]{1,0:T(8,128)(2,1)S(1)}, u32[]{:S(2)}, u32[]{:S(2)}) collective-permute-start(bf16[64,128]{1,0:T(8,128)(2,1)S(1)} %pad_maximum_fusion), channel_id=1, source_target_pairs={{0,4},{1,5},{2,6},{3,7},{4,0},{5,1},{6,2},{7,3},{8,12},{9,13},{10,... | collective-permute-start | bytes 49160 | tf_op jit(solution)/shard_map/ppermute | solution.py:38
  58.9 11.6 %collective-permute-start.18 = (bf16[512,128]{1,0:T(8,128)(2,1)S(1)}, bf16[512,128]{1,0:T(8,128)(2,1)S(1)}, u32[]{:S(2)}, u32[]{:S(2)}) collective-permute-start(bf16[512,128]{1,0:T(8,128)(2,1)S(1)} %compare_select_fusion.3), channel_id=1, source_target_pairs={{0,160},{32,192},{64,224},{96,0},{128,32},{160,64},{192,96},{224,1... | collective-permute-start | bytes 393224 | tf_op jit(solution)/shard_map/ppermute | solution.py:286
  61.3 11.9 %collective-permute-start.17 = (bf16[512,128]{1,0:T(8,128)(2,1)S(1)}, bf16[512,128]{1,0:T(8,128)(2,1)S(1)}, u32[]{:S(2)}, u32[]{:S(2)}) collective-permute-start(bf16[512,128]{1,0:T(8,128)(2,1)S(1)} %compare_select_fusion.3), channel_id=1, source_target_pairs={{0,96},{32,128},{64,160},{96,192},{128,224},{160,0},{192,32},{224,... | collective-permute-start | bytes 393224 | tf_op jit(solution)/shard_map/ppermute | solution.py:286
  62.8 10.6 %collective-permute-start.14 = (bf16[256,128]{1,0:T(8,128)(2,1)S(1)}, bf16[256,128]{1,0:T(8,128)(2,1)S(1)}, u32[]{:S(2)}, u32[]{:S(2)}) collective-permute-start(bf16[256,128]{1,0:T(8,128)(2,1)S(1)} %constant_dynamic-update-slice_fusion.4.own_ref), channel_id=1, source_target_pairs={{0,1},{1,0},{2,3},{3,2},{4,5},{5,4},{6,7},{7,6},{8,9},{9,8},{10,11... | collective-permute-start | bytes 196616 | tf_op jit(solution)/shard_map/ppermute | solution.py:38
  64.1 25.4 %collective-permute-start.21 = (bf16[32,24576]{1,0:T(8,128)(2,1)}, bf16[32,24576]{1,0:T(8,128)(2,1)}, u32[]{:S(2)}, u32[]{:S(2)}) collective-permute-start(bf16[32,24576]{1,0:T(8,128)(2,1)} %constant_dynamic-update-slice_fusion.refs_0_), channel_id=1, source_target_pairs={{0,1},{1,0},{2,3},{3,2},{4,5},{5,4},{6,7},{7,6},{8,9},{9,8},{10,11... | collective-permute-start | bytes 4718600 | tf_op jit(solution)/shard_map/ppermute | solution.py:38
  64.4 25.1 %copy-start.3 = (s32[256]{0:T(256)S(1)}, s32[256]{0:T(256)}, u32[]{:S(2)}) copy-start(s32[256]{0:T(256)} %piv_ref.3) | copy-start | bytes 3076
  64.5 11.3 %collective-permute-start.20 = (bf16[32,12288]{1,0:T(8,128)(2,1)S(1)}, bf16[32,12288]{1,0:T(8,128)(2,1)}, u32[]{:S(2)}, u32[]{:S(2)}) collective-permute-start(bf16[32,12288]{1,0:T(8,128)(2,1)S(1)} %slice.26), channel_id=1, source_target_pairs={{0,6},{1,25},{2,0},{3,27},{4,2},{5,29},{6,4},{7,31},{8,14},{9,1},{... | collective-permute-start | bytes 2359304 | tf_op jit(solution)/shard_map/ppermute | solution.py:38
  70.5 12.5 %copy-start.4 = (bf16[512,128]{1,0:T(8,128)(2,1)}, bf16[512,128]{1,0:T(8,128)(2,1)S(1)}, u32[]{:S(2)}) copy-start(bf16[512,128]{1,0:T(8,128)(2,1)S(1)} %collective-permute-done.18) | copy-start | bytes 393220
  70.5 12.5 %collective-permute-start.19 = (bf16[32,12288]{1,0:T(8,128)(2,1)S(1)}, bf16[32,12288]{1,0:T(8,128)(2,1)}, u32[]{:S(2)}, u32[]{:S(2)}) collective-permute-start(bf16[32,12288]{1,0:T(8,128)(2,1)S(1)} %slice.25), channel_id=1, source_target_pairs={{0,2},{1,9},{2,4},{3,11},{4,6},{5,13},{6,0},{7,15},{8,10},{9,17},{... | collective-permute-start | bytes 2359304 | tf_op jit(solution)/shard_map/ppermute | solution.py:38
  73.3 9.7 %copy-start.5 = (bf16[512,128]{1,0:T(8,128)(2,1)}, bf16[512,128]{1,0:T(8,128)(2,1)S(1)}, u32[]{:S(2)}) copy-start(bf16[512,128]{1,0:T(8,128)(2,1)S(1)} %collective-permute-done.17) | copy-start | bytes 393220
  73.3 16.3 %collective-permute-start.22 = (bf16[32,24576]{1,0:T(8,128)(2,1)S(1)}, bf16[32,24576]{1,0:T(8,128)(2,1)}, u32[]{:S(2)}, u32[]{:S(2)}) collective-permute-start(bf16[32,24576]{1,0:T(8,128)(2,1)S(1)} %collective-permute-done.12.refs_1_), channel_id=1, source_target_pairs={{0,1},{1,0},{2,3},{3,2},{4,5},{5,4},{6,7},{7,6},{8,9},{9,8},{10,11... | collective-permute-start | bytes 4718600 | tf_op jit(solution)/shard_map/ppermute | solution.py:38
  73.4 16.1 %collective-permute-start.23 = (bf16[32,24576]{1,0:T(8,128)(2,1)S(1)}, bf16[32,24576]{1,0:T(8,128)(2,1)}, u32[]{:S(2)}, u32[]{:S(2)}) collective-permute-start(bf16[32,24576]{1,0:T(8,128)(2,1)S(1)} %collective-permute-done.13.refs_2_), channel_id=1, source_target_pairs={{0,1},{1,0},{2,3},{3,2},{4,5},{5,4},{6,7},{7,6},{8,9},{9,8},{10,11... | collective-permute-start | bytes 4718600 | tf_op jit(solution)/shard_map/ppermute | solution.py:38
  75.8 13.7 %collective-permute-start.25 = (bf16[32,12288]{1,0:T(8,128)(2,1)}, bf16[32,12288]{1,0:T(8,128)(2,1)}, u32[]{:S(2)}, u32[]{:S(2)}) collective-permute-start(bf16[32,12288]{1,0:T(8,128)(2,1)} %collective-permute-done.20.refs_4_), channel_id=1, source_target_pairs={{0,1},{1,0},{2,3},{3,2},{4,5},{5,4},{6,7},{7,6},{8,9},{9,8},{10,11... | collective-permute-start | bytes 2359304 | tf_op jit(solution)/shard_map/ppermute | solution.py:38
  82.9 6.6 %collective-permute-start.24 = (bf16[32,12288]{1,0:T(8,128)(2,1)}, bf16[32,12288]{1,0:T(8,128)(2,1)}, u32[]{:S(2)}, u32[]{:S(2)}) collective-permute-start(bf16[32,12288]{1,0:T(8,128)(2,1)} %collective-permute-done.19.refs_3_), channel_id=1, source_target_pairs={{0,1},{1,0},{2,3},{3,2},{4,5},{5,4},{6,7},{7,6},{8,9},{9,8},{10,11... | collective-permute-start | bytes 2359304 | tf_op jit(solution)/shard_map/ppermute | solution.py:38
  89.6 2.8 %copy-start.1 = (bf16[24576,128]{1,0:T(8,128)(2,1)S(1)}, bf16[24576,128]{1,0:T(8,128)(2,1)}, u32[]{:S(2)}) copy-start(bf16[24576,128]{1,0:T(8,128)(2,1)} %copy-done) | copy-start | bytes 18874372

commit v3 on v2

v3 whole, which is shorter than its diff:
```python
import functools

import jax
import jax.numpy as jnp
from jax import lax
from jax.experimental import pallas as pl
from jax.experimental.pallas import tpu as pltpu
from jax.sharding import PartitionSpec as P

NX = 4
NY = 4
OFFSETS = (0, -1, 1, 2)
NBLK = 12
SMEM = pl.BlockSpec(memory_space=pltpu.SMEM)
VMEM = pl.BlockSpec(memory_space=pltpu.VMEM)
HIGHEST = lax.Precision.HIGHEST


def place(x, y, c):
    return ((x % NX) * NY + (y % NY)) * 2 + c


def hop(dx, dy, turn):
    pairs = []
    for x in range(NX):
        for y in range(NY):
            for c in range(2):
                a, b = (dy, dx) if turn and c == 1 else (dx, dy)
                pairs.append((place(x, y, c), place(x + a, y + b, c)))
    return pairs


CORES = [(p, p ^ 1) for p in range(NX * NY * 2)]


def send(block, pairs):
    return lax.ppermute(block, "pcol", pairs)


def params(mib):
    return pltpu.CompilerParams(vmem_limit_bytes=mib << 20)


def cost(us):
    return pl.CostEstimate(flops=int(us * 1.1e9), bytes_accessed=int(us * 3.5e6), transcendentals=0)


def stack_kernel(*refs):
    refs[-1][...] = jnp.concatenate([r[...] for r in refs[:-1]], axis=0)


def stack(parts, start, cols, name):
    rows = sum(p.shape[0] for p in parts)
    step = min(cols, 4096)
    return pl.pallas_call(
        stack_kernel,
        grid=(cols // step,),
        in_specs=[pl.BlockSpec((p.shape[0], step), lambda i: (0, i + start // step)) for p in parts],
        out_specs=pl.BlockSpec((rows, step), lambda i: (0, i)),
        out_shape=jax.ShapeDtypeStruct((rows, cols), jnp.bfloat16),
        compiler_params=params(6),
        name=name,
    )(*parts)


def add_kernel(a_ref, b_ref, out_ref):
    out_ref[...] = (a_ref[...].astype(jnp.float32) + b_ref[...].astype(jnp.float32)).astype(jnp.bfloat16)


def add(a, b):
    return pl.pallas_call(
        add_kernel,
        in_specs=[VMEM, VMEM],
        out_specs=VMEM,
        out_shape=jax.ShapeDtypeStruct(a.shape, a.dtype),
        compiler_params=params(2),
        name="add",
    )(a, b)


def choose_kernel(limit, first_ref, a_ref, b_ref, out_ref):
    @pl.when(first_ref[0] < limit)
    def _():
        out_ref[...] = a_ref[...]

    @pl.when(first_ref[0] >= limit)
    def _():
        out_ref[...] = b_ref[...]


def choose(first, limit, a, b):
    return pl.pallas_call(
        functools.partial(choose_kernel, limit),
        in_specs=[SMEM, VMEM, VMEM],
        out_specs=VMEM,
        out_shape=jax.ShapeDtypeStruct(a.shape, a.dtype),
        compiler_params=params(2),
        name="choose",
    )(first, a, b)


def pick_kernel(blk, piv_ref, first_ref, trailing_ref, out_ref, cnt_ref, lst_ref, own_ref, group_ref, rows_ref, sem):
    width = piv_ref.shape[0]
    rows = trailing_ref.shape[0]
    first = first_ref[0]
    nblk = cnt_ref.shape[0]
    for b in range(nblk):
        cnt_ref[b] = 0

    def filt(i, n):
        loc = piv_ref[i] - first
        own_ref[n] = i
        return n + ((loc >= 0) & (loc < rows)).astype(jnp.int32)

    n = lax.fori_loop(0, width, filt, 0, unroll=8)

    def group(k):
        loc = piv_ref[own_ref[k]] - first
        base = pl.multiple_of(loc & ~15, 16)
        return pltpu.make_async_copy(trailing_ref.at[pl.ds(base, 16)], group_ref.at[k], sem)

    def begin(k, carry):
        group(k).start()
        i = own_ref[k]
        b = lax.div(piv_ref[i] - first, blk)
        m = cnt_ref[b]
        lst_ref[b * width + m] = i
        cnt_ref[b] = m + 1
        return carry

    def finish(k, carry):
        group(k).wait()
        return carry

    lax.fori_loop(0, n, begin, 0)
    rows_ref[...] = jnp.zeros_like(rows_ref)
    lax.fori_loop(0, n, finish, 0)
    sub = lax.broadcasted_iota(jnp.int32, (16, 128), 0)

    def extract(k, carry):
        i = own_ref[k]
        loc = piv_ref[i] - first
        tile = group_ref[k].astype(jnp.float32)
        row = jnp.sum(jnp.where(sub == (loc & 15), tile, 0.0), axis=0, keepdims=True)
        rows_ref[pl.ds(i, 1), :] = row
        return carry

    lax.fori_loop(0, n, extract, 0)
    out_ref[...] = rows_ref[...].astype(jnp.bfloat16)


def pick(trailing, pivots, first, blk):
    rows, cols = trailing.shape
    width = pivots.shape[0]
    nblk = rows // blk
    return pl.pallas_call(
        functools.partial(pick_kernel, blk),
        in_specs=[SMEM, SMEM, pl.BlockSpec(memory_space=pltpu.HBM)],
        out_specs=[VMEM, SMEM, SMEM],
        out_shape=[
            jax.ShapeDtypeStruct((width, cols), jnp.bfloat16),
            jax.ShapeDtypeStruct((nblk,), jnp.int32),
            jax.ShapeDtypeStruct((nblk * width,), jnp.int32),
        ],
        scratch_shapes=[
            pltpu.SMEM((width + 8,), jnp.int32),
            pltpu.VMEM((width, 16, cols), jnp.bfloat16),
            pltpu.VMEM((width, cols), jnp.float32),
            pltpu.SemaphoreType.DMA,
        ],
        compiler_params=params(6),
        cost_estimate=cost(12),
        name="pick",
    )(pivots, first, trailing)


def dot(a, b):
    return lax.dot_general(
        a, b, (((1,), (0,)), ((), ())), precision=HIGHEST, preferred_element_type=jnp.float32
    )


def dot_exact(a, b):
    n = b.shape[1]
    hi = b.astype(jnp.bfloat16)
    rest = b - hi.astype(jnp.float32)
    mid = rest.astype(jnp.bfloat16)
    low = (rest - mid.astype(jnp.float32)).astype(jnp.bfloat16)
    r = lax.dot_general(
        a, jnp.concatenate([hi, mid, low], axis=1), (((1,), (0,)), ((), ())),
        preferred_element_type=jnp.float32,
    )
    return r[:, 2 * n :] + r[:, n : 2 * n] + r[:, :n]


def unit_inverse(strict):
    n = strict.shape[0]
    r = lax.broadcasted_iota(jnp.int32, (n, n), 0)
    c = lax.broadcasted_iota(jnp.int32, (n, n), 1)
    d = jnp.where((r >> 4) == (c >> 4), strict, 0.0)
    x = jnp.where(r == c, 1.0, 0.0) - d
    for step in range(3):
        d = dot_exact(d.astype(jnp.bfloat16), d) if step == 0 else dot(d, d)
        x = x + dot(x, d)
    for lg in (4, 5, 6):
        inside = ((r >> (lg + 1)) == (c >> (lg + 1))) & ((r >> lg) != (c >> lg))
        part = jnp.where(inside, strict, 0.0).astype(jnp.bfloat16)
        x = x - dot(x, dot_exact(part, x))
    return x


def blocks():
    return [(k, outer, inner) for k in range(2) for outer in OFFSETS for inner in OFFSETS]


def block_at(me, k, outer, inner):
    core = (me & 1) ^ k
    dx = jnp.where(core == 0, inner, outer)
    dy = jnp.where(core == 0, outer, inner)
    x = ((me >> 3) + dx) & 3
    y = ((me >> 1) + dy) & 3
    return pl.ds(pl.multiple_of(((x * 4 + y) * 2 + core) * 8, 8), 8)


def solve_kernel(me_ref, own_ref, other_ref, top_ref, more_ref, head_ref, out_ref, a_ref, g_ref):
    n = top_ref.shape[0]
    h = n // 2
    me = me_ref[0]
    g_ref[:h, :] = own_ref[...].astype(jnp.float32)
    g_ref[h:, :] = other_ref[...].astype(jnp.float32)
    for b, where in enumerate(blocks()):
        a_ref[block_at(me, *where), :] = g_ref[8 * b : 8 * b + 8, :]
    r = lax.broadcasted_iota(jnp.int32, (h, h), 0)
    c = lax.broadcasted_iota(jnp.int32, (h, h), 1)
    s11 = jnp.where(r > c, a_ref[:h, :h].T, 0.0)
    s22 = jnp.where(r > c, a_ref[h:, h:].T, 0.0)
    s21 = a_ref[:h, h:].T
    x1 = unit_inverse(s11)
    x2 = unit_inverse(s22)
    top = top_ref[...].astype(jnp.float32) + more_ref[...].astype(jnp.float32)
    u1 = dot(x1, top[:h])
    u2 = dot(x2, top[h:] - dot_exact(s21.astype(jnp.bfloat16), u1))
    out_ref[:n, :] = jnp.concatenate([u1, u2], axis=0).astype(jnp.bfloat16)
    out_ref[n:, :] = head_ref[...]


def solve(me, own, other, top, more, trailing):
    n, cols = top.shape
    whole = pl.BlockSpec((n // 2, n), lambda i: (0, 0))
    tall = pl.BlockSpec((n, cols), lambda i: (0, 0))
    return pl.pallas_call(
        solve_kernel,
        grid=(1,),
        in_specs=[SMEM, whole, whole, tall, tall, tall],
        out_specs=pl.BlockSpec((2 * n, cols), lambda i: (0, 0)),
        out_shape=jax.ShapeDtypeStruct((2 * n, cols), jnp.bfloat16),
        scratch_shapes=[pltpu.VMEM((n, n), jnp.float32), pltpu.VMEM((n, n), jnp.float32)],
        compiler_params=params(10),
        cost_estimate=cost(20),
        name="solve",
    )(me, own, other, top, more, trailing)


def update_kernel(nblk, late, cnt_ref, lst_ref, piv_ref, first_ref, me_ref, tr_ref, ud_ref, rest_ref, *refs):
    parts = refs[:16]
    out_ref, acc_ref, nat_ref, drow_ref, u_ref, tmp_ref = refs[16:]
    blk = out_ref.shape[0]
    width = nat_ref.shape[0]
    b = pl.program_id(0)
    first = first_ref[0]

    @pl.when(b == 0)
    def _():
        @pl.when(first < late)
        def _():
            nat_ref[...] = ud_ref[:width, :].astype(jnp.float32)
            drow_ref[...] = ud_ref[width:, :].astype(jnp.float32)

        @pl.when(first >= late)
        def _():
            nat_ref[...] = rest_ref[:width, :].astype(jnp.float32)
            drow_ref[...] = rest_ref[width:, :].astype(jnp.float32)

        for i, where in enumerate(blocks()):
            tmp_ref[8 * i : 8 * i + 8, :] = nat_ref[block_at(me_ref[0], *where), :]
        u_ref[...] = tmp_ref[...].astype(jnp.bfloat16)

    def compute(half):
        here = pl.ds(pl.multiple_of((b - half * (nblk // 2)) * blk, 128), blk)
        pieces = [r[:, here] for r in parts[half::2]]
        acc_ref[...] = lax.dot_general(
            jnp.concatenate(pieces, axis=0), u_ref[...], (((0,), (0,)), ((), ())),
            preferred_element_type=jnp.float32,
        )

    @pl.when(b < nblk // 2)
    def _():
        compute(0)

    @pl.when(b >= nblk // 2)
    def _():
        compute(1)

    out_ref[...] = (tr_ref[...].astype(jnp.float32) - acc_ref[...]).astype(jnp.bfloat16)
    sub = lax.broadcasted_iota(jnp.int32, (16, 128), 0)

    def fix(k, carry):
        i = lst_ref[b * width + k]
        loc = piv_ref[i] - first - b * blk
        at = pl.ds(pl.multiple_of(loc & ~15, 16), 16)
        new = drow_ref[pl.ds(i, 1), :] - acc_ref[at, :]
        old = out_ref[at, :].astype(jnp.float32)
        out_ref[at, :] = jnp.where(sub == (loc & 15), new, old).astype(jnp.bfloat16)
        return carry

    lax.fori_loop(0, cnt_ref[b], fix, 0)

    @pl.when((b == 0) & (first == 0))
    def _():
        out_ref[:width, :] = nat_ref[...].astype(jnp.bfloat16)


def update(cnt, lst, pivots, first, me, trailing, ud, rest, parts, blk):
    rows, cols = trailing.shape
    width = pivots.shape[0]
    nblk = rows // blk
    tall = pl.BlockSpec((blk, cols), lambda b: (b, 0))
    pair = pl.BlockSpec((2 * width, cols), lambda b: (0, 0))
    return pl.pallas_call(
        functools.partial(update_kernel, nblk, 4 * rows),
        grid=(nblk,),
        in_specs=[SMEM] * 5 + [tall, pair, pair] + [VMEM] * 16,
        out_specs=tall,
        scratch_shapes=[
            pltpu.VMEM((blk, cols), jnp.float32),
            pltpu.VMEM((width, cols), jnp.float32),
            pltpu.VMEM((width, cols), jnp.float32),
            pltpu.VMEM((width, cols), jnp.bfloat16),
            pltpu.VMEM((width, cols), jnp.float32),
        ],
        out_shape=jax.ShapeDtypeStruct((rows, cols), jnp.bfloat16),
        compiler_params=params(12),
        name="update",
    )(cnt, lst, pivots, first, me, trailing, ud, rest, *parts)


def body(trailing, panel_t, pivots):
    rows = trailing.shape[0]
    width = pivots.shape[0]
    blk = rows // NBLK
    half = rows // 2
    barrier = lax.optimization_barrier
    first = (lax.axis_index("prow") * rows).astype(jnp.int32).reshape(1)
    me = lax.axis_index("pcol").astype(jnp.int32).reshape(1)
    trailing = pltpu.with_memory_space_constraint(trailing, pltpu.HBM)

    def zsend(x, pairs):
        return lax.ppermute(x, "prow", pairs)

    p, m, q = [send(panel_t, hop(d, 0, True)) for d in (1, -1, 2)]

    top, cnt, lst = pick(trailing, pivots, first, blk)
    p, m, q, top = barrier((p, m, q, top))
    more = zsend(top, [(i + 4, i) for i in range(4)])

    up, down, across = hop(0, 1, True), hop(0, -1, True), hop(0, 2, True)
    diag = stack([panel_t, p, m, q], 0, width, "stack_d")
    diag_q, diag_m = send(diag, across), send(diag, down)
    p, m, q, diag_q = barrier((p, m, q, diag_q))
    xa = stack([panel_t, p, m, q], 0, half, "stack_a")
    p, m, q, diag_m, xa = barrier((p, m, q, diag_m, xa))
    xb = stack([panel_t, p, m, q], half, half, "stack_b")
    pa, mb = send(xa, up), send(xb, down)
    top = add(top, more)
    xa, xb, top = barrier((xa, xb, top))
    pb, ma = send(xb, up), send(xa, down)
    more = zsend(top, [(2, 0), (3, 1)])
    oxa, oxb = send(xa, CORES), send(xb, CORES)
    pa, mb, diag_q, diag_m = barrier((pa, mb, diag_q, diag_m))
    qa, qb = send(pa, up), send(mb, down)
    own = stack([diag, pa, diag_m, diag_q], 0, width, "stack_l")
    other = send(own, CORES)
    opa, omb = send(pa, CORES), send(mb, CORES)
    top = add(top, more)
    more = zsend(top, [(1, 0)])

    other, pb, ma = barrier((other, pb, ma))
    ud = solve(me, own, other, top, more, trailing)
    opb, oma = send(pb, CORES), send(ma, CORES)
    ud = choose(first, rows, ud, zsend(ud, [(0, 1)]))
    ud, qa, qb = barrier((ud, qa, qb))
    oqa, oqb = send(qa, CORES), send(qb, CORES)
    ud = choose(first, 2 * rows, ud, zsend(ud, [(0, 2), (1, 3)]))
    rest = zsend(ud, [(i, i + 4) for i in range(4)])

    parts = [xa, xb, pa, pb, ma, mb, qa, qb, oxa, oxb, opa, opb, oma, omb, oqa, oqb]
    return update(cnt, lst, pivots, first, me, trailing, ud, rest, parts, blk)


def solution(mesh):
    return jax.shard_map(
        body,
        mesh=mesh,
        in_specs=(P("prow", "pcol"), P("pcol", "prow"), P()),
        out_specs=P("prow", "pcol"),
        check_vma=False,
    )
```

time: 106 us -> 89.5 us (0.84)
  the two profiles are of different devices: /device:TPU:1 before, /device:TPU:225 now
where the time goes in v3:
time: 89.5 us; the launch traced here: 88.9 us
  starting transfers between devices  34.9 us (39%)
  waiting for transfers between devices  29.8 us (33%)
  Pallas kernels  23.3 us (26%)
    ppermute x20, starting transfers between devices, send(): return lax.ppermute(block, 'pcol', pairs)  27.9 us
    ppermute x20, waiting for transfers between devices, send(): return lax.ppermute(block, 'pcol', pairs)  18 us
    pallas_call x1, Pallas kernels, update(): pl.pallas_call(functools.partial(update_kernel, nblk, 4 * rows), grid=(nb...  13.8 us
    ppermute x6, waiting for transfers between devices, zsend(): return lax.ppermute(x, 'prow', pairs)  11.8 us
    ppermute x6, starting transfers between devices, zsend(): return lax.ppermute(x, 'prow', pairs)  6.98 us
    pallas_call x1, Pallas kernels, solve(): pl.pallas_call(solve_kernel, grid=(1,), in_specs=[SMEM, whole, whole, tal...  5.09 us
    pallas_call x1, Pallas kernels, pick(): pl.pallas_call(functools.partial(pick_kernel, blk), in_specs=[SMEM, SMEM,...  3.95 us
  transfers between devices with their start and end apart: 26, of which 9 were waited for; matrix products, arithmetic and copies ran while one was open for 0% of the time, Pallas kernels for 11%

profile of v3, /device:TPU:225, one launch (start us, length us, event | category | flops | bytes accessed | tf_op | source)
XLA Modules:
  0.0 88.9 jit_solution(8587096919096417637)
XLA Ops:
  0.0 2.9 %collective-permute-start.2 = (bf16[8,24576]{1,0:T(8,128)(2,1)}, bf16[8,24576]{1,0:T(8,128)(2,1)S(1)}, u32[]{:S(2)}, u32[]{:S(2)}) collective-permute-start(bf16[8,24576]{1,0:T(8,128)(2,1)} %refs_0_.5), channel_id=1, source_target_pairs={{0,16},{1,5},{2,18},{3,7},{4,20},{5,1},{6,22},{7,3},{8,24},{9,13},... | collective-permute-start | bytes 1179656 | tf_op jit(solution)/shard_map/ppermute | solution.py:37
  2.9 0.8 collective-permute-start.1
  3.7 0.7 collective-permute-start
  4.4 0.7 copy-done.1
  5.1 3.9 %pick.1 = (bf16[256,128]{1,0:T(8,128)(2,1)S(1)}, s32[12]{0:T(128)S(1)}, s32[3072]{0:T(1024)S(1)}) custom-call(s32[256]{0:T(256)S(1)} %copy-done.1, s32[1]{0:T(128)} %bitcast.first_ref, bf16[24576,128]{1,0:T(8,128)(2,1)} %tr_ref.1), custom_call_target="tpu_custom_call" | custom-call | flops 13200000000 | bytes 42000000 | tf_op jit(solution)/shard_map/pick/pallas_call | solution.py:156
  9.0 0.0 collective-permute-done.2.refs_3_
  9.0 4.2 %collective-permute-done.1.refs_2_ = bf16[8,24576]{1,0:T(8,128)(2,1)S(1)} collective-permute-done((bf16[8,24576]{1,0:T(8,128)(2,1)}, bf16[8,24576]{1,0:T(8,128)(2,1)S(1)}, u32[]{:S(2)}, u32[]{:S(2)}) %collective-permute-start.1) | collective-permute-done | bytes 393248 | tf_op jit(solution)/shard_map/ppermute | solution.py:37
  13.2 0.0 collective-permute-done.refs_1_
  13.3 2.8 %collective-permute-start.3 = (bf16[32,256]{1,0:T(8,128)(2,1)S(1)}, bf16[32,256]{1,0:T(8,128)(2,1)S(1)}, u32[]{:S(2)}, u32[]{:S(2)}) collective-permute-start(bf16[32,256]{1,0:T(8,128)(2,1)S(1)} %stack_d.1.refs_0_), channel_id=1, source_target_pairs={{0,4},{1,17},{2,6},{3,19},{4,0},{5,21},{6,2},{7,23},{8,12},{9,25},... | collective-permute-start | bytes 49160 | tf_op jit(solution)/shard_map/ppermute | solution.py:37
  16.1 0.9 collective-permute-start.4
  16.9 3.1 %collective-permute-start.8 = (bf16[256,128]{1,0:T(8,128)(2,1)S(1)}, bf16[256,128]{1,0:T(8,128)(2,1)S(1)}, u32[]{:S(2)}, u32[]{:S(2)}) collective-permute-start(bf16[256,128]{1,0:T(8,128)(2,1)S(1)} %get-tuple-element.52.a_ref), channel_id=1, source_target_pairs={{128,0},{160,32},{192,64},{224,96},{129,1},{161,33},{193,65},{225,... | collective-permute-start | bytes 196616 | tf_op jit(solution)/shard_map/ppermute | solution.py:358
  20.0 0.0 collective-permute-done.3.refs_3_
  20.0 0.2 stack_a.1.refs_0_
  20.3 0.0 collective-permute-done.4.refs_2_
  20.3 0.2 stack_b.1.refs_1_
  20.5 0.5 collective-permute-start.6
  21.0 1.0 %collective-permute-start.5 = (bf16[32,12288]{1,0:T(8,128)(2,1)S(1)}, bf16[32,12288]{1,0:T(8,128)(2,1)S(1)}, u32[]{:S(2)}, u32[]{:S(2)}) collective-permute-start(bf16[32,12288]{1,0:T(8,128)(2,1)S(1)} %stack_a.1.refs_0_), channel_id=1, source_target_pairs={{0,2},{1,9},{2,4},{3,11},{4,6},{5,13},{6,0},{7,15},{8,10},{9,17},{... | collective-permute-start | bytes 2359304 | tf_op jit(solution)/shard_map/ppermute | solution.py:37
  22.1 0.0 collective-permute-done.8.b_ref
  22.1 0.7 collective-permute-start.9
  22.8 2.1 %collective-permute-start.10 = (bf16[32,12288]{1,0:T(8,128)(2,1)S(1)}, bf16[32,12288]{1,0:T(8,128)(2,1)}, u32[]{:S(2)}, u32[]{:S(2)}) collective-permute-start(bf16[32,12288]{1,0:T(8,128)(2,1)S(1)} %stack_a.1.refs_0_), channel_id=1, source_target_pairs={{0,6},{1,25},{2,0},{3,27},{4,2},{5,29},{6,4},{7,31},{8,14},{9,1},{... | collective-permute-start | bytes 2359304 | tf_op jit(solution)/shard_map/ppermute | solution.py:37
  24.8 0.7 collective-permute-start.11
  25.5 6.2 %collective-permute-done.6.refs_5_ = bf16[32,12288]{1,0:T(8,128)(2,1)S(1)} collective-permute-done((bf16[32,12288]{1,0:T(8,128)(2,1)S(1)}, bf16[32,12288]{1,0:T(8,128)(2,1)S(1)}, u32[]{:S(2)}, u32[]{:S(2)}) %collective-permute-start.6) | collective-permute-done | bytes 786464 | tf_op jit(solution)/shard_map/ppermute | solution.py:37
  31.7 1.7 %collective-permute-done.5.refs_1_.refs_2_ = bf16[32,12288]{1,0:T(8,128)(2,1)S(1)} collective-permute-done((bf16[32,12288]{1,0:T(8,128)(2,1)S(1)}, bf16[32,12288]{1,0:T(8,128)(2,1)S(1)}, u32[]{:S(2)}, u32[]{:S(2)}) %collective-permute-start.5) | collective-permute-done | bytes 786464 | tf_op jit(solution)/shard_map/ppermute | solution.py:37
  33.4 3.9 %collective-permute-start.7 = (bf16[128,256]{1,0:T(8,128)(2,1)S(1)}, bf16[128,256]{1,0:T(8,128)(2,1)S(1)}, u32[]{:S(2)}, u32[]{:S(2)}) collective-permute-start(bf16[128,256]{1,0:T(8,128)(2,1)S(1)} %stack_l.1.own_ref), channel_id=1, source_target_pairs={{0,1},{1,0},{2,3},{3,2},{4,5},{5,4},{6,7},{7,6},{8,9},{9,8},{10,11... | collective-permute-start | bytes 196616 | tf_op jit(solution)/shard_map/ppermute | solution.py:37
  37.3 0.7 collective-permute-start.12
  38.0 1.2 %collective-permute-start.14 = (bf16[32,12288]{1,0:T(8,128)(2,1)S(1)}, bf16[32,12288]{1,0:T(8,128)(2,1)S(1)}, u32[]{:S(2)}, u32[]{:S(2)}) collective-permute-start(bf16[32,12288]{1,0:T(8,128)(2,1)S(1)} %collective-permute-done.5.refs_1_.refs_2_), channel_id=1, source_target_pairs={{0,2},{1,9},{2,4},{3,11},{4,6},{5,13},{6,0},{7,15},{8,10},{9,17},{... | collective-permute-start | bytes 2359304 | tf_op jit(solution)/shard_map/ppermute | solution.py:37
  39.2 2.7 %collective-permute-done.9.refs_3_ = bf16[32,12288]{1,0:T(8,128)(2,1)} collective-permute-done((bf16[32,12288]{1,0:T(8,128)(2,1)S(1)}, bf16[32,12288]{1,0:T(8,128)(2,1)}, u32[]{:S(2)}, u32[]{:S(2)}) %collective-permute-start.9) | collective-permute-done | bytes 786464 | tf_op jit(solution)/shard_map/ppermute | solution.py:37
  41.9 0.0 collective-permute-start.15
  41.9 0.0 collective-permute-done.10.refs_4_
  41.9 0.0 copy-start.2
  41.9 5.1 %solve.1.a_ref = bf16[512,128]{1,0:T(8,128)(2,1)S(1)} custom-call(s32[1]{0:T(128)} %bitcast.1.me_ref, bf16[128,256]{1,0:T(8,128)(2,1)S(1)} %stack_l.1.own_ref, bf16[128,256]{1,0:T(8,128)(2,1)S(1)} %collective-permute-done.7.other_ref, bf16[256,128]{1,0:T(8,128)(2,1)S(1)} %add.3.top_ref, bf16[256,128]{1,0:T(8,128)(2,1)S(1)} %collective-permute-done.12.more_ref, ...), custom_call_target="tpu_custom_call" | custom-call | flops 22000001024 | bytes 70000000 | tf_op jit(solution)/shard_map/solve/pallas_call | solution.py:251
  47.0 0.7 collective-permute-start.13
  47.7 4.0 %collective-permute-start.19 = (bf16[32,12288]{1,0:T(8,128)(2,1)S(1)}, bf16[32,12288]{1,0:T(8,128)(2,1)S(1)}, u32[]{:S(2)}, u32[]{:S(2)}) collective-permute-start(bf16[32,12288]{1,0:T(8,128)(2,1)S(1)} %stack_b.1.refs_1_), channel_id=1, source_target_pairs={{0,1},{1,0},{2,3},{3,2},{4,5},{5,4},{6,7},{7,6},{8,9},{9,8},{10,11... | collective-permute-start | bytes 2359304 | tf_op jit(solution)/shard_map/ppermute | solution.py:37
  51.7 0.3 collective-permute-start.18
  52.0 0.2 collective-permute-start.23
  52.3 0.8 collective-permute-done.15.refs_7_
  53.0 4.8 %collective-permute-start.20 = (bf16[32,12288]{1,0:T(8,128)(2,1)S(1)}, bf16[32,12288]{1,0:T(8,128)(2,1)S(1)}, u32[]{:S(2)}, u32[]{:S(2)}) collective-permute-start(bf16[32,12288]{1,0:T(8,128)(2,1)S(1)} %collective-permute-done.5.refs_1_.refs_2_), channel_id=1, source_target_pairs={{0,1},{1,0},{2,3},{3,2},{4,5},{5,4},{6,7},{7,6},{8,9},{9,8},{10,11... | collective-permute-start | bytes 2359304 | tf_op jit(solution)/shard_map/ppermute | solution.py:37
  57.8 0.7 collective-permute-start.16
  58.5 0.1 collective-permute-start.21
  58.6 0.5 collective-permute-start.22
  59.1 0.1 collective-permute-start.24
  59.2 0.4 collective-permute-start.25
  59.6 0.1 collective-permute-done.20.refs_10_
  59.7 1.3 %collective-permute-start.17 = (bf16[512,128]{1,0:T(8,128)(2,1)S(1)}, bf16[512,128]{1,0:T(8,128)(2,1)S(1)}, u32[]{:S(2)}, u32[]{:S(2)}) collective-permute-start(bf16[512,128]{1,0:T(8,128)(2,1)S(1)} %choose.3.ud_ref), channel_id=1, source_target_pairs={{0,128},{32,160},{64,192},{96,224},{1,129},{33,161},{65,193},{97,2... | collective-permute-start | bytes 393224 | tf_op jit(solution)/shard_map/ppermute | solution.py:358
  61.0 0.1 collective-permute-done.21.refs_11_
  61.1 2.2 %collective-permute-done.22.refs_12_ = bf16[32,12288]{1,0:T(8,128)(2,1)S(1)} collective-permute-done((bf16[32,12288]{1,0:T(8,128)(2,1)}, bf16[32,12288]{1,0:T(8,128)(2,1)S(1)}, u32[]{:S(2)}, u32[]{:S(2)}) %collective-permute-start.22) | collective-permute-done | bytes 786464 | tf_op jit(solution)/shard_map/ppermute | solution.py:37
  63.3 11.8 %collective-permute-done.17.rest_ref = bf16[512,128]{1,0:T(8,128)(2,1)S(1)} collective-permute-done((bf16[512,128]{1,0:T(8,128)(2,1)S(1)}, bf16[512,128]{1,0:T(8,128)(2,1)S(1)}, u32[]{:S(2)}, u32[]{:S(2)}) %collective-permute-start.17) | collective-permute-done | bytes 131104 | tf_op jit(solution)/shard_map/ppermute | solution.py:358
  75.2 13.8 %update.1 = bf16[24576,128]{1,0:T(8,128)(2,1)} custom-call(s32[12]{0:T(128)S(1)} %get-tuple-element.34.cnt_ref, s32[3072]{0:T(1024)S(1)} %get-tuple-element.35.lst_ref, s32[256]{0:T(256)S(1)} %copy-done.2, s32[1]{0:T(128)} %bitcast.first_ref, s32[1]{0:T(128)} %bitcast.1.me_ref, bf16[24576,128]{1,0:T(8,128)(2,1)} %tr_ref.1, ...), custom_call_target="tpu_custom_call" | custom-call | tf_op jit(solution)/shard_map/update/pallas_call | solution.py:329
  (21 shorter events, 0.1 us)
Async XLA Ops:
  0.0 9.0 %collective-permute-start.2 = (bf16[8,24576]{1,0:T(8,128)(2,1)}, bf16[8,24576]{1,0:T(8,128)(2,1)S(1)}, u32[]{:S(2)}, u32[]{:S(2)}) collective-permute-start(bf16[8,24576]{1,0:T(8,128)(2,1)} %refs_0_.5), channel_id=1, source_target_pairs={{0,16},{1,5},{2,18},{3,7},{4,20},{5,1},{6,22},{7,3},{8,24},{9,13},... | collective-permute-start | bytes 1179656 | tf_op jit(solution)/shard_map/ppermute | solution.py:37
  2.9 10.3 %collective-permute-start.1 = (bf16[8,24576]{1,0:T(8,128)(2,1)}, bf16[8,24576]{1,0:T(8,128)(2,1)S(1)}, u32[]{:S(2)}, u32[]{:S(2)}) collective-permute-start(bf16[8,24576]{1,0:T(8,128)(2,1)} %refs_0_.5), channel_id=1, source_target_pairs={{0,24},{1,7},{2,26},{3,1},{4,28},{5,3},{6,30},{7,5},{8,0},{9,15},{... | collective-permute-start | bytes 1179656 | tf_op jit(solution)/shard_map/ppermute | solution.py:37
  3.7 9.5 %collective-permute-start = (bf16[8,24576]{1,0:T(8,128)(2,1)}, bf16[8,24576]{1,0:T(8,128)(2,1)S(1)}, u32[]{:S(2)}, u32[]{:S(2)}) collective-permute-start(bf16[8,24576]{1,0:T(8,128)(2,1)} %refs_0_.5), channel_id=1, source_target_pairs={{0,8},{1,3},{2,10},{3,5},{4,12},{5,7},{6,14},{7,1},{8,16},{9,11},{... | collective-permute-start | bytes 1179656 | tf_op jit(solution)/shard_map/ppermute | solution.py:37
  4.4 0.7 copy-start.1
  5.1 8.2 %copy-start = (bf16[8,24576]{1,0:T(8,128)(2,1)S(1)}, bf16[8,24576]{1,0:T(8,128)(2,1)}, u32[]{:S(2)}) copy-start(bf16[8,24576]{1,0:T(8,128)(2,1)} %refs_0_.5) | copy-start | bytes 1179652
  13.3 6.8 %collective-permute-start.3 = (bf16[32,256]{1,0:T(8,128)(2,1)S(1)}, bf16[32,256]{1,0:T(8,128)(2,1)S(1)}, u32[]{:S(2)}, u32[]{:S(2)}) collective-permute-start(bf16[32,256]{1,0:T(8,128)(2,1)S(1)} %stack_d.1.refs_0_), channel_id=1, source_target_pairs={{0,4},{1,17},{2,6},{3,19},{4,0},{5,21},{6,2},{7,23},{8,12},{9,25},... | collective-permute-start | bytes 49160 | tf_op jit(solution)/shard_map/ppermute | solution.py:37
  16.1 4.2 %collective-permute-start.4 = (bf16[32,256]{1,0:T(8,128)(2,1)S(1)}, bf16[32,256]{1,0:T(8,128)(2,1)S(1)}, u32[]{:S(2)}, u32[]{:S(2)}) collective-permute-start(bf16[32,256]{1,0:T(8,128)(2,1)S(1)} %stack_d.1.refs_0_), channel_id=1, source_target_pairs={{0,6},{1,25},{2,0},{3,27},{4,2},{5,29},{6,4},{7,31},{8,14},{9,1},{... | collective-permute-start | bytes 49160 | tf_op jit(solution)/shard_map/ppermute | solution.py:37
  16.9 5.1 %collective-permute-start.8 = (bf16[256,128]{1,0:T(8,128)(2,1)S(1)}, bf16[256,128]{1,0:T(8,128)(2,1)S(1)}, u32[]{:S(2)}, u32[]{:S(2)}) collective-permute-start(bf16[256,128]{1,0:T(8,128)(2,1)S(1)} %get-tuple-element.52.a_ref), channel_id=1, source_target_pairs={{128,0},{160,32},{192,64},{224,96},{129,1},{161,33},{193,65},{225,... | collective-permute-start | bytes 196616 | tf_op jit(solution)/shard_map/ppermute | solution.py:358
  20.5 11.2 %collective-permute-start.6 = (bf16[32,12288]{1,0:T(8,128)(2,1)S(1)}, bf16[32,12288]{1,0:T(8,128)(2,1)S(1)}, u32[]{:S(2)}, u32[]{:S(2)}) collective-permute-start(bf16[32,12288]{1,0:T(8,128)(2,1)S(1)} %stack_b.1.refs_1_), channel_id=1, source_target_pairs={{0,6},{1,25},{2,0},{3,27},{4,2},{5,29},{6,4},{7,31},{8,14},{9,1},{... | collective-permute-start | bytes 2359304 | tf_op jit(solution)/shard_map/ppermute | solution.py:37
  21.0 12.3 %collective-permute-start.5 = (bf16[32,12288]{1,0:T(8,128)(2,1)S(1)}, bf16[32,12288]{1,0:T(8,128)(2,1)S(1)}, u32[]{:S(2)}, u32[]{:S(2)}) collective-permute-start(bf16[32,12288]{1,0:T(8,128)(2,1)S(1)} %stack_a.1.refs_0_), channel_id=1, source_target_pairs={{0,2},{1,9},{2,4},{3,11},{4,6},{5,13},{6,0},{7,15},{8,10},{9,17},{... | collective-permute-start | bytes 2359304 | tf_op jit(solution)/shard_map/ppermute | solution.py:37
  22.1 19.8 %collective-permute-start.9 = (bf16[32,12288]{1,0:T(8,128)(2,1)S(1)}, bf16[32,12288]{1,0:T(8,128)(2,1)}, u32[]{:S(2)}, u32[]{:S(2)}) collective-permute-start(bf16[32,12288]{1,0:T(8,128)(2,1)S(1)} %stack_b.1.refs_1_), channel_id=1, source_target_pairs={{0,2},{1,9},{2,4},{3,11},{4,6},{5,13},{6,0},{7,15},{8,10},{9,17},{... | collective-permute-start | bytes 2359304 | tf_op jit(solution)/shard_map/ppermute | solution.py:37
  22.8 19.2 %collective-permute-start.10 = (bf16[32,12288]{1,0:T(8,128)(2,1)S(1)}, bf16[32,12288]{1,0:T(8,128)(2,1)}, u32[]{:S(2)}, u32[]{:S(2)}) collective-permute-start(bf16[32,12288]{1,0:T(8,128)(2,1)S(1)} %stack_a.1.refs_0_), channel_id=1, source_target_pairs={{0,6},{1,25},{2,0},{3,27},{4,2},{5,29},{6,4},{7,31},{8,14},{9,1},{... | collective-permute-start | bytes 2359304 | tf_op jit(solution)/shard_map/ppermute | solution.py:37
  24.8 12.5 %collective-permute-start.11 = (bf16[256,128]{1,0:T(8,128)(2,1)S(1)}, bf16[256,128]{1,0:T(8,128)(2,1)S(1)}, u32[]{:S(2)}, u32[]{:S(2)}) collective-permute-start(bf16[256,128]{1,0:T(8,128)(2,1)S(1)} %add.2.a_ref), channel_id=1, source_target_pairs={{64,0},{96,32},{65,1},{97,33},{66,2},{98,34},{67,3},{99,35},{68,4}... | collective-permute-start | bytes 196616 | tf_op jit(solution)/shard_map/ppermute | solution.py:358
  33.4 8.5 %collective-permute-start.7 = (bf16[128,256]{1,0:T(8,128)(2,1)S(1)}, bf16[128,256]{1,0:T(8,128)(2,1)S(1)}, u32[]{:S(2)}, u32[]{:S(2)}) collective-permute-start(bf16[128,256]{1,0:T(8,128)(2,1)S(1)} %stack_l.1.own_ref), channel_id=1, source_target_pairs={{0,1},{1,0},{2,3},{3,2},{4,5},{5,4},{6,7},{7,6},{8,9},{9,8},{10,11... | collective-permute-start | bytes 196616 | tf_op jit(solution)/shard_map/ppermute | solution.py:37
  37.3 4.6 %collective-permute-start.12 = (bf16[256,128]{1,0:T(8,128)(2,1)S(1)}, bf16[256,128]{1,0:T(8,128)(2,1)S(1)}, u32[]{:S(2)}, u32[]{:S(2)}) collective-permute-start(bf16[256,128]{1,0:T(8,128)(2,1)S(1)} %add.3.top_ref), channel_id=1, source_target_pairs={{32,0},{33,1},{34,2},{35,3},{36,4},{37,5},{38,6},{39,7},{40,8},{41... | collective-permute-start | bytes 196616 | tf_op jit(solution)/shard_map/ppermute | solution.py:358
  38.0 19.8 %collective-permute-start.14 = (bf16[32,12288]{1,0:T(8,128)(2,1)S(1)}, bf16[32,12288]{1,0:T(8,128)(2,1)S(1)}, u32[]{:S(2)}, u32[]{:S(2)}) collective-permute-start(bf16[32,12288]{1,0:T(8,128)(2,1)S(1)} %collective-permute-done.5.refs_1_.refs_2_), channel_id=1, source_target_pairs={{0,2},{1,9},{2,4},{3,11},{4,6},{5,13},{6,0},{7,15},{8,10},{9,17},{... | collective-permute-start | bytes 2359304 | tf_op jit(solution)/shard_map/ppermute | solution.py:37
  41.9 11.1 %collective-permute-start.15 = (bf16[32,12288]{1,0:T(8,128)(2,1)S(1)}, bf16[32,12288]{1,0:T(8,128)(2,1)S(1)}, u32[]{:S(2)}, u32[]{:S(2)}) collective-permute-start(bf16[32,12288]{1,0:T(8,128)(2,1)S(1)} %collective-permute-done.6.refs_5_), channel_id=1, source_target_pairs={{0,6},{1,25},{2,0},{3,27},{4,2},{5,29},{6,4},{7,31},{8,14},{9,1},{... | collective-permute-start | bytes 2359304 | tf_op jit(solution)/shard_map/ppermute | solution.py:37
  41.9 33.2 %copy-start.2 = (s32[256]{0:T(256)S(1)}, s32[256]{0:T(256)}, u32[]{:S(2)}) copy-start(s32[256]{0:T(256)} %piv_ref.3) | copy-start | bytes 3076
  47.0 5.0 %collective-permute-start.13 = (bf16[512,128]{1,0:T(8,128)(2,1)S(1)}, bf16[512,128]{1,0:T(8,128)(2,1)S(1)}, u32[]{:S(2)}, u32[]{:S(2)}) collective-permute-start(bf16[512,128]{1,0:T(8,128)(2,1)S(1)} %solve.1.a_ref), channel_id=1, source_target_pairs={{0,32},{1,33},{2,34},{3,35},{4,36},{5,37},{6,38},{7,39},{8,40},{9,... | collective-permute-start | bytes 393224 | tf_op jit(solution)/shard_map/ppermute | solution.py:358
  47.7 10.8 %collective-permute-start.19 = (bf16[32,12288]{1,0:T(8,128)(2,1)S(1)}, bf16[32,12288]{1,0:T(8,128)(2,1)S(1)}, u32[]{:S(2)}, u32[]{:S(2)}) collective-permute-start(bf16[32,12288]{1,0:T(8,128)(2,1)S(1)} %stack_b.1.refs_1_), channel_id=1, source_target_pairs={{0,1},{1,0},{2,3},{3,2},{4,5},{5,4},{6,7},{7,6},{8,9},{9,8},{10,11... | collective-permute-start | bytes 2359304 | tf_op jit(solution)/shard_map/ppermute | solution.py:37
  51.7 6.9 %collective-permute-start.18 = (bf16[32,12288]{1,0:T(8,128)(2,1)S(1)}, bf16[32,12288]{1,0:T(8,128)(2,1)S(1)}, u32[]{:S(2)}, u32[]{:S(2)}) collective-permute-start(bf16[32,12288]{1,0:T(8,128)(2,1)S(1)} %stack_a.1.refs_0_), channel_id=1, source_target_pairs={{0,1},{1,0},{2,3},{3,2},{4,5},{5,4},{6,7},{7,6},{8,9},{9,8},{10,11... | collective-permute-start | bytes 2359304 | tf_op jit(solution)/shard_map/ppermute | solution.py:37
  52.0 7.1 %collective-permute-start.23 = (bf16[32,12288]{1,0:T(8,128)(2,1)S(1)}, bf16[32,12288]{1,0:T(8,128)(2,1)S(1)}, u32[]{:S(2)}, u32[]{:S(2)}) collective-permute-start(bf16[32,12288]{1,0:T(8,128)(2,1)S(1)} %collective-permute-done.6.refs_5_), channel_id=1, source_target_pairs={{0,1},{1,0},{2,3},{3,2},{4,5},{5,4},{6,7},{7,6},{8,9},{9,8},{10,11... | collective-permute-start | bytes 2359304 | tf_op jit(solution)/shard_map/ppermute | solution.py:37
  53.0 6.7 %collective-permute-start.20 = (bf16[32,12288]{1,0:T(8,128)(2,1)S(1)}, bf16[32,12288]{1,0:T(8,128)(2,1)S(1)}, u32[]{:S(2)}, u32[]{:S(2)}) collective-permute-start(bf16[32,12288]{1,0:T(8,128)(2,1)S(1)} %collective-permute-done.5.refs_1_.refs_2_), channel_id=1, source_target_pairs={{0,1},{1,0},{2,3},{3,2},{4,5},{5,4},{6,7},{7,6},{8,9},{9,8},{10,11... | collective-permute-start | bytes 2359304 | tf_op jit(solution)/shard_map/ppermute | solution.py:37
  57.8 1.4 %collective-permute-start.16 = (bf16[512,128]{1,0:T(8,128)(2,1)S(1)}, bf16[512,128]{1,0:T(8,128)(2,1)S(1)}, u32[]{:S(2)}, u32[]{:S(2)}) collective-permute-start(bf16[512,128]{1,0:T(8,128)(2,1)S(1)} %choose.2.a_ref), channel_id=1, source_target_pairs={{0,64},{32,96},{1,65},{33,97},{2,66},{34,98},{3,67},{35,99},{4,68}... | collective-permute-start | bytes 393224 | tf_op jit(solution)/shard_map/ppermute | solution.py:358
  58.5 2.6 %collective-permute-start.21 = (bf16[32,12288]{1,0:T(8,128)(2,1)}, bf16[32,12288]{1,0:T(8,128)(2,1)S(1)}, u32[]{:S(2)}, u32[]{:S(2)}) collective-permute-start(bf16[32,12288]{1,0:T(8,128)(2,1)} %collective-permute-done.9.refs_3_), channel_id=1, source_target_pairs={{0,1},{1,0},{2,3},{3,2},{4,5},{5,4},{6,7},{7,6},{8,9},{9,8},{10,11... | collective-permute-start | bytes 2359304 | tf_op jit(solution)/shard_map/ppermute | solution.py:37
  58.6 4.7 %collective-permute-start.22 = (bf16[32,12288]{1,0:T(8,128)(2,1)}, bf16[32,12288]{1,0:T(8,128)(2,1)S(1)}, u32[]{:S(2)}, u32[]{:S(2)}) collective-permute-start(bf16[32,12288]{1,0:T(8,128)(2,1)} %collective-permute-done.10.refs_4_), channel_id=1, source_target_pairs={{0,1},{1,0},{2,3},{3,2},{4,5},{5,4},{6,7},{7,6},{8,9},{9,8},{10,11... | collective-permute-start | bytes 2359304 | tf_op jit(solution)/shard_map/ppermute | solution.py:37
  59.1 16.0 %collective-permute-start.24 = (bf16[32,12288]{1,0:T(8,128)(2,1)S(1)}, bf16[32,12288]{1,0:T(8,128)(2,1)S(1)}, u32[]{:S(2)}, u32[]{:S(2)}) collective-permute-start(bf16[32,12288]{1,0:T(8,128)(2,1)S(1)} %collective-permute-done.14.refs_6_), channel_id=1, source_target_pairs={{0,1},{1,0},{2,3},{3,2},{4,5},{5,4},{6,7},{7,6},{8,9},{9,8},{10,11... | collective-permute-start | bytes 2359304 | tf_op jit(solution)/shard_map/ppermute | solution.py:37
  59.2 15.9 %collective-permute-start.25 = (bf16[32,12288]{1,0:T(8,128)(2,1)S(1)}, bf16[32,12288]{1,0:T(8,128)(2,1)S(1)}, u32[]{:S(2)}, u32[]{:S(2)}) collective-permute-start(bf16[32,12288]{1,0:T(8,128)(2,1)S(1)} %collective-permute-done.15.refs_7_), channel_id=1, source_target_pairs={{0,1},{1,0},{2,3},{3,2},{4,5},{5,4},{6,7},{7,6},{8,9},{9,8},{10,11... | collective-permute-start | bytes 2359304 | tf_op jit(solution)/shard_map/ppermute | solution.py:37
  59.7 15.4 %collective-permute-start.17 = (bf16[512,128]{1,0:T(8,128)(2,1)S(1)}, bf16[512,128]{1,0:T(8,128)(2,1)S(1)}, u32[]{:S(2)}, u32[]{:S(2)}) collective-permute-start(bf16[512,128]{1,0:T(8,128)(2,1)S(1)} %choose.3.ud_ref), channel_id=1, source_target_pairs={{0,128},{32,160},{64,192},{96,224},{1,129},{33,161},{65,193},{97,2... | collective-permute-start | bytes 393224 | tf_op jit(solution)/shard_map/ppermute | solution.py:358

commit v4 on v3

--- a/solution.py
+++ b/solution.py
@@ -10,7 +10,7 @@
 NX = 4
 NY = 4
 OFFSETS = (0, -1, 1, 2)
-NBLK = 12
+NBLK = 6
 SMEM = pl.BlockSpec(memory_space=pltpu.SMEM)
 VMEM = pl.BlockSpec(memory_space=pltpu.VMEM)
 HIGHEST = lax.Precision.HIGHEST
@@ -49,7 +49,7 @@
     refs[-1][...] = jnp.concatenate([r[...] for r in refs[:-1]], axis=0)
 
 
-def stack(parts, start, cols, name):
+def stack(parts, start, cols, name, us=1):
     rows = sum(p.shape[0] for p in parts)
     step = min(cols, 4096)
     return pl.pallas_call(
@@ -59,6 +59,7 @@
         out_specs=pl.BlockSpec((rows, step), lambda i: (0, i)),
         out_shape=jax.ShapeDtypeStruct((rows, cols), jnp.bfloat16),
         compiler_params=params(6),
+        cost_estimate=cost(us),
         name=name,
     )(*parts)
 
@@ -78,25 +79,24 @@
     )(a, b)
 
 
-def choose_kernel(limit, first_ref, a_ref, b_ref, out_ref):
-    @pl.when(first_ref[0] < limit)
-    def _():
-        out_ref[...] = a_ref[...]
-
-    @pl.when(first_ref[0] >= limit)
-    def _():
-        out_ref[...] = b_ref[...]
-
-
-def choose(first, limit, a, b):
-    return pl.pallas_call(
-        functools.partial(choose_kernel, limit),
-        in_specs=[SMEM, VMEM, VMEM],
+def choose_kernel(rows, first_ref, *refs):
+    z = lax.div(first_ref[0], rows)
+    for k, ref in enumerate(refs[:-1]):
+
+        @pl.when((z >> 1) == k)
+        def _():
+            refs[-1][...] = ref[...]
+
+
+def choose(first, rows, parts):
+    return pl.pallas_call(
+        functools.partial(choose_kernel, rows),
+        in_specs=[SMEM] + [VMEM] * len(parts),
         out_specs=VMEM,
-        out_shape=jax.ShapeDtypeStruct(a.shape, a.dtype),
+        out_shape=jax.ShapeDtypeStruct(parts[0].shape, parts[0].dtype),
         compiler_params=params(2),
         name="choose",
-    )(first, a, b)
+    )(first, *parts)
 
 
 def pick_kernel(blk, piv_ref, first_ref, trailing_ref, out_ref, cnt_ref, lst_ref, own_ref, group_ref, rows_ref, sem):
@@ -261,9 +261,9 @@
     )(me, own, other, top, more, trailing)
 
 
-def update_kernel(nblk, late, cnt_ref, lst_ref, piv_ref, first_ref, me_ref, tr_ref, ud_ref, rest_ref, *refs):
-    parts = refs[:16]
-    out_ref, acc_ref, nat_ref, drow_ref, u_ref, tmp_ref = refs[16:]
+def update_kernel(nblk, cnt_ref, lst_ref, piv_ref, first_ref, me_ref, tr_ref, ud_ref, rest_ref, *refs):
+    parts = refs[1:11]
+    out_ref, acc_ref, nat_ref, drow_ref, u_ref, tmp_ref = refs[11:]
     blk = out_ref.shape[0]
     width = nat_ref.shape[0]
     b = pl.program_id(0)
@@ -271,12 +271,14 @@
 
     @pl.when(b == 0)
     def _():
-        @pl.when(first < late)
+        odd = lax.div(first, nblk * blk) & 1
+
+        @pl.when(odd == 0)
         def _():
             nat_ref[...] = ud_ref[:width, :].astype(jnp.float32)
             drow_ref[...] = ud_ref[width:, :].astype(jnp.float32)
 
-        @pl.when(first >= late)
+        @pl.when(odd == 1)
         def _():
             nat_ref[...] = rest_ref[:width, :].astype(jnp.float32)
             drow_ref[...] = rest_ref[width:, :].astype(jnp.float32)
@@ -286,8 +288,11 @@
         u_ref[...] = tmp_ref[...].astype(jnp.bfloat16)
 
     def compute(half):
-        here = pl.ds(pl.multiple_of((b - half * (nblk // 2)) * blk, 128), blk)
-        pieces = [r[:, here] for r in parts[half::2]]
+        here = pl.ds(pl.multiple_of(b * blk, 128), blk)
+        there = pl.ds(pl.multiple_of((b - half * (nblk // 2)) * blk, 128), blk)
+        pieces = []
+        for s in (parts[:5], parts[5:]):
+            pieces += [s[0][:, here], s[1][:, here], s[2][:, here], s[3 + half][:, there]]
         acc_ref[...] = lax.dot_general(
             jnp.concatenate(pieces, axis=0), u_ref[...], (((0,), (0,)), ((), ())),
             preferred_element_type=jnp.float32,
@@ -320,16 +325,16 @@
         out_ref[:width, :] = nat_ref[...].astype(jnp.bfloat16)
 
 
-def update(cnt, lst, pivots, first, me, trailing, ud, rest, parts, blk):
+def update(cnt, lst, pivots, first, me, trailing, ud, rest, ahead, parts, blk):
     rows, cols = trailing.shape
     width = pivots.shape[0]
     nblk = rows // blk
     tall = pl.BlockSpec((blk, cols), lambda b: (b, 0))
     pair = pl.BlockSpec((2 * width, cols), lambda b: (0, 0))
     return pl.pallas_call(
-        functools.partial(update_kernel, nblk, 4 * rows),
+        functools.partial(update_kernel, nblk),
         grid=(nblk,),
-        in_specs=[SMEM] * 5 + [tall, pair, pair] + [VMEM] * 16,
+        in_specs=[SMEM] * 5 + [tall, pair, pair] + [VMEM] * 11,
         out_specs=tall,
         scratch_shapes=[
             pltpu.VMEM((blk, cols), jnp.float32),
@@ -339,9 +344,9 @@
             pltpu.VMEM((width, cols), jnp.float32),
         ],
         out_shape=jax.ShapeDtypeStruct((rows, cols), jnp.bfloat16),
-        compiler_params=params(12),
+        compiler_params=params(16),
         name="update",
-    )(cnt, lst, pivots, first, me, trailing, ud, rest, *parts)
+    )(cnt, lst, pivots, first, me, trailing, ud, rest, ahead, *parts)
 
 
 def body(trailing, panel_t, pivots):
@@ -360,41 +365,36 @@
     p, m, q = [send(panel_t, hop(d, 0, True)) for d in (1, -1, 2)]
 
     top, cnt, lst = pick(trailing, pivots, first, blk)
+    more = zsend(top, [(1, 0), (3, 2), (5, 4), (7, 6)])
+    top = add(top, more)
     p, m, q, top = barrier((p, m, q, top))
-    more = zsend(top, [(i + 4, i) for i in range(4)])
+    more = zsend(top, [(2, 0), (6, 4)])
 
     up, down, across = hop(0, 1, True), hop(0, -1, True), hop(0, 2, True)
     diag = stack([panel_t, p, m, q], 0, width, "stack_d")
-    diag_q, diag_m = send(diag, across), send(diag, down)
-    p, m, q, diag_q = barrier((p, m, q, diag_q))
-    xa = stack([panel_t, p, m, q], 0, half, "stack_a")
-    p, m, q, diag_m, xa = barrier((p, m, q, diag_m, xa))
-    xb = stack([panel_t, p, m, q], half, half, "stack_b")
-    pa, mb = send(xa, up), send(xb, down)
+    diag_q, diag_p, diag_m = send(diag, across), send(diag, up), send(diag, down)
     top = add(top, more)
-    xa, xb, top = barrier((xa, xb, top))
-    pb, ma = send(xb, up), send(xa, down)
-    more = zsend(top, [(2, 0), (3, 1)])
-    oxa, oxb = send(xa, CORES), send(xb, CORES)
-    pa, mb, diag_q, diag_m = barrier((pa, mb, diag_q, diag_m))
-    qa, qb = send(pa, up), send(mb, down)
-    own = stack([diag, pa, diag_m, diag_q], 0, width, "stack_l")
+    p, m, q, diag_q, diag_p, diag_m, top = barrier((p, m, q, diag_q, diag_p, diag_m, top))
+    more = zsend(top, [(4, 0)])
+    block = stack([panel_t, p, m, q], 0, rows, "stack_p")
+    near, far = send(block, up), send(block, down)
+    own = stack([diag, diag_p, diag_m, diag_q], 0, width, "stack_l")
     other = send(own, CORES)
-    opa, omb = send(pa, CORES), send(mb, CORES)
-    top = add(top, more)
-    more = zsend(top, [(1, 0)])
-
-    other, pb, ma = barrier((other, pb, ma))
     ud = solve(me, own, other, top, more, trailing)
-    opb, oma = send(pb, CORES), send(ma, CORES)
-    ud = choose(first, rows, ud, zsend(ud, [(0, 1)]))
-    ud, qa, qb = barrier((ud, qa, qb))
-    oqa, oqb = send(qa, CORES), send(qb, CORES)
-    ud = choose(first, 2 * rows, ud, zsend(ud, [(0, 2), (1, 3)]))
-    rest = zsend(ud, [(i, i + 4) for i in range(4)])
-
-    parts = [xa, xb, pa, pb, ma, mb, qa, qb, oxa, oxb, opa, opb, oma, omb, oqa, oqb]
-    return update(cnt, lst, pivots, first, me, trailing, ud, rest, parts, blk)
+    swap = send(block, CORES)
+    ud, near, far, swap = barrier((ud, near, far, swap))
+    fa, fb = stack([near], 0, half, "stack_a"), stack([far], half, half, "stack_b")
+    qa, qb = send(fa, up), send(fb, down)
+
+    spread = [zsend(ud, [(0, d)]) for d in (2, 4, 6)]
+    ud = choose(first, rows, [ud] + spread)
+    ud, near, far = barrier((ud, near, far))
+    rest = zsend(ud, [(0, 1), (2, 3), (4, 5), (6, 7)])
+    other_near, other_far = send(near, CORES), send(far, CORES)
+    ahead = stack([qa, qb], 0, 128, "stack_q", 30)
+    own = [block, near, far, qa, qb]
+    parts = own + [swap, other_near, other_far, send(qa, CORES), send(qb, CORES)]
+    return update(cnt, lst, pivots, first, me, trailing, ud, rest, ahead, parts, blk)
 
 
 def solution(mesh):

time: 89.5 us -> 93.1 us (1.040)
  the two profiles are of different devices: /device:TPU:225 before, /device:TPU:1 now
where the time goes in v4:
time: 93.1 us; the launch traced here: 92.6 us
  starting transfers between devices  40.8 us (44%)
  waiting for transfers between devices  30.9 us (33%)
  Pallas kernels  19.9 us (21%)
    ppermute x16, starting transfers between devices, send(): return lax.ppermute(block, 'pcol', pairs)  23.4 us
    ppermute x7, starting transfers between devices, zsend(): return lax.ppermute(x, 'prow', pairs)  17.5 us
    ppermute x16, waiting for transfers between devices, send(): return lax.ppermute(block, 'pcol', pairs)  17.5 us
    ppermute x7, waiting for transfers between devices, zsend(): return lax.ppermute(x, 'prow', pairs)  13.4 us
    pallas_call x1, Pallas kernels, update(): pl.pallas_call(functools.partial(update_kernel, nblk), grid=(nblk,), in_s...  10.2 us
    pallas_call x1, Pallas kernels, solve(): pl.pallas_call(solve_kernel, grid=(1,), in_specs=[SMEM, whole, whole, tal...  5.09 us
    pallas_call x1, Pallas kernels, pick(): pl.pallas_call(functools.partial(pick_kernel, blk), in_specs=[SMEM, SMEM,...  3.69 us
  transfers between devices with their start and end apart: 23, of which 11 were waited for; matrix products, arithmetic and copies ran while one was open for 0% of the time, Pallas kernels for 10%

profile of v4, /device:TPU:1, one launch (start us, length us, event | category | flops | bytes accessed | tf_op | source)
XLA Modules:
  0.0 92.6 jit_solution(14000800788998968500)
XLA Ops:
  0.0 3.7 %collective-permute-start.2 = (bf16[8,24576]{1,0:T(8,128)(2,1)}, bf16[8,24576]{1,0:T(8,128)(2,1)S(1)}, u32[]{:S(2)}, u32[]{:S(2)}) collective-permute-start(bf16[8,24576]{1,0:T(8,128)(2,1)} %refs_0_.3), channel_id=1, source_target_pairs={{0,16},{1,5},{2,18},{3,7},{4,20},{5,1},{6,22},{7,3},{8,24},{9,13},... | collective-permute-start | bytes 1179656 | tf_op jit(solution)/shard_map/ppermute | solution.py:37
  3.7 0.8 collective-permute-start.1
  4.5 0.7 collective-permute-start
  5.2 0.7 copy-done
  5.9 3.7 %pick.1 = (bf16[256,128]{1,0:T(8,128)(2,1)S(1)}, s32[6]{0:T(128)S(1)}, s32[1536]{0:T(1024)S(1)}) custom-call(s32[256]{0:T(256)S(1)} %copy-done, s32[1]{0:T(128)} %bitcast.first_ref, bf16[24576,128]{1,0:T(8,128)(2,1)} %tr_ref.1), custom_call_target="tpu_custom_call" | custom-call | flops 13200000000 | bytes 42000000 | tf_op jit(solution)/shard_map/pick/pallas_call | solution.py:156
  9.6 1.3 %collective-permute-start.3 = (bf16[256,128]{1,0:T(8,128)(2,1)S(1)}, bf16[256,128]{1,0:T(8,128)(2,1)S(1)}, u32[]{:S(2)}, u32[]{:S(2)}) collective-permute-start(bf16[256,128]{1,0:T(8,128)(2,1)S(1)} %get-tuple-element.28.a_ref), channel_id=1, source_target_pairs={{32,0},{96,64},{160,128},{224,192},{33,1},{97,65},{161,129},{225,1... | collective-permute-start | bytes 196616 | tf_op jit(solution)/shard_map/ppermute | solution.py:363
  10.9 4.0 %collective-permute-done.3.b_ref = bf16[256,128]{1,0:T(8,128)(2,1)S(1)} collective-permute-done((bf16[256,128]{1,0:T(8,128)(2,1)S(1)}, bf16[256,128]{1,0:T(8,128)(2,1)S(1)}, u32[]{:S(2)}, u32[]{:S(2)}) %collective-permute-start.3) | collective-permute-done | bytes 65568 | tf_op jit(solution)/shard_map/ppermute | solution.py:363
  14.9 0.0 collective-permute-done.2.refs_3_
  14.9 0.0 collective-permute-done.1.refs_2_
  14.9 1.3 %collective-permute-start.7 = (bf16[256,128]{1,0:T(8,128)(2,1)S(1)}, bf16[256,128]{1,0:T(8,128)(2,1)S(1)}, u32[]{:S(2)}, u32[]{:S(2)}) collective-permute-start(bf16[256,128]{1,0:T(8,128)(2,1)S(1)} %add.2.a_ref), channel_id=1, source_target_pairs={{64,0},{192,128},{65,1},{193,129},{66,2},{194,130},{67,3},{195,131... | collective-permute-start | bytes 196616 | tf_op jit(solution)/shard_map/ppermute | solution.py:363
  16.3 2.5 %collective-permute-start.6 = (bf16[32,256]{1,0:T(8,128)(2,1)S(1)}, bf16[32,256]{1,0:T(8,128)(2,1)S(1)}, u32[]{:S(2)}, u32[]{:S(2)}) collective-permute-start(bf16[32,256]{1,0:T(8,128)(2,1)S(1)} %stack_d.1.refs_0_), channel_id=1, source_target_pairs={{0,6},{1,25},{2,0},{3,27},{4,2},{5,29},{6,4},{7,31},{8,14},{9,1},{... | collective-permute-start | bytes 49160 | tf_op jit(solution)/shard_map/ppermute | solution.py:37
  18.8 0.0 collective-permute-start.5
  18.8 1.7 %collective-permute-start.4 = (bf16[32,256]{1,0:T(8,128)(2,1)S(1)}, bf16[32,256]{1,0:T(8,128)(2,1)S(1)}, u32[]{:S(2)}, u32[]{:S(2)}) collective-permute-start(bf16[32,256]{1,0:T(8,128)(2,1)S(1)} %stack_d.1.refs_0_), channel_id=1, source_target_pairs={{0,4},{1,17},{2,6},{3,19},{4,0},{5,21},{6,2},{7,23},{8,12},{9,25},... | collective-permute-start | bytes 49160 | tf_op jit(solution)/shard_map/ppermute | solution.py:37
  20.5 0.4 collective-permute-done.7.b_ref
  20.9 0.0 collective-permute-done.6.refs_2_
  21.0 1.6 %collective-permute-done.5.refs_1_ = bf16[32,256]{1,0:T(8,128)(2,1)S(1)} collective-permute-done((bf16[32,256]{1,0:T(8,128)(2,1)S(1)}, bf16[32,256]{1,0:T(8,128)(2,1)S(1)}, u32[]{:S(2)}, u32[]{:S(2)}) %collective-permute-start.5) | collective-permute-done | bytes 16416 | tf_op jit(solution)/shard_map/ppermute | solution.py:37
  22.6 0.3 collective-permute-done.4.refs_3_
  22.9 4.0 %collective-permute-start.8 = (bf16[128,256]{1,0:T(8,128)(2,1)S(1)}, bf16[128,256]{1,0:T(8,128)(2,1)S(1)}, u32[]{:S(2)}, u32[]{:S(2)}) collective-permute-start(bf16[128,256]{1,0:T(8,128)(2,1)S(1)} %stack_l.1.own_ref), channel_id=1, source_target_pairs={{0,1},{1,0},{2,3},{3,2},{4,5},{5,4},{6,7},{7,6},{8,9},{9,8},{10,11... | collective-permute-start | bytes 196616 | tf_op jit(solution)/shard_map/ppermute | solution.py:37
  26.8 1.3 %collective-permute-start.9 = (bf16[256,128]{1,0:T(8,128)(2,1)S(1)}, bf16[256,128]{1,0:T(8,128)(2,1)S(1)}, u32[]{:S(2)}, u32[]{:S(2)}) collective-permute-start(bf16[256,128]{1,0:T(8,128)(2,1)S(1)} %add.3.top_ref), channel_id=1, source_target_pairs={{128,0},{129,1},{130,2},{131,3},{132,4},{133,5},{134,6},{135,7},{1... | collective-permute-start | bytes 196616 | tf_op jit(solution)/shard_map/ppermute | solution.py:363
  28.1 0.4 stack_p.1.refs_1_
  28.6 0.1 collective-permute-start.12
  28.7 2.1 %collective-permute-start.11 = (bf16[32,24576]{1,0:T(8,128)(2,1)S(1)}, bf16[32,24576]{1,0:T(8,128)(2,1)S(1)}, u32[]{:S(2)}, u32[]{:S(2)}) collective-permute-start(bf16[32,24576]{1,0:T(8,128)(2,1)S(1)} %stack_p.1.refs_1_), channel_id=1, source_target_pairs={{0,6},{1,25},{2,0},{3,27},{4,2},{5,29},{6,4},{7,31},{8,14},{9,1},{... | collective-permute-start | bytes 4718600 | tf_op jit(solution)/shard_map/ppermute | solution.py:37
  30.8 0.0 collective-permute-start.10
  30.8 0.0 collective-permute-done.8.other_ref
  30.8 7.0 %collective-permute-done.9.more_ref = bf16[256,128]{1,0:T(8,128)(2,1)S(1)} collective-permute-done((bf16[256,128]{1,0:T(8,128)(2,1)S(1)}, bf16[256,128]{1,0:T(8,128)(2,1)S(1)}, u32[]{:S(2)}, u32[]{:S(2)}) %collective-permute-start.9) | collective-permute-done | bytes 65568 | tf_op jit(solution)/shard_map/ppermute | solution.py:363
  37.8 5.1 %solve.1.refs_0_ = bf16[512,128]{1,0:T(8,128)(2,1)S(1)} custom-call(s32[1]{0:T(128)} %bitcast.1.me_ref, bf16[128,256]{1,0:T(8,128)(2,1)S(1)} %stack_l.1.own_ref, bf16[128,256]{1,0:T(8,128)(2,1)S(1)} %collective-permute-done.8.other_ref, bf16[256,128]{1,0:T(8,128)(2,1)S(1)} %add.3.top_ref, bf16[256,128]{1,0:T(8,128)(2,1)S(1)} %collective-permute-done.9.more_ref, ...), custom_call_target="tpu_custom_call" | custom-call | flops 22000001024 | bytes 70000000 | tf_op jit(solution)/shard_map/solve/pallas_call | solution.py:251
  42.9 0.0 collective-permute-done.12.refs_6_
  42.9 5.4 %collective-permute-done.11.refs_0_.refs_3_ = bf16[32,24576]{1,0:T(8,128)(2,1)S(1)} collective-permute-done((bf16[32,24576]{1,0:T(8,128)(2,1)S(1)}, bf16[32,24576]{1,0:T(8,128)(2,1)S(1)}, u32[]{:S(2)}, u32[]{:S(2)}) %collective-permute-start.11) | collective-permute-done | bytes 1572896 | tf_op jit(solution)/shard_map/ppermute | solution.py:37
  48.3 3.3 %collective-permute-done.10.refs_0_.refs_2_ = bf16[32,24576]{1,0:T(8,128)(2,1)S(1)} collective-permute-done((bf16[32,24576]{1,0:T(8,128)(2,1)S(1)}, bf16[32,24576]{1,0:T(8,128)(2,1)S(1)}, u32[]{:S(2)}, u32[]{:S(2)}) %collective-permute-start.10) | collective-permute-done | bytes 1572896 | tf_op jit(solution)/shard_map/ppermute | solution.py:37
  51.6 0.2 stack_b.1
  51.8 0.1 collective-permute-start.18
  51.9 0.2 stack_a.1
  52.2 1.5 %collective-permute-start.17 = (bf16[32,12288]{1,0:T(8,128)(2,1)S(1)}, bf16[32,12288]{1,0:T(8,128)(2,1)S(1)}, u32[]{:S(2)}, u32[]{:S(2)}) collective-permute-start(bf16[32,12288]{1,0:T(8,128)(2,1)S(1)} %stack_a.1), channel_id=1, source_target_pairs={{0,2},{1,9},{2,4},{3,11},{4,6},{5,13},{6,0},{7,15},{8,10},{9,17},{... | collective-permute-start | bytes 2359304 | tf_op jit(solution)/shard_map/ppermute | solution.py:37
  53.7 9.7 %collective-permute-start.15 = (bf16[512,128]{1,0:T(8,128)(2,1)S(1)}, bf16[512,128]{1,0:T(8,128)(2,1)S(1)}, u32[]{:S(2)}, u32[]{:S(2)}) collective-permute-start(bf16[512,128]{1,0:T(8,128)(2,1)S(1)} %solve.1.refs_0_), channel_id=1, source_target_pairs={{0,192},{1,193},{2,194},{3,195},{4,196},{5,197},{6,198},{7,199},{8... | collective-permute-start | bytes 393224 | tf_op jit(solution)/shard_map/ppermute | solution.py:363
  63.4 1.3 %collective-permute-start.14 = (bf16[512,128]{1,0:T(8,128)(2,1)S(1)}, bf16[512,128]{1,0:T(8,128)(2,1)S(1)}, u32[]{:S(2)}, u32[]{:S(2)}) collective-permute-start(bf16[512,128]{1,0:T(8,128)(2,1)S(1)} %solve.1.refs_0_), channel_id=1, source_target_pairs={{0,128},{1,129},{2,130},{3,131},{4,132},{5,133},{6,134},{7,135},{8... | collective-permute-start | bytes 393224 | tf_op jit(solution)/shard_map/ppermute | solution.py:363
  64.7 1.3 %collective-permute-start.13 = (bf16[512,128]{1,0:T(8,128)(2,1)S(1)}, bf16[512,128]{1,0:T(8,128)(2,1)S(1)}, u32[]{:S(2)}, u32[]{:S(2)}) collective-permute-start(bf16[512,128]{1,0:T(8,128)(2,1)S(1)} %solve.1.refs_0_), channel_id=1, source_target_pairs={{0,64},{1,65},{2,66},{3,67},{4,68},{5,69},{6,70},{7,71},{8,72},{9,... | collective-permute-start | bytes 393224 | tf_op jit(solution)/shard_map/ppermute | solution.py:363
  66.0 0.6 collective-permute-done.14.refs_2_
  66.6 1.4 %collective-permute-done.13.refs_1_ = bf16[512,128]{1,0:T(8,128)(2,1)S(1)} collective-permute-done((bf16[512,128]{1,0:T(8,128)(2,1)S(1)}, bf16[512,128]{1,0:T(8,128)(2,1)S(1)}, u32[]{:S(2)}, u32[]{:S(2)}) %collective-permute-start.13) | collective-permute-done | bytes 131104 | tf_op jit(solution)/shard_map/ppermute | solution.py:363
  68.0 0.0 copy-start.1
  68.0 1.3 %collective-permute-start.16 = (bf16[512,128]{1,0:T(8,128)(2,1)S(1)}, bf16[512,128]{1,0:T(8,128)(2,1)S(1)}, u32[]{:S(2)}, u32[]{:S(2)}) collective-permute-start(bf16[512,128]{1,0:T(8,128)(2,1)S(1)} %choose.1.ud_ref), channel_id=1, source_target_pairs={{0,32},{64,96},{128,160},{192,224},{1,33},{65,97},{129,161},{193,2... | collective-permute-start | bytes 393224 | tf_op jit(solution)/shard_map/ppermute | solution.py:363
  69.4 5.5 %collective-permute-start.19 = (bf16[32,24576]{1,0:T(8,128)(2,1)S(1)}, bf16[32,24576]{1,0:T(8,128)(2,1)S(1)}, u32[]{:S(2)}, u32[]{:S(2)}) collective-permute-start(bf16[32,24576]{1,0:T(8,128)(2,1)S(1)} %collective-permute-done.10.refs_0_.refs_2_), channel_id=1, source_target_pairs={{0,1},{1,0},{2,3},{3,2},{4,5},{5,4},{6,7},{7,6},{8,9},{9,8},{10,11... | collective-permute-start | bytes 4718600 | tf_op jit(solution)/shard_map/ppermute | solution.py:37
  74.9 0.1 collective-permute-start.20
  75.0 0.0 collective-permute-done.18.refs_1_.refs_5_
  75.0 0.4 collective-permute-start.22
  75.4 0.1 collective-permute-start.21
  75.5 5.8 %collective-permute-done.22.refs_10_ = bf16[32,12288]{1,0:T(8,128)(2,1)S(1)} collective-permute-done((bf16[32,12288]{1,0:T(8,128)(2,1)S(1)}, bf16[32,12288]{1,0:T(8,128)(2,1)S(1)}, u32[]{:S(2)}, u32[]{:S(2)}) %collective-permute-start.22) | collective-permute-done | bytes 786464 | tf_op jit(solution)/shard_map/ppermute | solution.py:37
  81.3 1.1 %collective-permute-done.21.refs_9_ = bf16[32,12288]{1,0:T(8,128)(2,1)S(1)} collective-permute-done((bf16[32,12288]{1,0:T(8,128)(2,1)S(1)}, bf16[32,12288]{1,0:T(8,128)(2,1)S(1)}, u32[]{:S(2)}, u32[]{:S(2)}) %collective-permute-start.21) | collective-permute-done | bytes 786464 | tf_op jit(solution)/shard_map/ppermute | solution.py:37
  82.4 10.2 %update.1 = bf16[24576,128]{1,0:T(8,128)(2,1)} custom-call(s32[6]{0:T(128)S(1)} %get-tuple-element.26.cnt_ref, s32[1536]{0:T(1024)S(1)} %get-tuple-element.27.lst_ref, s32[256]{0:T(256)S(1)} %copy-done.1, s32[1]{0:T(128)} %bitcast.first_ref, s32[1]{0:T(128)} %bitcast.1.me_ref, bf16[24576,128]{1,0:T(8,128)(2,1)} %tr_ref.1, ...), custom_call_target="tpu_custom_call" | custom-call | tf_op jit(solution)/shard_map/update/pallas_call | solution.py:334
  (16 shorter events, 0.1 us)
Async XLA Ops:
  0.0 14.9 %collective-permute-start.2 = (bf16[8,24576]{1,0:T(8,128)(2,1)}, bf16[8,24576]{1,0:T(8,128)(2,1)S(1)}, u32[]{:S(2)}, u32[]{:S(2)}) collective-permute-start(bf16[8,24576]{1,0:T(8,128)(2,1)} %refs_0_.3), channel_id=1, source_target_pairs={{0,16},{1,5},{2,18},{3,7},{4,20},{5,1},{6,22},{7,3},{8,24},{9,13},... | collective-permute-start | bytes 1179656 | tf_op jit(solution)/shard_map/ppermute | solution.py:37
  3.7 11.2 %collective-permute-start.1 = (bf16[8,24576]{1,0:T(8,128)(2,1)}, bf16[8,24576]{1,0:T(8,128)(2,1)S(1)}, u32[]{:S(2)}, u32[]{:S(2)}) collective-permute-start(bf16[8,24576]{1,0:T(8,128)(2,1)} %refs_0_.3), channel_id=1, source_target_pairs={{0,24},{1,7},{2,26},{3,1},{4,28},{5,3},{6,30},{7,5},{8,0},{9,15},{... | collective-permute-start | bytes 1179656 | tf_op jit(solution)/shard_map/ppermute | solution.py:37
  4.5 10.4 %collective-permute-start = (bf16[8,24576]{1,0:T(8,128)(2,1)}, bf16[8,24576]{1,0:T(8,128)(2,1)S(1)}, u32[]{:S(2)}, u32[]{:S(2)}) collective-permute-start(bf16[8,24576]{1,0:T(8,128)(2,1)} %refs_0_.3), channel_id=1, source_target_pairs={{0,8},{1,3},{2,10},{3,5},{4,12},{5,7},{6,14},{7,1},{8,16},{9,11},{... | collective-permute-start | bytes 1179656 | tf_op jit(solution)/shard_map/ppermute | solution.py:37
  5.2 0.7 copy-start
  5.9 10.4 %copy-start.2 = (bf16[8,24576]{1,0:T(8,128)(2,1)S(1)}, bf16[8,24576]{1,0:T(8,128)(2,1)}, u32[]{:S(2)}) copy-start(bf16[8,24576]{1,0:T(8,128)(2,1)} %refs_0_.3) | copy-start | bytes 1179652
  9.6 5.3 %collective-permute-start.3 = (bf16[256,128]{1,0:T(8,128)(2,1)S(1)}, bf16[256,128]{1,0:T(8,128)(2,1)S(1)}, u32[]{:S(2)}, u32[]{:S(2)}) collective-permute-start(bf16[256,128]{1,0:T(8,128)(2,1)S(1)} %get-tuple-element.28.a_ref), channel_id=1, source_target_pairs={{32,0},{96,64},{160,128},{224,192},{33,1},{97,65},{161,129},{225,1... | collective-permute-start | bytes 196616 | tf_op jit(solution)/shard_map/ppermute | solution.py:363
  14.9 6.0 %collective-permute-start.7 = (bf16[256,128]{1,0:T(8,128)(2,1)S(1)}, bf16[256,128]{1,0:T(8,128)(2,1)S(1)}, u32[]{:S(2)}, u32[]{:S(2)}) collective-permute-start(bf16[256,128]{1,0:T(8,128)(2,1)S(1)} %add.2.a_ref), channel_id=1, source_target_pairs={{64,0},{192,128},{65,1},{193,129},{66,2},{194,130},{67,3},{195,131... | collective-permute-start | bytes 196616 | tf_op jit(solution)/shard_map/ppermute | solution.py:363
  16.3 4.7 %collective-permute-start.6 = (bf16[32,256]{1,0:T(8,128)(2,1)S(1)}, bf16[32,256]{1,0:T(8,128)(2,1)S(1)}, u32[]{:S(2)}, u32[]{:S(2)}) collective-permute-start(bf16[32,256]{1,0:T(8,128)(2,1)S(1)} %stack_d.1.refs_0_), channel_id=1, source_target_pairs={{0,6},{1,25},{2,0},{3,27},{4,2},{5,29},{6,4},{7,31},{8,14},{9,1},{... | collective-permute-start | bytes 49160 | tf_op jit(solution)/shard_map/ppermute | solution.py:37
  18.8 3.8 %collective-permute-start.5 = (bf16[32,256]{1,0:T(8,128)(2,1)S(1)}, bf16[32,256]{1,0:T(8,128)(2,1)S(1)}, u32[]{:S(2)}, u32[]{:S(2)}) collective-permute-start(bf16[32,256]{1,0:T(8,128)(2,1)S(1)} %stack_d.1.refs_0_), channel_id=1, source_target_pairs={{0,2},{1,9},{2,4},{3,11},{4,6},{5,13},{6,0},{7,15},{8,10},{9,17},{... | collective-permute-start | bytes 49160 | tf_op jit(solution)/shard_map/ppermute | solution.py:37
  18.8 4.1 %collective-permute-start.4 = (bf16[32,256]{1,0:T(8,128)(2,1)S(1)}, bf16[32,256]{1,0:T(8,128)(2,1)S(1)}, u32[]{:S(2)}, u32[]{:S(2)}) collective-permute-start(bf16[32,256]{1,0:T(8,128)(2,1)S(1)} %stack_d.1.refs_0_), channel_id=1, source_target_pairs={{0,4},{1,17},{2,6},{3,19},{4,0},{5,21},{6,2},{7,23},{8,12},{9,25},... | collective-permute-start | bytes 49160 | tf_op jit(solution)/shard_map/ppermute | solution.py:37
  22.9 8.0 %collective-permute-start.8 = (bf16[128,256]{1,0:T(8,128)(2,1)S(1)}, bf16[128,256]{1,0:T(8,128)(2,1)S(1)}, u32[]{:S(2)}, u32[]{:S(2)}) collective-permute-start(bf16[128,256]{1,0:T(8,128)(2,1)S(1)} %stack_l.1.own_ref), channel_id=1, source_target_pairs={{0,1},{1,0},{2,3},{3,2},{4,5},{5,4},{6,7},{7,6},{8,9},{9,8},{10,11... | collective-permute-start | bytes 196616 | tf_op jit(solution)/shard_map/ppermute | solution.py:37
  26.8 11.0 %collective-permute-start.9 = (bf16[256,128]{1,0:T(8,128)(2,1)S(1)}, bf16[256,128]{1,0:T(8,128)(2,1)S(1)}, u32[]{:S(2)}, u32[]{:S(2)}) collective-permute-start(bf16[256,128]{1,0:T(8,128)(2,1)S(1)} %add.3.top_ref), channel_id=1, source_target_pairs={{128,0},{129,1},{130,2},{131,3},{132,4},{133,5},{134,6},{135,7},{1... | collective-permute-start | bytes 196616 | tf_op jit(solution)/shard_map/ppermute | solution.py:363
  28.6 14.4 %collective-permute-start.12 = (bf16[32,24576]{1,0:T(8,128)(2,1)S(1)}, bf16[32,24576]{1,0:T(8,128)(2,1)S(1)}, u32[]{:S(2)}, u32[]{:S(2)}) collective-permute-start(bf16[32,24576]{1,0:T(8,128)(2,1)S(1)} %stack_p.1.refs_1_), channel_id=1, source_target_pairs={{0,1},{1,0},{2,3},{3,2},{4,5},{5,4},{6,7},{7,6},{8,9},{9,8},{10,11... | collective-permute-start | bytes 4718600 | tf_op jit(solution)/shard_map/ppermute | solution.py:37
  28.7 19.6 %collective-permute-start.11 = (bf16[32,24576]{1,0:T(8,128)(2,1)S(1)}, bf16[32,24576]{1,0:T(8,128)(2,1)S(1)}, u32[]{:S(2)}, u32[]{:S(2)}) collective-permute-start(bf16[32,24576]{1,0:T(8,128)(2,1)S(1)} %stack_p.1.refs_1_), channel_id=1, source_target_pairs={{0,6},{1,25},{2,0},{3,27},{4,2},{5,29},{6,4},{7,31},{8,14},{9,1},{... | collective-permute-start | bytes 4718600 | tf_op jit(solution)/shard_map/ppermute | solution.py:37
  30.8 20.8 %collective-permute-start.10 = (bf16[32,24576]{1,0:T(8,128)(2,1)S(1)}, bf16[32,24576]{1,0:T(8,128)(2,1)S(1)}, u32[]{:S(2)}, u32[]{:S(2)}) collective-permute-start(bf16[32,24576]{1,0:T(8,128)(2,1)S(1)} %stack_p.1.refs_1_), channel_id=1, source_target_pairs={{0,2},{1,9},{2,4},{3,11},{4,6},{5,13},{6,0},{7,15},{8,10},{9,17},{... | collective-permute-start | bytes 4718600 | tf_op jit(solution)/shard_map/ppermute | solution.py:37
  51.8 23.2 %collective-permute-start.18 = (bf16[32,12288]{1,0:T(8,128)(2,1)S(1)}, bf16[32,12288]{1,0:T(8,128)(2,1)S(1)}, u32[]{:S(2)}, u32[]{:S(2)}) collective-permute-start(bf16[32,12288]{1,0:T(8,128)(2,1)S(1)} %stack_b.1), channel_id=1, source_target_pairs={{0,6},{1,25},{2,0},{3,27},{4,2},{5,29},{6,4},{7,31},{8,14},{9,1},{... | collective-permute-start | bytes 2359304 | tf_op jit(solution)/shard_map/ppermute | solution.py:37
  52.2 23.2 %collective-permute-start.17 = (bf16[32,12288]{1,0:T(8,128)(2,1)S(1)}, bf16[32,12288]{1,0:T(8,128)(2,1)S(1)}, u32[]{:S(2)}, u32[]{:S(2)}) collective-permute-start(bf16[32,12288]{1,0:T(8,128)(2,1)S(1)} %stack_a.1), channel_id=1, source_target_pairs={{0,2},{1,9},{2,4},{3,11},{4,6},{5,13},{6,0},{7,15},{8,10},{9,17},{... | collective-permute-start | bytes 2359304 | tf_op jit(solution)/shard_map/ppermute | solution.py:37
  53.7 12.3 %collective-permute-start.15 = (bf16[512,128]{1,0:T(8,128)(2,1)S(1)}, bf16[512,128]{1,0:T(8,128)(2,1)S(1)}, u32[]{:S(2)}, u32[]{:S(2)}) collective-permute-start(bf16[512,128]{1,0:T(8,128)(2,1)S(1)} %solve.1.refs_0_), channel_id=1, source_target_pairs={{0,192},{1,193},{2,194},{3,195},{4,196},{5,197},{6,198},{7,199},{8... | collective-permute-start | bytes 393224 | tf_op jit(solution)/shard_map/ppermute | solution.py:363
  63.4 3.2 %collective-permute-start.14 = (bf16[512,128]{1,0:T(8,128)(2,1)S(1)}, bf16[512,128]{1,0:T(8,128)(2,1)S(1)}, u32[]{:S(2)}, u32[]{:S(2)}) collective-permute-start(bf16[512,128]{1,0:T(8,128)(2,1)S(1)} %solve.1.refs_0_), channel_id=1, source_target_pairs={{0,128},{1,129},{2,130},{3,131},{4,132},{5,133},{6,134},{7,135},{8... | collective-permute-start | bytes 393224 | tf_op jit(solution)/shard_map/ppermute | solution.py:363
  64.7 3.3 %collective-permute-start.13 = (bf16[512,128]{1,0:T(8,128)(2,1)S(1)}, bf16[512,128]{1,0:T(8,128)(2,1)S(1)}, u32[]{:S(2)}, u32[]{:S(2)}) collective-permute-start(bf16[512,128]{1,0:T(8,128)(2,1)S(1)} %solve.1.refs_0_), channel_id=1, source_target_pairs={{0,64},{1,65},{2,66},{3,67},{4,68},{5,69},{6,70},{7,71},{8,72},{9,... | collective-permute-start | bytes 393224 | tf_op jit(solution)/shard_map/ppermute | solution.py:363
  68.0 14.4 %copy-start.1 = (s32[256]{0:T(256)S(1)}, s32[256]{0:T(256)}, u32[]{:S(2)}) copy-start(s32[256]{0:T(256)} %piv_ref.3) | copy-start | bytes 3076
  68.0 7.5 %collective-permute-start.16 = (bf16[512,128]{1,0:T(8,128)(2,1)S(1)}, bf16[512,128]{1,0:T(8,128)(2,1)S(1)}, u32[]{:S(2)}, u32[]{:S(2)}) collective-permute-start(bf16[512,128]{1,0:T(8,128)(2,1)S(1)} %choose.1.ud_ref), channel_id=1, source_target_pairs={{0,32},{64,96},{128,160},{192,224},{1,33},{65,97},{129,161},{193,2... | collective-permute-start | bytes 393224 | tf_op jit(solution)/shard_map/ppermute | solution.py:363
  69.4 13.1 %collective-permute-start.19 = (bf16[32,24576]{1,0:T(8,128)(2,1)S(1)}, bf16[32,24576]{1,0:T(8,128)(2,1)S(1)}, u32[]{:S(2)}, u32[]{:S(2)}) collective-permute-start(bf16[32,24576]{1,0:T(8,128)(2,1)S(1)} %collective-permute-done.10.refs_0_.refs_2_), channel_id=1, source_target_pairs={{0,1},{1,0},{2,3},{3,2},{4,5},{5,4},{6,7},{7,6},{8,9},{9,8},{10,11... | collective-permute-start | bytes 4718600 | tf_op jit(solution)/shard_map/ppermute | solution.py:37
  74.9 7.5 %collective-permute-start.20 = (bf16[32,24576]{1,0:T(8,128)(2,1)S(1)}, bf16[32,24576]{1,0:T(8,128)(2,1)S(1)}, u32[]{:S(2)}, u32[]{:S(2)}) collective-permute-start(bf16[32,24576]{1,0:T(8,128)(2,1)S(1)} %collective-permute-done.11.refs_0_.refs_3_), channel_id=1, source_target_pairs={{0,1},{1,0},{2,3},{3,2},{4,5},{5,4},{6,7},{7,6},{8,9},{9,8},{10,11... | collective-permute-start | bytes 4718600 | tf_op jit(solution)/shard_map/ppermute | solution.py:37
  75.0 6.3 %collective-permute-start.22 = (bf16[32,12288]{1,0:T(8,128)(2,1)S(1)}, bf16[32,12288]{1,0:T(8,128)(2,1)S(1)}, u32[]{:S(2)}, u32[]{:S(2)}) collective-permute-start(bf16[32,12288]{1,0:T(8,128)(2,1)S(1)} %collective-permute-done.18.refs_1_.refs_5_), channel_id=1, source_target_pairs={{0,1},{1,0},{2,3},{3,2},{4,5},{5,4},{6,7},{7,6},{8,9},{9,8},{10,11... | collective-permute-start | bytes 2359304 | tf_op jit(solution)/shard_map/ppermute | solution.py:37
  75.4 7.0 %collective-permute-start.21 = (bf16[32,12288]{1,0:T(8,128)(2,1)S(1)}, bf16[32,12288]{1,0:T(8,128)(2,1)S(1)}, u32[]{:S(2)}, u32[]{:S(2)}) collective-permute-start(bf16[32,12288]{1,0:T(8,128)(2,1)S(1)} %collective-permute-done.17.refs_0_.refs_4_), channel_id=1, source_target_pairs={{0,1},{1,0},{2,3},{3,2},{4,5},{5,4},{6,7},{7,6},{8,9},{9,8},{10,11... | collective-permute-start | bytes 2359304 | tf_op jit(solution)/shard_map/ppermute | solution.py:37

commit v5 on v4

--- a/solution.py
+++ b/solution.py
@@ -79,24 +79,27 @@
     )(a, b)
 
 
-def choose_kernel(rows, first_ref, *refs):
-    z = lax.div(first_ref[0], rows)
-    for k, ref in enumerate(refs[:-1]):
-
-        @pl.when((z >> 1) == k)
-        def _():
-            refs[-1][...] = ref[...]
-
-
-def choose(first, rows, parts):
-    return pl.pallas_call(
-        functools.partial(choose_kernel, rows),
-        in_specs=[SMEM] + [VMEM] * len(parts),
+def choose_kernel(rows, mask, first_ref, a_ref, b_ref, out_ref):
+    other = (jnp.int32(mask) >> lax.div(first_ref[0], rows)) & 1
+
+    @pl.when(other == 0)
+    def _():
+        out_ref[...] = a_ref[...]
+
+    @pl.when(other == 1)
+    def _():
+        out_ref[...] = b_ref[...]
+
+
+def choose(first, rows, others, a, b):
+    return pl.pallas_call(
+        functools.partial(choose_kernel, rows, sum(1 << z for z in others)),
+        in_specs=[SMEM, VMEM, VMEM],
         out_specs=VMEM,
-        out_shape=jax.ShapeDtypeStruct(parts[0].shape, parts[0].dtype),
+        out_shape=jax.ShapeDtypeStruct(a.shape, a.dtype),
         compiler_params=params(2),
         name="choose",
-    )(first, *parts)
+    )(first, a, b)
 
 
 def pick_kernel(blk, piv_ref, first_ref, trailing_ref, out_ref, cnt_ref, lst_ref, own_ref, group_ref, rows_ref, sem):
@@ -237,7 +240,7 @@
     s21 = a_ref[:h, h:].T
     x1 = unit_inverse(s11)
     x2 = unit_inverse(s22)
-    top = top_ref[...].astype(jnp.float32) + more_ref[...].astype(jnp.float32)
+    top = sum(r[...].astype(jnp.float32) for r in (top_ref, more_ref))
     u1 = dot(x1, top[:h])
     u2 = dot(x2, top[h:] - dot_exact(s21.astype(jnp.bfloat16), u1))
     out_ref[:n, :] = jnp.concatenate([u1, u2], axis=0).astype(jnp.bfloat16)
@@ -251,12 +254,11 @@
     return pl.pallas_call(
         solve_kernel,
         grid=(1,),
-        in_specs=[SMEM, whole, whole, tall, tall, tall],
+        in_specs=[SMEM, whole, whole] + [tall] * 3,
         out_specs=pl.BlockSpec((2 * n, cols), lambda i: (0, 0)),
         out_shape=jax.ShapeDtypeStruct((2 * n, cols), jnp.bfloat16),
         scratch_shapes=[pltpu.VMEM((n, n), jnp.float32), pltpu.VMEM((n, n), jnp.float32)],
         compiler_params=params(10),
-        cost_estimate=cost(20),
         name="solve",
     )(me, own, other, top, more, trailing)
 
@@ -271,14 +273,14 @@
 
     @pl.when(b == 0)
     def _():
-        odd = lax.div(first, nblk * blk) & 1
-
-        @pl.when(odd == 0)
+        late = lax.div(first, nblk * blk) >> 2
+
+        @pl.when(late == 0)
         def _():
             nat_ref[...] = ud_ref[:width, :].astype(jnp.float32)
             drow_ref[...] = ud_ref[width:, :].astype(jnp.float32)
 
-        @pl.when(odd == 1)
+        @pl.when(late == 1)
         def _():
             nat_ref[...] = rest_ref[:width, :].astype(jnp.float32)
             drow_ref[...] = rest_ref[width:, :].astype(jnp.float32)
@@ -362,36 +364,40 @@
     def zsend(x, pairs):
         return lax.ppermute(x, "prow", pairs)
 
-    p, m, q = [send(panel_t, hop(d, 0, True)) for d in (1, -1, 2)]
+    two = hop(2, 0, True)
+    diag = stack([panel_t], 0, width, "stack_t")
+    diag_q = send(diag, two)
+    p, m = send(panel_t, hop(1, 0, True)), send(panel_t, hop(-1, 0, True))
+    long, diag_q = barrier((panel_t, diag_q))
+    q = send(long, two)
 
     top, cnt, lst = pick(trailing, pivots, first, blk)
     more = zsend(top, [(1, 0), (3, 2), (5, 4), (7, 6)])
-    top = add(top, more)
-    p, m, q, top = barrier((p, m, q, top))
-    more = zsend(top, [(2, 0), (6, 4)])
 
     up, down, across = hop(0, 1, True), hop(0, -1, True), hop(0, 2, True)
-    diag = stack([panel_t, p, m, q], 0, width, "stack_d")
+    p, m, diag_q, top = barrier((p, m, diag_q, top))
+    diag = stack([diag, p, m, diag_q], 0, width, "stack_d")
     diag_q, diag_p, diag_m = send(diag, across), send(diag, up), send(diag, down)
     top = add(top, more)
-    p, m, q, diag_q, diag_p, diag_m, top = barrier((p, m, q, diag_q, diag_p, diag_m, top))
+    more = zsend(top, [(2, 0), (6, 4)])
+    p, m, q, diag_q, diag_p, diag_m, top, more = barrier((p, m, q, diag_q, diag_p, diag_m, top, more))
+    top = add(top, more)
     more = zsend(top, [(4, 0)])
     block = stack([panel_t, p, m, q], 0, rows, "stack_p")
     near, far = send(block, up), send(block, down)
+    swap = send(block, CORES)
     own = stack([diag, diag_p, diag_m, diag_q], 0, width, "stack_l")
     other = send(own, CORES)
     ud = solve(me, own, other, top, more, trailing)
-    swap = send(block, CORES)
     ud, near, far, swap = barrier((ud, near, far, swap))
     fa, fb = stack([near], 0, half, "stack_a"), stack([far], half, half, "stack_b")
     qa, qb = send(fa, up), send(fb, down)
-
-    spread = [zsend(ud, [(0, d)]) for d in (2, 4, 6)]
-    ud = choose(first, rows, [ud] + spread)
+    ud = choose(first, rows, (2,), ud, zsend(ud, [(0, 2)]))
     ud, near, far = barrier((ud, near, far))
-    rest = zsend(ud, [(0, 1), (2, 3), (4, 5), (6, 7)])
     other_near, other_far = send(near, CORES), send(far, CORES)
-    ahead = stack([qa, qb], 0, 128, "stack_q", 30)
+    ud = choose(first, rows, (1, 3), ud, zsend(ud, [(0, 1), (2, 3)]))
+    rest = zsend(ud, [(i, i + 4) for i in range(4)])
+    ahead = stack([qa, qb], 0, 128, "stack_q", 60)
     own = [block, near, far, qa, qb]
     parts = own + [swap, other_near, other_far, send(qa, CORES), send(qb, CORES)]
     return update(cnt, lst, pivots, first, me, trailing, ud, rest, ahead, parts, blk)

time: 93.1 us -> 96.3 us (1.034)
  the two profiles are of different devices: /device:TPU:1 before, /device:TPU:224 now
where the time goes in v5:
time: 96.3 us; the launch traced here: 95.6 us
  waiting for transfers between devices  41.1 us (43%)
  Pallas kernels  27.6 us (29%)
  starting transfers between devices  26.7 us (28%)
    ppermute x17, waiting for transfers between devices, send(): return lax.ppermute(block, 'pcol', pairs)  29.4 us
    ppermute x17, starting transfers between devices, send(): return lax.ppermute(block, 'pcol', pairs)  19.8 us
    ppermute x6, waiting for transfers between devices, zsend(): return lax.ppermute(x, 'prow', pairs)  11.7 us
    pallas_call x1, Pallas kernels, update(): pl.pallas_call(functools.partial(update_kernel, nblk), grid=(nblk,), in_s...  11.1 us
    pallas_call x7, Pallas kernels, stack(): pl.pallas_call(stack_kernel, grid=(cols // step,), in_specs=[pl.BlockSpec...  7.55 us
    ppermute x6, starting transfers between devices, zsend(): return lax.ppermute(x, 'prow', pairs)  6.86 us
    pallas_call x1, Pallas kernels, solve(): pl.pallas_call(solve_kernel, grid=(1,), in_specs=[SMEM, whole, whole] + [...  5.09 us
    pallas_call x1, Pallas kernels, pick(): pl.pallas_call(functools.partial(pick_kernel, blk), in_specs=[SMEM, SMEM,...  3.75 us
  transfers between devices with their start and end apart: 23, of which 10 were waited for; matrix products, arithmetic and copies ran while one was open for 0% of the time, Pallas kernels for 11%

profile of v5, /device:TPU:224, one launch (start us, length us, event | category | flops | bytes accessed | tf_op | source)
XLA Modules:
  0.0 95.6 jit_solution(7125882856119298477)
XLA Ops:
  0.0 0.7 stack_t.1.refs_0_
  0.7 3.0 %collective-permute-start.2 = (bf16[8,256]{1,0:T(8,128)(2,1)S(1)}, bf16[8,256]{1,0:T(8,128)(2,1)S(1)}, u32[]{:S(2)}, u32[]{:S(2)}) collective-permute-start(bf16[8,256]{1,0:T(8,128)(2,1)S(1)} %stack_t.1.refs_0_), channel_id=1, source_target_pairs={{0,16},{1,5},{2,18},{3,7},{4,20},{5,1},{6,22},{7,3},{8,24},{9,13},... | collective-permute-start | bytes 12296 | tf_op jit(solution)/shard_map/ppermute | solution.py:37
  3.7 1.1 %collective-permute-start.1 = (bf16[8,24576]{1,0:T(8,128)(2,1)}, bf16[8,24576]{1,0:T(8,128)(2,1)S(1)}, u32[]{:S(2)}, u32[]{:S(2)}) collective-permute-start(bf16[8,24576]{1,0:T(8,128)(2,1)} %refs_0_.3), channel_id=1, source_target_pairs={{0,24},{1,7},{2,26},{3,1},{4,28},{5,3},{6,30},{7,5},{8,0},{9,15},{... | collective-permute-start | bytes 1179656 | tf_op jit(solution)/shard_map/ppermute | solution.py:37
  4.9 0.9 collective-permute-start
  5.8 0.1 collective-permute-done.2.refs_3_
  5.8 3.0 %collective-permute-start.3 = (bf16[8,24576]{1,0:T(8,128)(2,1)}, bf16[8,24576]{1,0:T(8,128)(2,1)S(1)}, u32[]{:S(2)}, u32[]{:S(2)}) collective-permute-start(bf16[8,24576]{1,0:T(8,128)(2,1)} %refs_0_.3), channel_id=1, source_target_pairs={{0,16},{1,5},{2,18},{3,7},{4,20},{5,1},{6,22},{7,3},{8,24},{9,13},... | collective-permute-start | bytes 1179656 | tf_op jit(solution)/shard_map/ppermute | solution.py:37
  8.8 3.8 %pick.1 = (bf16[256,128]{1,0:T(8,128)(2,1)S(1)}, s32[6]{0:T(128)S(1)}, s32[1536]{0:T(1024)S(1)}) custom-call(s32[256]{0:T(256)S(1)} %copy-done, s32[1]{0:T(128)} %bitcast.first_ref, bf16[24576,128]{1,0:T(8,128)(2,1)} %tr_ref.1), custom_call_target="tpu_custom_call" | custom-call | flops 13200000000 | bytes 42000000 | tf_op jit(solution)/shard_map/pick/pallas_call | solution.py:159
  12.6 2.9 %collective-permute-start.7 = (bf16[256,128]{1,0:T(8,128)(2,1)S(1)}, bf16[256,128]{1,0:T(8,128)(2,1)S(1)}, u32[]{:S(2)}, u32[]{:S(2)}) collective-permute-start(bf16[256,128]{1,0:T(8,128)(2,1)S(1)} %get-tuple-element.37.a_ref), channel_id=1, source_target_pairs={{32,0},{96,64},{160,128},{224,192},{33,1},{97,65},{161,129},{225,1... | collective-permute-start | bytes 196616 | tf_op jit(solution)/shard_map/ppermute | solution.py:365
  15.5 2.7 %collective-permute-done.refs_1_ = bf16[8,24576]{1,0:T(8,128)(2,1)S(1)} collective-permute-done((bf16[8,24576]{1,0:T(8,128)(2,1)}, bf16[8,24576]{1,0:T(8,128)(2,1)S(1)}, u32[]{:S(2)}, u32[]{:S(2)}) %collective-permute-start) | collective-permute-done | bytes 393248 | tf_op jit(solution)/shard_map/ppermute | solution.py:37
  18.3 0.7 collective-permute-start.8
  19.0 3.1 %collective-permute-start.6 = (bf16[32,256]{1,0:T(8,128)(2,1)S(1)}, bf16[32,256]{1,0:T(8,128)(2,1)S(1)}, u32[]{:S(2)}, u32[]{:S(2)}) collective-permute-start(bf16[32,256]{1,0:T(8,128)(2,1)S(1)} %stack_d.1.refs_0_), channel_id=1, source_target_pairs={{0,6},{1,25},{2,0},{3,27},{4,2},{5,29},{6,4},{7,31},{8,14},{9,1},{... | collective-permute-start | bytes 49160 | tf_op jit(solution)/shard_map/ppermute | solution.py:37
  22.1 0.0 collective-permute-start.5
  22.1 2.2 %collective-permute-start.4 = (bf16[32,256]{1,0:T(8,128)(2,1)S(1)}, bf16[32,256]{1,0:T(8,128)(2,1)S(1)}, u32[]{:S(2)}, u32[]{:S(2)}) collective-permute-start(bf16[32,256]{1,0:T(8,128)(2,1)S(1)} %stack_d.1.refs_0_), channel_id=1, source_target_pairs={{0,4},{1,17},{2,6},{3,19},{4,0},{5,21},{6,2},{7,23},{8,12},{9,25},... | collective-permute-start | bytes 49160 | tf_op jit(solution)/shard_map/ppermute | solution.py:37
  24.3 0.0 collective-permute-done.3.refs_3_
  24.3 0.0 collective-permute-done.6.refs_2_
  24.3 2.7 %collective-permute-done.5.refs_1_ = bf16[32,256]{1,0:T(8,128)(2,1)S(1)} collective-permute-done((bf16[32,256]{1,0:T(8,128)(2,1)S(1)}, bf16[32,256]{1,0:T(8,128)(2,1)S(1)}, u32[]{:S(2)}, u32[]{:S(2)}) %collective-permute-start.5) | collective-permute-done | bytes 16416 | tf_op jit(solution)/shard_map/ppermute | solution.py:37
  27.0 0.3 collective-permute-done.4.refs_3_
  27.3 0.0 collective-permute-done.8.b_ref
  27.3 2.8 %stack_p.1.refs_1_ = bf16[32,24576]{1,0:T(8,128)(2,1)S(1)} custom-call(bf16[8,24576]{1,0:T(8,128)(2,1)} %refs_0_.3, bf16[8,24576]{1,0:T(8,128)(2,1)S(1)} %collective-permute-done.refs_1_, bf16[8,24576]{1,0:T(8,128)(2,1)S(1)} %collective-permute-done.1.refs_2_, bf16[8,24576]{1,0:T(8,128)(2,1)S(1)} %collective-permute-done.3.refs_3_), custom_call_target="tpu_custom_call" | custom-call | flops 1100000000 | bytes 3500000 | tf_op jit(solution)/shard_map/stack_p/pallas_call | solution.py:55
  30.1 0.1 collective-permute-start.13
  30.2 3.3 %collective-permute-start.12 = (bf16[32,24576]{1,0:T(8,128)(2,1)S(1)}, bf16[32,24576]{1,0:T(8,128)(2,1)}, u32[]{:S(2)}, u32[]{:S(2)}) collective-permute-start(bf16[32,24576]{1,0:T(8,128)(2,1)S(1)} %stack_p.1.refs_1_), channel_id=1, source_target_pairs={{0,6},{1,25},{2,0},{3,27},{4,2},{5,29},{6,4},{7,31},{8,14},{9,1},{... | collective-permute-start | bytes 4718600 | tf_op jit(solution)/shard_map/ppermute | solution.py:37
  33.6 0.0 collective-permute-start.11
  33.6 0.7 collective-permute-start.10
  34.3 0.1 collective-permute-start.9
  34.4 0.0 collective-permute-done.10.more_ref
  34.4 1.2 %collective-permute-done.9.other_ref = bf16[128,256]{1,0:T(8,128)(2,1)S(1)} collective-permute-done((bf16[128,256]{1,0:T(8,128)(2,1)S(1)}, bf16[128,256]{1,0:T(8,128)(2,1)S(1)}, u32[]{:S(2)}, u32[]{:S(2)}) %collective-permute-start.9) | collective-permute-done | bytes 65568 | tf_op jit(solution)/shard_map/ppermute | solution.py:37
  35.6 5.1 %solve.1.a_ref = bf16[512,128]{1,0:T(8,128)(2,1)S(1)} custom-call(s32[1]{0:T(128)} %bitcast.1.me_ref, bf16[128,256]{1,0:T(8,128)(2,1)S(1)} %stack_l.1.own_ref, bf16[128,256]{1,0:T(8,128)(2,1)S(1)} %collective-permute-done.9.other_ref, bf16[256,128]{1,0:T(8,128)(2,1)S(1)} %add.3.top_ref, bf16[256,128]{1,0:T(8,128)(2,1)S(1)} %collective-permute-done.10.more_ref, ...), custom_call_target="tpu_custom_call" | custom-call | tf_op jit(solution)/shard_map/solve/pallas_call | solution.py:254
  40.7 0.0 collective-permute-done.13.refs_6_
  40.7 10.8 %collective-permute-done.12.refs_0_.refs_3_ = bf16[32,24576]{1,0:T(8,128)(2,1)} collective-permute-done((bf16[32,24576]{1,0:T(8,128)(2,1)S(1)}, bf16[32,24576]{1,0:T(8,128)(2,1)}, u32[]{:S(2)}, u32[]{:S(2)}) %collective-permute-start.12) | collective-permute-done | bytes 1572896 | tf_op jit(solution)/shard_map/ppermute | solution.py:37
  51.5 3.8 %collective-permute-done.11.refs_0_.refs_2_ = bf16[32,24576]{1,0:T(8,128)(2,1)} collective-permute-done((bf16[32,24576]{1,0:T(8,128)(2,1)S(1)}, bf16[32,24576]{1,0:T(8,128)(2,1)}, u32[]{:S(2)}, u32[]{:S(2)}) %collective-permute-start.11) | collective-permute-done | bytes 1572896 | tf_op jit(solution)/shard_map/ppermute | solution.py:37
  55.3 2.0 %stack_b.1 = bf16[32,12288]{1,0:T(8,128)(2,1)S(1)} custom-call(bf16[32,24576]{1,0:T(8,128)(2,1)} %collective-permute-done.12.refs_0_.refs_3_), custom_call_target="tpu_custom_call" | custom-call | flops 1100000000 | bytes 3500000 | tf_op jit(solution)/shard_map/stack_b/pallas_call | solution.py:55
  57.3 0.1 collective-permute-start.18
  57.4 2.0 %stack_a.1 = bf16[32,12288]{1,0:T(8,128)(2,1)S(1)} custom-call(bf16[32,24576]{1,0:T(8,128)(2,1)} %collective-permute-done.11.refs_0_.refs_2_), custom_call_target="tpu_custom_call" | custom-call | flops 1100000000 | bytes 3500000 | tf_op jit(solution)/shard_map/stack_a/pallas_call | solution.py:55
  59.4 2.1 %collective-permute-start.17 = (bf16[32,12288]{1,0:T(8,128)(2,1)S(1)}, bf16[32,12288]{1,0:T(8,128)(2,1)S(1)}, u32[]{:S(2)}, u32[]{:S(2)}) collective-permute-start(bf16[32,12288]{1,0:T(8,128)(2,1)S(1)} %stack_a.1), channel_id=1, source_target_pairs={{0,2},{1,9},{2,4},{3,11},{4,6},{5,13},{6,0},{7,15},{8,10},{9,17},{... | collective-permute-start | bytes 2359304 | tf_op jit(solution)/shard_map/ppermute | solution.py:37
  61.5 0.7 collective-permute-start.14
  62.2 0.0 collective-permute-done.14.b_ref
  62.2 0.7 collective-permute-start.15
  62.9 0.3 collective-permute-start.19
  63.2 0.5 collective-permute-start.20
  63.7 0.0 collective-permute-done.15.b_ref
  63.7 1.3 %collective-permute-start.16 = (bf16[512,128]{1,0:T(8,128)(2,1)S(1)}, bf16[512,128]{1,0:T(8,128)(2,1)S(1)}, u32[]{:S(2)}, u32[]{:S(2)}) collective-permute-start(bf16[512,128]{1,0:T(8,128)(2,1)S(1)} %choose.3.ud_ref), channel_id=1, source_target_pairs={{0,128},{32,160},{64,192},{96,224},{1,129},{33,161},{65,193},{97,2... | collective-permute-start | bytes 393224 | tf_op jit(solution)/shard_map/ppermute | solution.py:365
  65.0 4.4 %collective-permute-done.18.refs_1_.refs_5_ = bf16[32,12288]{1,0:T(8,128)(2,1)S(1)} collective-permute-done((bf16[32,12288]{1,0:T(8,128)(2,1)S(1)}, bf16[32,12288]{1,0:T(8,128)(2,1)S(1)}, u32[]{:S(2)}, u32[]{:S(2)}) %collective-permute-start.18) | collective-permute-done | bytes 786464 | tf_op jit(solution)/shard_map/ppermute | solution.py:37
  69.4 0.0 collective-permute-start.22
  69.4 3.3 %collective-permute-done.17.refs_0_.refs_4_ = bf16[32,12288]{1,0:T(8,128)(2,1)S(1)} collective-permute-done((bf16[32,12288]{1,0:T(8,128)(2,1)S(1)}, bf16[32,12288]{1,0:T(8,128)(2,1)S(1)}, u32[]{:S(2)}, u32[]{:S(2)}) %collective-permute-start.17) | collective-permute-done | bytes 786464 | tf_op jit(solution)/shard_map/ppermute | solution.py:37
  72.7 0.0 collective-permute-start.21
  72.7 11.7 %collective-permute-done.16.rest_ref = bf16[512,128]{1,0:T(8,128)(2,1)S(1)} collective-permute-done((bf16[512,128]{1,0:T(8,128)(2,1)S(1)}, bf16[512,128]{1,0:T(8,128)(2,1)S(1)}, u32[]{:S(2)}, u32[]{:S(2)}) %collective-permute-start.16) | collective-permute-done | bytes 131104 | tf_op jit(solution)/shard_map/ppermute | solution.py:365
  84.4 0.0 collective-permute-done.22.refs_10_
  84.5 11.1 %update.1 = bf16[24576,128]{1,0:T(8,128)(2,1)} custom-call(s32[6]{0:T(128)S(1)} %get-tuple-element.29.cnt_ref, s32[1536]{0:T(1024)S(1)} %get-tuple-element.30.lst_ref, s32[256]{0:T(256)S(1)} %copy-done, s32[1]{0:T(128)} %bitcast.first_ref, s32[1]{0:T(128)} %bitcast.1.me_ref, bf16[24576,128]{1,0:T(8,128)(2,1)} %tr_ref.1, bf16[512,128]{1,0:T(8,128)(2,1)S(1)} %choose.3.ud_ref, ...), custom_call_target="tpu_custom_call" | custom-call | tf_op jit(solution)/shard_map/update/pallas_call | solution.py:336
  (14 shorter events, 0.1 us)
Async XLA Ops:
  0.0 8.8 %copy-start = (s32[256]{0:T(256)S(1)}, s32[256]{0:T(256)}, u32[]{:S(2)}) copy-start(s32[256]{0:T(256)} %piv_ref.3) | copy-start | bytes 3076
  0.7 5.1 %collective-permute-start.2 = (bf16[8,256]{1,0:T(8,128)(2,1)S(1)}, bf16[8,256]{1,0:T(8,128)(2,1)S(1)}, u32[]{:S(2)}, u32[]{:S(2)}) collective-permute-start(bf16[8,256]{1,0:T(8,128)(2,1)S(1)} %stack_t.1.refs_0_), channel_id=1, source_target_pairs={{0,16},{1,5},{2,18},{3,7},{4,20},{5,1},{6,22},{7,3},{8,24},{9,13},... | collective-permute-start | bytes 12296 | tf_op jit(solution)/shard_map/ppermute | solution.py:37
  3.7 11.8 %collective-permute-start.1 = (bf16[8,24576]{1,0:T(8,128)(2,1)}, bf16[8,24576]{1,0:T(8,128)(2,1)S(1)}, u32[]{:S(2)}, u32[]{:S(2)}) collective-permute-start(bf16[8,24576]{1,0:T(8,128)(2,1)} %refs_0_.3), channel_id=1, source_target_pairs={{0,24},{1,7},{2,26},{3,1},{4,28},{5,3},{6,30},{7,5},{8,0},{9,15},{... | collective-permute-start | bytes 1179656 | tf_op jit(solution)/shard_map/ppermute | solution.py:37
  4.9 13.4 %collective-permute-start = (bf16[8,24576]{1,0:T(8,128)(2,1)}, bf16[8,24576]{1,0:T(8,128)(2,1)S(1)}, u32[]{:S(2)}, u32[]{:S(2)}) collective-permute-start(bf16[8,24576]{1,0:T(8,128)(2,1)} %refs_0_.3), channel_id=1, source_target_pairs={{0,8},{1,3},{2,10},{3,5},{4,12},{5,7},{6,14},{7,1},{8,16},{9,11},{... | collective-permute-start | bytes 1179656 | tf_op jit(solution)/shard_map/ppermute | solution.py:37
  5.8 18.5 %collective-permute-start.3 = (bf16[8,24576]{1,0:T(8,128)(2,1)}, bf16[8,24576]{1,0:T(8,128)(2,1)S(1)}, u32[]{:S(2)}, u32[]{:S(2)}) collective-permute-start(bf16[8,24576]{1,0:T(8,128)(2,1)} %refs_0_.3), channel_id=1, source_target_pairs={{0,16},{1,5},{2,18},{3,7},{4,20},{5,1},{6,22},{7,3},{8,24},{9,13},... | collective-permute-start | bytes 1179656 | tf_op jit(solution)/shard_map/ppermute | solution.py:37
  12.6 5.7 %collective-permute-start.7 = (bf16[256,128]{1,0:T(8,128)(2,1)S(1)}, bf16[256,128]{1,0:T(8,128)(2,1)S(1)}, u32[]{:S(2)}, u32[]{:S(2)}) collective-permute-start(bf16[256,128]{1,0:T(8,128)(2,1)S(1)} %get-tuple-element.37.a_ref), channel_id=1, source_target_pairs={{32,0},{96,64},{160,128},{224,192},{33,1},{97,65},{161,129},{225,1... | collective-permute-start | bytes 196616 | tf_op jit(solution)/shard_map/ppermute | solution.py:365
  18.3 9.0 %collective-permute-start.8 = (bf16[256,128]{1,0:T(8,128)(2,1)S(1)}, bf16[256,128]{1,0:T(8,128)(2,1)S(1)}, u32[]{:S(2)}, u32[]{:S(2)}) collective-permute-start(bf16[256,128]{1,0:T(8,128)(2,1)S(1)} %add.2.a_ref), channel_id=1, source_target_pairs={{64,0},{192,128},{65,1},{193,129},{66,2},{194,130},{67,3},{195,131... | collective-permute-start | bytes 196616 | tf_op jit(solution)/shard_map/ppermute | solution.py:365
  19.0 5.3 %collective-permute-start.6 = (bf16[32,256]{1,0:T(8,128)(2,1)S(1)}, bf16[32,256]{1,0:T(8,128)(2,1)S(1)}, u32[]{:S(2)}, u32[]{:S(2)}) collective-permute-start(bf16[32,256]{1,0:T(8,128)(2,1)S(1)} %stack_d.1.refs_0_), channel_id=1, source_target_pairs={{0,6},{1,25},{2,0},{3,27},{4,2},{5,29},{6,4},{7,31},{8,14},{9,1},{... | collective-permute-start | bytes 49160 | tf_op jit(solution)/shard_map/ppermute | solution.py:37
  22.1 4.9 %collective-permute-start.5 = (bf16[32,256]{1,0:T(8,128)(2,1)S(1)}, bf16[32,256]{1,0:T(8,128)(2,1)S(1)}, u32[]{:S(2)}, u32[]{:S(2)}) collective-permute-start(bf16[32,256]{1,0:T(8,128)(2,1)S(1)} %stack_d.1.refs_0_), channel_id=1, source_target_pairs={{0,2},{1,9},{2,4},{3,11},{4,6},{5,13},{6,0},{7,15},{8,10},{9,17},{... | collective-permute-start | bytes 49160 | tf_op jit(solution)/shard_map/ppermute | solution.py:37
  22.1 5.2 %collective-permute-start.4 = (bf16[32,256]{1,0:T(8,128)(2,1)S(1)}, bf16[32,256]{1,0:T(8,128)(2,1)S(1)}, u32[]{:S(2)}, u32[]{:S(2)}) collective-permute-start(bf16[32,256]{1,0:T(8,128)(2,1)S(1)} %stack_d.1.refs_0_), channel_id=1, source_target_pairs={{0,4},{1,17},{2,6},{3,19},{4,0},{5,21},{6,2},{7,23},{8,12},{9,25},... | collective-permute-start | bytes 49160 | tf_op jit(solution)/shard_map/ppermute | solution.py:37
  30.1 10.6 %collective-permute-start.13 = (bf16[32,24576]{1,0:T(8,128)(2,1)S(1)}, bf16[32,24576]{1,0:T(8,128)(2,1)S(1)}, u32[]{:S(2)}, u32[]{:S(2)}) collective-permute-start(bf16[32,24576]{1,0:T(8,128)(2,1)S(1)} %stack_p.1.refs_1_), channel_id=1, source_target_pairs={{0,1},{1,0},{2,3},{3,2},{4,5},{5,4},{6,7},{7,6},{8,9},{9,8},{10,11... | collective-permute-start | bytes 4718600 | tf_op jit(solution)/shard_map/ppermute | solution.py:37
  30.2 21.2 %collective-permute-start.12 = (bf16[32,24576]{1,0:T(8,128)(2,1)S(1)}, bf16[32,24576]{1,0:T(8,128)(2,1)}, u32[]{:S(2)}, u32[]{:S(2)}) collective-permute-start(bf16[32,24576]{1,0:T(8,128)(2,1)S(1)} %stack_p.1.refs_1_), channel_id=1, source_target_pairs={{0,6},{1,25},{2,0},{3,27},{4,2},{5,29},{6,4},{7,31},{8,14},{9,1},{... | collective-permute-start | bytes 4718600 | tf_op jit(solution)/shard_map/ppermute | solution.py:37
  33.6 21.7 %collective-permute-start.11 = (bf16[32,24576]{1,0:T(8,128)(2,1)S(1)}, bf16[32,24576]{1,0:T(8,128)(2,1)}, u32[]{:S(2)}, u32[]{:S(2)}) collective-permute-start(bf16[32,24576]{1,0:T(8,128)(2,1)S(1)} %stack_p.1.refs_1_), channel_id=1, source_target_pairs={{0,2},{1,9},{2,4},{3,11},{4,6},{5,13},{6,0},{7,15},{8,10},{9,17},{... | collective-permute-start | bytes 4718600 | tf_op jit(solution)/shard_map/ppermute | solution.py:37
  33.6 0.8 collective-permute-start.10
  34.3 1.3 %collective-permute-start.9 = (bf16[128,256]{1,0:T(8,128)(2,1)S(1)}, bf16[128,256]{1,0:T(8,128)(2,1)S(1)}, u32[]{:S(2)}, u32[]{:S(2)}) collective-permute-start(bf16[128,256]{1,0:T(8,128)(2,1)S(1)} %stack_l.1.own_ref), channel_id=1, source_target_pairs={{0,1},{1,0},{2,3},{3,2},{4,5},{5,4},{6,7},{7,6},{8,9},{9,8},{10,11... | collective-permute-start | bytes 196616 | tf_op jit(solution)/shard_map/ppermute | solution.py:37
  57.3 12.1 %collective-permute-start.18 = (bf16[32,12288]{1,0:T(8,128)(2,1)S(1)}, bf16[32,12288]{1,0:T(8,128)(2,1)S(1)}, u32[]{:S(2)}, u32[]{:S(2)}) collective-permute-start(bf16[32,12288]{1,0:T(8,128)(2,1)S(1)} %stack_b.1), channel_id=1, source_target_pairs={{0,6},{1,25},{2,0},{3,27},{4,2},{5,29},{6,4},{7,31},{8,14},{9,1},{... | collective-permute-start | bytes 2359304 | tf_op jit(solution)/shard_map/ppermute | solution.py:37
  59.4 13.3 %collective-permute-start.17 = (bf16[32,12288]{1,0:T(8,128)(2,1)S(1)}, bf16[32,12288]{1,0:T(8,128)(2,1)S(1)}, u32[]{:S(2)}, u32[]{:S(2)}) collective-permute-start(bf16[32,12288]{1,0:T(8,128)(2,1)S(1)} %stack_a.1), channel_id=1, source_target_pairs={{0,2},{1,9},{2,4},{3,11},{4,6},{5,13},{6,0},{7,15},{8,10},{9,17},{... | collective-permute-start | bytes 2359304 | tf_op jit(solution)/shard_map/ppermute | solution.py:37
  61.5 0.7 collective-permute-start.14
  62.2 1.5 %collective-permute-start.15 = (bf16[512,128]{1,0:T(8,128)(2,1)S(1)}, bf16[512,128]{1,0:T(8,128)(2,1)S(1)}, u32[]{:S(2)}, u32[]{:S(2)}) collective-permute-start(bf16[512,128]{1,0:T(8,128)(2,1)S(1)} %choose.2.a_ref), channel_id=1, source_target_pairs={{0,32},{64,96},{1,33},{65,97},{2,34},{66,98},{3,35},{67,99},{4,36}... | collective-permute-start | bytes 393224 | tf_op jit(solution)/shard_map/ppermute | solution.py:365
  62.9 21.6 %collective-permute-start.19 = (bf16[32,24576]{1,0:T(8,128)(2,1)}, bf16[32,24576]{1,0:T(8,128)(2,1)S(1)}, u32[]{:S(2)}, u32[]{:S(2)}) collective-permute-start(bf16[32,24576]{1,0:T(8,128)(2,1)} %collective-permute-done.11.refs_0_.refs_2_), channel_id=1, source_target_pairs={{0,1},{1,0},{2,3},{3,2},{4,5},{5,4},{6,7},{7,6},{8,9},{9,8},{10,11... | collective-permute-start | bytes 4718600 | tf_op jit(solution)/shard_map/ppermute | solution.py:37
  63.2 21.3 %collective-permute-start.20 = (bf16[32,24576]{1,0:T(8,128)(2,1)}, bf16[32,24576]{1,0:T(8,128)(2,1)S(1)}, u32[]{:S(2)}, u32[]{:S(2)}) collective-permute-start(bf16[32,24576]{1,0:T(8,128)(2,1)} %collective-permute-done.12.refs_0_.refs_3_), channel_id=1, source_target_pairs={{0,1},{1,0},{2,3},{3,2},{4,5},{5,4},{6,7},{7,6},{8,9},{9,8},{10,11... | collective-permute-start | bytes 4718600 | tf_op jit(solution)/shard_map/ppermute | solution.py:37
  63.7 20.8 %collective-permute-start.16 = (bf16[512,128]{1,0:T(8,128)(2,1)S(1)}, bf16[512,128]{1,0:T(8,128)(2,1)S(1)}, u32[]{:S(2)}, u32[]{:S(2)}) collective-permute-start(bf16[512,128]{1,0:T(8,128)(2,1)S(1)} %choose.3.ud_ref), channel_id=1, source_target_pairs={{0,128},{32,160},{64,192},{96,224},{1,129},{33,161},{65,193},{97,2... | collective-permute-start | bytes 393224 | tf_op jit(solution)/shard_map/ppermute | solution.py:365
  69.4 15.1 %collective-permute-start.22 = (bf16[32,12288]{1,0:T(8,128)(2,1)S(1)}, bf16[32,12288]{1,0:T(8,128)(2,1)S(1)}, u32[]{:S(2)}, u32[]{:S(2)}) collective-permute-start(bf16[32,12288]{1,0:T(8,128)(2,1)S(1)} %collective-permute-done.18.refs_1_.refs_5_), channel_id=1, source_target_pairs={{0,1},{1,0},{2,3},{3,2},{4,5},{5,4},{6,7},{7,6},{8,9},{9,8},{10,11... | collective-permute-start | bytes 2359304 | tf_op jit(solution)/shard_map/ppermute | solution.py:37
  72.7 11.7 %collective-permute-start.21 = (bf16[32,12288]{1,0:T(8,128)(2,1)S(1)}, bf16[32,12288]{1,0:T(8,128)(2,1)S(1)}, u32[]{:S(2)}, u32[]{:S(2)}) collective-permute-start(bf16[32,12288]{1,0:T(8,128)(2,1)S(1)} %collective-permute-done.17.refs_0_.refs_4_), channel_id=1, source_target_pairs={{0,1},{1,0},{2,3},{3,2},{4,5},{5,4},{6,7},{7,6},{8,9},{9,8},{10,11... | collective-permute-start | bytes 2359304 | tf_op jit(solution)/shard_map/ppermute | solution.py:37

commit v6 on v5

--- a/solution.py
+++ b/solution.py
@@ -45,20 +45,24 @@
     return pl.CostEstimate(flops=int(us * 1.1e9), bytes_accessed=int(us * 3.5e6), transcendentals=0)
 
 
-def stack_kernel(*refs):
-    refs[-1][...] = jnp.concatenate([r[...] for r in refs[:-1]], axis=0)
+def stack_kernel(start, step, *refs):
+    def chunk(i, carry):
+        src = pl.ds(pl.multiple_of(start + i * step, 128), step)
+        dst = pl.ds(pl.multiple_of(i * step, 128), step)
+        refs[-1][:, dst] = jnp.concatenate([r[:, src] for r in refs[:-1]], axis=0)
+        return carry
+
+    lax.fori_loop(0, refs[-1].shape[1] // step, chunk, 0)
 
 
 def stack(parts, start, cols, name, us=1):
     rows = sum(p.shape[0] for p in parts)
-    step = min(cols, 4096)
-    return pl.pallas_call(
-        stack_kernel,
-        grid=(cols // step,),
-        in_specs=[pl.BlockSpec((p.shape[0], step), lambda i: (0, i + start // step)) for p in parts],
-        out_specs=pl.BlockSpec((rows, step), lambda i: (0, i)),
+    return pl.pallas_call(
+        functools.partial(stack_kernel, start, min(cols, 1024)),
+        in_specs=[VMEM] * len(parts),
+        out_specs=VMEM,
         out_shape=jax.ShapeDtypeStruct((rows, cols), jnp.bfloat16),
-        compiler_params=params(6),
+        compiler_params=params(2),
         cost_estimate=cost(us),
         name=name,
     )(*parts)
@@ -364,34 +368,30 @@
     def zsend(x, pairs):
         return lax.ppermute(x, "prow", pairs)
 
-    two = hop(2, 0, True)
-    diag = stack([panel_t], 0, width, "stack_t")
-    diag_q = send(diag, two)
-    p, m = send(panel_t, hop(1, 0, True)), send(panel_t, hop(-1, 0, True))
-    long, diag_q = barrier((panel_t, diag_q))
-    q = send(long, two)
+    p, m, q = [send(panel_t, hop(d, 0, True)) for d in (1, -1, 2)]
 
     top, cnt, lst = pick(trailing, pivots, first, blk)
     more = zsend(top, [(1, 0), (3, 2), (5, 4), (7, 6)])
+    p, m, q, top, more = barrier((p, m, q, top, more))
 
     up, down, across = hop(0, 1, True), hop(0, -1, True), hop(0, 2, True)
-    p, m, diag_q, top = barrier((p, m, diag_q, top))
-    diag = stack([diag, p, m, diag_q], 0, width, "stack_d")
-    diag_q, diag_p, diag_m = send(diag, across), send(diag, up), send(diag, down)
+    diag = stack([panel_t, p, m, q], 0, width, "stack_d")
+    diag_q = send(diag, across)
+    block = stack([panel_t, p, m, q], 0, rows, "stack_p")
     top = add(top, more)
+    block, diag_q, top = barrier((block, diag_q, top))
+    near, far = send(block, up), send(block, down)
     more = zsend(top, [(2, 0), (6, 4)])
-    p, m, q, diag_q, diag_p, diag_m, top, more = barrier((p, m, q, diag_q, diag_p, diag_m, top, more))
     top = add(top, more)
+    top, block2 = barrier((top, block))
+    swap = send(block2, CORES)
     more = zsend(top, [(4, 0)])
-    block = stack([panel_t, p, m, q], 0, rows, "stack_p")
-    near, far = send(block, up), send(block, down)
-    swap = send(block, CORES)
-    own = stack([diag, diag_p, diag_m, diag_q], 0, width, "stack_l")
+    more, near, far, swap = barrier((more, near, far, swap))
+    own = stack([diag, near, far, diag_q], 0, width, "stack_l")
     other = send(own, CORES)
-    ud = solve(me, own, other, top, more, trailing)
-    ud, near, far, swap = barrier((ud, near, far, swap))
     fa, fb = stack([near], 0, half, "stack_a"), stack([far], half, half, "stack_b")
     qa, qb = send(fa, up), send(fb, down)
+    ud = solve(me, own, other, top, more, trailing)
     ud = choose(first, rows, (2,), ud, zsend(ud, [(0, 2)]))
     ud, near, far = barrier((ud, near, far))
     other_near, other_far = send(near, CORES), send(far, CORES)

time: 96.3 us -> 91.1 us (0.946)
  starting transfers between devices: 26.7 us -> 21 us
  Pallas kernels: 27.6 us -> 23.8 us
  waiting for transfers between devices: 41.1 us -> 44.5 us
  local copies, waits for them, and re-layouts: 0.01 us -> 1.05 us
    ppermute x6, waiting for transfers between devices: 11.7 us -> 19.5 us  [zsend(): return lax.ppermute(x, 'prow', pairs)]
    ppermute x17 -> x14, starting transfers between devices: 19.8 us -> 14.5 us  [send(): return lax.ppermute(block, 'pcol', pairs)]
    ppermute x17 -> x14, waiting for transfers between devices: 29.4 us -> 25 us  [send(): return lax.ppermute(block, 'pcol', pairs)]
    pallas_call x7 -> x6, Pallas kernels: 7.55 us -> 3.74 us  [stack(): pl.pallas_call(functools.partial(stack_kernel, start, min(cols, 1024)), i...]
    unnamed x2 -> x14, local copies, waits for them, and re-layouts: 0.01 us -> 1.05 us
  transfers between devices with their start and end apart: 23 -> 20, of which waited for: 10 -> 7; matrix products, arithmetic and copies ran while one was open for 0% -> 0% of each run, Pallas kernels for 11% -> 13%
where the time goes in v6:
time: 91.1 us; the launch traced here: 90.6 us
  waiting for transfers between devices  44.5 us (49%)
  Pallas kernels  23.8 us (26%)
  starting transfers between devices  21 us (23%)
  local copies, waits for them, and re-layouts  1.05 us (1%)
    ppermute x14, waiting for transfers between devices, send(): return lax.ppermute(block, 'pcol', pairs)  25 us
    ppermute x6, waiting for transfers between devices, zsend(): return lax.ppermute(x, 'prow', pairs)  19.5 us
    ppermute x14, starting transfers between devices, send(): return lax.ppermute(block, 'pcol', pairs)  14.5 us
    pallas_call x1, Pallas kernels, update(): pl.pallas_call(functools.partial(update_kernel, nblk), grid=(nblk,), in_s...  10.7 us
    ppermute x6, starting transfers between devices, zsend(): return lax.ppermute(x, 'prow', pairs)  6.5 us
    pallas_call x1, Pallas kernels, solve(): pl.pallas_call(solve_kernel, grid=(1,), in_specs=[SMEM, whole, whole] + [...  5.21 us
    pallas_call x1, Pallas kernels, pick(): pl.pallas_call(functools.partial(pick_kernel, blk), in_specs=[SMEM, SMEM,...  4.09 us
    pallas_call x6, Pallas kernels, stack(): pl.pallas_call(functools.partial(stack_kernel, start, min(cols, 1024)), i...  3.74 us
  transfers between devices with their start and end apart: 20, of which 7 were waited for; matrix products, arithmetic and copies ran while one was open for 0% of the time, Pallas kernels for 13%

profile of v6, /device:TPU:224, one launch (start us, length us, event | category | flops | bytes accessed | tf_op | source)
XLA Modules:
  0.0 90.6 jit_solution(1041583497341623)
XLA Ops:
  0.0 3.0 %collective-permute-start.2 = (bf16[8,24576]{1,0:T(8,128)(2,1)}, bf16[8,24576]{1,0:T(8,128)(2,1)S(1)}, u32[]{:S(2)}, u32[]{:S(2)}) collective-permute-start(bf16[8,24576]{1,0:T(8,128)(2,1)} %refs_0_.3), channel_id=1, source_target_pairs={{0,16},{1,5},{2,18},{3,7},{4,20},{5,1},{6,22},{7,3},{8,24},{9,13},... | collective-permute-start | bytes 1179656 | tf_op jit(solution)/shard_map/ppermute | solution.py:37
  3.0 1.1 %collective-permute-start.1 = (bf16[8,24576]{1,0:T(8,128)(2,1)}, bf16[8,24576]{1,0:T(8,128)(2,1)S(1)}, u32[]{:S(2)}, u32[]{:S(2)}) collective-permute-start(bf16[8,24576]{1,0:T(8,128)(2,1)} %refs_0_.3), channel_id=1, source_target_pairs={{0,24},{1,7},{2,26},{3,1},{4,28},{5,3},{6,30},{7,5},{8,0},{9,15},{... | collective-permute-start | bytes 1179656 | tf_op jit(solution)/shard_map/ppermute | solution.py:37
  4.2 0.9 collective-permute-start
  5.1 0.7 copy-done.4
  5.7 4.1 %pick.1 = (bf16[256,128]{1,0:T(8,128)(2,1)S(1)}, s32[6]{0:T(128)S(1)}, s32[1536]{0:T(1024)S(1)}) custom-call(s32[256]{0:T(256)S(1)} %copy-done.4, s32[1]{0:T(128)} %bitcast.first_ref, bf16[24576,128]{1,0:T(8,128)(2,1)} %tr_ref.1), custom_call_target="tpu_custom_call" | custom-call | flops 13200000000 | bytes 42000000 | tf_op jit(solution)/shard_map/pick/pallas_call | solution.py:163
  9.8 2.4 %collective-permute-start.3 = (bf16[256,128]{1,0:T(8,128)(2,1)S(1)}, bf16[256,128]{1,0:T(8,128)(2,1)S(1)}, u32[]{:S(2)}, u32[]{:S(2)}) collective-permute-start(bf16[256,128]{1,0:T(8,128)(2,1)S(1)} %get-tuple-element.31.a_ref), channel_id=1, source_target_pairs={{32,0},{96,64},{160,128},{224,192},{33,1},{97,65},{161,129},{225,1... | collective-permute-start | bytes 196616 | tf_op jit(solution)/shard_map/ppermute | solution.py:369
  12.3 1.9 %collective-permute-done.3.b_ref = bf16[256,128]{1,0:T(8,128)(2,1)S(1)} collective-permute-done((bf16[256,128]{1,0:T(8,128)(2,1)S(1)}, bf16[256,128]{1,0:T(8,128)(2,1)S(1)}, u32[]{:S(2)}, u32[]{:S(2)}) %collective-permute-start.3) | collective-permute-done | bytes 65568 | tf_op jit(solution)/shard_map/ppermute | solution.py:369
  14.1 0.0 collective-permute-done.2.refs_3_
  14.1 0.0 collective-permute-done.1.refs_2_
  14.2 0.0 collective-permute-done.refs_1_
  14.2 3.3 %collective-permute-start.4 = (bf16[32,256]{1,0:T(8,128)(2,1)S(1)}, bf16[32,256]{1,0:T(8,128)(2,1)S(1)}, u32[]{:S(2)}, u32[]{:S(2)}) collective-permute-start(bf16[32,256]{1,0:T(8,128)(2,1)S(1)} %stack_d.1.refs_0_), channel_id=1, source_target_pairs={{0,4},{1,17},{2,6},{3,19},{4,0},{5,21},{6,2},{7,23},{8,12},{9,25},... | collective-permute-start | bytes 49160 | tf_op jit(solution)/shard_map/ppermute | solution.py:37
  17.5 0.3 stack_p.1.refs_1_
  17.8 1.7 %collective-permute-done.4.refs_3_ = bf16[32,256]{1,0:T(8,128)(2,1)S(1)} collective-permute-done((bf16[32,256]{1,0:T(8,128)(2,1)S(1)}, bf16[32,256]{1,0:T(8,128)(2,1)S(1)}, u32[]{:S(2)}, u32[]{:S(2)}) %collective-permute-start.4) | collective-permute-done | bytes 16416 | tf_op jit(solution)/shard_map/ppermute | solution.py:37
  19.5 0.7 collective-permute-start.5
  20.2 3.1 %collective-permute-start.8 = (bf16[32,24576]{1,0:T(8,128)(2,1)S(1)}, bf16[32,24576]{1,0:T(8,128)(2,1)S(1)}, u32[]{:S(2)}, u32[]{:S(2)}) collective-permute-start(bf16[32,24576]{1,0:T(8,128)(2,1)S(1)} %stack_p.1.refs_1_), channel_id=1, source_target_pairs={{0,6},{1,25},{2,0},{3,27},{4,2},{5,29},{6,4},{7,31},{8,14},{9,1},{... | collective-permute-start | bytes 4718600 | tf_op jit(solution)/shard_map/ppermute | solution.py:37
  23.3 0.0 collective-permute-start.7
  23.3 0.0 collective-permute-done.5.b_ref
  23.3 0.1 collective-permute-start.9
  23.4 0.7 collective-permute-start.6
  24.1 0.0 collective-permute-done.6.more_ref
  24.1 17.1 %collective-permute-done.8.refs_2_.refs_0_.refs_3_ = bf16[32,24576]{1,0:T(8,128)(2,1)S(1)} collective-permute-done((bf16[32,24576]{1,0:T(8,128)(2,1)S(1)}, bf16[32,24576]{1,0:T(8,128)(2,1)S(1)}, u32[]{:S(2)}, u32[]{:S(2)}) %collective-permute-start.8) | collective-permute-done | bytes 1572896 | tf_op jit(solution)/shard_map/ppermute | solution.py:37
  41.2 3.7 %collective-permute-done.7.refs_1_.refs_0_.refs_2_ = bf16[32,24576]{1,0:T(8,128)(2,1)S(1)} collective-permute-done((bf16[32,24576]{1,0:T(8,128)(2,1)S(1)}, bf16[32,24576]{1,0:T(8,128)(2,1)S(1)}, u32[]{:S(2)}, u32[]{:S(2)}) %collective-permute-start.7) | collective-permute-done | bytes 1572896 | tf_op jit(solution)/shard_map/ppermute | solution.py:37
  44.9 0.0 collective-permute-done.9.refs_6_
  44.9 1.1 %stack_b.1 = bf16[32,12288]{1,0:T(8,128)(2,1)} custom-call(bf16[32,24576]{1,0:T(8,128)(2,1)S(1)} %collective-permute-done.8.refs_2_.refs_0_.refs_3_), custom_call_target="tpu_custom_call" | custom-call | flops 1100000000 | bytes 3500000 | tf_op jit(solution)/shard_map/stack_b/pallas_call | solution.py:60
  46.0 0.4 copy-done.2
  46.3 0.0 collective-permute-start.15
  46.3 1.0 %stack_a.1 = bf16[32,12288]{1,0:T(8,128)(2,1)} custom-call(bf16[32,24576]{1,0:T(8,128)(2,1)S(1)} %collective-permute-done.7.refs_1_.refs_0_.refs_2_), custom_call_target="tpu_custom_call" | custom-call | flops 1100000000 | bytes 3500000 | tf_op jit(solution)/shard_map/stack_a/pallas_call | solution.py:60
  47.3 2.0 %collective-permute-start.14 = (bf16[32,12288]{1,0:T(8,128)(2,1)}, bf16[32,12288]{1,0:T(8,128)(2,1)}, u32[]{:S(2)}, u32[]{:S(2)}) collective-permute-start(bf16[32,12288]{1,0:T(8,128)(2,1)} %stack_a.1), channel_id=1, source_target_pairs={{0,2},{1,9},{2,4},{3,11},{4,6},{5,13},{6,0},{7,15},{8,10},{9,17},{... | collective-permute-start | bytes 2359304 | tf_op jit(solution)/shard_map/ppermute | solution.py:37
  49.3 0.1 collective-permute-start.10
  49.4 1.2 %collective-permute-done.10.other_ref = bf16[128,256]{1,0:T(8,128)(2,1)S(1)} collective-permute-done((bf16[128,256]{1,0:T(8,128)(2,1)S(1)}, bf16[128,256]{1,0:T(8,128)(2,1)S(1)}, u32[]{:S(2)}, u32[]{:S(2)}) %collective-permute-start.10) | collective-permute-done | bytes 65568 | tf_op jit(solution)/shard_map/ppermute | solution.py:37
  50.7 5.2 %solve.1.a_ref = bf16[512,128]{1,0:T(8,128)(2,1)S(1)} custom-call(s32[1]{0:T(128)} %bitcast.1.me_ref, bf16[128,256]{1,0:T(8,128)(2,1)S(1)} %stack_l.1.own_ref, bf16[128,256]{1,0:T(8,128)(2,1)S(1)} %collective-permute-done.10.other_ref, bf16[256,128]{1,0:T(8,128)(2,1)S(1)} %add.3.top_ref, bf16[256,128]{1,0:T(8,128)(2,1)S(1)} %collective-permute-done.6.more_ref, ...), custom_call_target="tpu_custom_call" | custom-call | tf_op jit(solution)/shard_map/solve/pallas_call | solution.py:258
  55.9 0.7 collective-permute-start.11
  56.6 0.0 collective-permute-done.11.b_ref
  56.6 0.7 collective-permute-start.12
  57.3 0.2 collective-permute-start.16
  57.5 0.4 collective-permute-start.17
  57.9 0.0 collective-permute-done.12.b_ref
  57.9 0.0 copy-start.5
  57.9 1.4 %collective-permute-start.13 = (bf16[512,128]{1,0:T(8,128)(2,1)S(1)}, bf16[512,128]{1,0:T(8,128)(2,1)S(1)}, u32[]{:S(2)}, u32[]{:S(2)}) collective-permute-start(bf16[512,128]{1,0:T(8,128)(2,1)S(1)} %choose.3.ud_ref), channel_id=1, source_target_pairs={{0,128},{32,160},{64,192},{96,224},{1,129},{33,161},{65,193},{97,2... | collective-permute-start | bytes 393224 | tf_op jit(solution)/shard_map/ppermute | solution.py:369
  59.4 0.0 collective-permute-done.15.refs_1_.refs_5_
  59.4 0.2 collective-permute-start.19
  59.6 1.2 %collective-permute-done.14.refs_0_.refs_4_ = bf16[32,12288]{1,0:T(8,128)(2,1)} collective-permute-done((bf16[32,12288]{1,0:T(8,128)(2,1)}, bf16[32,12288]{1,0:T(8,128)(2,1)}, u32[]{:S(2)}, u32[]{:S(2)}) %collective-permute-start.14) | collective-permute-done | bytes 786464 | tf_op jit(solution)/shard_map/ppermute | solution.py:37
  60.8 1.4 %stack_q.1.refs_0_ = bf16[64,128]{1,0:T(8,128)(2,1)S(1)} custom-call(bf16[32,12288]{1,0:T(8,128)(2,1)} %collective-permute-done.14.refs_0_.refs_4_, bf16[32,12288]{1,0:T(8,128)(2,1)} %collective-permute-done.15.refs_1_.refs_5_), custom_call_target="tpu_custom_call" | custom-call | flops 65999998976 | bytes 210000000 | tf_op jit(solution)/shard_map/stack_q/pallas_call | solution.py:60
  62.2 17.6 %collective-permute-done.13.rest_ref = bf16[512,128]{1,0:T(8,128)(2,1)S(1)} collective-permute-done((bf16[512,128]{1,0:T(8,128)(2,1)S(1)}, bf16[512,128]{1,0:T(8,128)(2,1)S(1)}, u32[]{:S(2)}, u32[]{:S(2)}) %collective-permute-start.13) | collective-permute-done | bytes 131104 | tf_op jit(solution)/shard_map/ppermute | solution.py:369
  79.8 0.0 collective-permute-done.18.refs_9_
  79.8 0.0 collective-permute-done.16.refs_7_
  79.8 0.0 collective-permute-done.17.refs_8_
  79.9 10.7 %update.1 = bf16[24576,128]{1,0:T(8,128)(2,1)} custom-call(s32[6]{0:T(128)S(1)} %get-tuple-element.25.cnt_ref, s32[1536]{0:T(1024)S(1)} %get-tuple-element.26.lst_ref, s32[256]{0:T(256)S(1)} %copy-done.5, s32[1]{0:T(128)} %bitcast.first_ref, s32[1]{0:T(128)} %bitcast.1.me_ref, bf16[24576,128]{1,0:T(8,128)(2,1)} %tr_ref.1, ...), custom_call_target="tpu_custom_call" | custom-call | tf_op jit(solution)/shard_map/update/pallas_call | solution.py:340
  (19 shorter events, 0.1 us)
Async XLA Ops:
  0.0 14.1 %collective-permute-start.2 = (bf16[8,24576]{1,0:T(8,128)(2,1)}, bf16[8,24576]{1,0:T(8,128)(2,1)S(1)}, u32[]{:S(2)}, u32[]{:S(2)}) collective-permute-start(bf16[8,24576]{1,0:T(8,128)(2,1)} %refs_0_.3), channel_id=1, source_target_pairs={{0,16},{1,5},{2,18},{3,7},{4,20},{5,1},{6,22},{7,3},{8,24},{9,13},... | collective-permute-start | bytes 1179656 | tf_op jit(solution)/shard_map/ppermute | solution.py:37
  3.0 11.1 %collective-permute-start.1 = (bf16[8,24576]{1,0:T(8,128)(2,1)}, bf16[8,24576]{1,0:T(8,128)(2,1)S(1)}, u32[]{:S(2)}, u32[]{:S(2)}) collective-permute-start(bf16[8,24576]{1,0:T(8,128)(2,1)} %refs_0_.3), channel_id=1, source_target_pairs={{0,24},{1,7},{2,26},{3,1},{4,28},{5,3},{6,30},{7,5},{8,0},{9,15},{... | collective-permute-start | bytes 1179656 | tf_op jit(solution)/shard_map/ppermute | solution.py:37
  4.2 10.0 %collective-permute-start = (bf16[8,24576]{1,0:T(8,128)(2,1)}, bf16[8,24576]{1,0:T(8,128)(2,1)S(1)}, u32[]{:S(2)}, u32[]{:S(2)}) collective-permute-start(bf16[8,24576]{1,0:T(8,128)(2,1)} %refs_0_.3), channel_id=1, source_target_pairs={{0,8},{1,3},{2,10},{3,5},{4,12},{5,7},{6,14},{7,1},{8,16},{9,11},{... | collective-permute-start | bytes 1179656 | tf_op jit(solution)/shard_map/ppermute | solution.py:37
  5.1 0.7 copy-start.4
  5.7 8.4 %copy-start.6 = (bf16[8,24576]{1,0:T(8,128)(2,1)S(1)}, bf16[8,24576]{1,0:T(8,128)(2,1)}, u32[]{:S(2)}) copy-start(bf16[8,24576]{1,0:T(8,128)(2,1)} %refs_0_.3) | copy-start | bytes 1179652
  9.8 4.3 %collective-permute-start.3 = (bf16[256,128]{1,0:T(8,128)(2,1)S(1)}, bf16[256,128]{1,0:T(8,128)(2,1)S(1)}, u32[]{:S(2)}, u32[]{:S(2)}) collective-permute-start(bf16[256,128]{1,0:T(8,128)(2,1)S(1)} %get-tuple-element.31.a_ref), channel_id=1, source_target_pairs={{32,0},{96,64},{160,128},{224,192},{33,1},{97,65},{161,129},{225,1... | collective-permute-start | bytes 196616 | tf_op jit(solution)/shard_map/ppermute | solution.py:369
  14.2 5.3 %collective-permute-start.4 = (bf16[32,256]{1,0:T(8,128)(2,1)S(1)}, bf16[32,256]{1,0:T(8,128)(2,1)S(1)}, u32[]{:S(2)}, u32[]{:S(2)}) collective-permute-start(bf16[32,256]{1,0:T(8,128)(2,1)S(1)} %stack_d.1.refs_0_), channel_id=1, source_target_pairs={{0,4},{1,17},{2,6},{3,19},{4,0},{5,21},{6,2},{7,23},{8,12},{9,25},... | collective-permute-start | bytes 49160 | tf_op jit(solution)/shard_map/ppermute | solution.py:37
  19.5 3.8 %collective-permute-start.5 = (bf16[256,128]{1,0:T(8,128)(2,1)S(1)}, bf16[256,128]{1,0:T(8,128)(2,1)S(1)}, u32[]{:S(2)}, u32[]{:S(2)}) collective-permute-start(bf16[256,128]{1,0:T(8,128)(2,1)S(1)} %add.2.a_ref), channel_id=1, source_target_pairs={{64,0},{192,128},{65,1},{193,129},{66,2},{194,130},{67,3},{195,131... | collective-permute-start | bytes 196616 | tf_op jit(solution)/shard_map/ppermute | solution.py:369
  20.2 21.0 %collective-permute-start.8 = (bf16[32,24576]{1,0:T(8,128)(2,1)S(1)}, bf16[32,24576]{1,0:T(8,128)(2,1)S(1)}, u32[]{:S(2)}, u32[]{:S(2)}) collective-permute-start(bf16[32,24576]{1,0:T(8,128)(2,1)S(1)} %stack_p.1.refs_1_), channel_id=1, source_target_pairs={{0,6},{1,25},{2,0},{3,27},{4,2},{5,29},{6,4},{7,31},{8,14},{9,1},{... | collective-permute-start | bytes 4718600 | tf_op jit(solution)/shard_map/ppermute | solution.py:37
  23.3 21.6 %collective-permute-start.7 = (bf16[32,24576]{1,0:T(8,128)(2,1)S(1)}, bf16[32,24576]{1,0:T(8,128)(2,1)S(1)}, u32[]{:S(2)}, u32[]{:S(2)}) collective-permute-start(bf16[32,24576]{1,0:T(8,128)(2,1)S(1)} %stack_p.1.refs_1_), channel_id=1, source_target_pairs={{0,2},{1,9},{2,4},{3,11},{4,6},{5,13},{6,0},{7,15},{8,10},{9,17},{... | collective-permute-start | bytes 4718600 | tf_op jit(solution)/shard_map/ppermute | solution.py:37
  23.3 21.6 %collective-permute-start.9 = (bf16[32,24576]{1,0:T(8,128)(2,1)S(1)}, bf16[32,24576]{1,0:T(8,128)(2,1)S(1)}, u32[]{:S(2)}, u32[]{:S(2)}) collective-permute-start(bf16[32,24576]{1,0:T(8,128)(2,1)S(1)} %stack_p.1.refs_1_), channel_id=1, source_target_pairs={{0,1},{1,0},{2,3},{3,2},{4,5},{5,4},{6,7},{7,6},{8,9},{9,8},{10,11... | collective-permute-start | bytes 4718600 | tf_op jit(solution)/shard_map/ppermute | solution.py:37
  23.4 0.7 collective-permute-start.6
  44.9 4.4 %copy-start = (bf16[32,24576]{1,0:T(8,128)(2,1)}, bf16[32,24576]{1,0:T(8,128)(2,1)S(1)}, u32[]{:S(2)}) copy-start(bf16[32,24576]{1,0:T(8,128)(2,1)S(1)} %collective-permute-done.7.refs_1_.refs_0_.refs_2_) | copy-start | bytes 4718596
  44.9 1.4 %copy-start.2 = (bf16[32,24576]{1,0:T(8,128)(2,1)}, bf16[32,24576]{1,0:T(8,128)(2,1)S(1)}, u32[]{:S(2)}) copy-start(bf16[32,24576]{1,0:T(8,128)(2,1)S(1)} %collective-permute-done.9.refs_6_) | copy-start | bytes 4718596
  46.3 13.0 %collective-permute-start.15 = (bf16[32,12288]{1,0:T(8,128)(2,1)}, bf16[32,12288]{1,0:T(8,128)(2,1)}, u32[]{:S(2)}, u32[]{:S(2)}) collective-permute-start(bf16[32,12288]{1,0:T(8,128)(2,1)} %stack_b.1), channel_id=1, source_target_pairs={{0,6},{1,25},{2,0},{3,27},{4,2},{5,29},{6,4},{7,31},{8,14},{9,1},{... | collective-permute-start | bytes 2359304 | tf_op jit(solution)/shard_map/ppermute | solution.py:37
  47.3 13.5 %collective-permute-start.14 = (bf16[32,12288]{1,0:T(8,128)(2,1)}, bf16[32,12288]{1,0:T(8,128)(2,1)}, u32[]{:S(2)}, u32[]{:S(2)}) collective-permute-start(bf16[32,12288]{1,0:T(8,128)(2,1)} %stack_a.1), channel_id=1, source_target_pairs={{0,2},{1,9},{2,4},{3,11},{4,6},{5,13},{6,0},{7,15},{8,10},{9,17},{... | collective-permute-start | bytes 2359304 | tf_op jit(solution)/shard_map/ppermute | solution.py:37
  49.3 1.3 %collective-permute-start.10 = (bf16[128,256]{1,0:T(8,128)(2,1)S(1)}, bf16[128,256]{1,0:T(8,128)(2,1)S(1)}, u32[]{:S(2)}, u32[]{:S(2)}) collective-permute-start(bf16[128,256]{1,0:T(8,128)(2,1)S(1)} %stack_l.1.own_ref), channel_id=1, source_target_pairs={{0,1},{1,0},{2,3},{3,2},{4,5},{5,4},{6,7},{7,6},{8,9},{9,8},{10,11... | collective-permute-start | bytes 196616 | tf_op jit(solution)/shard_map/ppermute | solution.py:37
  50.7 6.6 %copy-start.1 = (bf16[32,24576]{1,0:T(8,128)(2,1)S(1)}, bf16[32,24576]{1,0:T(8,128)(2,1)}, u32[]{:S(2)}) copy-start(bf16[32,24576]{1,0:T(8,128)(2,1)} %copy-done) | copy-start | bytes 4718596
  55.9 0.7 collective-permute-start.11
  56.6 1.3 %collective-permute-start.12 = (bf16[512,128]{1,0:T(8,128)(2,1)S(1)}, bf16[512,128]{1,0:T(8,128)(2,1)S(1)}, u32[]{:S(2)}, u32[]{:S(2)}) collective-permute-start(bf16[512,128]{1,0:T(8,128)(2,1)S(1)} %choose.2.a_ref), channel_id=1, source_target_pairs={{0,32},{64,96},{1,33},{65,97},{2,34},{66,98},{3,35},{67,99},{4,36}... | collective-permute-start | bytes 393224 | tf_op jit(solution)/shard_map/ppermute | solution.py:369
  57.3 22.5 %collective-permute-start.16 = (bf16[32,24576]{1,0:T(8,128)(2,1)S(1)}, bf16[32,24576]{1,0:T(8,128)(2,1)S(1)}, u32[]{:S(2)}, u32[]{:S(2)}) collective-permute-start(bf16[32,24576]{1,0:T(8,128)(2,1)S(1)} %copy-done.1), channel_id=1, source_target_pairs={{0,1},{1,0},{2,3},{3,2},{4,5},{5,4},{6,7},{7,6},{8,9},{9,8},{10,11... | collective-permute-start | bytes 4718600 | tf_op jit(solution)/shard_map/ppermute | solution.py:37
  57.5 22.3 %collective-permute-start.17 = (bf16[32,24576]{1,0:T(8,128)(2,1)S(1)}, bf16[32,24576]{1,0:T(8,128)(2,1)S(1)}, u32[]{:S(2)}, u32[]{:S(2)}) collective-permute-start(bf16[32,24576]{1,0:T(8,128)(2,1)S(1)} %collective-permute-done.8.refs_2_.refs_0_.refs_3_), channel_id=1, source_target_pairs={{0,1},{1,0},{2,3},{3,2},{4,5},{5,4},{6,7},{7,6},{8,9},{9,8},{10,11... | collective-permute-start | bytes 4718600 | tf_op jit(solution)/shard_map/ppermute | solution.py:37
  57.9 21.9 %copy-start.3 = (bf16[32,24576]{1,0:T(8,128)(2,1)S(1)}, bf16[32,24576]{1,0:T(8,128)(2,1)}, u32[]{:S(2)}) copy-start(bf16[32,24576]{1,0:T(8,128)(2,1)} %copy-done.2) | copy-start | bytes 4718596
  57.9 21.9 %copy-start.5 = (s32[256]{0:T(256)S(1)}, s32[256]{0:T(256)}, u32[]{:S(2)}) copy-start(s32[256]{0:T(256)} %piv_ref.3) | copy-start | bytes 3076
  57.9 21.9 %collective-permute-start.13 = (bf16[512,128]{1,0:T(8,128)(2,1)S(1)}, bf16[512,128]{1,0:T(8,128)(2,1)S(1)}, u32[]{:S(2)}, u32[]{:S(2)}) collective-permute-start(bf16[512,128]{1,0:T(8,128)(2,1)S(1)} %choose.3.ud_ref), channel_id=1, source_target_pairs={{0,128},{32,160},{64,192},{96,224},{1,129},{33,161},{65,193},{97,2... | collective-permute-start | bytes 393224 | tf_op jit(solution)/shard_map/ppermute | solution.py:369
  59.4 20.5 %collective-permute-start.19 = (bf16[32,12288]{1,0:T(8,128)(2,1)}, bf16[32,12288]{1,0:T(8,128)(2,1)S(1)}, u32[]{:S(2)}, u32[]{:S(2)}) collective-permute-start(bf16[32,12288]{1,0:T(8,128)(2,1)} %collective-permute-done.15.refs_1_.refs_5_), channel_id=1, source_target_pairs={{0,1},{1,0},{2,3},{3,2},{4,5},{5,4},{6,7},{7,6},{8,9},{9,8},{10,11... | collective-permute-start | bytes 2359304 | tf_op jit(solution)/shard_map/ppermute | solution.py:37
  60.8 19.0 %collective-permute-start.18 = (bf16[32,12288]{1,0:T(8,128)(2,1)}, bf16[32,12288]{1,0:T(8,128)(2,1)S(1)}, u32[]{:S(2)}, u32[]{:S(2)}) collective-permute-start(bf16[32,12288]{1,0:T(8,128)(2,1)} %collective-permute-done.14.refs_0_.refs_4_), channel_id=1, source_target_pairs={{0,1},{1,0},{2,3},{3,2},{4,5},{5,4},{6,7},{7,6},{8,9},{9,8},{10,11... | collective-permute-start | bytes 2359304 | tf_op jit(solution)/shard_map/ppermute | solution.py:37

commit v7 on v6

--- a/solution.py
+++ b/solution.py
@@ -106,11 +106,31 @@
     )(first, a, b)
 
 
-def pick_kernel(blk, piv_ref, first_ref, trailing_ref, out_ref, cnt_ref, lst_ref, own_ref, group_ref, rows_ref, sem):
+def join_kernel(rows, mask, first_ref, a_ref, b_ref, below_ref, out_ref):
+    width = a_ref.shape[0]
+    choose_kernel(rows, mask, first_ref, a_ref, b_ref, out_ref.at[pl.ds(0, width)])
+    out_ref[width:, :] = below_ref[...]
+
+
+def join(first, rows, others, a, b, below):
+    width, cols = a.shape
+    return pl.pallas_call(
+        functools.partial(join_kernel, rows, sum(1 << z for z in others)),
+        in_specs=[SMEM] + [VMEM] * 3,
+        out_specs=VMEM,
+        out_shape=jax.ShapeDtypeStruct((2 * width, cols), a.dtype),
+        compiler_params=params(2),
+        name="join",
+    )(first, a, b, below)
+
+
+def pick_kernel(blk, piv_ref, first_ref, trailing_ref, out_ref, head_ref, cnt_ref, lst_ref, own_ref, group_ref, rows_ref, sem, head_sem):
     width = piv_ref.shape[0]
     rows = trailing_ref.shape[0]
     first = first_ref[0]
     nblk = cnt_ref.shape[0]
+    head = pltpu.make_async_copy(trailing_ref.at[pl.ds(0, width)], head_ref, head_sem)
+    head.start()
     for b in range(nblk):
         cnt_ref[b] = 0
 
@@ -154,6 +174,7 @@
 
     lax.fori_loop(0, n, extract, 0)
     out_ref[...] = rows_ref[...].astype(jnp.bfloat16)
+    head.wait()
 
 
 def pick(trailing, pivots, first, blk):
@@ -163,8 +184,9 @@
     return pl.pallas_call(
         functools.partial(pick_kernel, blk),
         in_specs=[SMEM, SMEM, pl.BlockSpec(memory_space=pltpu.HBM)],
-        out_specs=[VMEM, SMEM, SMEM],
+        out_specs=[VMEM, VMEM, SMEM, SMEM],
         out_shape=[
+            jax.ShapeDtypeStruct((width, cols), jnp.bfloat16),
             jax.ShapeDtypeStruct((width, cols), jnp.bfloat16),
             jax.ShapeDtypeStruct((nblk,), jnp.int32),
             jax.ShapeDtypeStruct((nblk * width,), jnp.int32),
@@ -173,6 +195,7 @@
             pltpu.SMEM((width + 8,), jnp.int32),
             pltpu.VMEM((width, 16, cols), jnp.bfloat16),
             pltpu.VMEM((width, cols), jnp.float32),
+            pltpu.SemaphoreType.DMA,
             pltpu.SemaphoreType.DMA,
         ],
         compiler_params=params(6),
@@ -229,7 +252,7 @@
     return pl.ds(pl.multiple_of(((x * 4 + y) * 2 + core) * 8, 8), 8)
 
 
-def solve_kernel(me_ref, own_ref, other_ref, top_ref, more_ref, head_ref, out_ref, a_ref, g_ref):
+def solve_kernel(me_ref, own_ref, other_ref, top_ref, more_ref, out_ref, a_ref, g_ref):
     n = top_ref.shape[0]
     h = n // 2
     me = me_ref[0]
@@ -247,24 +270,20 @@
     top = sum(r[...].astype(jnp.float32) for r in (top_ref, more_ref))
     u1 = dot(x1, top[:h])
     u2 = dot(x2, top[h:] - dot_exact(s21.astype(jnp.bfloat16), u1))
-    out_ref[:n, :] = jnp.concatenate([u1, u2], axis=0).astype(jnp.bfloat16)
-    out_ref[n:, :] = head_ref[...]
-
-
-def solve(me, own, other, top, more, trailing):
+    out_ref[...] = jnp.concatenate([u1, u2], axis=0).astype(jnp.bfloat16)
+
+
+def solve(me, own, other, top, more):
     n, cols = top.shape
-    whole = pl.BlockSpec((n // 2, n), lambda i: (0, 0))
-    tall = pl.BlockSpec((n, cols), lambda i: (0, 0))
     return pl.pallas_call(
         solve_kernel,
-        grid=(1,),
-        in_specs=[SMEM, whole, whole] + [tall] * 3,
-        out_specs=pl.BlockSpec((2 * n, cols), lambda i: (0, 0)),
-        out_shape=jax.ShapeDtypeStruct((2 * n, cols), jnp.bfloat16),
+        in_specs=[SMEM] + [VMEM] * 4,
+        out_specs=VMEM,
+        out_shape=jax.ShapeDtypeStruct((n, cols), jnp.bfloat16),
         scratch_shapes=[pltpu.VMEM((n, n), jnp.float32), pltpu.VMEM((n, n), jnp.float32)],
         compiler_params=params(10),
         name="solve",
-    )(me, own, other, top, more, trailing)
+    )(me, own, other, top, more)
 
 
 def update_kernel(nblk, cnt_ref, lst_ref, piv_ref, first_ref, me_ref, tr_ref, ud_ref, rest_ref, *refs):
@@ -370,32 +389,35 @@
 
     p, m, q = [send(panel_t, hop(d, 0, True)) for d in (1, -1, 2)]
 
-    top, cnt, lst = pick(trailing, pivots, first, blk)
+    top, disp, cnt, lst = pick(trailing, pivots, first, blk)
     more = zsend(top, [(1, 0), (3, 2), (5, 4), (7, 6)])
-    p, m, q, top, more = barrier((p, m, q, top, more))
+    lower = zsend(disp, [(0, 2)])
+    p, m, q, top, more, lower = barrier((p, m, q, top, more, lower))
 
     up, down, across = hop(0, 1, True), hop(0, -1, True), hop(0, 2, True)
     diag = stack([panel_t, p, m, q], 0, width, "stack_d")
-    diag_q = send(diag, across)
+    diag_q, diag_p, diag_m = send(diag, across), send(diag, up), send(diag, down)
     block = stack([panel_t, p, m, q], 0, rows, "stack_p")
+    block, diag_q, diag_p, diag_m = barrier((block, diag_q, diag_p, diag_m))
+    near, far = send(block, up), send(block, down)
+    own = stack([diag, diag_p, diag_m, diag_q], 0, width, "stack_l")
+    top, more, block2 = barrier((top, more, block))
     top = add(top, more)
-    block, diag_q, top = barrier((block, diag_q, top))
-    near, far = send(block, up), send(block, down)
     more = zsend(top, [(2, 0), (6, 4)])
     top = add(top, more)
-    top, block2 = barrier((top, block))
-    swap = send(block2, CORES)
     more = zsend(top, [(4, 0)])
-    more, near, far, swap = barrier((more, near, far, swap))
-    own = stack([diag, near, far, diag_q], 0, width, "stack_l")
     other = send(own, CORES)
+    disp = choose(first, rows, (2,), disp, lower)
+    disp = choose(first, rows, (1, 3), disp, zsend(disp, [(0, 1), (2, 3)]))
+    swap = send(block, CORES)
+    u = solve(me, own, other, top, more)
+    u, near, far, swap, disp = barrier((u, near, far, swap, disp))
     fa, fb = stack([near], 0, half, "stack_a"), stack([far], half, half, "stack_b")
     qa, qb = send(fa, up), send(fb, down)
-    ud = solve(me, own, other, top, more, trailing)
-    ud = choose(first, rows, (2,), ud, zsend(ud, [(0, 2)]))
-    ud, near, far = barrier((ud, near, far))
+    u = choose(first, rows, (2,), u, zsend(u, [(0, 2)]))
+    u, near, far = barrier((u, near, far))
     other_near, other_far = send(near, CORES), send(far, CORES)
-    ud = choose(first, rows, (1, 3), ud, zsend(ud, [(0, 1), (2, 3)]))
+    ud = join(first, rows, (1, 3), u, zsend(u, [(0, 1), (2, 3)]), disp)
     rest = zsend(ud, [(i, i + 4) for i in range(4)])
     ahead = stack([qa, qb], 0, 128, "stack_q", 60)
     own = [block, near, far, qa, qb]

time: 91.1 us -> 87 us (0.955)
  the two profiles are of different devices: /device:TPU:224 before, /device:TPU:1 now
where the time goes in v7:
time: 87 us; the launch traced here: 86.4 us
  starting transfers between devices  42.1 us (48%)
  Pallas kernels  22.5 us (26%)
  waiting for transfers between devices  20.9 us (24%)
    ppermute x16, starting transfers between devices, send(): return lax.ppermute(block, 'pcol', pairs)  27.9 us
    ppermute x8, waiting for transfers between devices, zsend(): return lax.ppermute(x, 'prow', pairs)  15.8 us
    ppermute x8, starting transfers between devices, zsend(): return lax.ppermute(x, 'prow', pairs)  14.2 us
    pallas_call x1, Pallas kernels, update(): pl.pallas_call(functools.partial(update_kernel, nblk), grid=(nblk,), in_s...  11.1 us
    ppermute x16, waiting for transfers between devices, send(): return lax.ppermute(block, 'pcol', pairs)  5.07 us
    pallas_call x1, Pallas kernels, solve(): pl.pallas_call(solve_kernel, in_specs=[SMEM] + [VMEM] * 4, out_specs=VMEM...  4.25 us
    pallas_call x1, Pallas kernels, pick(): pl.pallas_call(functools.partial(pick_kernel, blk), in_specs=[SMEM, SMEM,...  3.74 us
    pallas_call x6, Pallas kernels, stack(): pl.pallas_call(functools.partial(stack_kernel, start, min(cols, 1024)), i...  3.3 us
  transfers between devices with their start and end apart: 24, of which 8 were waited for; matrix products, arithmetic and copies ran while one was open for 0% of the time, Pallas kernels for 11%

profile of v7, /device:TPU:1, one launch (start us, length us, event | category | flops | bytes accessed | tf_op | source)
XLA Modules:
  0.0 86.4 jit_solution(3137254288176215667)
XLA Ops:
  0.0 3.7 %collective-permute-start.2 = (bf16[8,24576]{1,0:T(8,128)(2,1)}, bf16[8,24576]{1,0:T(8,128)(2,1)S(1)}, u32[]{:S(2)}, u32[]{:S(2)}) collective-permute-start(bf16[8,24576]{1,0:T(8,128)(2,1)} %refs_0_.3), channel_id=1, source_target_pairs={{0,16},{1,5},{2,18},{3,7},{4,20},{5,1},{6,22},{7,3},{8,24},{9,13},... | collective-permute-start | bytes 1179656 | tf_op jit(solution)/shard_map/ppermute | solution.py:37
  3.7 0.8 collective-permute-start.1
  4.5 0.7 collective-permute-start
  5.2 0.7 copy-done
  5.9 3.7 %pick.1 = (bf16[256,128]{1,0:T(8,128)(2,1)S(1)}, bf16[256,128]{1,0:T(8,128)(2,1)S(1)}, s32[6]{0:T(128)S(1)}, s32[1536]{0:T(1024)S(1)}) custom-call(s32[256]{0:T(256)S(1)} %copy-done, s32[1]{0:T(128)} %bitcast.first_ref, bf16[24576,128]{1,0:T(8,128)(2,1)} %tr_ref.1), custom_call_target="tpu_custom_call" | custom-call | flops 13200000000 | bytes 42000000 | tf_op jit(solution)/shard_map/pick/pallas_call | solution.py:184
  9.6 1.3 %collective-permute-start.3 = (bf16[256,128]{1,0:T(8,128)(2,1)S(1)}, bf16[256,128]{1,0:T(8,128)(2,1)S(1)}, u32[]{:S(2)}, u32[]{:S(2)}) collective-permute-start(bf16[256,128]{1,0:T(8,128)(2,1)S(1)} %get-tuple-element.42.a_ref), channel_id=1, source_target_pairs={{32,0},{96,64},{160,128},{224,192},{33,1},{97,65},{161,129},{225,1... | collective-permute-start | bytes 196616 | tf_op jit(solution)/shard_map/ppermute | solution.py:388
  10.9 4.7 %collective-permute-start.4 = (bf16[256,128]{1,0:T(8,128)(2,1)S(1)}, bf16[256,128]{1,0:T(8,128)(2,1)S(1)}, u32[]{:S(2)}, u32[]{:S(2)}) collective-permute-start(bf16[256,128]{1,0:T(8,128)(2,1)S(1)} %get-tuple-element.32.a_ref), channel_id=1, source_target_pairs={{0,64},{1,65},{2,66},{3,67},{4,68},{5,69},{6,70},{7,71},{8,72},{9,... | collective-permute-start | bytes 196616 | tf_op jit(solution)/shard_map/ppermute | solution.py:388
  15.7 1.3 %collective-permute-done.4.b_ref = bf16[256,128]{1,0:T(8,128)(2,1)S(1)} collective-permute-done((bf16[256,128]{1,0:T(8,128)(2,1)S(1)}, bf16[256,128]{1,0:T(8,128)(2,1)S(1)}, u32[]{:S(2)}, u32[]{:S(2)}) %collective-permute-start.4) | collective-permute-done | bytes 65568 | tf_op jit(solution)/shard_map/ppermute | solution.py:388
  17.0 0.0 collective-permute-done.refs_1_
  17.0 2.6 %collective-permute-start.7 = (bf16[32,256]{1,0:T(8,128)(2,1)S(1)}, bf16[32,256]{1,0:T(8,128)(2,1)S(1)}, u32[]{:S(2)}, u32[]{:S(2)}) collective-permute-start(bf16[32,256]{1,0:T(8,128)(2,1)S(1)} %stack_d.1.refs_0_), channel_id=1, source_target_pairs={{0,6},{1,25},{2,0},{3,27},{4,2},{5,29},{6,4},{7,31},{8,14},{9,1},{... | collective-permute-start | bytes 49160 | tf_op jit(solution)/shard_map/ppermute | solution.py:37
  19.6 1.7 %collective-permute-start.5 = (bf16[32,256]{1,0:T(8,128)(2,1)S(1)}, bf16[32,256]{1,0:T(8,128)(2,1)S(1)}, u32[]{:S(2)}, u32[]{:S(2)}) collective-permute-start(bf16[32,256]{1,0:T(8,128)(2,1)S(1)} %stack_d.1.refs_0_), channel_id=1, source_target_pairs={{0,4},{1,17},{2,6},{3,19},{4,0},{5,21},{6,2},{7,23},{8,12},{9,25},... | collective-permute-start | bytes 49160 | tf_op jit(solution)/shard_map/ppermute | solution.py:37
  21.3 0.3 stack_p.1.refs_1_
  21.6 0.0 collective-permute-done.7.refs_2_
  21.7 1.7 %collective-permute-done.6.refs_1_ = bf16[32,256]{1,0:T(8,128)(2,1)S(1)} collective-permute-done((bf16[32,256]{1,0:T(8,128)(2,1)S(1)}, bf16[32,256]{1,0:T(8,128)(2,1)S(1)}, u32[]{:S(2)}, u32[]{:S(2)}) %collective-permute-start.6) | collective-permute-done | bytes 16416 | tf_op jit(solution)/shard_map/ppermute | solution.py:37
  23.4 0.3 collective-permute-done.5.refs_3_
  23.7 3.9 %collective-permute-start.13 = (bf16[32,24576]{1,0:T(8,128)(2,1)S(1)}, bf16[32,24576]{1,0:T(8,128)(2,1)S(1)}, u32[]{:S(2)}, u32[]{:S(2)}) collective-permute-start(bf16[32,24576]{1,0:T(8,128)(2,1)S(1)} %stack_p.1.refs_1_), channel_id=1, source_target_pairs={{0,1},{1,0},{2,3},{3,2},{4,5},{5,4},{6,7},{7,6},{8,9},{9,8},{10,11... | collective-permute-start | bytes 4718600 | tf_op jit(solution)/shard_map/ppermute | solution.py:37
  27.6 2.1 %collective-permute-start.12 = (bf16[32,24576]{1,0:T(8,128)(2,1)S(1)}, bf16[32,24576]{1,0:T(8,128)(2,1)}, u32[]{:S(2)}, u32[]{:S(2)}) collective-permute-start(bf16[32,24576]{1,0:T(8,128)(2,1)S(1)} %stack_p.1.refs_1_), channel_id=1, source_target_pairs={{0,6},{1,25},{2,0},{3,27},{4,2},{5,29},{6,4},{7,31},{8,14},{9,1},{... | collective-permute-start | bytes 4718600 | tf_op jit(solution)/shard_map/ppermute | solution.py:37
  29.7 0.0 collective-permute-start.11
  29.7 1.3 %collective-permute-start.14 = (bf16[256,128]{1,0:T(8,128)(2,1)S(1)}, bf16[256,128]{1,0:T(8,128)(2,1)S(1)}, u32[]{:S(2)}, u32[]{:S(2)}) collective-permute-start(bf16[256,128]{1,0:T(8,128)(2,1)S(1)} %choose.3.a_ref), channel_id=1, source_target_pairs={{0,32},{64,96},{1,33},{65,97},{2,34},{66,98},{3,35},{67,99},{4,36}... | collective-permute-start | bytes 196616 | tf_op jit(solution)/shard_map/ppermute | solution.py:388
  31.0 1.3 %collective-permute-start.9 = (bf16[256,128]{1,0:T(8,128)(2,1)S(1)}, bf16[256,128]{1,0:T(8,128)(2,1)S(1)}, u32[]{:S(2)}, u32[]{:S(2)}) collective-permute-start(bf16[256,128]{1,0:T(8,128)(2,1)S(1)} %add.2.a_ref), channel_id=1, source_target_pairs={{64,0},{192,128},{65,1},{193,129},{66,2},{194,130},{67,3},{195,131... | collective-permute-start | bytes 196616 | tf_op jit(solution)/shard_map/ppermute | solution.py:388
  32.3 5.0 %collective-permute-done.9.b_ref = bf16[256,128]{1,0:T(8,128)(2,1)S(1)} collective-permute-done((bf16[256,128]{1,0:T(8,128)(2,1)S(1)}, bf16[256,128]{1,0:T(8,128)(2,1)S(1)}, u32[]{:S(2)}, u32[]{:S(2)}) %collective-permute-start.9) | collective-permute-done | bytes 65568 | tf_op jit(solution)/shard_map/ppermute | solution.py:388
  37.3 1.9 %collective-permute-start.8 = (bf16[128,256]{1,0:T(8,128)(2,1)S(1)}, bf16[128,256]{1,0:T(8,128)(2,1)S(1)}, u32[]{:S(2)}, u32[]{:S(2)}) collective-permute-start(bf16[128,256]{1,0:T(8,128)(2,1)S(1)} %stack_l.1.own_ref), channel_id=1, source_target_pairs={{0,1},{1,0},{2,3},{3,2},{4,5},{5,4},{6,7},{7,6},{8,9},{9,8},{10,11... | collective-permute-start | bytes 196616 | tf_op jit(solution)/shard_map/ppermute | solution.py:37
  39.2 0.0 collective-permute-done.14.b_ref
  39.3 1.3 %collective-permute-start.10 = (bf16[256,128]{1,0:T(8,128)(2,1)S(1)}, bf16[256,128]{1,0:T(8,128)(2,1)S(1)}, u32[]{:S(2)}, u32[]{:S(2)}) collective-permute-start(bf16[256,128]{1,0:T(8,128)(2,1)S(1)} %add.3.top_ref), channel_id=1, source_target_pairs={{128,0},{129,1},{130,2},{131,3},{132,4},{133,5},{134,6},{135,7},{1... | collective-permute-start | bytes 196616 | tf_op jit(solution)/shard_map/ppermute | solution.py:388
  40.6 8.2 %collective-permute-done.10.more_ref = bf16[256,128]{1,0:T(8,128)(2,1)S(1)} collective-permute-done((bf16[256,128]{1,0:T(8,128)(2,1)S(1)}, bf16[256,128]{1,0:T(8,128)(2,1)S(1)}, u32[]{:S(2)}, u32[]{:S(2)}) %collective-permute-start.10) | collective-permute-done | bytes 65568 | tf_op jit(solution)/shard_map/ppermute | solution.py:388
  48.8 4.2 %solve.1.a_ref = bf16[256,128]{1,0:T(8,128)(2,1)S(1)} custom-call(s32[1]{0:T(128)} %bitcast.1.me_ref, bf16[128,256]{1,0:T(8,128)(2,1)S(1)} %stack_l.1.own_ref, bf16[128,256]{1,0:T(8,128)(2,1)S(1)} %collective-permute-done.8.other_ref, bf16[256,128]{1,0:T(8,128)(2,1)S(1)} %add.3.top_ref, bf16[256,128]{1,0:T(8,128)(2,1)S(1)} %collective-permute-done.10.more_ref), custom_call_target="tpu_custom_call" | custom-call | tf_op jit(solution)/shard_map/solve/pallas_call | solution.py:278
  53.0 0.0 collective-permute-done.13.refs_6_
  53.0 0.0 collective-permute-done.12.refs_0_.refs_3_
  53.1 0.0 collective-permute-done.11.refs_0_.refs_2_
  53.1 1.5 %stack_b.1 = bf16[32,12288]{1,0:T(8,128)(2,1)S(1)} custom-call(bf16[32,24576]{1,0:T(8,128)(2,1)} %collective-permute-done.12.refs_0_.refs_3_), custom_call_target="tpu_custom_call" | custom-call | flops 1100000000 | bytes 3500000 | tf_op jit(solution)/shard_map/stack_b/pallas_call | solution.py:60
  54.6 2.2 %collective-permute-start.19 = (bf16[32,12288]{1,0:T(8,128)(2,1)S(1)}, bf16[32,12288]{1,0:T(8,128)(2,1)S(1)}, u32[]{:S(2)}, u32[]{:S(2)}) collective-permute-start(bf16[32,12288]{1,0:T(8,128)(2,1)S(1)} %stack_b.1), channel_id=1, source_target_pairs={{0,6},{1,25},{2,0},{3,27},{4,2},{5,29},{6,4},{7,31},{8,14},{9,1},{... | collective-permute-start | bytes 2359304 | tf_op jit(solution)/shard_map/ppermute | solution.py:37
  56.7 1.5 %stack_a.1 = bf16[32,12288]{1,0:T(8,128)(2,1)S(1)} custom-call(bf16[32,24576]{1,0:T(8,128)(2,1)} %collective-permute-done.11.refs_0_.refs_2_), custom_call_target="tpu_custom_call" | custom-call | flops 1100000000 | bytes 3500000 | tf_op jit(solution)/shard_map/stack_a/pallas_call | solution.py:60
  58.2 0.1 collective-permute-start.18
  58.3 1.7 %collective-permute-start.15 = (bf16[256,128]{1,0:T(8,128)(2,1)S(1)}, bf16[256,128]{1,0:T(8,128)(2,1)S(1)}, u32[]{:S(2)}, u32[]{:S(2)}) collective-permute-start(bf16[256,128]{1,0:T(8,128)(2,1)S(1)} %solve.1.a_ref), channel_id=1, source_target_pairs={{0,64},{1,65},{2,66},{3,67},{4,68},{5,69},{6,70},{7,71},{8,72},{9,... | collective-permute-start | bytes 196616 | tf_op jit(solution)/shard_map/ppermute | solution.py:388
  60.0 1.3 %collective-permute-done.15.b_ref = bf16[256,128]{1,0:T(8,128)(2,1)S(1)} collective-permute-done((bf16[256,128]{1,0:T(8,128)(2,1)S(1)}, bf16[256,128]{1,0:T(8,128)(2,1)S(1)}, u32[]{:S(2)}, u32[]{:S(2)}) %collective-permute-start.15) | collective-permute-done | bytes 65568 | tf_op jit(solution)/shard_map/ppermute | solution.py:388
  61.3 1.3 %collective-permute-start.16 = (bf16[256,128]{1,0:T(8,128)(2,1)S(1)}, bf16[256,128]{1,0:T(8,128)(2,1)S(1)}, u32[]{:S(2)}, u32[]{:S(2)}) collective-permute-start(bf16[256,128]{1,0:T(8,128)(2,1)S(1)} %choose.5.a_ref), channel_id=1, source_target_pairs={{0,32},{64,96},{1,33},{65,97},{2,34},{66,98},{3,35},{67,99},{4,36}... | collective-permute-start | bytes 196616 | tf_op jit(solution)/shard_map/ppermute | solution.py:388
  62.6 3.7 %collective-permute-start.20 = (bf16[32,24576]{1,0:T(8,128)(2,1)}, bf16[32,24576]{1,0:T(8,128)(2,1)S(1)}, u32[]{:S(2)}, u32[]{:S(2)}) collective-permute-start(bf16[32,24576]{1,0:T(8,128)(2,1)} %collective-permute-done.11.refs_0_.refs_2_), channel_id=1, source_target_pairs={{0,1},{1,0},{2,3},{3,2},{4,5},{5,4},{6,7},{7,6},{8,9},{9,8},{10,11... | collective-permute-start | bytes 4718600 | tf_op jit(solution)/shard_map/ppermute | solution.py:37
  66.3 0.3 collective-permute-start.21
  66.6 0.0 collective-permute-done.16.b_ref
  66.6 0.0 copy-start.1
  66.6 1.3 %collective-permute-start.17 = (bf16[512,128]{1,0:T(8,128)(2,1)S(1)}, bf16[512,128]{1,0:T(8,128)(2,1)S(1)}, u32[]{:S(2)}, u32[]{:S(2)}) collective-permute-start(bf16[512,128]{1,0:T(8,128)(2,1)S(1)} %join.1.ud_ref), channel_id=1, source_target_pairs={{0,128},{32,160},{64,192},{96,224},{1,129},{33,161},{65,193},{97,2... | collective-permute-start | bytes 393224 | tf_op jit(solution)/shard_map/ppermute | solution.py:388
  67.9 0.0 collective-permute-done.19.refs_1_.refs_5_
  67.9 1.6 %collective-permute-start.23 = (bf16[32,12288]{1,0:T(8,128)(2,1)S(1)}, bf16[32,12288]{1,0:T(8,128)(2,1)S(1)}, u32[]{:S(2)}, u32[]{:S(2)}) collective-permute-start(bf16[32,12288]{1,0:T(8,128)(2,1)S(1)} %collective-permute-done.19.refs_1_.refs_5_), channel_id=1, source_target_pairs={{0,1},{1,0},{2,3},{3,2},{4,5},{5,4},{6,7},{7,6},{8,9},{9,8},{10,11... | collective-permute-start | bytes 2359304 | tf_op jit(solution)/shard_map/ppermute | solution.py:37
  69.5 1.1 %collective-permute-done.18.refs_0_.refs_4_ = bf16[32,12288]{1,0:T(8,128)(2,1)S(1)} collective-permute-done((bf16[32,12288]{1,0:T(8,128)(2,1)S(1)}, bf16[32,12288]{1,0:T(8,128)(2,1)S(1)}, u32[]{:S(2)}, u32[]{:S(2)}) %collective-permute-start.18) | collective-permute-done | bytes 786464 | tf_op jit(solution)/shard_map/ppermute | solution.py:37
  70.6 2.8 %collective-permute-start.22 = (bf16[32,12288]{1,0:T(8,128)(2,1)S(1)}, bf16[32,12288]{1,0:T(8,128)(2,1)S(1)}, u32[]{:S(2)}, u32[]{:S(2)}) collective-permute-start(bf16[32,12288]{1,0:T(8,128)(2,1)S(1)} %collective-permute-done.18.refs_0_.refs_4_), channel_id=1, source_target_pairs={{0,1},{1,0},{2,3},{3,2},{4,5},{5,4},{6,7},{7,6},{8,9},{9,8},{10,11... | collective-permute-start | bytes 2359304 | tf_op jit(solution)/shard_map/ppermute | solution.py:37
  73.4 0.0 collective-permute-done.17.rest_ref
  73.4 1.9 %collective-permute-done.22.refs_9_ = bf16[32,12288]{1,0:T(8,128)(2,1)S(1)} collective-permute-done((bf16[32,12288]{1,0:T(8,128)(2,1)S(1)}, bf16[32,12288]{1,0:T(8,128)(2,1)S(1)}, u32[]{:S(2)}, u32[]{:S(2)}) %collective-permute-start.22) | collective-permute-done | bytes 786464 | tf_op jit(solution)/shard_map/ppermute | solution.py:37
  75.3 11.1 %update.1 = bf16[24576,128]{1,0:T(8,128)(2,1)} custom-call(s32[6]{0:T(128)S(1)} %get-tuple-element.29.cnt_ref, s32[1536]{0:T(1024)S(1)} %get-tuple-element.30.lst_ref, s32[256]{0:T(256)S(1)} %copy-done.1, s32[1]{0:T(128)} %bitcast.first_ref, s32[1]{0:T(128)} %bitcast.1.me_ref, bf16[24576,128]{1,0:T(8,128)(2,1)} %tr_ref.1, bf16[512,128]{1,0:T(8,128)(2,1)S(1)} %join.1.ud_ref, ...), custom_call_target="tpu_custom_call" | custom-call | tf_op jit(solution)/shard_map/update/pallas_call | solution.py:359
  (21 shorter events, 0.1 us)
Async XLA Ops:
  0.0 17.0 %collective-permute-start.2 = (bf16[8,24576]{1,0:T(8,128)(2,1)}, bf16[8,24576]{1,0:T(8,128)(2,1)S(1)}, u32[]{:S(2)}, u32[]{:S(2)}) collective-permute-start(bf16[8,24576]{1,0:T(8,128)(2,1)} %refs_0_.3), channel_id=1, source_target_pairs={{0,16},{1,5},{2,18},{3,7},{4,20},{5,1},{6,22},{7,3},{8,24},{9,13},... | collective-permute-start | bytes 1179656 | tf_op jit(solution)/shard_map/ppermute | solution.py:37
  3.7 13.3 %collective-permute-start.1 = (bf16[8,24576]{1,0:T(8,128)(2,1)}, bf16[8,24576]{1,0:T(8,128)(2,1)S(1)}, u32[]{:S(2)}, u32[]{:S(2)}) collective-permute-start(bf16[8,24576]{1,0:T(8,128)(2,1)} %refs_0_.3), channel_id=1, source_target_pairs={{0,24},{1,7},{2,26},{3,1},{4,28},{5,3},{6,30},{7,5},{8,0},{9,15},{... | collective-permute-start | bytes 1179656 | tf_op jit(solution)/shard_map/ppermute | solution.py:37
  4.5 12.5 %collective-permute-start = (bf16[8,24576]{1,0:T(8,128)(2,1)}, bf16[8,24576]{1,0:T(8,128)(2,1)S(1)}, u32[]{:S(2)}, u32[]{:S(2)}) collective-permute-start(bf16[8,24576]{1,0:T(8,128)(2,1)} %refs_0_.3), channel_id=1, source_target_pairs={{0,8},{1,3},{2,10},{3,5},{4,12},{5,7},{6,14},{7,1},{8,16},{9,11},{... | collective-permute-start | bytes 1179656 | tf_op jit(solution)/shard_map/ppermute | solution.py:37
  5.2 0.7 copy-start
  5.9 11.1 %copy-start.2 = (bf16[8,24576]{1,0:T(8,128)(2,1)S(1)}, bf16[8,24576]{1,0:T(8,128)(2,1)}, u32[]{:S(2)}) copy-start(bf16[8,24576]{1,0:T(8,128)(2,1)} %refs_0_.3) | copy-start | bytes 1179652
  9.6 6.1 %collective-permute-start.3 = (bf16[256,128]{1,0:T(8,128)(2,1)S(1)}, bf16[256,128]{1,0:T(8,128)(2,1)S(1)}, u32[]{:S(2)}, u32[]{:S(2)}) collective-permute-start(bf16[256,128]{1,0:T(8,128)(2,1)S(1)} %get-tuple-element.42.a_ref), channel_id=1, source_target_pairs={{32,0},{96,64},{160,128},{224,192},{33,1},{97,65},{161,129},{225,1... | collective-permute-start | bytes 196616 | tf_op jit(solution)/shard_map/ppermute | solution.py:388
  10.9 6.1 %collective-permute-start.4 = (bf16[256,128]{1,0:T(8,128)(2,1)S(1)}, bf16[256,128]{1,0:T(8,128)(2,1)S(1)}, u32[]{:S(2)}, u32[]{:S(2)}) collective-permute-start(bf16[256,128]{1,0:T(8,128)(2,1)S(1)} %get-tuple-element.32.a_ref), channel_id=1, source_target_pairs={{0,64},{1,65},{2,66},{3,67},{4,68},{5,69},{6,70},{7,71},{8,72},{9,... | collective-permute-start | bytes 196616 | tf_op jit(solution)/shard_map/ppermute | solution.py:388
  17.0 4.6 %collective-permute-start.7 = (bf16[32,256]{1,0:T(8,128)(2,1)S(1)}, bf16[32,256]{1,0:T(8,128)(2,1)S(1)}, u32[]{:S(2)}, u32[]{:S(2)}) collective-permute-start(bf16[32,256]{1,0:T(8,128)(2,1)S(1)} %stack_d.1.refs_0_), channel_id=1, source_target_pairs={{0,6},{1,25},{2,0},{3,27},{4,2},{5,29},{6,4},{7,31},{8,14},{9,1},{... | collective-permute-start | bytes 49160 | tf_op jit(solution)/shard_map/ppermute | solution.py:37
  19.6 3.8 %collective-permute-start.6 = (bf16[32,256]{1,0:T(8,128)(2,1)S(1)}, bf16[32,256]{1,0:T(8,128)(2,1)S(1)}, u32[]{:S(2)}, u32[]{:S(2)}) collective-permute-start(bf16[32,256]{1,0:T(8,128)(2,1)S(1)} %stack_d.1.refs_0_), channel_id=1, source_target_pairs={{0,2},{1,9},{2,4},{3,11},{4,6},{5,13},{6,0},{7,15},{8,10},{9,17},{... | collective-permute-start | bytes 49160 | tf_op jit(solution)/shard_map/ppermute | solution.py:37
  19.6 4.1 %collective-permute-start.5 = (bf16[32,256]{1,0:T(8,128)(2,1)S(1)}, bf16[32,256]{1,0:T(8,128)(2,1)S(1)}, u32[]{:S(2)}, u32[]{:S(2)}) collective-permute-start(bf16[32,256]{1,0:T(8,128)(2,1)S(1)} %stack_d.1.refs_0_), channel_id=1, source_target_pairs={{0,4},{1,17},{2,6},{3,19},{4,0},{5,21},{6,2},{7,23},{8,12},{9,25},... | collective-permute-start | bytes 49160 | tf_op jit(solution)/shard_map/ppermute | solution.py:37
  23.7 29.3 %collective-permute-start.13 = (bf16[32,24576]{1,0:T(8,128)(2,1)S(1)}, bf16[32,24576]{1,0:T(8,128)(2,1)S(1)}, u32[]{:S(2)}, u32[]{:S(2)}) collective-permute-start(bf16[32,24576]{1,0:T(8,128)(2,1)S(1)} %stack_p.1.refs_1_), channel_id=1, source_target_pairs={{0,1},{1,0},{2,3},{3,2},{4,5},{5,4},{6,7},{7,6},{8,9},{9,8},{10,11... | collective-permute-start | bytes 4718600 | tf_op jit(solution)/shard_map/ppermute | solution.py:37
  27.6 25.5 %collective-permute-start.12 = (bf16[32,24576]{1,0:T(8,128)(2,1)S(1)}, bf16[32,24576]{1,0:T(8,128)(2,1)}, u32[]{:S(2)}, u32[]{:S(2)}) collective-permute-start(bf16[32,24576]{1,0:T(8,128)(2,1)S(1)} %stack_p.1.refs_1_), channel_id=1, source_target_pairs={{0,6},{1,25},{2,0},{3,27},{4,2},{5,29},{6,4},{7,31},{8,14},{9,1},{... | collective-permute-start | bytes 4718600 | tf_op jit(solution)/shard_map/ppermute | solution.py:37
  29.7 23.4 %collective-permute-start.11 = (bf16[32,24576]{1,0:T(8,128)(2,1)S(1)}, bf16[32,24576]{1,0:T(8,128)(2,1)}, u32[]{:S(2)}, u32[]{:S(2)}) collective-permute-start(bf16[32,24576]{1,0:T(8,128)(2,1)S(1)} %stack_p.1.refs_1_), channel_id=1, source_target_pairs={{0,2},{1,9},{2,4},{3,11},{4,6},{5,13},{6,0},{7,15},{8,10},{9,17},{... | collective-permute-start | bytes 4718600 | tf_op jit(solution)/shard_map/ppermute | solution.py:37
  29.7 9.6 %collective-permute-start.14 = (bf16[256,128]{1,0:T(8,128)(2,1)S(1)}, bf16[256,128]{1,0:T(8,128)(2,1)S(1)}, u32[]{:S(2)}, u32[]{:S(2)}) collective-permute-start(bf16[256,128]{1,0:T(8,128)(2,1)S(1)} %choose.3.a_ref), channel_id=1, source_target_pairs={{0,32},{64,96},{1,33},{65,97},{2,34},{66,98},{3,35},{67,99},{4,36}... | collective-permute-start | bytes 196616 | tf_op jit(solution)/shard_map/ppermute | solution.py:388
  31.0 6.3 %collective-permute-start.9 = (bf16[256,128]{1,0:T(8,128)(2,1)S(1)}, bf16[256,128]{1,0:T(8,128)(2,1)S(1)}, u32[]{:S(2)}, u32[]{:S(2)}) collective-permute-start(bf16[256,128]{1,0:T(8,128)(2,1)S(1)} %add.2.a_ref), channel_id=1, source_target_pairs={{64,0},{192,128},{65,1},{193,129},{66,2},{194,130},{67,3},{195,131... | collective-permute-start | bytes 196616 | tf_op jit(solution)/shard_map/ppermute | solution.py:388
  37.3 3.3 %collective-permute-start.8 = (bf16[128,256]{1,0:T(8,128)(2,1)S(1)}, bf16[128,256]{1,0:T(8,128)(2,1)S(1)}, u32[]{:S(2)}, u32[]{:S(2)}) collective-permute-start(bf16[128,256]{1,0:T(8,128)(2,1)S(1)} %stack_l.1.own_ref), channel_id=1, source_target_pairs={{0,1},{1,0},{2,3},{3,2},{4,5},{5,4},{6,7},{7,6},{8,9},{9,8},{10,11... | collective-permute-start | bytes 196616 | tf_op jit(solution)/shard_map/ppermute | solution.py:37
  39.3 9.5 %collective-permute-start.10 = (bf16[256,128]{1,0:T(8,128)(2,1)S(1)}, bf16[256,128]{1,0:T(8,128)(2,1)S(1)}, u32[]{:S(2)}, u32[]{:S(2)}) collective-permute-start(bf16[256,128]{1,0:T(8,128)(2,1)S(1)} %add.3.top_ref), channel_id=1, source_target_pairs={{128,0},{129,1},{130,2},{131,3},{132,4},{133,5},{134,6},{135,7},{1... | collective-permute-start | bytes 196616 | tf_op jit(solution)/shard_map/ppermute | solution.py:388
  54.6 13.3 %collective-permute-start.19 = (bf16[32,12288]{1,0:T(8,128)(2,1)S(1)}, bf16[32,12288]{1,0:T(8,128)(2,1)S(1)}, u32[]{:S(2)}, u32[]{:S(2)}) collective-permute-start(bf16[32,12288]{1,0:T(8,128)(2,1)S(1)} %stack_b.1), channel_id=1, source_target_pairs={{0,6},{1,25},{2,0},{3,27},{4,2},{5,29},{6,4},{7,31},{8,14},{9,1},{... | collective-permute-start | bytes 2359304 | tf_op jit(solution)/shard_map/ppermute | solution.py:37
  58.2 12.4 %collective-permute-start.18 = (bf16[32,12288]{1,0:T(8,128)(2,1)S(1)}, bf16[32,12288]{1,0:T(8,128)(2,1)S(1)}, u32[]{:S(2)}, u32[]{:S(2)}) collective-permute-start(bf16[32,12288]{1,0:T(8,128)(2,1)S(1)} %stack_a.1), channel_id=1, source_target_pairs={{0,2},{1,9},{2,4},{3,11},{4,6},{5,13},{6,0},{7,15},{8,10},{9,17},{... | collective-permute-start | bytes 2359304 | tf_op jit(solution)/shard_map/ppermute | solution.py:37
  58.3 3.0 %collective-permute-start.15 = (bf16[256,128]{1,0:T(8,128)(2,1)S(1)}, bf16[256,128]{1,0:T(8,128)(2,1)S(1)}, u32[]{:S(2)}, u32[]{:S(2)}) collective-permute-start(bf16[256,128]{1,0:T(8,128)(2,1)S(1)} %solve.1.a_ref), channel_id=1, source_target_pairs={{0,64},{1,65},{2,66},{3,67},{4,68},{5,69},{6,70},{7,71},{8,72},{9,... | collective-permute-start | bytes 196616 | tf_op jit(solution)/shard_map/ppermute | solution.py:388
  61.3 5.2 %collective-permute-start.16 = (bf16[256,128]{1,0:T(8,128)(2,1)S(1)}, bf16[256,128]{1,0:T(8,128)(2,1)S(1)}, u32[]{:S(2)}, u32[]{:S(2)}) collective-permute-start(bf16[256,128]{1,0:T(8,128)(2,1)S(1)} %choose.5.a_ref), channel_id=1, source_target_pairs={{0,32},{64,96},{1,33},{65,97},{2,34},{66,98},{3,35},{67,99},{4,36}... | collective-permute-start | bytes 196616 | tf_op jit(solution)/shard_map/ppermute | solution.py:388
  62.6 12.7 %collective-permute-start.20 = (bf16[32,24576]{1,0:T(8,128)(2,1)}, bf16[32,24576]{1,0:T(8,128)(2,1)S(1)}, u32[]{:S(2)}, u32[]{:S(2)}) collective-permute-start(bf16[32,24576]{1,0:T(8,128)(2,1)} %collective-permute-done.11.refs_0_.refs_2_), channel_id=1, source_target_pairs={{0,1},{1,0},{2,3},{3,2},{4,5},{5,4},{6,7},{7,6},{8,9},{9,8},{10,11... | collective-permute-start | bytes 4718600 | tf_op jit(solution)/shard_map/ppermute | solution.py:37
  66.3 9.0 %collective-permute-start.21 = (bf16[32,24576]{1,0:T(8,128)(2,1)}, bf16[32,24576]{1,0:T(8,128)(2,1)S(1)}, u32[]{:S(2)}, u32[]{:S(2)}) collective-permute-start(bf16[32,24576]{1,0:T(8,128)(2,1)} %collective-permute-done.12.refs_0_.refs_3_), channel_id=1, source_target_pairs={{0,1},{1,0},{2,3},{3,2},{4,5},{5,4},{6,7},{7,6},{8,9},{9,8},{10,11... | collective-permute-start | bytes 4718600 | tf_op jit(solution)/shard_map/ppermute | solution.py:37
  66.6 8.7 %copy-start.1 = (s32[256]{0:T(256)S(1)}, s32[256]{0:T(256)}, u32[]{:S(2)}) copy-start(s32[256]{0:T(256)} %piv_ref.3) | copy-start | bytes 3076
  66.6 6.8 %collective-permute-start.17 = (bf16[512,128]{1,0:T(8,128)(2,1)S(1)}, bf16[512,128]{1,0:T(8,128)(2,1)S(1)}, u32[]{:S(2)}, u32[]{:S(2)}) collective-permute-start(bf16[512,128]{1,0:T(8,128)(2,1)S(1)} %join.1.ud_ref), channel_id=1, source_target_pairs={{0,128},{32,160},{64,192},{96,224},{1,129},{33,161},{65,193},{97,2... | collective-permute-start | bytes 393224 | tf_op jit(solution)/shard_map/ppermute | solution.py:388
  67.9 5.5 %collective-permute-start.23 = (bf16[32,12288]{1,0:T(8,128)(2,1)S(1)}, bf16[32,12288]{1,0:T(8,128)(2,1)S(1)}, u32[]{:S(2)}, u32[]{:S(2)}) collective-permute-start(bf16[32,12288]{1,0:T(8,128)(2,1)S(1)} %collective-permute-done.19.refs_1_.refs_5_), channel_id=1, source_target_pairs={{0,1},{1,0},{2,3},{3,2},{4,5},{5,4},{6,7},{7,6},{8,9},{9,8},{10,11... | collective-permute-start | bytes 2359304 | tf_op jit(solution)/shard_map/ppermute | solution.py:37
  70.6 4.7 %collective-permute-start.22 = (bf16[32,12288]{1,0:T(8,128)(2,1)S(1)}, bf16[32,12288]{1,0:T(8,128)(2,1)S(1)}, u32[]{:S(2)}, u32[]{:S(2)}) collective-permute-start(bf16[32,12288]{1,0:T(8,128)(2,1)S(1)} %collective-permute-done.18.refs_0_.refs_4_), channel_id=1, source_target_pairs={{0,1},{1,0},{2,3},{3,2},{4,5},{5,4},{6,7},{7,6},{8,9},{9,8},{10,11... | collective-permute-start | bytes 2359304 | tf_op jit(solution)/shard_map/ppermute | solution.py:37

commit v8 on v7

--- a/solution.py
+++ b/solution.py
@@ -390,27 +390,29 @@
     p, m, q = [send(panel_t, hop(d, 0, True)) for d in (1, -1, 2)]
 
     top, disp, cnt, lst = pick(trailing, pivots, first, blk)
-    more = zsend(top, [(1, 0), (3, 2), (5, 4), (7, 6)])
-    lower = zsend(disp, [(0, 2)])
-    p, m, q, top, more, lower = barrier((p, m, q, top, more, lower))
+    more = zsend(top, [(i + 4, i) for i in range(4)])
+    p, m, q, top = barrier((p, m, q, top))
 
     up, down, across = hop(0, 1, True), hop(0, -1, True), hop(0, 2, True)
     diag = stack([panel_t, p, m, q], 0, width, "stack_d")
     diag_q, diag_p, diag_m = send(diag, across), send(diag, up), send(diag, down)
     block = stack([panel_t, p, m, q], 0, rows, "stack_p")
-    block, diag_q, diag_p, diag_m = barrier((block, diag_q, diag_p, diag_m))
+    block, diag_q, diag_p, diag_m, top, more = barrier((block, diag_q, diag_p, diag_m, top, more))
     near, far = send(block, up), send(block, down)
     own = stack([diag, diag_p, diag_m, diag_q], 0, width, "stack_l")
-    top, more, block2 = barrier((top, more, block))
     top = add(top, more)
-    more = zsend(top, [(2, 0), (6, 4)])
+    more = zsend(top, [(2, 0), (3, 1)])
+    other = send(own, CORES)
     top = add(top, more)
-    more = zsend(top, [(4, 0)])
-    other = send(own, CORES)
+    top, disp, other = barrier((top, disp, other))
+    more = zsend(top, [(1, 0)])
+    lower = zsend(disp, [(0, 2)])
+    top, block2 = barrier((top, block))
+    swap = send(block2, CORES)
+    more, disp, lower = barrier((more, disp, lower))
+    u = solve(me, own, other, top, more)
     disp = choose(first, rows, (2,), disp, lower)
     disp = choose(first, rows, (1, 3), disp, zsend(disp, [(0, 1), (2, 3)]))
-    swap = send(block, CORES)
-    u = solve(me, own, other, top, more)
     u, near, far, swap, disp = barrier((u, near, far, swap, disp))
     fa, fb = stack([near], 0, half, "stack_a"), stack([far], half, half, "stack_b")
     qa, qb = send(fa, up), send(fb, down)

time: 87 us -> 82.6 us (0.949)
  starting transfers between devices: 42.1 us -> 40.4 us
  waiting for transfers between devices: 20.9 us -> 19.2 us
  Pallas kernels: 22.5 us -> 21.2 us
    ppermute x8, waiting for transfers between devices: 15.8 us -> 4.91 us  [zsend(): return lax.ppermute(x, 'prow', pairs)]
    ppermute x16, waiting for transfers between devices: 5.07 us -> 14.3 us  [send(): return lax.ppermute(block, 'pcol', pairs)]
    ppermute x16, starting transfers between devices: 27.9 us -> 25.9 us  [send(): return lax.ppermute(block, 'pcol', pairs)]
    pallas_call x6, Pallas kernels: 3.3 us -> 1.89 us  [stack(): pl.pallas_call(functools.partial(stack_kernel, start, min(cols, 1024)), i...]
  transfers between devices with their start and end apart: 24 -> 24, of which waited for: 8 -> 11; matrix products, arithmetic and copies ran while one was open for 0% -> 0% of each run, Pallas kernels for 11% -> 12%
where the time goes in v8:
time: 82.6 us; the launch traced here: 81.7 us
  starting transfers between devices  40.4 us (49%)
  Pallas kernels  21.2 us (26%)
  waiting for transfers between devices  19.2 us (23%)
    ppermute x16, starting transfers between devices, send(): return lax.ppermute(block, 'pcol', pairs)  25.9 us
    ppermute x8, starting transfers between devices, zsend(): return lax.ppermute(x, 'prow', pairs)  14.5 us
    ppermute x16, waiting for transfers between devices, send(): return lax.ppermute(block, 'pcol', pairs)  14.3 us
    pallas_call x1, Pallas kernels, update(): pl.pallas_call(functools.partial(update_kernel, nblk), grid=(nblk,), in_s...  11.1 us
    ppermute x8, waiting for transfers between devices, zsend(): return lax.ppermute(x, 'prow', pairs)  4.91 us
    pallas_call x1, Pallas kernels, solve(): pl.pallas_call(solve_kernel, in_specs=[SMEM] + [VMEM] * 4, out_specs=VMEM...  4.26 us
    pallas_call x1, Pallas kernels, pick(): pl.pallas_call(functools.partial(pick_kernel, blk), in_specs=[SMEM, SMEM,...  3.86 us
    pallas_call x6, Pallas kernels, stack(): pl.pallas_call(functools.partial(stack_kernel, start, min(cols, 1024)), i...  1.89 us
  transfers between devices with their start and end apart: 24, of which 11 were waited for; matrix products, arithmetic and copies ran while one was open for 0% of the time, Pallas kernels for 12%

profile of v8, /device:TPU:1, one launch (start us, length us, event | category | flops | bytes accessed | tf_op | source)
XLA Modules:
  0.0 81.7 jit_solution(4634075457073961731)
XLA Ops:
  0.0 3.7 %collective-permute-start.2 = (bf16[8,24576]{1,0:T(8,128)(2,1)}, bf16[8,24576]{1,0:T(8,128)(2,1)S(1)}, u32[]{:S(2)}, u32[]{:S(2)}) collective-permute-start(bf16[8,24576]{1,0:T(8,128)(2,1)} %refs_0_.3), channel_id=1, source_target_pairs={{0,16},{1,5},{2,18},{3,7},{4,20},{5,1},{6,22},{7,3},{8,24},{9,13},... | collective-permute-start | bytes 1179656 | tf_op jit(solution)/shard_map/ppermute | solution.py:37
  3.7 0.8 collective-permute-start.1
  4.5 0.7 collective-permute-start
  5.2 0.7 copy-done
  5.9 3.9 %pick.1 = (bf16[256,128]{1,0:T(8,128)(2,1)S(1)}, bf16[256,128]{1,0:T(8,128)(2,1)S(1)}, s32[6]{0:T(128)S(1)}, s32[1536]{0:T(1024)S(1)}) custom-call(s32[256]{0:T(256)S(1)} %copy-done, s32[1]{0:T(128)} %bitcast.first_ref, bf16[24576,128]{1,0:T(8,128)(2,1)} %tr_ref.1), custom_call_target="tpu_custom_call" | custom-call | flops 13200000000 | bytes 42000000 | tf_op jit(solution)/shard_map/pick/pallas_call | solution.py:184
  9.8 1.3 %collective-permute-start.6 = (bf16[256,128]{1,0:T(8,128)(2,1)S(1)}, bf16[256,128]{1,0:T(8,128)(2,1)S(1)}, u32[]{:S(2)}, u32[]{:S(2)}) collective-permute-start(bf16[256,128]{1,0:T(8,128)(2,1)S(1)} %get-tuple-element.45.a_ref), channel_id=1, source_target_pairs={{128,0},{160,32},{192,64},{224,96},{129,1},{161,33},{193,65},{225,... | collective-permute-start | bytes 196616 | tf_op jit(solution)/shard_map/ppermute | solution.py:388
  11.1 0.0 collective-permute-done.2.refs_3_
  11.1 3.0 %collective-permute-done.1.refs_2_ = bf16[8,24576]{1,0:T(8,128)(2,1)S(1)} collective-permute-done((bf16[8,24576]{1,0:T(8,128)(2,1)}, bf16[8,24576]{1,0:T(8,128)(2,1)S(1)}, u32[]{:S(2)}, u32[]{:S(2)}) %collective-permute-start.1) | collective-permute-done | bytes 393248 | tf_op jit(solution)/shard_map/ppermute | solution.py:37
  14.1 0.0 collective-permute-done.refs_1_
  14.1 2.6 %collective-permute-start.5 = (bf16[32,256]{1,0:T(8,128)(2,1)S(1)}, bf16[32,256]{1,0:T(8,128)(2,1)S(1)}, u32[]{:S(2)}, u32[]{:S(2)}) collective-permute-start(bf16[32,256]{1,0:T(8,128)(2,1)S(1)} %stack_d.1.refs_0_), channel_id=1, source_target_pairs={{0,6},{1,25},{2,0},{3,27},{4,2},{5,29},{6,4},{7,31},{8,14},{9,1},{... | collective-permute-start | bytes 49160 | tf_op jit(solution)/shard_map/ppermute | solution.py:37
  16.6 0.0 collective-permute-start.4
  16.6 1.7 %collective-permute-start.3 = (bf16[32,256]{1,0:T(8,128)(2,1)S(1)}, bf16[32,256]{1,0:T(8,128)(2,1)S(1)}, u32[]{:S(2)}, u32[]{:S(2)}) collective-permute-start(bf16[32,256]{1,0:T(8,128)(2,1)S(1)} %stack_d.1.refs_0_), channel_id=1, source_target_pairs={{0,4},{1,17},{2,6},{3,19},{4,0},{5,21},{6,2},{7,23},{8,12},{9,25},... | collective-permute-start | bytes 49160 | tf_op jit(solution)/shard_map/ppermute | solution.py:37
  18.4 0.3 stack_p.1.refs_1_
  18.7 0.6 collective-permute-done.6.b_ref
  19.3 0.0 collective-permute-done.5.refs_2_
  19.3 1.4 %collective-permute-done.4.refs_1_ = bf16[32,256]{1,0:T(8,128)(2,1)S(1)} collective-permute-done((bf16[32,256]{1,0:T(8,128)(2,1)S(1)}, bf16[32,256]{1,0:T(8,128)(2,1)S(1)}, u32[]{:S(2)}, u32[]{:S(2)}) %collective-permute-start.4) | collective-permute-done | bytes 16416 | tf_op jit(solution)/shard_map/ppermute | solution.py:37
  20.7 0.3 collective-permute-done.3.refs_3_
  21.1 1.3 %collective-permute-start.7 = (bf16[256,128]{1,0:T(8,128)(2,1)S(1)}, bf16[256,128]{1,0:T(8,128)(2,1)S(1)}, u32[]{:S(2)}, u32[]{:S(2)}) collective-permute-start(bf16[256,128]{1,0:T(8,128)(2,1)S(1)} %add.2.a_ref), channel_id=1, source_target_pairs={{64,0},{96,32},{65,1},{97,33},{66,2},{98,34},{67,3},{99,35},{68,4}... | collective-permute-start | bytes 196616 | tf_op jit(solution)/shard_map/ppermute | solution.py:388
  22.4 3.4 %collective-permute-start.8 = (bf16[128,256]{1,0:T(8,128)(2,1)S(1)}, bf16[128,256]{1,0:T(8,128)(2,1)S(1)}, u32[]{:S(2)}, u32[]{:S(2)}) collective-permute-start(bf16[128,256]{1,0:T(8,128)(2,1)S(1)} %stack_l.1.own_ref), channel_id=1, source_target_pairs={{0,1},{1,0},{2,3},{3,2},{4,5},{5,4},{6,7},{7,6},{8,9},{9,8},{10,11... | collective-permute-start | bytes 196616 | tf_op jit(solution)/shard_map/ppermute | solution.py:37
  25.7 1.7 %collective-permute-start.12 = (bf16[32,24576]{1,0:T(8,128)(2,1)S(1)}, bf16[32,24576]{1,0:T(8,128)(2,1)S(1)}, u32[]{:S(2)}, u32[]{:S(2)}) collective-permute-start(bf16[32,24576]{1,0:T(8,128)(2,1)S(1)} %stack_p.1.refs_1_), channel_id=1, source_target_pairs={{0,6},{1,25},{2,0},{3,27},{4,2},{5,29},{6,4},{7,31},{8,14},{9,1},{... | collective-permute-start | bytes 4718600 | tf_op jit(solution)/shard_map/ppermute | solution.py:37
  27.5 0.0 collective-permute-start.11
  27.5 0.0 collective-permute-done.7.b_ref
  27.5 4.0 %collective-permute-start.13 = (bf16[32,24576]{1,0:T(8,128)(2,1)S(1)}, bf16[32,24576]{1,0:T(8,128)(2,1)}, u32[]{:S(2)}, u32[]{:S(2)}) collective-permute-start(bf16[32,24576]{1,0:T(8,128)(2,1)S(1)} %stack_p.1.refs_1_), channel_id=1, source_target_pairs={{0,1},{1,0},{2,3},{3,2},{4,5},{5,4},{6,7},{7,6},{8,9},{9,8},{10,11... | collective-permute-start | bytes 4718600 | tf_op jit(solution)/shard_map/ppermute | solution.py:37
  31.5 1.3 %collective-permute-start.9 = (bf16[256,128]{1,0:T(8,128)(2,1)S(1)}, bf16[256,128]{1,0:T(8,128)(2,1)S(1)}, u32[]{:S(2)}, u32[]{:S(2)}) collective-permute-start(bf16[256,128]{1,0:T(8,128)(2,1)S(1)} %add.3.top_ref), channel_id=1, source_target_pairs={{32,0},{33,1},{34,2},{35,3},{36,4},{37,5},{38,6},{39,7},{40,8},{41... | collective-permute-start | bytes 196616 | tf_op jit(solution)/shard_map/ppermute | solution.py:388
  32.8 1.6 %collective-permute-start.10 = (bf16[256,128]{1,0:T(8,128)(2,1)S(1)}, bf16[256,128]{1,0:T(8,128)(2,1)S(1)}, u32[]{:S(2)}, u32[]{:S(2)}) collective-permute-start(bf16[256,128]{1,0:T(8,128)(2,1)S(1)} %get-tuple-element.55.a_ref), channel_id=1, source_target_pairs={{0,64},{1,65},{2,66},{3,67},{4,68},{5,69},{6,70},{7,71},{8,72},{9,... | collective-permute-start | bytes 196616 | tf_op jit(solution)/shard_map/ppermute | solution.py:388
  34.4 2.8 %collective-permute-done.9.more_ref = bf16[256,128]{1,0:T(8,128)(2,1)S(1)} collective-permute-done((bf16[256,128]{1,0:T(8,128)(2,1)S(1)}, bf16[256,128]{1,0:T(8,128)(2,1)S(1)}, u32[]{:S(2)}, u32[]{:S(2)}) %collective-permute-start.9) | collective-permute-done | bytes 65568 | tf_op jit(solution)/shard_map/ppermute | solution.py:388
  37.2 1.3 %collective-permute-start.14 = (bf16[256,128]{1,0:T(8,128)(2,1)S(1)}, bf16[256,128]{1,0:T(8,128)(2,1)S(1)}, u32[]{:S(2)}, u32[]{:S(2)}) collective-permute-start(bf16[256,128]{1,0:T(8,128)(2,1)S(1)} %choose.3.a_ref), channel_id=1, source_target_pairs={{0,32},{64,96},{1,33},{65,97},{2,34},{66,98},{3,35},{67,99},{4,36}... | collective-permute-start | bytes 196616 | tf_op jit(solution)/shard_map/ppermute | solution.py:388
  38.5 4.3 %solve.1.a_ref = bf16[256,128]{1,0:T(8,128)(2,1)S(1)} custom-call(s32[1]{0:T(128)} %bitcast.1.me_ref, bf16[128,256]{1,0:T(8,128)(2,1)S(1)} %stack_l.1.own_ref, bf16[128,256]{1,0:T(8,128)(2,1)S(1)} %collective-permute-done.8.other_ref, bf16[256,128]{1,0:T(8,128)(2,1)S(1)} %add.3.top_ref, bf16[256,128]{1,0:T(8,128)(2,1)S(1)} %collective-permute-done.9.more_ref), custom_call_target="tpu_custom_call" | custom-call | tf_op jit(solution)/shard_map/solve/pallas_call | solution.py:278
  42.8 0.0 collective-permute-done.14.b_ref
  42.8 2.6 %collective-permute-done.12.refs_0_.refs_3_ = bf16[32,24576]{1,0:T(8,128)(2,1)S(1)} collective-permute-done((bf16[32,24576]{1,0:T(8,128)(2,1)S(1)}, bf16[32,24576]{1,0:T(8,128)(2,1)S(1)}, u32[]{:S(2)}, u32[]{:S(2)}) %collective-permute-start.12) | collective-permute-done | bytes 1572896 | tf_op jit(solution)/shard_map/ppermute | solution.py:37
  45.4 2.9 %collective-permute-done.11.refs_0_.refs_2_ = bf16[32,24576]{1,0:T(8,128)(2,1)} collective-permute-done((bf16[32,24576]{1,0:T(8,128)(2,1)S(1)}, bf16[32,24576]{1,0:T(8,128)(2,1)}, u32[]{:S(2)}, u32[]{:S(2)}) %collective-permute-start.11) | collective-permute-done | bytes 1572896 | tf_op jit(solution)/shard_map/ppermute | solution.py:37
  48.3 0.1 stack_b.1
  48.4 0.1 collective-permute-start.19
  48.5 1.5 %stack_a.1 = bf16[32,12288]{1,0:T(8,128)(2,1)S(1)} custom-call(bf16[32,24576]{1,0:T(8,128)(2,1)} %collective-permute-done.11.refs_0_.refs_2_), custom_call_target="tpu_custom_call" | custom-call | flops 1100000000 | bytes 3500000 | tf_op jit(solution)/shard_map/stack_a/pallas_call | solution.py:60
  50.0 1.5 %collective-permute-start.18 = (bf16[32,12288]{1,0:T(8,128)(2,1)S(1)}, bf16[32,12288]{1,0:T(8,128)(2,1)S(1)}, u32[]{:S(2)}, u32[]{:S(2)}) collective-permute-start(bf16[32,12288]{1,0:T(8,128)(2,1)S(1)} %stack_a.1), channel_id=1, source_target_pairs={{0,2},{1,9},{2,4},{3,11},{4,6},{5,13},{6,0},{7,15},{8,10},{9,17},{... | collective-permute-start | bytes 2359304 | tf_op jit(solution)/shard_map/ppermute | solution.py:37
  51.6 5.2 %collective-permute-start.15 = (bf16[256,128]{1,0:T(8,128)(2,1)S(1)}, bf16[256,128]{1,0:T(8,128)(2,1)S(1)}, u32[]{:S(2)}, u32[]{:S(2)}) collective-permute-start(bf16[256,128]{1,0:T(8,128)(2,1)S(1)} %solve.1.a_ref), channel_id=1, source_target_pairs={{0,64},{1,65},{2,66},{3,67},{4,68},{5,69},{6,70},{7,71},{8,72},{9,... | collective-permute-start | bytes 196616 | tf_op jit(solution)/shard_map/ppermute | solution.py:388
  56.7 1.3 %collective-permute-done.15.b_ref = bf16[256,128]{1,0:T(8,128)(2,1)S(1)} collective-permute-done((bf16[256,128]{1,0:T(8,128)(2,1)S(1)}, bf16[256,128]{1,0:T(8,128)(2,1)S(1)}, u32[]{:S(2)}, u32[]{:S(2)}) %collective-permute-start.15) | collective-permute-done | bytes 65568 | tf_op jit(solution)/shard_map/ppermute | solution.py:388
  58.0 1.3 %collective-permute-start.16 = (bf16[256,128]{1,0:T(8,128)(2,1)S(1)}, bf16[256,128]{1,0:T(8,128)(2,1)S(1)}, u32[]{:S(2)}, u32[]{:S(2)}) collective-permute-start(bf16[256,128]{1,0:T(8,128)(2,1)S(1)} %choose.5.a_ref), channel_id=1, source_target_pairs={{0,32},{64,96},{1,33},{65,97},{2,34},{66,98},{3,35},{67,99},{4,36}... | collective-permute-start | bytes 196616 | tf_op jit(solution)/shard_map/ppermute | solution.py:388
  59.3 3.7 %collective-permute-start.20 = (bf16[32,24576]{1,0:T(8,128)(2,1)}, bf16[32,24576]{1,0:T(8,128)(2,1)S(1)}, u32[]{:S(2)}, u32[]{:S(2)}) collective-permute-start(bf16[32,24576]{1,0:T(8,128)(2,1)} %collective-permute-done.11.refs_0_.refs_2_), channel_id=1, source_target_pairs={{0,1},{1,0},{2,3},{3,2},{4,5},{5,4},{6,7},{7,6},{8,9},{9,8},{10,11... | collective-permute-start | bytes 4718600 | tf_op jit(solution)/shard_map/ppermute | solution.py:37
  63.0 0.3 collective-permute-start.21
  63.3 0.0 copy-start.1
  63.3 1.3 %collective-permute-start.17 = (bf16[512,128]{1,0:T(8,128)(2,1)S(1)}, bf16[512,128]{1,0:T(8,128)(2,1)S(1)}, u32[]{:S(2)}, u32[]{:S(2)}) collective-permute-start(bf16[512,128]{1,0:T(8,128)(2,1)S(1)} %join.1.ud_ref), channel_id=1, source_target_pairs={{0,128},{32,160},{64,192},{96,224},{1,129},{33,161},{65,193},{97,2... | collective-permute-start | bytes 393224 | tf_op jit(solution)/shard_map/ppermute | solution.py:388
  64.6 1.6 %collective-permute-start.23 = (bf16[32,12288]{1,0:T(8,128)(2,1)S(1)}, bf16[32,12288]{1,0:T(8,128)(2,1)S(1)}, u32[]{:S(2)}, u32[]{:S(2)}) collective-permute-start(bf16[32,12288]{1,0:T(8,128)(2,1)S(1)} %collective-permute-done.19.refs_1_.refs_5_), channel_id=1, source_target_pairs={{0,1},{1,0},{2,3},{3,2},{4,5},{5,4},{6,7},{7,6},{8,9},{9,8},{10,11... | collective-permute-start | bytes 2359304 | tf_op jit(solution)/shard_map/ppermute | solution.py:37
  66.2 0.1 collective-permute-start.22
  66.3 0.2 collective-permute-done.17.rest_ref
  66.5 2.9 %collective-permute-done.23.refs_10_ = bf16[32,12288]{1,0:T(8,128)(2,1)S(1)} collective-permute-done((bf16[32,12288]{1,0:T(8,128)(2,1)S(1)}, bf16[32,12288]{1,0:T(8,128)(2,1)S(1)}, u32[]{:S(2)}, u32[]{:S(2)}) %collective-permute-start.23) | collective-permute-done | bytes 786464 | tf_op jit(solution)/shard_map/ppermute | solution.py:37
  69.4 1.1 %collective-permute-done.22.refs_9_ = bf16[32,12288]{1,0:T(8,128)(2,1)S(1)} collective-permute-done((bf16[32,12288]{1,0:T(8,128)(2,1)S(1)}, bf16[32,12288]{1,0:T(8,128)(2,1)S(1)}, u32[]{:S(2)}, u32[]{:S(2)}) %collective-permute-start.22) | collective-permute-done | bytes 786464 | tf_op jit(solution)/shard_map/ppermute | solution.py:37
  70.5 11.1 %update.1 = bf16[24576,128]{1,0:T(8,128)(2,1)} custom-call(s32[6]{0:T(128)S(1)} %get-tuple-element.35.cnt_ref, s32[1536]{0:T(1024)S(1)} %get-tuple-element.36.lst_ref, s32[256]{0:T(256)S(1)} %copy-done.1, s32[1]{0:T(128)} %bitcast.first_ref, s32[1]{0:T(128)} %bitcast.1.me_ref, bf16[24576,128]{1,0:T(8,128)(2,1)} %tr_ref.1, bf16[512,128]{1,0:T(8,128)(2,1)S(1)} %join.1.ud_ref, ...), custom_call_target="tpu_custom_call" | custom-call | tf_op jit(solution)/shard_map/update/pallas_call | solution.py:359
  (21 shorter events, 0.1 us)
Async XLA Ops:
  0.0 11.1 %collective-permute-start.2 = (bf16[8,24576]{1,0:T(8,128)(2,1)}, bf16[8,24576]{1,0:T(8,128)(2,1)S(1)}, u32[]{:S(2)}, u32[]{:S(2)}) collective-permute-start(bf16[8,24576]{1,0:T(8,128)(2,1)} %refs_0_.3), channel_id=1, source_target_pairs={{0,16},{1,5},{2,18},{3,7},{4,20},{5,1},{6,22},{7,3},{8,24},{9,13},... | collective-permute-start | bytes 1179656 | tf_op jit(solution)/shard_map/ppermute | solution.py:37
  3.7 10.3 %collective-permute-start.1 = (bf16[8,24576]{1,0:T(8,128)(2,1)}, bf16[8,24576]{1,0:T(8,128)(2,1)S(1)}, u32[]{:S(2)}, u32[]{:S(2)}) collective-permute-start(bf16[8,24576]{1,0:T(8,128)(2,1)} %refs_0_.3), channel_id=1, source_target_pairs={{0,24},{1,7},{2,26},{3,1},{4,28},{5,3},{6,30},{7,5},{8,0},{9,15},{... | collective-permute-start | bytes 1179656 | tf_op jit(solution)/shard_map/ppermute | solution.py:37
  4.5 9.5 %collective-permute-start = (bf16[8,24576]{1,0:T(8,128)(2,1)}, bf16[8,24576]{1,0:T(8,128)(2,1)S(1)}, u32[]{:S(2)}, u32[]{:S(2)}) collective-permute-start(bf16[8,24576]{1,0:T(8,128)(2,1)} %refs_0_.3), channel_id=1, source_target_pairs={{0,8},{1,3},{2,10},{3,5},{4,12},{5,7},{6,14},{7,1},{8,16},{9,11},{... | collective-permute-start | bytes 1179656 | tf_op jit(solution)/shard_map/ppermute | solution.py:37
  5.2 0.7 copy-start
  5.9 8.2 %copy-start.2 = (bf16[8,24576]{1,0:T(8,128)(2,1)S(1)}, bf16[8,24576]{1,0:T(8,128)(2,1)}, u32[]{:S(2)}) copy-start(bf16[8,24576]{1,0:T(8,128)(2,1)} %refs_0_.3) | copy-start | bytes 1179652
  9.8 9.5 %collective-permute-start.6 = (bf16[256,128]{1,0:T(8,128)(2,1)S(1)}, bf16[256,128]{1,0:T(8,128)(2,1)S(1)}, u32[]{:S(2)}, u32[]{:S(2)}) collective-permute-start(bf16[256,128]{1,0:T(8,128)(2,1)S(1)} %get-tuple-element.45.a_ref), channel_id=1, source_target_pairs={{128,0},{160,32},{192,64},{224,96},{129,1},{161,33},{193,65},{225,... | collective-permute-start | bytes 196616 | tf_op jit(solution)/shard_map/ppermute | solution.py:388
  14.1 5.2 %collective-permute-start.5 = (bf16[32,256]{1,0:T(8,128)(2,1)S(1)}, bf16[32,256]{1,0:T(8,128)(2,1)S(1)}, u32[]{:S(2)}, u32[]{:S(2)}) collective-permute-start(bf16[32,256]{1,0:T(8,128)(2,1)S(1)} %stack_d.1.refs_0_), channel_id=1, source_target_pairs={{0,6},{1,25},{2,0},{3,27},{4,2},{5,29},{6,4},{7,31},{8,14},{9,1},{... | collective-permute-start | bytes 49160 | tf_op jit(solution)/shard_map/ppermute | solution.py:37
  16.6 4.1 %collective-permute-start.4 = (bf16[32,256]{1,0:T(8,128)(2,1)S(1)}, bf16[32,256]{1,0:T(8,128)(2,1)S(1)}, u32[]{:S(2)}, u32[]{:S(2)}) collective-permute-start(bf16[32,256]{1,0:T(8,128)(2,1)S(1)} %stack_d.1.refs_0_), channel_id=1, source_target_pairs={{0,2},{1,9},{2,4},{3,11},{4,6},{5,13},{6,0},{7,15},{8,10},{9,17},{... | collective-permute-start | bytes 49160 | tf_op jit(solution)/shard_map/ppermute | solution.py:37
  16.6 4.4 %collective-permute-start.3 = (bf16[32,256]{1,0:T(8,128)(2,1)S(1)}, bf16[32,256]{1,0:T(8,128)(2,1)S(1)}, u32[]{:S(2)}, u32[]{:S(2)}) collective-permute-start(bf16[32,256]{1,0:T(8,128)(2,1)S(1)} %stack_d.1.refs_0_), channel_id=1, source_target_pairs={{0,4},{1,17},{2,6},{3,19},{4,0},{5,21},{6,2},{7,23},{8,12},{9,25},... | collective-permute-start | bytes 49160 | tf_op jit(solution)/shard_map/ppermute | solution.py:37
  21.1 6.4 %collective-permute-start.7 = (bf16[256,128]{1,0:T(8,128)(2,1)S(1)}, bf16[256,128]{1,0:T(8,128)(2,1)S(1)}, u32[]{:S(2)}, u32[]{:S(2)}) collective-permute-start(bf16[256,128]{1,0:T(8,128)(2,1)S(1)} %add.2.a_ref), channel_id=1, source_target_pairs={{64,0},{96,32},{65,1},{97,33},{66,2},{98,34},{67,3},{99,35},{68,4}... | collective-permute-start | bytes 196616 | tf_op jit(solution)/shard_map/ppermute | solution.py:388
  22.4 5.1 %collective-permute-start.8 = (bf16[128,256]{1,0:T(8,128)(2,1)S(1)}, bf16[128,256]{1,0:T(8,128)(2,1)S(1)}, u32[]{:S(2)}, u32[]{:S(2)}) collective-permute-start(bf16[128,256]{1,0:T(8,128)(2,1)S(1)} %stack_l.1.own_ref), channel_id=1, source_target_pairs={{0,1},{1,0},{2,3},{3,2},{4,5},{5,4},{6,7},{7,6},{8,9},{9,8},{10,11... | collective-permute-start | bytes 196616 | tf_op jit(solution)/shard_map/ppermute | solution.py:37
  25.7 19.7 %collective-permute-start.12 = (bf16[32,24576]{1,0:T(8,128)(2,1)S(1)}, bf16[32,24576]{1,0:T(8,128)(2,1)S(1)}, u32[]{:S(2)}, u32[]{:S(2)}) collective-permute-start(bf16[32,24576]{1,0:T(8,128)(2,1)S(1)} %stack_p.1.refs_1_), channel_id=1, source_target_pairs={{0,6},{1,25},{2,0},{3,27},{4,2},{5,29},{6,4},{7,31},{8,14},{9,1},{... | collective-permute-start | bytes 4718600 | tf_op jit(solution)/shard_map/ppermute | solution.py:37
  27.5 20.9 %collective-permute-start.11 = (bf16[32,24576]{1,0:T(8,128)(2,1)S(1)}, bf16[32,24576]{1,0:T(8,128)(2,1)}, u32[]{:S(2)}, u32[]{:S(2)}) collective-permute-start(bf16[32,24576]{1,0:T(8,128)(2,1)S(1)} %stack_p.1.refs_1_), channel_id=1, source_target_pairs={{0,2},{1,9},{2,4},{3,11},{4,6},{5,13},{6,0},{7,15},{8,10},{9,17},{... | collective-permute-start | bytes 4718600 | tf_op jit(solution)/shard_map/ppermute | solution.py:37
  27.5 20.8 %collective-permute-start.13 = (bf16[32,24576]{1,0:T(8,128)(2,1)S(1)}, bf16[32,24576]{1,0:T(8,128)(2,1)}, u32[]{:S(2)}, u32[]{:S(2)}) collective-permute-start(bf16[32,24576]{1,0:T(8,128)(2,1)S(1)} %stack_p.1.refs_1_), channel_id=1, source_target_pairs={{0,1},{1,0},{2,3},{3,2},{4,5},{5,4},{6,7},{7,6},{8,9},{9,8},{10,11... | collective-permute-start | bytes 4718600 | tf_op jit(solution)/shard_map/ppermute | solution.py:37
  31.5 5.7 %collective-permute-start.9 = (bf16[256,128]{1,0:T(8,128)(2,1)S(1)}, bf16[256,128]{1,0:T(8,128)(2,1)S(1)}, u32[]{:S(2)}, u32[]{:S(2)}) collective-permute-start(bf16[256,128]{1,0:T(8,128)(2,1)S(1)} %add.3.top_ref), channel_id=1, source_target_pairs={{32,0},{33,1},{34,2},{35,3},{36,4},{37,5},{38,6},{39,7},{40,8},{41... | collective-permute-start | bytes 196616 | tf_op jit(solution)/shard_map/ppermute | solution.py:388
  32.8 4.4 %collective-permute-start.10 = (bf16[256,128]{1,0:T(8,128)(2,1)S(1)}, bf16[256,128]{1,0:T(8,128)(2,1)S(1)}, u32[]{:S(2)}, u32[]{:S(2)}) collective-permute-start(bf16[256,128]{1,0:T(8,128)(2,1)S(1)} %get-tuple-element.55.a_ref), channel_id=1, source_target_pairs={{0,64},{1,65},{2,66},{3,67},{4,68},{5,69},{6,70},{7,71},{8,72},{9,... | collective-permute-start | bytes 196616 | tf_op jit(solution)/shard_map/ppermute | solution.py:388
  37.2 5.6 %collective-permute-start.14 = (bf16[256,128]{1,0:T(8,128)(2,1)S(1)}, bf16[256,128]{1,0:T(8,128)(2,1)S(1)}, u32[]{:S(2)}, u32[]{:S(2)}) collective-permute-start(bf16[256,128]{1,0:T(8,128)(2,1)S(1)} %choose.3.a_ref), channel_id=1, source_target_pairs={{0,32},{64,96},{1,33},{65,97},{2,34},{66,98},{3,35},{67,99},{4,36}... | collective-permute-start | bytes 196616 | tf_op jit(solution)/shard_map/ppermute | solution.py:388
  48.4 16.2 %collective-permute-start.19 = (bf16[32,12288]{1,0:T(8,128)(2,1)S(1)}, bf16[32,12288]{1,0:T(8,128)(2,1)S(1)}, u32[]{:S(2)}, u32[]{:S(2)}) collective-permute-start(bf16[32,12288]{1,0:T(8,128)(2,1)S(1)} %stack_b.1), channel_id=1, source_target_pairs={{0,6},{1,25},{2,0},{3,27},{4,2},{5,29},{6,4},{7,31},{8,14},{9,1},{... | collective-permute-start | bytes 2359304 | tf_op jit(solution)/shard_map/ppermute | solution.py:37
  50.0 16.2 %collective-permute-start.18 = (bf16[32,12288]{1,0:T(8,128)(2,1)S(1)}, bf16[32,12288]{1,0:T(8,128)(2,1)S(1)}, u32[]{:S(2)}, u32[]{:S(2)}) collective-permute-start(bf16[32,12288]{1,0:T(8,128)(2,1)S(1)} %stack_a.1), channel_id=1, source_target_pairs={{0,2},{1,9},{2,4},{3,11},{4,6},{5,13},{6,0},{7,15},{8,10},{9,17},{... | collective-permute-start | bytes 2359304 | tf_op jit(solution)/shard_map/ppermute | solution.py:37
  51.6 6.5 %collective-permute-start.15 = (bf16[256,128]{1,0:T(8,128)(2,1)S(1)}, bf16[256,128]{1,0:T(8,128)(2,1)S(1)}, u32[]{:S(2)}, u32[]{:S(2)}) collective-permute-start(bf16[256,128]{1,0:T(8,128)(2,1)S(1)} %solve.1.a_ref), channel_id=1, source_target_pairs={{0,64},{1,65},{2,66},{3,67},{4,68},{5,69},{6,70},{7,71},{8,72},{9,... | collective-permute-start | bytes 196616 | tf_op jit(solution)/shard_map/ppermute | solution.py:388
  58.0 5.2 %collective-permute-start.16 = (bf16[256,128]{1,0:T(8,128)(2,1)S(1)}, bf16[256,128]{1,0:T(8,128)(2,1)S(1)}, u32[]{:S(2)}, u32[]{:S(2)}) collective-permute-start(bf16[256,128]{1,0:T(8,128)(2,1)S(1)} %choose.5.a_ref), channel_id=1, source_target_pairs={{0,32},{64,96},{1,33},{65,97},{2,34},{66,98},{3,35},{67,99},{4,36}... | collective-permute-start | bytes 196616 | tf_op jit(solution)/shard_map/ppermute | solution.py:388
  59.3 11.2 %collective-permute-start.20 = (bf16[32,24576]{1,0:T(8,128)(2,1)}, bf16[32,24576]{1,0:T(8,128)(2,1)S(1)}, u32[]{:S(2)}, u32[]{:S(2)}) collective-permute-start(bf16[32,24576]{1,0:T(8,128)(2,1)} %collective-permute-done.11.refs_0_.refs_2_), channel_id=1, source_target_pairs={{0,1},{1,0},{2,3},{3,2},{4,5},{5,4},{6,7},{7,6},{8,9},{9,8},{10,11... | collective-permute-start | bytes 4718600 | tf_op jit(solution)/shard_map/ppermute | solution.py:37
  63.0 7.5 %collective-permute-start.21 = (bf16[32,24576]{1,0:T(8,128)(2,1)S(1)}, bf16[32,24576]{1,0:T(8,128)(2,1)S(1)}, u32[]{:S(2)}, u32[]{:S(2)}) collective-permute-start(bf16[32,24576]{1,0:T(8,128)(2,1)S(1)} %collective-permute-done.12.refs_0_.refs_3_), channel_id=1, source_target_pairs={{0,1},{1,0},{2,3},{3,2},{4,5},{5,4},{6,7},{7,6},{8,9},{9,8},{10,11... | collective-permute-start | bytes 4718600 | tf_op jit(solution)/shard_map/ppermute | solution.py:37
  63.3 7.2 %copy-start.1 = (s32[256]{0:T(256)S(1)}, s32[256]{0:T(256)}, u32[]{:S(2)}) copy-start(s32[256]{0:T(256)} %piv_ref.3) | copy-start | bytes 3076
  63.3 3.2 %collective-permute-start.17 = (bf16[512,128]{1,0:T(8,128)(2,1)S(1)}, bf16[512,128]{1,0:T(8,128)(2,1)S(1)}, u32[]{:S(2)}, u32[]{:S(2)}) collective-permute-start(bf16[512,128]{1,0:T(8,128)(2,1)S(1)} %join.1.ud_ref), channel_id=1, source_target_pairs={{0,128},{32,160},{64,192},{96,224},{1,129},{33,161},{65,193},{97,2... | collective-permute-start | bytes 393224 | tf_op jit(solution)/shard_map/ppermute | solution.py:388
  64.6 4.8 %collective-permute-start.23 = (bf16[32,12288]{1,0:T(8,128)(2,1)S(1)}, bf16[32,12288]{1,0:T(8,128)(2,1)S(1)}, u32[]{:S(2)}, u32[]{:S(2)}) collective-permute-start(bf16[32,12288]{1,0:T(8,128)(2,1)S(1)} %collective-permute-done.19.refs_1_.refs_5_), channel_id=1, source_target_pairs={{0,1},{1,0},{2,3},{3,2},{4,5},{5,4},{6,7},{7,6},{8,9},{9,8},{10,11... | collective-permute-start | bytes 2359304 | tf_op jit(solution)/shard_map/ppermute | solution.py:37
  66.2 4.3 %collective-permute-start.22 = (bf16[32,12288]{1,0:T(8,128)(2,1)S(1)}, bf16[32,12288]{1,0:T(8,128)(2,1)S(1)}, u32[]{:S(2)}, u32[]{:S(2)}) collective-permute-start(bf16[32,12288]{1,0:T(8,128)(2,1)S(1)} %collective-permute-done.18.refs_0_.refs_4_), channel_id=1, source_target_pairs={{0,1},{1,0},{2,3},{3,2},{4,5},{5,4},{6,7},{7,6},{8,9},{9,8},{10,11... | collective-permute-start | bytes 2359304 | tf_op jit(solution)/shard_map/ppermute | solution.py:37

commit v9 on v8

--- a/solution.py
+++ b/solution.py
@@ -281,103 +281,119 @@
         out_specs=VMEM,
         out_shape=jax.ShapeDtypeStruct((n, cols), jnp.bfloat16),
         scratch_shapes=[pltpu.VMEM((n, n), jnp.float32), pltpu.VMEM((n, n), jnp.float32)],
-        compiler_params=params(10),
+        compiler_params=params(6),
         name="solve",
     )(me, own, other, top, more)
 
 
-def update_kernel(nblk, cnt_ref, lst_ref, piv_ref, first_ref, me_ref, tr_ref, ud_ref, rest_ref, *refs):
+def fetch_kernel(src_ref, dst_ref, sem):
+    n = sem.shape[0]
+    step = src_ref.shape[0] // n
+    copies = [
+        pltpu.make_async_copy(src_ref.at[pl.ds(i * step, step)], dst_ref.at[pl.ds(i * step, step)], sem.at[i])
+        for i in range(n)
+    ]
+    for copy in copies:
+        copy.start()
+    for copy in copies:
+        copy.wait()
+
+
+def fetch(x):
+    return pl.pallas_call(
+        fetch_kernel,
+        in_specs=[pl.BlockSpec(memory_space=pltpu.HBM)],
+        out_specs=VMEM,
+        out_shape=jax.ShapeDtypeStruct(x.shape, x.dtype),
+        scratch_shapes=[pltpu.SemaphoreType.DMA((4,))],
+        compiler_params=params(2),
+        name="fetch",
+    )(x)
+
+
+def update_kernel(cnt_ref, lst_ref, piv_ref, first_ref, me_ref, tr_ref, ud_ref, rest_ref, *refs):
     parts = refs[1:11]
-    out_ref, acc_ref, nat_ref, drow_ref, u_ref, tmp_ref = refs[11:]
-    blk = out_ref.shape[0]
+    out_ref, buf_ref, nat_ref, drow_ref, tmp_ref, sem = refs[11:]
+    rows = buf_ref.shape[0]
+    nblk = sem.shape[0]
+    blk = rows // nblk
     width = nat_ref.shape[0]
-    b = pl.program_id(0)
     first = first_ref[0]
-
-    @pl.when(b == 0)
+    late = lax.div(first, rows) >> 2
+
+    @pl.when(late == 0)
     def _():
-        late = lax.div(first, nblk * blk) >> 2
-
-        @pl.when(late == 0)
-        def _():
-            nat_ref[...] = ud_ref[:width, :].astype(jnp.float32)
-            drow_ref[...] = ud_ref[width:, :].astype(jnp.float32)
-
-        @pl.when(late == 1)
-        def _():
-            nat_ref[...] = rest_ref[:width, :].astype(jnp.float32)
-            drow_ref[...] = rest_ref[width:, :].astype(jnp.float32)
-
-        for i, where in enumerate(blocks()):
-            tmp_ref[8 * i : 8 * i + 8, :] = nat_ref[block_at(me_ref[0], *where), :]
-        u_ref[...] = tmp_ref[...].astype(jnp.bfloat16)
-
-    def compute(half):
-        here = pl.ds(pl.multiple_of(b * blk, 128), blk)
-        there = pl.ds(pl.multiple_of((b - half * (nblk // 2)) * blk, 128), blk)
+        nat_ref[...] = ud_ref[:width, :].astype(jnp.float32)
+        drow_ref[...] = ud_ref[width:, :].astype(jnp.float32)
+
+    @pl.when(late == 1)
+    def _():
+        nat_ref[...] = rest_ref[:width, :].astype(jnp.float32)
+        drow_ref[...] = rest_ref[width:, :].astype(jnp.float32)
+
+    sub = lax.broadcasted_iota(jnp.int32, (16, 128), 0)
+
+    def fix(k, carry):
+        i = lst_ref[k]
+        loc = piv_ref[i] - first
+        at = pl.ds(pl.multiple_of(loc & ~15, 16), 16)
+        old = buf_ref[at, :].astype(jnp.float32)
+        row = drow_ref[pl.ds(i, 1), :]
+        buf_ref[at, :] = jnp.where(sub == (loc & 15), row, old).astype(jnp.bfloat16)
+        return carry
+
+    lax.fori_loop(0, cnt_ref[0], fix, 0)
+    for i, where in enumerate(blocks()):
+        tmp_ref[8 * i : 8 * i + 8, :] = nat_ref[block_at(me_ref[0], *where), :]
+    ut = tmp_ref[...].T.astype(jnp.bfloat16)
+    copies = []
+    for b in range(nblk):
+        half = b // (nblk // 2)
+        here = pl.ds(b * blk, blk)
+        there = pl.ds((b - half * (nblk // 2)) * blk, blk)
         pieces = []
         for s in (parts[:5], parts[5:]):
             pieces += [s[0][:, here], s[1][:, here], s[2][:, here], s[3 + half][:, there]]
-        acc_ref[...] = lax.dot_general(
-            jnp.concatenate(pieces, axis=0), u_ref[...], (((0,), (0,)), ((), ())),
+        product = lax.dot_general(
+            ut, jnp.concatenate(pieces, axis=0), (((1,), (0,)), ((), ())),
             preferred_element_type=jnp.float32,
-        )
-
-    @pl.when(b < nblk // 2)
-    def _():
-        compute(0)
-
-    @pl.when(b >= nblk // 2)
-    def _():
-        compute(1)
-
-    out_ref[...] = (tr_ref[...].astype(jnp.float32) - acc_ref[...]).astype(jnp.bfloat16)
-    sub = lax.broadcasted_iota(jnp.int32, (16, 128), 0)
-
-    def fix(k, carry):
-        i = lst_ref[b * width + k]
-        loc = piv_ref[i] - first - b * blk
-        at = pl.ds(pl.multiple_of(loc & ~15, 16), 16)
-        new = drow_ref[pl.ds(i, 1), :] - acc_ref[at, :]
-        old = out_ref[at, :].astype(jnp.float32)
-        out_ref[at, :] = jnp.where(sub == (loc & 15), new, old).astype(jnp.bfloat16)
-        return carry
-
-    lax.fori_loop(0, cnt_ref[b], fix, 0)
-
-    @pl.when((b == 0) & (first == 0))
-    def _():
-        out_ref[:width, :] = nat_ref[...].astype(jnp.bfloat16)
-
-
-def update(cnt, lst, pivots, first, me, trailing, ud, rest, ahead, parts, blk):
+        ).T
+        new = buf_ref[here, :].astype(jnp.float32) - product
+        if b == 0:
+            head = jnp.where(first == 0, nat_ref[...], new[:width])
+            buf_ref[:width, :] = head.astype(jnp.bfloat16)
+            buf_ref[width:blk, :] = new[width:].astype(jnp.bfloat16)
+        else:
+            buf_ref[here, :] = new.astype(jnp.bfloat16)
+        copies.append(pltpu.make_async_copy(buf_ref.at[here], out_ref.at[here], sem.at[b]))
+        copies[-1].start()
+    for copy in copies:
+        copy.wait()
+
+
+def update(cnt, lst, pivots, first, me, trailing, ud, rest, ahead, parts, nblk):
     rows, cols = trailing.shape
     width = pivots.shape[0]
-    nblk = rows // blk
-    tall = pl.BlockSpec((blk, cols), lambda b: (b, 0))
-    pair = pl.BlockSpec((2 * width, cols), lambda b: (0, 0))
-    return pl.pallas_call(
-        functools.partial(update_kernel, nblk),
-        grid=(nblk,),
-        in_specs=[SMEM] * 5 + [tall, pair, pair] + [VMEM] * 11,
-        out_specs=tall,
+    return pl.pallas_call(
+        update_kernel,
+        in_specs=[SMEM] * 5 + [VMEM] * 14,
+        out_specs=[pl.BlockSpec(memory_space=pltpu.HBM), VMEM],
         scratch_shapes=[
-            pltpu.VMEM((blk, cols), jnp.float32),
             pltpu.VMEM((width, cols), jnp.float32),
             pltpu.VMEM((width, cols), jnp.float32),
-            pltpu.VMEM((width, cols), jnp.bfloat16),
             pltpu.VMEM((width, cols), jnp.float32),
+            pltpu.SemaphoreType.DMA((nblk,)),
         ],
-        out_shape=jax.ShapeDtypeStruct((rows, cols), jnp.bfloat16),
-        compiler_params=params(16),
+        out_shape=[jax.ShapeDtypeStruct((rows, cols), jnp.bfloat16)] * 2,
+        input_output_aliases={5: 1},
+        compiler_params=params(28),
         name="update",
-    )(cnt, lst, pivots, first, me, trailing, ud, rest, ahead, *parts)
+    )(cnt, lst, pivots, first, me, trailing, ud, rest, ahead, *parts)[0]
 
 
 def body(trailing, panel_t, pivots):
     rows = trailing.shape[0]
     width = pivots.shape[0]
-    blk = rows // NBLK
     half = rows // 2
     barrier = lax.optimization_barrier
     first = (lax.axis_index("prow") * rows).astype(jnp.int32).reshape(1)
@@ -389,7 +405,7 @@
 
     p, m, q = [send(panel_t, hop(d, 0, True)) for d in (1, -1, 2)]
 
-    top, disp, cnt, lst = pick(trailing, pivots, first, blk)
+    top, disp, cnt, lst = pick(trailing, pivots, first, rows)
     more = zsend(top, [(i + 4, i) for i in range(4)])
     p, m, q, top = barrier((p, m, q, top))
 
@@ -413,10 +429,13 @@
     u = solve(me, own, other, top, more)
     disp = choose(first, rows, (2,), disp, lower)
     disp = choose(first, rows, (1, 3), disp, zsend(disp, [(0, 1), (2, 3)]))
-    u, near, far, swap, disp = barrier((u, near, far, swap, disp))
+    ru = zsend(u, [(0, 2)])
+    u, source = barrier((u, trailing))
+    copy = fetch(pltpu.with_memory_space_constraint(source, pltpu.HBM))
+    ru, near, far, swap, disp, copy = barrier((ru, near, far, swap, disp, copy))
     fa, fb = stack([near], 0, half, "stack_a"), stack([far], half, half, "stack_b")
     qa, qb = send(fa, up), send(fb, down)
-    u = choose(first, rows, (2,), u, zsend(u, [(0, 2)]))
+    u = choose(first, rows, (2,), u, ru)
     u, near, far = barrier((u, near, far))
     other_near, other_far = send(near, CORES), send(far, CORES)
     ud = join(first, rows, (1, 3), u, zsend(u, [(0, 1), (2, 3)]), disp)
@@ -424,7 +443,7 @@
     ahead = stack([qa, qb], 0, 128, "stack_q", 60)
     own = [block, near, far, qa, qb]
     parts = own + [swap, other_near, other_far, send(qa, CORES), send(qb, CORES)]
-    return update(cnt, lst, pivots, first, me, trailing, ud, rest, ahead, parts, blk)
+    return update(cnt, lst, pivots, first, me, copy, ud, rest, ahead, parts, NBLK)
 
 
 def solution(mesh):

time: 82.6 us -> 78.9 us (0.955)
  waiting for transfers between devices: 19.2 us -> 12.1 us
  starting transfers between devices: 40.4 us -> 44.5 us
    ppermute x16, waiting for transfers between devices: 14.3 us -> 8.61 us  [send(): return lax.ppermute(block, 'pcol', pairs)]
    ppermute x8, starting transfers between devices: 14.5 us -> 17 us  [zsend(): return lax.ppermute(x, 'prow', pairs)]
    ppermute x16, starting transfers between devices: 25.9 us -> 27.5 us  [send(): return lax.ppermute(block, 'pcol', pairs)]
    ppermute x8, waiting for transfers between devices: 4.91 us -> 3.51 us  [zsend(): return lax.ppermute(x, 'prow', pairs)]
    pallas_call x1 -> x2, Pallas kernels: 11.1 us -> 10.7 us  [the longest x1 7.86 us: update(): pl.pallas_call(update_kernel, in_specs=[SMEM] * 5 + [VMEM] * 14, out_spec...]
  transfers between devices with their start and end apart: 24 -> 24, of which waited for: 11 -> 7; matrix products, arithmetic and copies ran while one was open for 0% -> 0% of each run, Pallas kernels for 12% -> 16%
where the time goes in v9:
time: 78.9 us; the launch traced here: 78.6 us
  starting transfers between devices  44.5 us (56%)
  Pallas kernels  20.9 us (26%)
  waiting for transfers between devices  12.1 us (15%)
    ppermute x16, starting transfers between devices, send(): return lax.ppermute(block, 'pcol', pairs)  27.5 us
    ppermute x8, starting transfers between devices, zsend(): return lax.ppermute(x, 'prow', pairs)  17 us
    ppermute x16, waiting for transfers between devices, send(): return lax.ppermute(block, 'pcol', pairs)  8.61 us
    pallas_call x1, Pallas kernels, update(): pl.pallas_call(update_kernel, in_specs=[SMEM] * 5 + [VMEM] * 14, out_spec...  7.86 us
    pallas_call x1, Pallas kernels, solve(): pl.pallas_call(solve_kernel, in_specs=[SMEM] + [VMEM] * 4, out_specs=VMEM...  4.26 us
    pallas_call x1, Pallas kernels, pick(): pl.pallas_call(functools.partial(pick_kernel, blk), in_specs=[SMEM, SMEM,...  3.94 us
    ppermute x8, waiting for transfers between devices, zsend(): return lax.ppermute(x, 'prow', pairs)  3.51 us
    pallas_call x1, Pallas kernels, fetch(): pl.pallas_call(fetch_kernel, in_specs=[pl.BlockSpec(memory_space=pltpu.HB...  2.87 us
  transfers between devices with their start and end apart: 24, of which 7 were waited for; matrix products, arithmetic and copies ran while one was open for 0% of the time, Pallas kernels for 16%

profile of v9, /device:TPU:1, one launch (start us, length us, event | category | flops | bytes accessed | tf_op | source)
XLA Modules:
  0.0 78.6 jit_solution(8831345422992740463)
XLA Ops:
  0.0 3.7 %collective-permute-start.2 = (bf16[8,24576]{1,0:T(8,128)(2,1)}, bf16[8,24576]{1,0:T(8,128)(2,1)S(1)}, u32[]{:S(2)}, u32[]{:S(2)}) collective-permute-start(bf16[8,24576]{1,0:T(8,128)(2,1)} %refs_0_.3), channel_id=1, source_target_pairs={{0,16},{1,5},{2,18},{3,7},{4,20},{5,1},{6,22},{7,3},{8,24},{9,13},... | collective-permute-start | bytes 1179656 | tf_op jit(solution)/shard_map/ppermute | solution.py:37
  3.7 0.8 collective-permute-start.1
  4.5 0.7 collective-permute-start
  5.2 0.7 copy-done
  5.9 3.9 %pick.1 = (bf16[256,128]{1,0:T(8,128)(2,1)S(1)}, bf16[256,128]{1,0:T(8,128)(2,1)S(1)}, s32[1]{0:T(128)}, s32[256]{0:T(256)S(1)}) custom-call(s32[256]{0:T(256)S(1)} %copy-done, s32[1]{0:T(128)} %bitcast.first_ref, bf16[24576,128]{1,0:T(8,128)(2,1)} %src_ref), custom_call_target="tpu_custom_call" | custom-call | flops 13200000000 | bytes 42000000 | tf_op jit(solution)/shard_map/pick/pallas_call | solution.py:184
  9.8 1.3 %collective-permute-start.6 = (bf16[256,128]{1,0:T(8,128)(2,1)S(1)}, bf16[256,128]{1,0:T(8,128)(2,1)S(1)}, u32[]{:S(2)}, u32[]{:S(2)}) collective-permute-start(bf16[256,128]{1,0:T(8,128)(2,1)S(1)} %get-tuple-element.49.a_ref), channel_id=1, source_target_pairs={{128,0},{160,32},{192,64},{224,96},{129,1},{161,33},{193,65},{225,... | collective-permute-start | bytes 196616 | tf_op jit(solution)/shard_map/ppermute | solution.py:404
  11.1 0.0 collective-permute-done.2.refs_3_
  11.2 2.9 %collective-permute-done.1.refs_2_ = bf16[8,24576]{1,0:T(8,128)(2,1)S(1)} collective-permute-done((bf16[8,24576]{1,0:T(8,128)(2,1)}, bf16[8,24576]{1,0:T(8,128)(2,1)S(1)}, u32[]{:S(2)}, u32[]{:S(2)}) %collective-permute-start.1) | collective-permute-done | bytes 393248 | tf_op jit(solution)/shard_map/ppermute | solution.py:37
  14.1 0.0 collective-permute-done.refs_1_
  14.1 2.6 %collective-permute-start.5 = (bf16[32,256]{1,0:T(8,128)(2,1)S(1)}, bf16[32,256]{1,0:T(8,128)(2,1)S(1)}, u32[]{:S(2)}, u32[]{:S(2)}) collective-permute-start(bf16[32,256]{1,0:T(8,128)(2,1)S(1)} %stack_d.1.refs_0_), channel_id=1, source_target_pairs={{0,6},{1,25},{2,0},{3,27},{4,2},{5,29},{6,4},{7,31},{8,14},{9,1},{... | collective-permute-start | bytes 49160 | tf_op jit(solution)/shard_map/ppermute | solution.py:37
  16.6 1.7 %collective-permute-start.3 = (bf16[32,256]{1,0:T(8,128)(2,1)S(1)}, bf16[32,256]{1,0:T(8,128)(2,1)S(1)}, u32[]{:S(2)}, u32[]{:S(2)}) collective-permute-start(bf16[32,256]{1,0:T(8,128)(2,1)S(1)} %stack_d.1.refs_0_), channel_id=1, source_target_pairs={{0,4},{1,17},{2,6},{3,19},{4,0},{5,21},{6,2},{7,23},{8,12},{9,25},... | collective-permute-start | bytes 49160 | tf_op jit(solution)/shard_map/ppermute | solution.py:37
  18.4 0.3 stack_p.1.refs_1_
  18.7 0.7 collective-permute-done.6.b_ref
  19.4 0.0 collective-permute-done.5.refs_2_
  19.4 1.3 %collective-permute-done.4.refs_1_ = bf16[32,256]{1,0:T(8,128)(2,1)S(1)} collective-permute-done((bf16[32,256]{1,0:T(8,128)(2,1)S(1)}, bf16[32,256]{1,0:T(8,128)(2,1)S(1)}, u32[]{:S(2)}, u32[]{:S(2)}) %collective-permute-start.4) | collective-permute-done | bytes 16416 | tf_op jit(solution)/shard_map/ppermute | solution.py:37
  20.7 0.3 collective-permute-done.3.refs_3_
  21.1 1.3 %collective-permute-start.7 = (bf16[256,128]{1,0:T(8,128)(2,1)S(1)}, bf16[256,128]{1,0:T(8,128)(2,1)S(1)}, u32[]{:S(2)}, u32[]{:S(2)}) collective-permute-start(bf16[256,128]{1,0:T(8,128)(2,1)S(1)} %add.2.a_ref), channel_id=1, source_target_pairs={{64,0},{96,32},{65,1},{97,33},{66,2},{98,34},{67,3},{99,35},{68,4}... | collective-permute-start | bytes 196616 | tf_op jit(solution)/shard_map/ppermute | solution.py:404
  22.4 3.4 %collective-permute-start.8 = (bf16[128,256]{1,0:T(8,128)(2,1)S(1)}, bf16[128,256]{1,0:T(8,128)(2,1)S(1)}, u32[]{:S(2)}, u32[]{:S(2)}) collective-permute-start(bf16[128,256]{1,0:T(8,128)(2,1)S(1)} %stack_l.1.own_ref), channel_id=1, source_target_pairs={{0,1},{1,0},{2,3},{3,2},{4,5},{5,4},{6,7},{7,6},{8,9},{9,8},{10,11... | collective-permute-start | bytes 196616 | tf_op jit(solution)/shard_map/ppermute | solution.py:37
  25.7 1.7 %collective-permute-start.13 = (bf16[32,24576]{1,0:T(8,128)(2,1)S(1)}, bf16[32,24576]{1,0:T(8,128)(2,1)S(1)}, u32[]{:S(2)}, u32[]{:S(2)}) collective-permute-start(bf16[32,24576]{1,0:T(8,128)(2,1)S(1)} %stack_p.1.refs_1_), channel_id=1, source_target_pairs={{0,6},{1,25},{2,0},{3,27},{4,2},{5,29},{6,4},{7,31},{8,14},{9,1},{... | collective-permute-start | bytes 4718600 | tf_op jit(solution)/shard_map/ppermute | solution.py:37
  27.5 0.0 collective-permute-start.12
  27.5 0.0 collective-permute-done.8.other_ref
  27.5 4.0 %collective-permute-start.14 = (bf16[32,24576]{1,0:T(8,128)(2,1)S(1)}, bf16[32,24576]{1,0:T(8,128)(2,1)}, u32[]{:S(2)}, u32[]{:S(2)}) collective-permute-start(bf16[32,24576]{1,0:T(8,128)(2,1)S(1)} %stack_p.1.refs_1_), channel_id=1, source_target_pairs={{0,1},{1,0},{2,3},{3,2},{4,5},{5,4},{6,7},{7,6},{8,9},{9,8},{10,11... | collective-permute-start | bytes 4718600 | tf_op jit(solution)/shard_map/ppermute | solution.py:37
  31.5 1.3 %collective-permute-start.9 = (bf16[256,128]{1,0:T(8,128)(2,1)S(1)}, bf16[256,128]{1,0:T(8,128)(2,1)S(1)}, u32[]{:S(2)}, u32[]{:S(2)}) collective-permute-start(bf16[256,128]{1,0:T(8,128)(2,1)S(1)} %add.3.top_ref), channel_id=1, source_target_pairs={{32,0},{33,1},{34,2},{35,3},{36,4},{37,5},{38,6},{39,7},{40,8},{41... | collective-permute-start | bytes 196616 | tf_op jit(solution)/shard_map/ppermute | solution.py:404
  32.8 1.6 %collective-permute-start.10 = (bf16[256,128]{1,0:T(8,128)(2,1)S(1)}, bf16[256,128]{1,0:T(8,128)(2,1)S(1)}, u32[]{:S(2)}, u32[]{:S(2)}) collective-permute-start(bf16[256,128]{1,0:T(8,128)(2,1)S(1)} %get-tuple-element.59.a_ref), channel_id=1, source_target_pairs={{0,64},{1,65},{2,66},{3,67},{4,68},{5,69},{6,70},{7,71},{8,72},{9,... | collective-permute-start | bytes 196616 | tf_op jit(solution)/shard_map/ppermute | solution.py:404
  34.4 2.8 %collective-permute-done.9.more_ref = bf16[256,128]{1,0:T(8,128)(2,1)S(1)} collective-permute-done((bf16[256,128]{1,0:T(8,128)(2,1)S(1)}, bf16[256,128]{1,0:T(8,128)(2,1)S(1)}, u32[]{:S(2)}, u32[]{:S(2)}) %collective-permute-start.9) | collective-permute-done | bytes 65568 | tf_op jit(solution)/shard_map/ppermute | solution.py:404
  37.2 0.0 collective-permute-done.10.b_ref
  37.2 1.3 %collective-permute-start.15 = (bf16[256,128]{1,0:T(8,128)(2,1)S(1)}, bf16[256,128]{1,0:T(8,128)(2,1)S(1)}, u32[]{:S(2)}, u32[]{:S(2)}) collective-permute-start(bf16[256,128]{1,0:T(8,128)(2,1)S(1)} %choose.3.a_ref), channel_id=1, source_target_pairs={{0,32},{64,96},{1,33},{65,97},{2,34},{66,98},{3,35},{67,99},{4,36}... | collective-permute-start | bytes 196616 | tf_op jit(solution)/shard_map/ppermute | solution.py:404
  38.5 4.3 %solve.1.a_ref = bf16[256,128]{1,0:T(8,128)(2,1)S(1)} custom-call(s32[1]{0:T(128)} %bitcast.1.me_ref, bf16[128,256]{1,0:T(8,128)(2,1)S(1)} %stack_l.1.own_ref, bf16[128,256]{1,0:T(8,128)(2,1)S(1)} %collective-permute-done.8.other_ref, bf16[256,128]{1,0:T(8,128)(2,1)S(1)} %add.3.top_ref, bf16[256,128]{1,0:T(8,128)(2,1)S(1)} %collective-permute-done.9.more_ref), custom_call_target="tpu_custom_call" | custom-call | tf_op jit(solution)/shard_map/solve/pallas_call | solution.py:278
  42.8 3.8 %collective-permute-start.11 = (bf16[256,128]{1,0:T(8,128)(2,1)S(1)}, bf16[256,128]{1,0:T(8,128)(2,1)S(1)}, u32[]{:S(2)}, u32[]{:S(2)}) collective-permute-start(bf16[256,128]{1,0:T(8,128)(2,1)S(1)} %solve.1.a_ref), channel_id=1, source_target_pairs={{0,64},{1,65},{2,66},{3,67},{4,68},{5,69},{6,70},{7,71},{8,72},{9,... | collective-permute-start | bytes 196616 | tf_op jit(solution)/shard_map/ppermute | solution.py:404
  46.6 2.9 %fetch.1.tr_ref = bf16[24576,128]{1,0:T(8,128)(2,1)S(1)} custom-call(bf16[24576,128]{1,0:T(8,128)(2,1)} %src_ref), custom_call_target="tpu_custom_call" | custom-call | tf_op jit(solution)/shard_map/fetch/pallas_call | solution.py:303
  49.5 0.0 collective-permute-done.12.refs_0_.refs_2_
  49.5 0.1 stack_b.1
  49.6 2.4 %collective-permute-start.19 = (bf16[32,12288]{1,0:T(8,128)(2,1)S(1)}, bf16[32,12288]{1,0:T(8,128)(2,1)S(1)}, u32[]{:S(2)}, u32[]{:S(2)}) collective-permute-start(bf16[32,12288]{1,0:T(8,128)(2,1)S(1)} %stack_b.1), channel_id=1, source_target_pairs={{0,6},{1,25},{2,0},{3,27},{4,2},{5,29},{6,4},{7,31},{8,14},{9,1},{... | collective-permute-start | bytes 2359304 | tf_op jit(solution)/shard_map/ppermute | solution.py:37
  52.1 1.5 %stack_a.1 = bf16[32,12288]{1,0:T(8,128)(2,1)S(1)} custom-call(bf16[32,24576]{1,0:T(8,128)(2,1)} %collective-permute-done.12.refs_0_.refs_2_), custom_call_target="tpu_custom_call" | custom-call | flops 1100000000 | bytes 3500000 | tf_op jit(solution)/shard_map/stack_a/pallas_call | solution.py:60
  53.5 0.1 collective-permute-start.18
  53.7 1.4 %collective-permute-start.16 = (bf16[256,128]{1,0:T(8,128)(2,1)S(1)}, bf16[256,128]{1,0:T(8,128)(2,1)S(1)}, u32[]{:S(2)}, u32[]{:S(2)}) collective-permute-start(bf16[256,128]{1,0:T(8,128)(2,1)S(1)} %choose.5.a_ref), channel_id=1, source_target_pairs={{0,32},{64,96},{1,33},{65,97},{2,34},{66,98},{3,35},{67,99},{4,36}... | collective-permute-start | bytes 196616 | tf_op jit(solution)/shard_map/ppermute | solution.py:404
  55.1 2.8 %collective-permute-start.20 = (bf16[32,24576]{1,0:T(8,128)(2,1)}, bf16[32,24576]{1,0:T(8,128)(2,1)S(1)}, u32[]{:S(2)}, u32[]{:S(2)}) collective-permute-start(bf16[32,24576]{1,0:T(8,128)(2,1)} %collective-permute-done.12.refs_0_.refs_2_), channel_id=1, source_target_pairs={{0,1},{1,0},{2,3},{3,2},{4,5},{5,4},{6,7},{7,6},{8,9},{9,8},{10,11... | collective-permute-start | bytes 4718600 | tf_op jit(solution)/shard_map/ppermute | solution.py:37
  57.9 0.3 collective-permute-start.21
  58.2 0.0 copy-start.1
  58.2 5.0 %collective-permute-start.17 = (bf16[512,128]{1,0:T(8,128)(2,1)S(1)}, bf16[512,128]{1,0:T(8,128)(2,1)S(1)}, u32[]{:S(2)}, u32[]{:S(2)}) collective-permute-start(bf16[512,128]{1,0:T(8,128)(2,1)S(1)} %join.1.ud_ref), channel_id=1, source_target_pairs={{0,128},{32,160},{64,192},{96,224},{1,129},{33,161},{65,193},{97,2... | collective-permute-start | bytes 393224 | tf_op jit(solution)/shard_map/ppermute | solution.py:404
  63.2 0.6 collective-permute-start.23
  63.8 2.1 %collective-permute-done.18.refs_0_.refs_4_ = bf16[32,12288]{1,0:T(8,128)(2,1)S(1)} collective-permute-done((bf16[32,12288]{1,0:T(8,128)(2,1)S(1)}, bf16[32,12288]{1,0:T(8,128)(2,1)S(1)}, u32[]{:S(2)}, u32[]{:S(2)}) %collective-permute-start.18) | collective-permute-done | bytes 786464 | tf_op jit(solution)/shard_map/ppermute | solution.py:37
  66.0 2.7 %collective-permute-start.22 = (bf16[32,12288]{1,0:T(8,128)(2,1)S(1)}, bf16[32,12288]{1,0:T(8,128)(2,1)S(1)}, u32[]{:S(2)}, u32[]{:S(2)}) collective-permute-start(bf16[32,12288]{1,0:T(8,128)(2,1)S(1)} %collective-permute-done.18.refs_0_.refs_4_), channel_id=1, source_target_pairs={{0,1},{1,0},{2,3},{3,2},{4,5},{5,4},{6,7},{7,6},{8,9},{9,8},{10,11... | collective-permute-start | bytes 2359304 | tf_op jit(solution)/shard_map/ppermute | solution.py:37
  68.7 0.0 collective-permute-done.17.rest_ref
  68.7 1.9 %collective-permute-done.22.refs_9_ = bf16[32,12288]{1,0:T(8,128)(2,1)S(1)} collective-permute-done((bf16[32,12288]{1,0:T(8,128)(2,1)S(1)}, bf16[32,12288]{1,0:T(8,128)(2,1)S(1)}, u32[]{:S(2)}, u32[]{:S(2)}) %collective-permute-start.22) | collective-permute-done | bytes 786464 | tf_op jit(solution)/shard_map/ppermute | solution.py:37
  70.6 0.0 collective-permute-done.20.refs_7_
  70.6 0.0 collective-permute-done.21.refs_8_
  70.6 7.9 %update.1 = (bf16[24576,128]{1,0:T(8,128)(2,1)}, bf16[24576,128]{1,0:T(8,128)(2,1)S(1)}) custom-call(s32[1]{0:T(128)} %get-tuple-element.39.cnt_ref, s32[256]{0:T(256)S(1)} %get-tuple-element.40.lst_ref, s32[256]{0:T(256)S(1)} %copy-done.1, s32[1]{0:T(128)} %bitcast.first_ref, s32[1]{0:T(128)} %bitcast.1.me_ref, ...), custom_call_target="tpu_custom_call", output_to_operand_aliasing={{1}: (5, {})} | custom-call | tf_op jit(solution)/shard_map/update/pallas_call | solution.py:377
  (22 shorter events, 0.1 us)
Async XLA Ops:
  0.0 11.1 %collective-permute-start.2 = (bf16[8,24576]{1,0:T(8,128)(2,1)}, bf16[8,24576]{1,0:T(8,128)(2,1)S(1)}, u32[]{:S(2)}, u32[]{:S(2)}) collective-permute-start(bf16[8,24576]{1,0:T(8,128)(2,1)} %refs_0_.3), channel_id=1, source_target_pairs={{0,16},{1,5},{2,18},{3,7},{4,20},{5,1},{6,22},{7,3},{8,24},{9,13},... | collective-permute-start | bytes 1179656 | tf_op jit(solution)/shard_map/ppermute | solution.py:37
  3.7 10.3 %collective-permute-start.1 = (bf16[8,24576]{1,0:T(8,128)(2,1)}, bf16[8,24576]{1,0:T(8,128)(2,1)S(1)}, u32[]{:S(2)}, u32[]{:S(2)}) collective-permute-start(bf16[8,24576]{1,0:T(8,128)(2,1)} %refs_0_.3), channel_id=1, source_target_pairs={{0,24},{1,7},{2,26},{3,1},{4,28},{5,3},{6,30},{7,5},{8,0},{9,15},{... | collective-permute-start | bytes 1179656 | tf_op jit(solution)/shard_map/ppermute | solution.py:37
  4.5 9.5 %collective-permute-start = (bf16[8,24576]{1,0:T(8,128)(2,1)}, bf16[8,24576]{1,0:T(8,128)(2,1)S(1)}, u32[]{:S(2)}, u32[]{:S(2)}) collective-permute-start(bf16[8,24576]{1,0:T(8,128)(2,1)} %refs_0_.3), channel_id=1, source_target_pairs={{0,8},{1,3},{2,10},{3,5},{4,12},{5,7},{6,14},{7,1},{8,16},{9,11},{... | collective-permute-start | bytes 1179656 | tf_op jit(solution)/shard_map/ppermute | solution.py:37
  5.2 0.7 copy-start
  5.9 8.2 %copy-start.2 = (bf16[8,24576]{1,0:T(8,128)(2,1)S(1)}, bf16[8,24576]{1,0:T(8,128)(2,1)}, u32[]{:S(2)}) copy-start(bf16[8,24576]{1,0:T(8,128)(2,1)} %refs_0_.3) | copy-start | bytes 1179652
  9.8 9.6 %collective-permute-start.6 = (bf16[256,128]{1,0:T(8,128)(2,1)S(1)}, bf16[256,128]{1,0:T(8,128)(2,1)S(1)}, u32[]{:S(2)}, u32[]{:S(2)}) collective-permute-start(bf16[256,128]{1,0:T(8,128)(2,1)S(1)} %get-tuple-element.49.a_ref), channel_id=1, source_target_pairs={{128,0},{160,32},{192,64},{224,96},{129,1},{161,33},{193,65},{225,... | collective-permute-start | bytes 196616 | tf_op jit(solution)/shard_map/ppermute | solution.py:404
  14.1 5.3 %collective-permute-start.5 = (bf16[32,256]{1,0:T(8,128)(2,1)S(1)}, bf16[32,256]{1,0:T(8,128)(2,1)S(1)}, u32[]{:S(2)}, u32[]{:S(2)}) collective-permute-start(bf16[32,256]{1,0:T(8,128)(2,1)S(1)} %stack_d.1.refs_0_), channel_id=1, source_target_pairs={{0,6},{1,25},{2,0},{3,27},{4,2},{5,29},{6,4},{7,31},{8,14},{9,1},{... | collective-permute-start | bytes 49160 | tf_op jit(solution)/shard_map/ppermute | solution.py:37
  16.6 4.1 %collective-permute-start.4 = (bf16[32,256]{1,0:T(8,128)(2,1)S(1)}, bf16[32,256]{1,0:T(8,128)(2,1)S(1)}, u32[]{:S(2)}, u32[]{:S(2)}) collective-permute-start(bf16[32,256]{1,0:T(8,128)(2,1)S(1)} %stack_d.1.refs_0_), channel_id=1, source_target_pairs={{0,2},{1,9},{2,4},{3,11},{4,6},{5,13},{6,0},{7,15},{8,10},{9,17},{... | collective-permute-start | bytes 49160 | tf_op jit(solution)/shard_map/ppermute | solution.py:37
  16.6 4.4 %collective-permute-start.3 = (bf16[32,256]{1,0:T(8,128)(2,1)S(1)}, bf16[32,256]{1,0:T(8,128)(2,1)S(1)}, u32[]{:S(2)}, u32[]{:S(2)}) collective-permute-start(bf16[32,256]{1,0:T(8,128)(2,1)S(1)} %stack_d.1.refs_0_), channel_id=1, source_target_pairs={{0,4},{1,17},{2,6},{3,19},{4,0},{5,21},{6,2},{7,23},{8,12},{9,25},... | collective-permute-start | bytes 49160 | tf_op jit(solution)/shard_map/ppermute | solution.py:37
  21.1 6.4 %collective-permute-start.7 = (bf16[256,128]{1,0:T(8,128)(2,1)S(1)}, bf16[256,128]{1,0:T(8,128)(2,1)S(1)}, u32[]{:S(2)}, u32[]{:S(2)}) collective-permute-start(bf16[256,128]{1,0:T(8,128)(2,1)S(1)} %add.2.a_ref), channel_id=1, source_target_pairs={{64,0},{96,32},{65,1},{97,33},{66,2},{98,34},{67,3},{99,35},{68,4}... | collective-permute-start | bytes 196616 | tf_op jit(solution)/shard_map/ppermute | solution.py:404
  22.4 5.1 %collective-permute-start.8 = (bf16[128,256]{1,0:T(8,128)(2,1)S(1)}, bf16[128,256]{1,0:T(8,128)(2,1)S(1)}, u32[]{:S(2)}, u32[]{:S(2)}) collective-permute-start(bf16[128,256]{1,0:T(8,128)(2,1)S(1)} %stack_l.1.own_ref), channel_id=1, source_target_pairs={{0,1},{1,0},{2,3},{3,2},{4,5},{5,4},{6,7},{7,6},{8,9},{9,8},{10,11... | collective-permute-start | bytes 196616 | tf_op jit(solution)/shard_map/ppermute | solution.py:37
  25.7 23.8 %collective-permute-start.13 = (bf16[32,24576]{1,0:T(8,128)(2,1)S(1)}, bf16[32,24576]{1,0:T(8,128)(2,1)S(1)}, u32[]{:S(2)}, u32[]{:S(2)}) collective-permute-start(bf16[32,24576]{1,0:T(8,128)(2,1)S(1)} %stack_p.1.refs_1_), channel_id=1, source_target_pairs={{0,6},{1,25},{2,0},{3,27},{4,2},{5,29},{6,4},{7,31},{8,14},{9,1},{... | collective-permute-start | bytes 4718600 | tf_op jit(solution)/shard_map/ppermute | solution.py:37
  27.5 22.0 %collective-permute-start.12 = (bf16[32,24576]{1,0:T(8,128)(2,1)S(1)}, bf16[32,24576]{1,0:T(8,128)(2,1)}, u32[]{:S(2)}, u32[]{:S(2)}) collective-permute-start(bf16[32,24576]{1,0:T(8,128)(2,1)S(1)} %stack_p.1.refs_1_), channel_id=1, source_target_pairs={{0,2},{1,9},{2,4},{3,11},{4,6},{5,13},{6,0},{7,15},{8,10},{9,17},{... | collective-permute-start | bytes 4718600 | tf_op jit(solution)/shard_map/ppermute | solution.py:37
  27.5 22.0 %collective-permute-start.14 = (bf16[32,24576]{1,0:T(8,128)(2,1)S(1)}, bf16[32,24576]{1,0:T(8,128)(2,1)}, u32[]{:S(2)}, u32[]{:S(2)}) collective-permute-start(bf16[32,24576]{1,0:T(8,128)(2,1)S(1)} %stack_p.1.refs_1_), channel_id=1, source_target_pairs={{0,1},{1,0},{2,3},{3,2},{4,5},{5,4},{6,7},{7,6},{8,9},{9,8},{10,11... | collective-permute-start | bytes 4718600 | tf_op jit(solution)/shard_map/ppermute | solution.py:37
  31.5 5.7 %collective-permute-start.9 = (bf16[256,128]{1,0:T(8,128)(2,1)S(1)}, bf16[256,128]{1,0:T(8,128)(2,1)S(1)}, u32[]{:S(2)}, u32[]{:S(2)}) collective-permute-start(bf16[256,128]{1,0:T(8,128)(2,1)S(1)} %add.3.top_ref), channel_id=1, source_target_pairs={{32,0},{33,1},{34,2},{35,3},{36,4},{37,5},{38,6},{39,7},{40,8},{41... | collective-permute-start | bytes 196616 | tf_op jit(solution)/shard_map/ppermute | solution.py:404
  32.8 4.4 %collective-permute-start.10 = (bf16[256,128]{1,0:T(8,128)(2,1)S(1)}, bf16[256,128]{1,0:T(8,128)(2,1)S(1)}, u32[]{:S(2)}, u32[]{:S(2)}) collective-permute-start(bf16[256,128]{1,0:T(8,128)(2,1)S(1)} %get-tuple-element.59.a_ref), channel_id=1, source_target_pairs={{0,64},{1,65},{2,66},{3,67},{4,68},{5,69},{6,70},{7,71},{8,72},{9,... | collective-permute-start | bytes 196616 | tf_op jit(solution)/shard_map/ppermute | solution.py:404
  37.2 12.2 %collective-permute-start.15 = (bf16[256,128]{1,0:T(8,128)(2,1)S(1)}, bf16[256,128]{1,0:T(8,128)(2,1)S(1)}, u32[]{:S(2)}, u32[]{:S(2)}) collective-permute-start(bf16[256,128]{1,0:T(8,128)(2,1)S(1)} %choose.3.a_ref), channel_id=1, source_target_pairs={{0,32},{64,96},{1,33},{65,97},{2,34},{66,98},{3,35},{67,99},{4,36}... | collective-permute-start | bytes 196616 | tf_op jit(solution)/shard_map/ppermute | solution.py:404
  42.8 6.7 %collective-permute-start.11 = (bf16[256,128]{1,0:T(8,128)(2,1)S(1)}, bf16[256,128]{1,0:T(8,128)(2,1)S(1)}, u32[]{:S(2)}, u32[]{:S(2)}) collective-permute-start(bf16[256,128]{1,0:T(8,128)(2,1)S(1)} %solve.1.a_ref), channel_id=1, source_target_pairs={{0,64},{1,65},{2,66},{3,67},{4,68},{5,69},{6,70},{7,71},{8,72},{9,... | collective-permute-start | bytes 196616 | tf_op jit(solution)/shard_map/ppermute | solution.py:404
  49.6 13.6 %collective-permute-start.19 = (bf16[32,12288]{1,0:T(8,128)(2,1)S(1)}, bf16[32,12288]{1,0:T(8,128)(2,1)S(1)}, u32[]{:S(2)}, u32[]{:S(2)}) collective-permute-start(bf16[32,12288]{1,0:T(8,128)(2,1)S(1)} %stack_b.1), channel_id=1, source_target_pairs={{0,6},{1,25},{2,0},{3,27},{4,2},{5,29},{6,4},{7,31},{8,14},{9,1},{... | collective-permute-start | bytes 2359304 | tf_op jit(solution)/shard_map/ppermute | solution.py:37
  53.5 12.4 %collective-permute-start.18 = (bf16[32,12288]{1,0:T(8,128)(2,1)S(1)}, bf16[32,12288]{1,0:T(8,128)(2,1)S(1)}, u32[]{:S(2)}, u32[]{:S(2)}) collective-permute-start(bf16[32,12288]{1,0:T(8,128)(2,1)S(1)} %stack_a.1), channel_id=1, source_target_pairs={{0,2},{1,9},{2,4},{3,11},{4,6},{5,13},{6,0},{7,15},{8,10},{9,17},{... | collective-permute-start | bytes 2359304 | tf_op jit(solution)/shard_map/ppermute | solution.py:37
  53.7 4.5 %collective-permute-start.16 = (bf16[256,128]{1,0:T(8,128)(2,1)S(1)}, bf16[256,128]{1,0:T(8,128)(2,1)S(1)}, u32[]{:S(2)}, u32[]{:S(2)}) collective-permute-start(bf16[256,128]{1,0:T(8,128)(2,1)S(1)} %choose.5.a_ref), channel_id=1, source_target_pairs={{0,32},{64,96},{1,33},{65,97},{2,34},{66,98},{3,35},{67,99},{4,36}... | collective-permute-start | bytes 196616 | tf_op jit(solution)/shard_map/ppermute | solution.py:404
  55.1 15.5 %collective-permute-start.20 = (bf16[32,24576]{1,0:T(8,128)(2,1)}, bf16[32,24576]{1,0:T(8,128)(2,1)S(1)}, u32[]{:S(2)}, u32[]{:S(2)}) collective-permute-start(bf16[32,24576]{1,0:T(8,128)(2,1)} %collective-permute-done.12.refs_0_.refs_2_), channel_id=1, source_target_pairs={{0,1},{1,0},{2,3},{3,2},{4,5},{5,4},{6,7},{7,6},{8,9},{9,8},{10,11... | collective-permute-start | bytes 4718600 | tf_op jit(solution)/shard_map/ppermute | solution.py:37
  57.9 12.7 %collective-permute-start.21 = (bf16[32,24576]{1,0:T(8,128)(2,1)S(1)}, bf16[32,24576]{1,0:T(8,128)(2,1)S(1)}, u32[]{:S(2)}, u32[]{:S(2)}) collective-permute-start(bf16[32,24576]{1,0:T(8,128)(2,1)S(1)} %collective-permute-done.13.refs_0_.refs_3_), channel_id=1, source_target_pairs={{0,1},{1,0},{2,3},{3,2},{4,5},{5,4},{6,7},{7,6},{8,9},{9,8},{10,11... | collective-permute-start | bytes 4718600 | tf_op jit(solution)/shard_map/ppermute | solution.py:37
  58.2 12.4 %copy-start.1 = (s32[256]{0:T(256)S(1)}, s32[256]{0:T(256)}, u32[]{:S(2)}) copy-start(s32[256]{0:T(256)} %piv_ref.3) | copy-start | bytes 3076
  58.2 10.5 %collective-permute-start.17 = (bf16[512,128]{1,0:T(8,128)(2,1)S(1)}, bf16[512,128]{1,0:T(8,128)(2,1)S(1)}, u32[]{:S(2)}, u32[]{:S(2)}) collective-permute-start(bf16[512,128]{1,0:T(8,128)(2,1)S(1)} %join.1.ud_ref), channel_id=1, source_target_pairs={{0,128},{32,160},{64,192},{96,224},{1,129},{33,161},{65,193},{97,2... | collective-permute-start | bytes 393224 | tf_op jit(solution)/shard_map/ppermute | solution.py:404
  63.2 5.5 %collective-permute-start.23 = (bf16[32,12288]{1,0:T(8,128)(2,1)S(1)}, bf16[32,12288]{1,0:T(8,128)(2,1)S(1)}, u32[]{:S(2)}, u32[]{:S(2)}) collective-permute-start(bf16[32,12288]{1,0:T(8,128)(2,1)S(1)} %collective-permute-done.19.refs_1_.refs_5_), channel_id=1, source_target_pairs={{0,1},{1,0},{2,3},{3,2},{4,5},{5,4},{6,7},{7,6},{8,9},{9,8},{10,11... | collective-permute-start | bytes 2359304 | tf_op jit(solution)/shard_map/ppermute | solution.py:37
  66.0 4.6 %collective-permute-start.22 = (bf16[32,12288]{1,0:T(8,128)(2,1)S(1)}, bf16[32,12288]{1,0:T(8,128)(2,1)S(1)}, u32[]{:S(2)}, u32[]{:S(2)}) collective-permute-start(bf16[32,12288]{1,0:T(8,128)(2,1)S(1)} %collective-permute-done.18.refs_0_.refs_4_), channel_id=1, source_target_pairs={{0,1},{1,0},{2,3},{3,2},{4,5},{5,4},{6,7},{7,6},{8,9},{9,8},{10,11... | collective-permute-start | bytes 2359304 | tf_op jit(solution)/shard_map/ppermute | solution.py:37

commit v10 on v9

--- a/solution.py
+++ b/solution.py
@@ -10,7 +10,7 @@
 NX = 4
 NY = 4
 OFFSETS = (0, -1, 1, 2)
-NBLK = 6
+NBLK = 12
 SMEM = pl.BlockSpec(memory_space=pltpu.SMEM)
 VMEM = pl.BlockSpec(memory_space=pltpu.VMEM)
 HIGHEST = lax.Precision.HIGHEST
@@ -386,7 +386,7 @@
         ],
         out_shape=[jax.ShapeDtypeStruct((rows, cols), jnp.bfloat16)] * 2,
         input_output_aliases={5: 1},
-        compiler_params=params(28),
+        compiler_params=params(16),
         name="update",
     )(cnt, lst, pivots, first, me, trailing, ud, rest, ahead, *parts)[0]
 
@@ -420,18 +420,17 @@
     more = zsend(top, [(2, 0), (3, 1)])
     other = send(own, CORES)
     top = add(top, more)
-    top, disp, other = barrier((top, disp, other))
+    top, disp, other, source = barrier((top, disp, other, trailing))
+    copy = fetch(pltpu.with_memory_space_constraint(source, pltpu.HBM))
     more = zsend(top, [(1, 0)])
     lower = zsend(disp, [(0, 2)])
     top, block2 = barrier((top, block))
     swap = send(block2, CORES)
-    more, disp, lower = barrier((more, disp, lower))
+    more, disp, lower, copy = barrier((more, disp, lower, copy))
     u = solve(me, own, other, top, more)
     disp = choose(first, rows, (2,), disp, lower)
     disp = choose(first, rows, (1, 3), disp, zsend(disp, [(0, 1), (2, 3)]))
     ru = zsend(u, [(0, 2)])
-    u, source = barrier((u, trailing))
-    copy = fetch(pltpu.with_memory_space_constraint(source, pltpu.HBM))
     ru, near, far, swap, disp, copy = barrier((ru, near, far, swap, disp, copy))
     fa, fb = stack([near], 0, half, "stack_a"), stack([far], half, half, "stack_b")
     qa, qb = send(fa, up), send(fb, down)

time: 78.9 us -> 77.7 us (0.985)
  waiting for transfers between devices: 12.1 us -> 9.46 us
  starting transfers between devices: 44.5 us -> 46.1 us
    ppermute x8, starting transfers between devices: 17 us -> 18.5 us  [zsend(): return lax.ppermute(x, 'prow', pairs)]
    ppermute x8, waiting for transfers between devices: 3.51 us -> 2.01 us  [zsend(): return lax.ppermute(x, 'prow', pairs)]
    ppermute x16, waiting for transfers between devices: 8.61 us -> 7.46 us  [send(): return lax.ppermute(block, 'pcol', pairs)]
  transfers between devices with their start and end apart: 24 -> 24, of which waited for: 7 -> 8; matrix products, arithmetic and copies ran while one was open for 0% -> 0% of each run, Pallas kernels for 16% -> 17%
where the time goes in v10:
time: 77.7 us; the launch traced here: 77.4 us
  starting transfers between devices  46.1 us (59%)
  Pallas kernels  20.8 us (27%)
  waiting for transfers between devices  9.46 us (12%)
    ppermute x16, starting transfers between devices, send(): return lax.ppermute(block, 'pcol', pairs)  27.6 us
    ppermute x8, starting transfers between devices, zsend(): return lax.ppermute(x, 'prow', pairs)  18.5 us
    pallas_call x1, Pallas kernels, update(): pl.pallas_call(update_kernel, in_specs=[SMEM] * 5 + [VMEM] * 14, out_spec...  7.73 us
    ppermute x16, waiting for transfers between devices, send(): return lax.ppermute(block, 'pcol', pairs)  7.46 us
    pallas_call x1, Pallas kernels, solve(): pl.pallas_call(solve_kernel, in_specs=[SMEM] + [VMEM] * 4, out_specs=VMEM...  4.26 us
    pallas_call x1, Pallas kernels, pick(): pl.pallas_call(functools.partial(pick_kernel, blk), in_specs=[SMEM, SMEM,...  3.91 us
    pallas_call x1, Pallas kernels, fetch(): pl.pallas_call(fetch_kernel, in_specs=[pl.BlockSpec(memory_space=pltpu.HB...  2.87 us
    ppermute x8, waiting for transfers between devices, zsend(): return lax.ppermute(x, 'prow', pairs)  2.01 us
  transfers between devices with their start and end apart: 24, of which 8 were waited for; matrix products, arithmetic and copies ran while one was open for 0% of the time, Pallas kernels for 17%

profile of v10, /device:TPU:1, one launch (start us, length us, event | category | flops | bytes accessed | tf_op | source)
XLA Modules:
  0.0 77.4 jit_solution(18081211264397960148)
XLA Ops:
  0.0 3.7 %collective-permute-start.2 = (bf16[8,24576]{1,0:T(8,128)(2,1)}, bf16[8,24576]{1,0:T(8,128)(2,1)S(1)}, u32[]{:S(2)}, u32[]{:S(2)}) collective-permute-start(bf16[8,24576]{1,0:T(8,128)(2,1)} %refs_0_.3), channel_id=1, source_target_pairs={{0,16},{1,5},{2,18},{3,7},{4,20},{5,1},{6,22},{7,3},{8,24},{9,13},... | collective-permute-start | bytes 1179656 | tf_op jit(solution)/shard_map/ppermute | solution.py:37
  3.7 0.8 %collective-permute-start.1 = (bf16[8,24576]{1,0:T(8,128)(2,1)}, bf16[8,24576]{1,0:T(8,128)(2,1)S(1)}, u32[]{:S(2)}, u32[]{:S(2)}) collective-permute-start(bf16[8,24576]{1,0:T(8,128)(2,1)} %refs_0_.3), channel_id=1, source_target_pairs={{0,24},{1,7},{2,26},{3,1},{4,28},{5,3},{6,30},{7,5},{8,0},{9,15},{... | collective-permute-start | bytes 1179656 | tf_op jit(solution)/shard_map/ppermute | solution.py:37
  4.5 0.7 collective-permute-start
  5.2 0.7 copy-done
  5.9 3.9 %pick.1 = (bf16[256,128]{1,0:T(8,128)(2,1)S(1)}, bf16[256,128]{1,0:T(8,128)(2,1)S(1)}, s32[1]{0:T(128)}, s32[256]{0:T(256)S(1)}) custom-call(s32[256]{0:T(256)S(1)} %copy-done, s32[1]{0:T(128)} %bitcast.first_ref, bf16[24576,128]{1,0:T(8,128)(2,1)} %src_ref), custom_call_target="tpu_custom_call" | custom-call | flops 13200000000 | bytes 42000000 | tf_op jit(solution)/shard_map/pick/pallas_call | solution.py:184
  9.8 1.3 %collective-permute-start.6 = (bf16[256,128]{1,0:T(8,128)(2,1)S(1)}, bf16[256,128]{1,0:T(8,128)(2,1)S(1)}, u32[]{:S(2)}, u32[]{:S(2)}) collective-permute-start(bf16[256,128]{1,0:T(8,128)(2,1)S(1)} %get-tuple-element.49.a_ref), channel_id=1, source_target_pairs={{128,0},{160,32},{192,64},{224,96},{129,1},{161,33},{193,65},{225,... | collective-permute-start | bytes 196616 | tf_op jit(solution)/shard_map/ppermute | solution.py:404
  11.1 2.9 %collective-permute-done.1.refs_2_ = bf16[8,24576]{1,0:T(8,128)(2,1)S(1)} collective-permute-done((bf16[8,24576]{1,0:T(8,128)(2,1)}, bf16[8,24576]{1,0:T(8,128)(2,1)S(1)}, u32[]{:S(2)}, u32[]{:S(2)}) %collective-permute-start.1) | collective-permute-done | bytes 393248 | tf_op jit(solution)/shard_map/ppermute | solution.py:37
  14.1 0.0 collective-permute-done.refs_1_
  14.1 2.6 %collective-permute-start.5 = (bf16[32,256]{1,0:T(8,128)(2,1)S(1)}, bf16[32,256]{1,0:T(8,128)(2,1)S(1)}, u32[]{:S(2)}, u32[]{:S(2)}) collective-permute-start(bf16[32,256]{1,0:T(8,128)(2,1)S(1)} %stack_d.1.refs_0_), channel_id=1, source_target_pairs={{0,6},{1,25},{2,0},{3,27},{4,2},{5,29},{6,4},{7,31},{8,14},{9,1},{... | collective-permute-start | bytes 49160 | tf_op jit(solution)/shard_map/ppermute | solution.py:37
  16.6 0.0 collective-permute-start.4
  16.6 1.7 %collective-permute-start.3 = (bf16[32,256]{1,0:T(8,128)(2,1)S(1)}, bf16[32,256]{1,0:T(8,128)(2,1)S(1)}, u32[]{:S(2)}, u32[]{:S(2)}) collective-permute-start(bf16[32,256]{1,0:T(8,128)(2,1)S(1)} %stack_d.1.refs_0_), channel_id=1, source_target_pairs={{0,4},{1,17},{2,6},{3,19},{4,0},{5,21},{6,2},{7,23},{8,12},{9,25},... | collective-permute-start | bytes 49160 | tf_op jit(solution)/shard_map/ppermute | solution.py:37
  18.4 0.3 stack_p.1.refs_1_
  18.7 0.7 collective-permute-done.6.b_ref
  19.4 0.0 collective-permute-done.5.refs_2_
  19.4 1.3 %collective-permute-done.4.refs_1_ = bf16[32,256]{1,0:T(8,128)(2,1)S(1)} collective-permute-done((bf16[32,256]{1,0:T(8,128)(2,1)S(1)}, bf16[32,256]{1,0:T(8,128)(2,1)S(1)}, u32[]{:S(2)}, u32[]{:S(2)}) %collective-permute-start.4) | collective-permute-done | bytes 16416 | tf_op jit(solution)/shard_map/ppermute | solution.py:37
  20.7 0.3 collective-permute-done.3.refs_3_
  21.1 1.3 %collective-permute-start.7 = (bf16[256,128]{1,0:T(8,128)(2,1)S(1)}, bf16[256,128]{1,0:T(8,128)(2,1)S(1)}, u32[]{:S(2)}, u32[]{:S(2)}) collective-permute-start(bf16[256,128]{1,0:T(8,128)(2,1)S(1)} %add.2.a_ref), channel_id=1, source_target_pairs={{64,0},{96,32},{65,1},{97,33},{66,2},{98,34},{67,3},{99,35},{68,4}... | collective-permute-start | bytes 196616 | tf_op jit(solution)/shard_map/ppermute | solution.py:404
  22.4 3.4 %collective-permute-start.8 = (bf16[128,256]{1,0:T(8,128)(2,1)S(1)}, bf16[128,256]{1,0:T(8,128)(2,1)S(1)}, u32[]{:S(2)}, u32[]{:S(2)}) collective-permute-start(bf16[128,256]{1,0:T(8,128)(2,1)S(1)} %stack_l.1.own_ref), channel_id=1, source_target_pairs={{0,1},{1,0},{2,3},{3,2},{4,5},{5,4},{6,7},{7,6},{8,9},{9,8},{10,11... | collective-permute-start | bytes 196616 | tf_op jit(solution)/shard_map/ppermute | solution.py:37
  25.7 1.7 %collective-permute-start.13 = (bf16[32,24576]{1,0:T(8,128)(2,1)S(1)}, bf16[32,24576]{1,0:T(8,128)(2,1)S(1)}, u32[]{:S(2)}, u32[]{:S(2)}) collective-permute-start(bf16[32,24576]{1,0:T(8,128)(2,1)S(1)} %stack_p.1.refs_1_), channel_id=1, source_target_pairs={{0,6},{1,25},{2,0},{3,27},{4,2},{5,29},{6,4},{7,31},{8,14},{9,1},{... | collective-permute-start | bytes 4718600 | tf_op jit(solution)/shard_map/ppermute | solution.py:37
  27.5 0.0 collective-permute-start.12
  27.5 0.0 collective-permute-done.7.b_ref
  27.5 0.0 collective-permute-done.8.other_ref
  27.5 4.0 %collective-permute-start.14 = (bf16[32,24576]{1,0:T(8,128)(2,1)S(1)}, bf16[32,24576]{1,0:T(8,128)(2,1)}, u32[]{:S(2)}, u32[]{:S(2)}) collective-permute-start(bf16[32,24576]{1,0:T(8,128)(2,1)S(1)} %stack_p.1.refs_1_), channel_id=1, source_target_pairs={{0,1},{1,0},{2,3},{3,2},{4,5},{5,4},{6,7},{7,6},{8,9},{9,8},{10,11... | collective-permute-start | bytes 4718600 | tf_op jit(solution)/shard_map/ppermute | solution.py:37
  31.5 1.3 %collective-permute-start.9 = (bf16[256,128]{1,0:T(8,128)(2,1)S(1)}, bf16[256,128]{1,0:T(8,128)(2,1)S(1)}, u32[]{:S(2)}, u32[]{:S(2)}) collective-permute-start(bf16[256,128]{1,0:T(8,128)(2,1)S(1)} %add.3.top_ref), channel_id=1, source_target_pairs={{32,0},{33,1},{34,2},{35,3},{36,4},{37,5},{38,6},{39,7},{40,8},{41... | collective-permute-start | bytes 196616 | tf_op jit(solution)/shard_map/ppermute | solution.py:404
  32.8 1.6 %collective-permute-start.10 = (bf16[256,128]{1,0:T(8,128)(2,1)S(1)}, bf16[256,128]{1,0:T(8,128)(2,1)S(1)}, u32[]{:S(2)}, u32[]{:S(2)}) collective-permute-start(bf16[256,128]{1,0:T(8,128)(2,1)S(1)} %get-tuple-element.60.a_ref), channel_id=1, source_target_pairs={{0,64},{1,65},{2,66},{3,67},{4,68},{5,69},{6,70},{7,71},{8,72},{9,... | collective-permute-start | bytes 196616 | tf_op jit(solution)/shard_map/ppermute | solution.py:404
  34.4 2.9 %fetch.1.tr_ref = bf16[24576,128]{1,0:T(8,128)(2,1)S(1)} custom-call(bf16[24576,128]{1,0:T(8,128)(2,1)} %src_ref), custom_call_target="tpu_custom_call" | custom-call | tf_op jit(solution)/shard_map/fetch/pallas_call | solution.py:303
  37.3 3.0 %collective-permute-start.15 = (bf16[256,128]{1,0:T(8,128)(2,1)S(1)}, bf16[256,128]{1,0:T(8,128)(2,1)S(1)}, u32[]{:S(2)}, u32[]{:S(2)}) collective-permute-start(bf16[256,128]{1,0:T(8,128)(2,1)S(1)} %choose.3.a_ref), channel_id=1, source_target_pairs={{0,32},{64,96},{1,33},{65,97},{2,34},{66,98},{3,35},{67,99},{4,36}... | collective-permute-start | bytes 196616 | tf_op jit(solution)/shard_map/ppermute | solution.py:404
  40.4 4.3 %solve.1.a_ref = bf16[256,128]{1,0:T(8,128)(2,1)S(1)} custom-call(s32[1]{0:T(128)} %bitcast.1.me_ref, bf16[128,256]{1,0:T(8,128)(2,1)S(1)} %stack_l.1.own_ref, bf16[128,256]{1,0:T(8,128)(2,1)S(1)} %collective-permute-done.8.other_ref, bf16[256,128]{1,0:T(8,128)(2,1)S(1)} %add.3.top_ref, bf16[256,128]{1,0:T(8,128)(2,1)S(1)} %collective-permute-done.9.more_ref), custom_call_target="tpu_custom_call" | custom-call | tf_op jit(solution)/shard_map/solve/pallas_call | solution.py:278
  44.7 1.9 %collective-permute-start.11 = (bf16[256,128]{1,0:T(8,128)(2,1)S(1)}, bf16[256,128]{1,0:T(8,128)(2,1)S(1)}, u32[]{:S(2)}, u32[]{:S(2)}) collective-permute-start(bf16[256,128]{1,0:T(8,128)(2,1)S(1)} %solve.1.a_ref), channel_id=1, source_target_pairs={{0,64},{1,65},{2,66},{3,67},{4,68},{5,69},{6,70},{7,71},{8,72},{9,... | collective-permute-start | bytes 196616 | tf_op jit(solution)/shard_map/ppermute | solution.py:404
  46.6 1.3 %collective-permute-done.11.b_ref = bf16[256,128]{1,0:T(8,128)(2,1)S(1)} collective-permute-done((bf16[256,128]{1,0:T(8,128)(2,1)S(1)}, bf16[256,128]{1,0:T(8,128)(2,1)S(1)}, u32[]{:S(2)}, u32[]{:S(2)}) %collective-permute-start.11) | collective-permute-done | bytes 65568 | tf_op jit(solution)/shard_map/ppermute | solution.py:404
  47.9 0.5 collective-permute-done.12.refs_0_.refs_2_
  48.3 0.0 collective-permute-done.14.refs_6_
  48.3 0.1 stack_b.1
  48.4 2.0 %collective-permute-start.19 = (bf16[32,12288]{1,0:T(8,128)(2,1)S(1)}, bf16[32,12288]{1,0:T(8,128)(2,1)S(1)}, u32[]{:S(2)}, u32[]{:S(2)}) collective-permute-start(bf16[32,12288]{1,0:T(8,128)(2,1)S(1)} %stack_b.1), channel_id=1, source_target_pairs={{0,6},{1,25},{2,0},{3,27},{4,2},{5,29},{6,4},{7,31},{8,14},{9,1},{... | collective-permute-start | bytes 2359304 | tf_op jit(solution)/shard_map/ppermute | solution.py:37
  50.4 1.5 %stack_a.1 = bf16[32,12288]{1,0:T(8,128)(2,1)S(1)} custom-call(bf16[32,24576]{1,0:T(8,128)(2,1)} %collective-permute-done.12.refs_0_.refs_2_), custom_call_target="tpu_custom_call" | custom-call | flops 1100000000 | bytes 3500000 | tf_op jit(solution)/shard_map/stack_a/pallas_call | solution.py:60
  51.9 0.1 collective-permute-start.18
  52.0 3.1 %collective-permute-start.16 = (bf16[256,128]{1,0:T(8,128)(2,1)S(1)}, bf16[256,128]{1,0:T(8,128)(2,1)S(1)}, u32[]{:S(2)}, u32[]{:S(2)}) collective-permute-start(bf16[256,128]{1,0:T(8,128)(2,1)S(1)} %choose.5.a_ref), channel_id=1, source_target_pairs={{0,32},{64,96},{1,33},{65,97},{2,34},{66,98},{3,35},{67,99},{4,36}... | collective-permute-start | bytes 196616 | tf_op jit(solution)/shard_map/ppermute | solution.py:404
  55.1 2.8 %collective-permute-start.20 = (bf16[32,24576]{1,0:T(8,128)(2,1)}, bf16[32,24576]{1,0:T(8,128)(2,1)S(1)}, u32[]{:S(2)}, u32[]{:S(2)}) collective-permute-start(bf16[32,24576]{1,0:T(8,128)(2,1)} %collective-permute-done.12.refs_0_.refs_2_), channel_id=1, source_target_pairs={{0,1},{1,0},{2,3},{3,2},{4,5},{5,4},{6,7},{7,6},{8,9},{9,8},{10,11... | collective-permute-start | bytes 4718600 | tf_op jit(solution)/shard_map/ppermute | solution.py:37
  57.9 0.3 collective-permute-start.21
  58.1 0.0 collective-permute-done.16.b_ref
  58.2 0.0 copy-start.1
  58.2 5.0 %collective-permute-start.17 = (bf16[512,128]{1,0:T(8,128)(2,1)S(1)}, bf16[512,128]{1,0:T(8,128)(2,1)S(1)}, u32[]{:S(2)}, u32[]{:S(2)}) collective-permute-start(bf16[512,128]{1,0:T(8,128)(2,1)S(1)} %join.1.ud_ref), channel_id=1, source_target_pairs={{0,128},{32,160},{64,192},{96,224},{1,129},{33,161},{65,193},{97,2... | collective-permute-start | bytes 393224 | tf_op jit(solution)/shard_map/ppermute | solution.py:404
  63.2 0.0 collective-permute-done.19.refs_1_.refs_5_
  63.2 0.6 collective-permute-start.23
  63.8 0.5 collective-permute-done.18.refs_0_.refs_4_
  64.3 3.3 %collective-permute-start.22 = (bf16[32,12288]{1,0:T(8,128)(2,1)S(1)}, bf16[32,12288]{1,0:T(8,128)(2,1)S(1)}, u32[]{:S(2)}, u32[]{:S(2)}) collective-permute-start(bf16[32,12288]{1,0:T(8,128)(2,1)S(1)} %collective-permute-done.18.refs_0_.refs_4_), channel_id=1, source_target_pairs={{0,1},{1,0},{2,3},{3,2},{4,5},{5,4},{6,7},{7,6},{8,9},{9,8},{10,11... | collective-permute-start | bytes 2359304 | tf_op jit(solution)/shard_map/ppermute | solution.py:37
  67.6 1.9 %collective-permute-done.22.refs_9_ = bf16[32,12288]{1,0:T(8,128)(2,1)S(1)} collective-permute-done((bf16[32,12288]{1,0:T(8,128)(2,1)S(1)}, bf16[32,12288]{1,0:T(8,128)(2,1)S(1)}, u32[]{:S(2)}, u32[]{:S(2)}) %collective-permute-start.22) | collective-permute-done | bytes 786464 | tf_op jit(solution)/shard_map/ppermute | solution.py:37
  69.5 7.7 %update.1 = (bf16[24576,128]{1,0:T(8,128)(2,1)}, bf16[24576,128]{1,0:T(8,128)(2,1)S(1)}) custom-call(s32[1]{0:T(128)} %get-tuple-element.39.cnt_ref, s32[256]{0:T(256)S(1)} %get-tuple-element.40.lst_ref, s32[256]{0:T(256)S(1)} %copy-done.1, s32[1]{0:T(128)} %bitcast.first_ref, s32[1]{0:T(128)} %bitcast.1.me_ref, ...), custom_call_target="tpu_custom_call", output_to_operand_aliasing={{1}: (5, {})} | custom-call | tf_op jit(solution)/shard_map/update/pallas_call | solution.py:377
  (22 shorter events, 0.2 us)
Async XLA Ops:
  0.0 11.1 %collective-permute-start.2 = (bf16[8,24576]{1,0:T(8,128)(2,1)}, bf16[8,24576]{1,0:T(8,128)(2,1)S(1)}, u32[]{:S(2)}, u32[]{:S(2)}) collective-permute-start(bf16[8,24576]{1,0:T(8,128)(2,1)} %refs_0_.3), channel_id=1, source_target_pairs={{0,16},{1,5},{2,18},{3,7},{4,20},{5,1},{6,22},{7,3},{8,24},{9,13},... | collective-permute-start | bytes 1179656 | tf_op jit(solution)/shard_map/ppermute | solution.py:37
  3.7 10.3 %collective-permute-start.1 = (bf16[8,24576]{1,0:T(8,128)(2,1)}, bf16[8,24576]{1,0:T(8,128)(2,1)S(1)}, u32[]{:S(2)}, u32[]{:S(2)}) collective-permute-start(bf16[8,24576]{1,0:T(8,128)(2,1)} %refs_0_.3), channel_id=1, source_target_pairs={{0,24},{1,7},{2,26},{3,1},{4,28},{5,3},{6,30},{7,5},{8,0},{9,15},{... | collective-permute-start | bytes 1179656 | tf_op jit(solution)/shard_map/ppermute | solution.py:37
  4.5 9.5 %collective-permute-start = (bf16[8,24576]{1,0:T(8,128)(2,1)}, bf16[8,24576]{1,0:T(8,128)(2,1)S(1)}, u32[]{:S(2)}, u32[]{:S(2)}) collective-permute-start(bf16[8,24576]{1,0:T(8,128)(2,1)} %refs_0_.3), channel_id=1, source_target_pairs={{0,8},{1,3},{2,10},{3,5},{4,12},{5,7},{6,14},{7,1},{8,16},{9,11},{... | collective-permute-start | bytes 1179656 | tf_op jit(solution)/shard_map/ppermute | solution.py:37
  5.2 0.7 copy-start
  5.9 8.2 %copy-start.2 = (bf16[8,24576]{1,0:T(8,128)(2,1)S(1)}, bf16[8,24576]{1,0:T(8,128)(2,1)}, u32[]{:S(2)}) copy-start(bf16[8,24576]{1,0:T(8,128)(2,1)} %refs_0_.3) | copy-start | bytes 1179652
  9.8 9.6 %collective-permute-start.6 = (bf16[256,128]{1,0:T(8,128)(2,1)S(1)}, bf16[256,128]{1,0:T(8,128)(2,1)S(1)}, u32[]{:S(2)}, u32[]{:S(2)}) collective-permute-start(bf16[256,128]{1,0:T(8,128)(2,1)S(1)} %get-tuple-element.49.a_ref), channel_id=1, source_target_pairs={{128,0},{160,32},{192,64},{224,96},{129,1},{161,33},{193,65},{225,... | collective-permute-start | bytes 196616 | tf_op jit(solution)/shard_map/ppermute | solution.py:404
  14.1 5.3 %collective-permute-start.5 = (bf16[32,256]{1,0:T(8,128)(2,1)S(1)}, bf16[32,256]{1,0:T(8,128)(2,1)S(1)}, u32[]{:S(2)}, u32[]{:S(2)}) collective-permute-start(bf16[32,256]{1,0:T(8,128)(2,1)S(1)} %stack_d.1.refs_0_), channel_id=1, source_target_pairs={{0,6},{1,25},{2,0},{3,27},{4,2},{5,29},{6,4},{7,31},{8,14},{9,1},{... | collective-permute-start | bytes 49160 | tf_op jit(solution)/shard_map/ppermute | solution.py:37
  16.6 4.1 %collective-permute-start.4 = (bf16[32,256]{1,0:T(8,128)(2,1)S(1)}, bf16[32,256]{1,0:T(8,128)(2,1)S(1)}, u32[]{:S(2)}, u32[]{:S(2)}) collective-permute-start(bf16[32,256]{1,0:T(8,128)(2,1)S(1)} %stack_d.1.refs_0_), channel_id=1, source_target_pairs={{0,2},{1,9},{2,4},{3,11},{4,6},{5,13},{6,0},{7,15},{8,10},{9,17},{... | collective-permute-start | bytes 49160 | tf_op jit(solution)/shard_map/ppermute | solution.py:37
  16.6 4.4 %collective-permute-start.3 = (bf16[32,256]{1,0:T(8,128)(2,1)S(1)}, bf16[32,256]{1,0:T(8,128)(2,1)S(1)}, u32[]{:S(2)}, u32[]{:S(2)}) collective-permute-start(bf16[32,256]{1,0:T(8,128)(2,1)S(1)} %stack_d.1.refs_0_), channel_id=1, source_target_pairs={{0,4},{1,17},{2,6},{3,19},{4,0},{5,21},{6,2},{7,23},{8,12},{9,25},... | collective-permute-start | bytes 49160 | tf_op jit(solution)/shard_map/ppermute | solution.py:37
  21.1 6.4 %collective-permute-start.7 = (bf16[256,128]{1,0:T(8,128)(2,1)S(1)}, bf16[256,128]{1,0:T(8,128)(2,1)S(1)}, u32[]{:S(2)}, u32[]{:S(2)}) collective-permute-start(bf16[256,128]{1,0:T(8,128)(2,1)S(1)} %add.2.a_ref), channel_id=1, source_target_pairs={{64,0},{96,32},{65,1},{97,33},{66,2},{98,34},{67,3},{99,35},{68,4}... | collective-permute-start | bytes 196616 | tf_op jit(solution)/shard_map/ppermute | solution.py:404
  22.4 5.1 %collective-permute-start.8 = (bf16[128,256]{1,0:T(8,128)(2,1)S(1)}, bf16[128,256]{1,0:T(8,128)(2,1)S(1)}, u32[]{:S(2)}, u32[]{:S(2)}) collective-permute-start(bf16[128,256]{1,0:T(8,128)(2,1)S(1)} %stack_l.1.own_ref), channel_id=1, source_target_pairs={{0,1},{1,0},{2,3},{3,2},{4,5},{5,4},{6,7},{7,6},{8,9},{9,8},{10,11... | collective-permute-start | bytes 196616 | tf_op jit(solution)/shard_map/ppermute | solution.py:37
  25.7 22.1 %collective-permute-start.13 = (bf16[32,24576]{1,0:T(8,128)(2,1)S(1)}, bf16[32,24576]{1,0:T(8,128)(2,1)S(1)}, u32[]{:S(2)}, u32[]{:S(2)}) collective-permute-start(bf16[32,24576]{1,0:T(8,128)(2,1)S(1)} %stack_p.1.refs_1_), channel_id=1, source_target_pairs={{0,6},{1,25},{2,0},{3,27},{4,2},{5,29},{6,4},{7,31},{8,14},{9,1},{... | collective-permute-start | bytes 4718600 | tf_op jit(solution)/shard_map/ppermute | solution.py:37
  27.5 20.9 %collective-permute-start.12 = (bf16[32,24576]{1,0:T(8,128)(2,1)S(1)}, bf16[32,24576]{1,0:T(8,128)(2,1)}, u32[]{:S(2)}, u32[]{:S(2)}) collective-permute-start(bf16[32,24576]{1,0:T(8,128)(2,1)S(1)} %stack_p.1.refs_1_), channel_id=1, source_target_pairs={{0,2},{1,9},{2,4},{3,11},{4,6},{5,13},{6,0},{7,15},{8,10},{9,17},{... | collective-permute-start | bytes 4718600 | tf_op jit(solution)/shard_map/ppermute | solution.py:37
  27.5 20.8 %collective-permute-start.14 = (bf16[32,24576]{1,0:T(8,128)(2,1)S(1)}, bf16[32,24576]{1,0:T(8,128)(2,1)}, u32[]{:S(2)}, u32[]{:S(2)}) collective-permute-start(bf16[32,24576]{1,0:T(8,128)(2,1)S(1)} %stack_p.1.refs_1_), channel_id=1, source_target_pairs={{0,1},{1,0},{2,3},{3,2},{4,5},{5,4},{6,7},{7,6},{8,9},{9,8},{10,11... | collective-permute-start | bytes 4718600 | tf_op jit(solution)/shard_map/ppermute | solution.py:37
  31.5 5.8 %collective-permute-start.9 = (bf16[256,128]{1,0:T(8,128)(2,1)S(1)}, bf16[256,128]{1,0:T(8,128)(2,1)S(1)}, u32[]{:S(2)}, u32[]{:S(2)}) collective-permute-start(bf16[256,128]{1,0:T(8,128)(2,1)S(1)} %add.3.top_ref), channel_id=1, source_target_pairs={{32,0},{33,1},{34,2},{35,3},{36,4},{37,5},{38,6},{39,7},{40,8},{41... | collective-permute-start | bytes 196616 | tf_op jit(solution)/shard_map/ppermute | solution.py:404
  32.8 4.5 %collective-permute-start.10 = (bf16[256,128]{1,0:T(8,128)(2,1)S(1)}, bf16[256,128]{1,0:T(8,128)(2,1)S(1)}, u32[]{:S(2)}, u32[]{:S(2)}) collective-permute-start(bf16[256,128]{1,0:T(8,128)(2,1)S(1)} %get-tuple-element.60.a_ref), channel_id=1, source_target_pairs={{0,64},{1,65},{2,66},{3,67},{4,68},{5,69},{6,70},{7,71},{8,72},{9,... | collective-permute-start | bytes 196616 | tf_op jit(solution)/shard_map/ppermute | solution.py:404
  37.3 9.2 %collective-permute-start.15 = (bf16[256,128]{1,0:T(8,128)(2,1)S(1)}, bf16[256,128]{1,0:T(8,128)(2,1)S(1)}, u32[]{:S(2)}, u32[]{:S(2)}) collective-permute-start(bf16[256,128]{1,0:T(8,128)(2,1)S(1)} %choose.3.a_ref), channel_id=1, source_target_pairs={{0,32},{64,96},{1,33},{65,97},{2,34},{66,98},{3,35},{67,99},{4,36}... | collective-permute-start | bytes 196616 | tf_op jit(solution)/shard_map/ppermute | solution.py:404
  44.7 3.2 %collective-permute-start.11 = (bf16[256,128]{1,0:T(8,128)(2,1)S(1)}, bf16[256,128]{1,0:T(8,128)(2,1)S(1)}, u32[]{:S(2)}, u32[]{:S(2)}) collective-permute-start(bf16[256,128]{1,0:T(8,128)(2,1)S(1)} %solve.1.a_ref), channel_id=1, source_target_pairs={{0,64},{1,65},{2,66},{3,67},{4,68},{5,69},{6,70},{7,71},{8,72},{9,... | collective-permute-start | bytes 196616 | tf_op jit(solution)/shard_map/ppermute | solution.py:404
  48.4 14.8 %collective-permute-start.19 = (bf16[32,12288]{1,0:T(8,128)(2,1)S(1)}, bf16[32,12288]{1,0:T(8,128)(2,1)S(1)}, u32[]{:S(2)}, u32[]{:S(2)}) collective-permute-start(bf16[32,12288]{1,0:T(8,128)(2,1)S(1)} %stack_b.1), channel_id=1, source_target_pairs={{0,6},{1,25},{2,0},{3,27},{4,2},{5,29},{6,4},{7,31},{8,14},{9,1},{... | collective-permute-start | bytes 2359304 | tf_op jit(solution)/shard_map/ppermute | solution.py:37
  51.9 12.4 %collective-permute-start.18 = (bf16[32,12288]{1,0:T(8,128)(2,1)S(1)}, bf16[32,12288]{1,0:T(8,128)(2,1)S(1)}, u32[]{:S(2)}, u32[]{:S(2)}) collective-permute-start(bf16[32,12288]{1,0:T(8,128)(2,1)S(1)} %stack_a.1), channel_id=1, source_target_pairs={{0,2},{1,9},{2,4},{3,11},{4,6},{5,13},{6,0},{7,15},{8,10},{9,17},{... | collective-permute-start | bytes 2359304 | tf_op jit(solution)/shard_map/ppermute | solution.py:37
  52.0 6.1 %collective-permute-start.16 = (bf16[256,128]{1,0:T(8,128)(2,1)S(1)}, bf16[256,128]{1,0:T(8,128)(2,1)S(1)}, u32[]{:S(2)}, u32[]{:S(2)}) collective-permute-start(bf16[256,128]{1,0:T(8,128)(2,1)S(1)} %choose.5.a_ref), channel_id=1, source_target_pairs={{0,32},{64,96},{1,33},{65,97},{2,34},{66,98},{3,35},{67,99},{4,36}... | collective-permute-start | bytes 196616 | tf_op jit(solution)/shard_map/ppermute | solution.py:404
  55.1 14.4 %collective-permute-start.20 = (bf16[32,24576]{1,0:T(8,128)(2,1)}, bf16[32,24576]{1,0:T(8,128)(2,1)S(1)}, u32[]{:S(2)}, u32[]{:S(2)}) collective-permute-start(bf16[32,24576]{1,0:T(8,128)(2,1)} %collective-permute-done.12.refs_0_.refs_2_), channel_id=1, source_target_pairs={{0,1},{1,0},{2,3},{3,2},{4,5},{5,4},{6,7},{7,6},{8,9},{9,8},{10,11... | collective-permute-start | bytes 4718600 | tf_op jit(solution)/shard_map/ppermute | solution.py:37
  57.9 11.7 %collective-permute-start.21 = (bf16[32,24576]{1,0:T(8,128)(2,1)S(1)}, bf16[32,24576]{1,0:T(8,128)(2,1)S(1)}, u32[]{:S(2)}, u32[]{:S(2)}) collective-permute-start(bf16[32,24576]{1,0:T(8,128)(2,1)S(1)} %collective-permute-done.13.refs_0_.refs_3_), channel_id=1, source_target_pairs={{0,1},{1,0},{2,3},{3,2},{4,5},{5,4},{6,7},{7,6},{8,9},{9,8},{10,11... | collective-permute-start | bytes 4718600 | tf_op jit(solution)/shard_map/ppermute | solution.py:37
  58.2 11.4 %copy-start.1 = (s32[256]{0:T(256)S(1)}, s32[256]{0:T(256)}, u32[]{:S(2)}) copy-start(s32[256]{0:T(256)} %piv_ref.3) | copy-start | bytes 3076
  58.2 9.5 %collective-permute-start.17 = (bf16[512,128]{1,0:T(8,128)(2,1)S(1)}, bf16[512,128]{1,0:T(8,128)(2,1)S(1)}, u32[]{:S(2)}, u32[]{:S(2)}) collective-permute-start(bf16[512,128]{1,0:T(8,128)(2,1)S(1)} %join.1.ud_ref), channel_id=1, source_target_pairs={{0,128},{32,160},{64,192},{96,224},{1,129},{33,161},{65,193},{97,2... | collective-permute-start | bytes 393224 | tf_op jit(solution)/shard_map/ppermute | solution.py:404
  63.2 4.4 %collective-permute-start.23 = (bf16[32,12288]{1,0:T(8,128)(2,1)S(1)}, bf16[32,12288]{1,0:T(8,128)(2,1)S(1)}, u32[]{:S(2)}, u32[]{:S(2)}) collective-permute-start(bf16[32,12288]{1,0:T(8,128)(2,1)S(1)} %collective-permute-done.19.refs_1_.refs_5_), channel_id=1, source_target_pairs={{0,1},{1,0},{2,3},{3,2},{4,5},{5,4},{6,7},{7,6},{8,9},{9,8},{10,11... | collective-permute-start | bytes 2359304 | tf_op jit(solution)/shard_map/ppermute | solution.py:37
  64.3 5.2 %collective-permute-start.22 = (bf16[32,12288]{1,0:T(8,128)(2,1)S(1)}, bf16[32,12288]{1,0:T(8,128)(2,1)S(1)}, u32[]{:S(2)}, u32[]{:S(2)}) collective-permute-start(bf16[32,12288]{1,0:T(8,128)(2,1)S(1)} %collective-permute-done.18.refs_0_.refs_4_), channel_id=1, source_target_pairs={{0,1},{1,0},{2,3},{3,2},{4,5},{5,4},{6,7},{7,6},{8,9},{9,8},{10,11... | collective-permute-start | bytes 2359304 | tf_op jit(solution)/shard_map/ppermute | solution.py:37

commit v11 on v10

--- a/solution.py
+++ b/solution.py
@@ -418,9 +418,10 @@
     own = stack([diag, diag_p, diag_m, diag_q], 0, width, "stack_l")
     top = add(top, more)
     more = zsend(top, [(2, 0), (3, 1)])
+    top = add(top, more)
+    top, disp, own = barrier((top, disp, own))
     other = send(own, CORES)
-    top = add(top, more)
-    top, disp, other, source = barrier((top, disp, other, trailing))
+    other, source = barrier((other, trailing))
     copy = fetch(pltpu.with_memory_space_constraint(source, pltpu.HBM))
     more = zsend(top, [(1, 0)])
     lower = zsend(disp, [(0, 2)])
@@ -435,10 +436,10 @@
     fa, fb = stack([near], 0, half, "stack_a"), stack([far], half, half, "stack_b")
     qa, qb = send(fa, up), send(fb, down)
     u = choose(first, rows, (2,), u, ru)
-    u, near, far = barrier((u, near, far))
+    ud = join(first, rows, (1, 3), u, zsend(u, [(0, 1), (2, 3)]), disp)
+    ud, near, far = barrier((ud, near, far))
+    rest = zsend(ud, [(i, i + 4) for i in range(4)])
     other_near, other_far = send(near, CORES), send(far, CORES)
-    ud = join(first, rows, (1, 3), u, zsend(u, [(0, 1), (2, 3)]), disp)
-    rest = zsend(ud, [(i, i + 4) for i in range(4)])
     ahead = stack([qa, qb], 0, 128, "stack_q", 60)
     own = [block, near, far, qa, qb]
     parts = own + [swap, other_near, other_far, send(qa, CORES), send(qb, CORES)]

time: 77.7 us -> 81.8 us (1.053)
  waiting for transfers between devices: 9.46 us -> 18 us
  starting transfers between devices: 46.1 us -> 41.8 us
    ppermute x8, waiting for transfers between devices: 2.01 us -> 8.22 us  [zsend(): return lax.ppermute(x, 'prow', pairs)]
    ppermute x8, starting transfers between devices: 18.5 us -> 12.5 us  [zsend(): return lax.ppermute(x, 'prow', pairs)]
    ppermute x16, waiting for transfers between devices: 7.46 us -> 9.79 us  [send(): return lax.ppermute(block, 'pcol', pairs)]
    ppermute x16, starting transfers between devices: 27.6 us -> 29.2 us  [send(): return lax.ppermute(block, 'pcol', pairs)]
  transfers between devices with their start and end apart: 24 -> 24, of which waited for: 8 -> 10; matrix products, arithmetic and copies ran while one was open for 0% -> 0% of each run, Pallas kernels for 17% -> 16%
where the time goes in v11:
time: 81.8 us; the launch traced here: 81.4 us
  starting transfers between devices  41.8 us (51%)
  Pallas kernels  20.5 us (25%)
  waiting for transfers between devices  18 us (22%)
    ppermute x16, starting transfers between devices, send(): return lax.ppermute(block, 'pcol', pairs)  29.2 us
    ppermute x8, starting transfers between devices, zsend(): return lax.ppermute(x, 'prow', pairs)  12.5 us
    ppermute x16, waiting for transfers between devices, send(): return lax.ppermute(block, 'pcol', pairs)  9.79 us
    ppermute x8, waiting for transfers between devices, zsend(): return lax.ppermute(x, 'prow', pairs)  8.22 us
    pallas_call x1, Pallas kernels, update(): pl.pallas_call(update_kernel, in_specs=[SMEM] * 5 + [VMEM] * 14, out_spec...  7.65 us
    pallas_call x1, Pallas kernels, solve(): pl.pallas_call(solve_kernel, in_specs=[SMEM] + [VMEM] * 4, out_specs=VMEM...  4.26 us
    pallas_call x1, Pallas kernels, pick(): pl.pallas_call(functools.partial(pick_kernel, blk), in_specs=[SMEM, SMEM,...  3.72 us
    pallas_call x1, Pallas kernels, fetch(): pl.pallas_call(fetch_kernel, in_specs=[pl.BlockSpec(memory_space=pltpu.HB...  2.87 us
  transfers between devices with their start and end apart: 24, of which 10 were waited for; matrix products, arithmetic and copies ran while one was open for 0% of the time, Pallas kernels for 16%

profile of v11, /device:TPU:1, one launch (start us, length us, event | category | flops | bytes accessed | tf_op | source)
XLA Modules:
  0.0 81.4 jit_solution(3089553205288472867)
XLA Ops:
  0.0 3.7 %collective-permute-start.2 = (bf16[8,24576]{1,0:T(8,128)(2,1)}, bf16[8,24576]{1,0:T(8,128)(2,1)S(1)}, u32[]{:S(2)}, u32[]{:S(2)}) collective-permute-start(bf16[8,24576]{1,0:T(8,128)(2,1)} %refs_0_.3), channel_id=1, source_target_pairs={{0,16},{1,5},{2,18},{3,7},{4,20},{5,1},{6,22},{7,3},{8,24},{9,13},... | collective-permute-start | bytes 1179656 | tf_op jit(solution)/shard_map/ppermute | solution.py:37
  3.7 0.8 collective-permute-start.1
  4.5 0.7 collective-permute-start
  5.2 0.7 copy-done
  5.9 3.7 %pick.1 = (bf16[256,128]{1,0:T(8,128)(2,1)S(1)}, bf16[256,128]{1,0:T(8,128)(2,1)S(1)}, s32[1]{0:T(128)}, s32[256]{0:T(256)S(1)}) custom-call(s32[256]{0:T(256)S(1)} %copy-done, s32[1]{0:T(128)} %bitcast.first_ref, bf16[24576,128]{1,0:T(8,128)(2,1)} %src_ref), custom_call_target="tpu_custom_call" | custom-call | flops 13200000000 | bytes 42000000 | tf_op jit(solution)/shard_map/pick/pallas_call | solution.py:184
  9.6 1.3 %collective-permute-start.6 = (bf16[256,128]{1,0:T(8,128)(2,1)S(1)}, bf16[256,128]{1,0:T(8,128)(2,1)S(1)}, u32[]{:S(2)}, u32[]{:S(2)}) collective-permute-start(bf16[256,128]{1,0:T(8,128)(2,1)S(1)} %get-tuple-element.47.a_ref), channel_id=1, source_target_pairs={{128,0},{160,32},{192,64},{224,96},{129,1},{161,33},{193,65},{225,... | collective-permute-start | bytes 196616 | tf_op jit(solution)/shard_map/ppermute | solution.py:404
  10.9 0.0 collective-permute-done.2.refs_3_
  10.9 3.1 %collective-permute-done.1.refs_2_ = bf16[8,24576]{1,0:T(8,128)(2,1)S(1)} collective-permute-done((bf16[8,24576]{1,0:T(8,128)(2,1)}, bf16[8,24576]{1,0:T(8,128)(2,1)S(1)}, u32[]{:S(2)}, u32[]{:S(2)}) %collective-permute-start.1) | collective-permute-done | bytes 393248 | tf_op jit(solution)/shard_map/ppermute | solution.py:37
  14.1 2.6 %collective-permute-start.5 = (bf16[32,256]{1,0:T(8,128)(2,1)S(1)}, bf16[32,256]{1,0:T(8,128)(2,1)S(1)}, u32[]{:S(2)}, u32[]{:S(2)}) collective-permute-start(bf16[32,256]{1,0:T(8,128)(2,1)S(1)} %stack_d.1.refs_0_), channel_id=1, source_target_pairs={{0,6},{1,25},{2,0},{3,27},{4,2},{5,29},{6,4},{7,31},{8,14},{9,1},{... | collective-permute-start | bytes 49160 | tf_op jit(solution)/shard_map/ppermute | solution.py:37
  16.6 0.0 collective-permute-start.4
  16.6 1.7 %collective-permute-start.3 = (bf16[32,256]{1,0:T(8,128)(2,1)S(1)}, bf16[32,256]{1,0:T(8,128)(2,1)S(1)}, u32[]{:S(2)}, u32[]{:S(2)}) collective-permute-start(bf16[32,256]{1,0:T(8,128)(2,1)S(1)} %stack_d.1.refs_0_), channel_id=1, source_target_pairs={{0,4},{1,17},{2,6},{3,19},{4,0},{5,21},{6,2},{7,23},{8,12},{9,25},... | collective-permute-start | bytes 49160 | tf_op jit(solution)/shard_map/ppermute | solution.py:37
  18.4 0.3 stack_p.1.refs_1_
  18.7 1.0 %collective-permute-done.6.b_ref = bf16[256,128]{1,0:T(8,128)(2,1)S(1)} collective-permute-done((bf16[256,128]{1,0:T(8,128)(2,1)S(1)}, bf16[256,128]{1,0:T(8,128)(2,1)S(1)}, u32[]{:S(2)}, u32[]{:S(2)}) %collective-permute-start.6) | collective-permute-done | bytes 65568 | tf_op jit(solution)/shard_map/ppermute | solution.py:404
  19.7 1.0 %collective-permute-done.4.refs_1_ = bf16[32,256]{1,0:T(8,128)(2,1)S(1)} collective-permute-done((bf16[32,256]{1,0:T(8,128)(2,1)S(1)}, bf16[32,256]{1,0:T(8,128)(2,1)S(1)}, u32[]{:S(2)}, u32[]{:S(2)}) %collective-permute-start.4) | collective-permute-done | bytes 16416 | tf_op jit(solution)/shard_map/ppermute | solution.py:37
  20.7 0.3 collective-permute-done.3.refs_3_
  21.0 2.5 %collective-permute-start.13 = (bf16[32,24576]{1,0:T(8,128)(2,1)S(1)}, bf16[32,24576]{1,0:T(8,128)(2,1)S(1)}, u32[]{:S(2)}, u32[]{:S(2)}) collective-permute-start(bf16[32,24576]{1,0:T(8,128)(2,1)S(1)} %stack_p.1.refs_1_), channel_id=1, source_target_pairs={{0,6},{1,25},{2,0},{3,27},{4,2},{5,29},{6,4},{7,31},{8,14},{9,1},{... | collective-permute-start | bytes 4718600 | tf_op jit(solution)/shard_map/ppermute | solution.py:37
  23.5 0.0 collective-permute-start.12
  23.5 1.3 %collective-permute-start.7 = (bf16[256,128]{1,0:T(8,128)(2,1)S(1)}, bf16[256,128]{1,0:T(8,128)(2,1)S(1)}, u32[]{:S(2)}, u32[]{:S(2)}) collective-permute-start(bf16[256,128]{1,0:T(8,128)(2,1)S(1)} %add.2.a_ref), channel_id=1, source_target_pairs={{64,0},{96,32},{65,1},{97,33},{66,2},{98,34},{67,3},{99,35},{68,4}... | collective-permute-start | bytes 196616 | tf_op jit(solution)/shard_map/ppermute | solution.py:404
  24.8 4.6 %collective-permute-done.7.b_ref = bf16[256,128]{1,0:T(8,128)(2,1)S(1)} collective-permute-done((bf16[256,128]{1,0:T(8,128)(2,1)S(1)}, bf16[256,128]{1,0:T(8,128)(2,1)S(1)}, u32[]{:S(2)}, u32[]{:S(2)}) %collective-permute-start.7) | collective-permute-done | bytes 65568 | tf_op jit(solution)/shard_map/ppermute | solution.py:404
  29.5 4.7 %collective-permute-start.14 = (bf16[32,24576]{1,0:T(8,128)(2,1)S(1)}, bf16[32,24576]{1,0:T(8,128)(2,1)}, u32[]{:S(2)}, u32[]{:S(2)}) collective-permute-start(bf16[32,24576]{1,0:T(8,128)(2,1)S(1)} %stack_p.1.refs_1_), channel_id=1, source_target_pairs={{0,1},{1,0},{2,3},{3,2},{4,5},{5,4},{6,7},{7,6},{8,9},{9,8},{10,11... | collective-permute-start | bytes 4718600 | tf_op jit(solution)/shard_map/ppermute | solution.py:37
  34.1 0.1 collective-permute-start.8
  34.2 1.3 %collective-permute-start.9 = (bf16[256,128]{1,0:T(8,128)(2,1)S(1)}, bf16[256,128]{1,0:T(8,128)(2,1)S(1)}, u32[]{:S(2)}, u32[]{:S(2)}) collective-permute-start(bf16[256,128]{1,0:T(8,128)(2,1)S(1)} %add.3.top_ref), channel_id=1, source_target_pairs={{32,0},{33,1},{34,2},{35,3},{36,4},{37,5},{38,6},{39,7},{40,8},{41... | collective-permute-start | bytes 196616 | tf_op jit(solution)/shard_map/ppermute | solution.py:404
  35.5 1.6 %collective-permute-done.8.other_ref = bf16[128,256]{1,0:T(8,128)(2,1)S(1)} collective-permute-done((bf16[128,256]{1,0:T(8,128)(2,1)S(1)}, bf16[128,256]{1,0:T(8,128)(2,1)S(1)}, u32[]{:S(2)}, u32[]{:S(2)}) %collective-permute-start.8) | collective-permute-done | bytes 65568 | tf_op jit(solution)/shard_map/ppermute | solution.py:37
  37.1 1.3 %collective-permute-start.10 = (bf16[256,128]{1,0:T(8,128)(2,1)S(1)}, bf16[256,128]{1,0:T(8,128)(2,1)S(1)}, u32[]{:S(2)}, u32[]{:S(2)}) collective-permute-start(bf16[256,128]{1,0:T(8,128)(2,1)S(1)} %get-tuple-element.62.a_ref), channel_id=1, source_target_pairs={{0,64},{1,65},{2,66},{3,67},{4,68},{5,69},{6,70},{7,71},{8,72},{9,... | collective-permute-start | bytes 196616 | tf_op jit(solution)/shard_map/ppermute | solution.py:404
  38.4 2.9 %fetch.1.tr_ref = bf16[24576,128]{1,0:T(8,128)(2,1)S(1)} custom-call(bf16[24576,128]{1,0:T(8,128)(2,1)} %src_ref), custom_call_target="tpu_custom_call" | custom-call | tf_op jit(solution)/shard_map/fetch/pallas_call | solution.py:303
  41.3 2.9 %collective-permute-start.15 = (bf16[256,128]{1,0:T(8,128)(2,1)S(1)}, bf16[256,128]{1,0:T(8,128)(2,1)S(1)}, u32[]{:S(2)}, u32[]{:S(2)}) collective-permute-start(bf16[256,128]{1,0:T(8,128)(2,1)S(1)} %choose.3.a_ref), channel_id=1, source_target_pairs={{0,32},{64,96},{1,33},{65,97},{2,34},{66,98},{3,35},{67,99},{4,36}... | collective-permute-start | bytes 196616 | tf_op jit(solution)/shard_map/ppermute | solution.py:404
  44.3 4.3 %solve.1.a_ref = bf16[256,128]{1,0:T(8,128)(2,1)S(1)} custom-call(s32[1]{0:T(128)} %bitcast.1.me_ref, bf16[128,256]{1,0:T(8,128)(2,1)S(1)} %stack_l.1.own_ref, bf16[128,256]{1,0:T(8,128)(2,1)S(1)} %collective-permute-done.8.other_ref, bf16[256,128]{1,0:T(8,128)(2,1)S(1)} %add.3.top_ref, bf16[256,128]{1,0:T(8,128)(2,1)S(1)} %collective-permute-done.9.more_ref), custom_call_target="tpu_custom_call" | custom-call | tf_op jit(solution)/shard_map/solve/pallas_call | solution.py:278
  48.5 1.9 %collective-permute-start.11 = (bf16[256,128]{1,0:T(8,128)(2,1)S(1)}, bf16[256,128]{1,0:T(8,128)(2,1)S(1)}, u32[]{:S(2)}, u32[]{:S(2)}) collective-permute-start(bf16[256,128]{1,0:T(8,128)(2,1)S(1)} %solve.1.a_ref), channel_id=1, source_target_pairs={{0,64},{1,65},{2,66},{3,67},{4,68},{5,69},{6,70},{7,71},{8,72},{9,... | collective-permute-start | bytes 196616 | tf_op jit(solution)/shard_map/ppermute | solution.py:404
  50.4 0.0 collective-permute-done.15.b_ref
  50.5 1.3 %collective-permute-done.11.b_ref = bf16[256,128]{1,0:T(8,128)(2,1)S(1)} collective-permute-done((bf16[256,128]{1,0:T(8,128)(2,1)S(1)}, bf16[256,128]{1,0:T(8,128)(2,1)S(1)}, u32[]{:S(2)}, u32[]{:S(2)}) %collective-permute-start.11) | collective-permute-done | bytes 65568 | tf_op jit(solution)/shard_map/ppermute | solution.py:404
  51.7 0.0 collective-permute-done.13.refs_0_.refs_3_
  51.7 0.0 collective-permute-done.12.refs_0_.refs_2_
  51.7 0.1 stack_b.1
  51.8 2.4 %collective-permute-start.19 = (bf16[32,12288]{1,0:T(8,128)(2,1)S(1)}, bf16[32,12288]{1,0:T(8,128)(2,1)S(1)}, u32[]{:S(2)}, u32[]{:S(2)}) collective-permute-start(bf16[32,12288]{1,0:T(8,128)(2,1)S(1)} %stack_b.1), channel_id=1, source_target_pairs={{0,6},{1,25},{2,0},{3,27},{4,2},{5,29},{6,4},{7,31},{8,14},{9,1},{... | collective-permute-start | bytes 2359304 | tf_op jit(solution)/shard_map/ppermute | solution.py:37
  54.3 1.5 %stack_a.1 = bf16[32,12288]{1,0:T(8,128)(2,1)S(1)} custom-call(bf16[32,24576]{1,0:T(8,128)(2,1)} %collective-permute-done.12.refs_0_.refs_2_), custom_call_target="tpu_custom_call" | custom-call | flops 1100000000 | bytes 3500000 | tf_op jit(solution)/shard_map/stack_a/pallas_call | solution.py:60
  55.8 0.1 collective-permute-start.18
  55.9 1.3 %collective-permute-start.16 = (bf16[256,128]{1,0:T(8,128)(2,1)S(1)}, bf16[256,128]{1,0:T(8,128)(2,1)S(1)}, u32[]{:S(2)}, u32[]{:S(2)}) collective-permute-start(bf16[256,128]{1,0:T(8,128)(2,1)S(1)} %choose.5.a_ref), channel_id=1, source_target_pairs={{0,32},{64,96},{1,33},{65,97},{2,34},{66,98},{3,35},{67,99},{4,36}... | collective-permute-start | bytes 196616 | tf_op jit(solution)/shard_map/ppermute | solution.py:404
  57.2 1.3 %collective-permute-done.16.b_ref = bf16[256,128]{1,0:T(8,128)(2,1)S(1)} collective-permute-done((bf16[256,128]{1,0:T(8,128)(2,1)S(1)}, bf16[256,128]{1,0:T(8,128)(2,1)S(1)}, u32[]{:S(2)}, u32[]{:S(2)}) %collective-permute-start.16) | collective-permute-done | bytes 65568 | tf_op jit(solution)/shard_map/ppermute | solution.py:404
  58.5 0.0 copy-start.1
  58.5 1.3 %collective-permute-start.17 = (bf16[512,128]{1,0:T(8,128)(2,1)S(1)}, bf16[512,128]{1,0:T(8,128)(2,1)S(1)}, u32[]{:S(2)}, u32[]{:S(2)}) collective-permute-start(bf16[512,128]{1,0:T(8,128)(2,1)S(1)} %join.1.ud_ref), channel_id=1, source_target_pairs={{0,128},{32,160},{64,192},{96,224},{1,129},{33,161},{65,193},{97,2... | collective-permute-start | bytes 393224 | tf_op jit(solution)/shard_map/ppermute | solution.py:404
  59.8 3.8 %collective-permute-start.20 = (bf16[32,24576]{1,0:T(8,128)(2,1)}, bf16[32,24576]{1,0:T(8,128)(2,1)S(1)}, u32[]{:S(2)}, u32[]{:S(2)}) collective-permute-start(bf16[32,24576]{1,0:T(8,128)(2,1)} %collective-permute-done.12.refs_0_.refs_2_), channel_id=1, source_target_pairs={{0,1},{1,0},{2,3},{3,2},{4,5},{5,4},{6,7},{7,6},{8,9},{9,8},{10,11... | collective-permute-start | bytes 4718600 | tf_op jit(solution)/shard_map/ppermute | solution.py:37
  63.7 0.3 collective-permute-start.21
  63.9 0.0 collective-permute-done.19.refs_1_.refs_5_
  63.9 2.4 %collective-permute-start.23 = (bf16[32,12288]{1,0:T(8,128)(2,1)S(1)}, bf16[32,12288]{1,0:T(8,128)(2,1)S(1)}, u32[]{:S(2)}, u32[]{:S(2)}) collective-permute-start(bf16[32,12288]{1,0:T(8,128)(2,1)S(1)} %collective-permute-done.19.refs_1_.refs_5_), channel_id=1, source_target_pairs={{0,1},{1,0},{2,3},{3,2},{4,5},{5,4},{6,7},{7,6},{8,9},{9,8},{10,11... | collective-permute-start | bytes 2359304 | tf_op jit(solution)/shard_map/ppermute | solution.py:37
  66.4 1.8 %collective-permute-done.18.refs_0_.refs_4_ = bf16[32,12288]{1,0:T(8,128)(2,1)S(1)} collective-permute-done((bf16[32,12288]{1,0:T(8,128)(2,1)S(1)}, bf16[32,12288]{1,0:T(8,128)(2,1)S(1)}, u32[]{:S(2)}, u32[]{:S(2)}) %collective-permute-start.18) | collective-permute-done | bytes 786464 | tf_op jit(solution)/shard_map/ppermute | solution.py:37
  68.2 3.4 %collective-permute-start.22 = (bf16[32,12288]{1,0:T(8,128)(2,1)S(1)}, bf16[32,12288]{1,0:T(8,128)(2,1)S(1)}, u32[]{:S(2)}, u32[]{:S(2)}) collective-permute-start(bf16[32,12288]{1,0:T(8,128)(2,1)S(1)} %collective-permute-done.18.refs_0_.refs_4_), channel_id=1, source_target_pairs={{0,1},{1,0},{2,3},{3,2},{4,5},{5,4},{6,7},{7,6},{8,9},{9,8},{10,11... | collective-permute-start | bytes 2359304 | tf_op jit(solution)/shard_map/ppermute | solution.py:37
  71.7 1.9 %collective-permute-done.22.refs_9_ = bf16[32,12288]{1,0:T(8,128)(2,1)S(1)} collective-permute-done((bf16[32,12288]{1,0:T(8,128)(2,1)S(1)}, bf16[32,12288]{1,0:T(8,128)(2,1)S(1)}, u32[]{:S(2)}, u32[]{:S(2)}) %collective-permute-start.22) | collective-permute-done | bytes 786464 | tf_op jit(solution)/shard_map/ppermute | solution.py:37
  73.6 7.6 %update.1 = (bf16[24576,128]{1,0:T(8,128)(2,1)}, bf16[24576,128]{1,0:T(8,128)(2,1)S(1)}) custom-call(s32[1]{0:T(128)} %get-tuple-element.40.cnt_ref, s32[256]{0:T(256)S(1)} %get-tuple-element.41.lst_ref, s32[256]{0:T(256)S(1)} %copy-done.1, s32[1]{0:T(128)} %bitcast.first_ref, s32[1]{0:T(128)} %bitcast.1.me_ref, ...), custom_call_target="tpu_custom_call", output_to_operand_aliasing={{1}: (5, {})} | custom-call | tf_op jit(solution)/shard_map/update/pallas_call | solution.py:377
  (22 shorter events, 0.2 us)
Async XLA Ops:
  0.0 10.9 %collective-permute-start.2 = (bf16[8,24576]{1,0:T(8,128)(2,1)}, bf16[8,24576]{1,0:T(8,128)(2,1)S(1)}, u32[]{:S(2)}, u32[]{:S(2)}) collective-permute-start(bf16[8,24576]{1,0:T(8,128)(2,1)} %refs_0_.3), channel_id=1, source_target_pairs={{0,16},{1,5},{2,18},{3,7},{4,20},{5,1},{6,22},{7,3},{8,24},{9,13},... | collective-permute-start | bytes 1179656 | tf_op jit(solution)/shard_map/ppermute | solution.py:37
  3.7 10.3 %collective-permute-start.1 = (bf16[8,24576]{1,0:T(8,128)(2,1)}, bf16[8,24576]{1,0:T(8,128)(2,1)S(1)}, u32[]{:S(2)}, u32[]{:S(2)}) collective-permute-start(bf16[8,24576]{1,0:T(8,128)(2,1)} %refs_0_.3), channel_id=1, source_target_pairs={{0,24},{1,7},{2,26},{3,1},{4,28},{5,3},{6,30},{7,5},{8,0},{9,15},{... | collective-permute-start | bytes 1179656 | tf_op jit(solution)/shard_map/ppermute | solution.py:37
  4.5 9.5 %collective-permute-start = (bf16[8,24576]{1,0:T(8,128)(2,1)}, bf16[8,24576]{1,0:T(8,128)(2,1)S(1)}, u32[]{:S(2)}, u32[]{:S(2)}) collective-permute-start(bf16[8,24576]{1,0:T(8,128)(2,1)} %refs_0_.3), channel_id=1, source_target_pairs={{0,8},{1,3},{2,10},{3,5},{4,12},{5,7},{6,14},{7,1},{8,16},{9,11},{... | collective-permute-start | bytes 1179656 | tf_op jit(solution)/shard_map/ppermute | solution.py:37
  5.2 0.7 copy-start
  5.9 8.2 %copy-start.2 = (bf16[8,24576]{1,0:T(8,128)(2,1)S(1)}, bf16[8,24576]{1,0:T(8,128)(2,1)}, u32[]{:S(2)}) copy-start(bf16[8,24576]{1,0:T(8,128)(2,1)} %refs_0_.3) | copy-start | bytes 1179652
  9.6 10.1 %collective-permute-start.6 = (bf16[256,128]{1,0:T(8,128)(2,1)S(1)}, bf16[256,128]{1,0:T(8,128)(2,1)S(1)}, u32[]{:S(2)}, u32[]{:S(2)}) collective-permute-start(bf16[256,128]{1,0:T(8,128)(2,1)S(1)} %get-tuple-element.47.a_ref), channel_id=1, source_target_pairs={{128,0},{160,32},{192,64},{224,96},{129,1},{161,33},{193,65},{225,... | collective-permute-start | bytes 196616 | tf_op jit(solution)/shard_map/ppermute | solution.py:404
  14.1 5.6 %collective-permute-start.5 = (bf16[32,256]{1,0:T(8,128)(2,1)S(1)}, bf16[32,256]{1,0:T(8,128)(2,1)S(1)}, u32[]{:S(2)}, u32[]{:S(2)}) collective-permute-start(bf16[32,256]{1,0:T(8,128)(2,1)S(1)} %stack_d.1.refs_0_), channel_id=1, source_target_pairs={{0,6},{1,25},{2,0},{3,27},{4,2},{5,29},{6,4},{7,31},{8,14},{9,1},{... | collective-permute-start | bytes 49160 | tf_op jit(solution)/shard_map/ppermute | solution.py:37
  16.6 4.1 %collective-permute-start.4 = (bf16[32,256]{1,0:T(8,128)(2,1)S(1)}, bf16[32,256]{1,0:T(8,128)(2,1)S(1)}, u32[]{:S(2)}, u32[]{:S(2)}) collective-permute-start(bf16[32,256]{1,0:T(8,128)(2,1)S(1)} %stack_d.1.refs_0_), channel_id=1, source_target_pairs={{0,2},{1,9},{2,4},{3,11},{4,6},{5,13},{6,0},{7,15},{8,10},{9,17},{... | collective-permute-start | bytes 49160 | tf_op jit(solution)/shard_map/ppermute | solution.py:37
  16.6 4.4 %collective-permute-start.3 = (bf16[32,256]{1,0:T(8,128)(2,1)S(1)}, bf16[32,256]{1,0:T(8,128)(2,1)S(1)}, u32[]{:S(2)}, u32[]{:S(2)}) collective-permute-start(bf16[32,256]{1,0:T(8,128)(2,1)S(1)} %stack_d.1.refs_0_), channel_id=1, source_target_pairs={{0,4},{1,17},{2,6},{3,19},{4,0},{5,21},{6,2},{7,23},{8,12},{9,25},... | collective-permute-start | bytes 49160 | tf_op jit(solution)/shard_map/ppermute | solution.py:37
  21.0 30.7 %collective-permute-start.13 = (bf16[32,24576]{1,0:T(8,128)(2,1)S(1)}, bf16[32,24576]{1,0:T(8,128)(2,1)S(1)}, u32[]{:S(2)}, u32[]{:S(2)}) collective-permute-start(bf16[32,24576]{1,0:T(8,128)(2,1)S(1)} %stack_p.1.refs_1_), channel_id=1, source_target_pairs={{0,6},{1,25},{2,0},{3,27},{4,2},{5,29},{6,4},{7,31},{8,14},{9,1},{... | collective-permute-start | bytes 4718600 | tf_op jit(solution)/shard_map/ppermute | solution.py:37
  23.5 28.2 %collective-permute-start.12 = (bf16[32,24576]{1,0:T(8,128)(2,1)S(1)}, bf16[32,24576]{1,0:T(8,128)(2,1)}, u32[]{:S(2)}, u32[]{:S(2)}) collective-permute-start(bf16[32,24576]{1,0:T(8,128)(2,1)S(1)} %stack_p.1.refs_1_), channel_id=1, source_target_pairs={{0,2},{1,9},{2,4},{3,11},{4,6},{5,13},{6,0},{7,15},{8,10},{9,17},{... | collective-permute-start | bytes 4718600 | tf_op jit(solution)/shard_map/ppermute | solution.py:37
  23.5 5.9 %collective-permute-start.7 = (bf16[256,128]{1,0:T(8,128)(2,1)S(1)}, bf16[256,128]{1,0:T(8,128)(2,1)S(1)}, u32[]{:S(2)}, u32[]{:S(2)}) collective-permute-start(bf16[256,128]{1,0:T(8,128)(2,1)S(1)} %add.2.a_ref), channel_id=1, source_target_pairs={{64,0},{96,32},{65,1},{97,33},{66,2},{98,34},{67,3},{99,35},{68,4}... | collective-permute-start | bytes 196616 | tf_op jit(solution)/shard_map/ppermute | solution.py:404
  29.5 22.3 %collective-permute-start.14 = (bf16[32,24576]{1,0:T(8,128)(2,1)S(1)}, bf16[32,24576]{1,0:T(8,128)(2,1)}, u32[]{:S(2)}, u32[]{:S(2)}) collective-permute-start(bf16[32,24576]{1,0:T(8,128)(2,1)S(1)} %stack_p.1.refs_1_), channel_id=1, source_target_pairs={{0,1},{1,0},{2,3},{3,2},{4,5},{5,4},{6,7},{7,6},{8,9},{9,8},{10,11... | collective-permute-start | bytes 4718600 | tf_op jit(solution)/shard_map/ppermute | solution.py:37
  34.1 3.0 %collective-permute-start.8 = (bf16[128,256]{1,0:T(8,128)(2,1)S(1)}, bf16[128,256]{1,0:T(8,128)(2,1)S(1)}, u32[]{:S(2)}, u32[]{:S(2)}) collective-permute-start(bf16[128,256]{1,0:T(8,128)(2,1)S(1)} %stack_l.1.own_ref), channel_id=1, source_target_pairs={{0,1},{1,0},{2,3},{3,2},{4,5},{5,4},{6,7},{7,6},{8,9},{9,8},{10,11... | collective-permute-start | bytes 196616 | tf_op jit(solution)/shard_map/ppermute | solution.py:37
  34.2 7.1 %collective-permute-start.9 = (bf16[256,128]{1,0:T(8,128)(2,1)S(1)}, bf16[256,128]{1,0:T(8,128)(2,1)S(1)}, u32[]{:S(2)}, u32[]{:S(2)}) collective-permute-start(bf16[256,128]{1,0:T(8,128)(2,1)S(1)} %add.3.top_ref), channel_id=1, source_target_pairs={{32,0},{33,1},{34,2},{35,3},{36,4},{37,5},{38,6},{39,7},{40,8},{41... | collective-permute-start | bytes 196616 | tf_op jit(solution)/shard_map/ppermute | solution.py:404
  37.1 4.2 %collective-permute-start.10 = (bf16[256,128]{1,0:T(8,128)(2,1)S(1)}, bf16[256,128]{1,0:T(8,128)(2,1)S(1)}, u32[]{:S(2)}, u32[]{:S(2)}) collective-permute-start(bf16[256,128]{1,0:T(8,128)(2,1)S(1)} %get-tuple-element.62.a_ref), channel_id=1, source_target_pairs={{0,64},{1,65},{2,66},{3,67},{4,68},{5,69},{6,70},{7,71},{8,72},{9,... | collective-permute-start | bytes 196616 | tf_op jit(solution)/shard_map/ppermute | solution.py:404
  41.3 9.1 %collective-permute-start.15 = (bf16[256,128]{1,0:T(8,128)(2,1)S(1)}, bf16[256,128]{1,0:T(8,128)(2,1)S(1)}, u32[]{:S(2)}, u32[]{:S(2)}) collective-permute-start(bf16[256,128]{1,0:T(8,128)(2,1)S(1)} %choose.3.a_ref), channel_id=1, source_target_pairs={{0,32},{64,96},{1,33},{65,97},{2,34},{66,98},{3,35},{67,99},{4,36}... | collective-permute-start | bytes 196616 | tf_op jit(solution)/shard_map/ppermute | solution.py:404
  48.5 3.2 %collective-permute-start.11 = (bf16[256,128]{1,0:T(8,128)(2,1)S(1)}, bf16[256,128]{1,0:T(8,128)(2,1)S(1)}, u32[]{:S(2)}, u32[]{:S(2)}) collective-permute-start(bf16[256,128]{1,0:T(8,128)(2,1)S(1)} %solve.1.a_ref), channel_id=1, source_target_pairs={{0,64},{1,65},{2,66},{3,67},{4,68},{5,69},{6,70},{7,71},{8,72},{9,... | collective-permute-start | bytes 196616 | tf_op jit(solution)/shard_map/ppermute | solution.py:404
  51.8 12.1 %collective-permute-start.19 = (bf16[32,12288]{1,0:T(8,128)(2,1)S(1)}, bf16[32,12288]{1,0:T(8,128)(2,1)S(1)}, u32[]{:S(2)}, u32[]{:S(2)}) collective-permute-start(bf16[32,12288]{1,0:T(8,128)(2,1)S(1)} %stack_b.1), channel_id=1, source_target_pairs={{0,6},{1,25},{2,0},{3,27},{4,2},{5,29},{6,4},{7,31},{8,14},{9,1},{... | collective-permute-start | bytes 2359304 | tf_op jit(solution)/shard_map/ppermute | solution.py:37
  55.8 12.4 %collective-permute-start.18 = (bf16[32,12288]{1,0:T(8,128)(2,1)S(1)}, bf16[32,12288]{1,0:T(8,128)(2,1)S(1)}, u32[]{:S(2)}, u32[]{:S(2)}) collective-permute-start(bf16[32,12288]{1,0:T(8,128)(2,1)S(1)} %stack_a.1), channel_id=1, source_target_pairs={{0,2},{1,9},{2,4},{3,11},{4,6},{5,13},{6,0},{7,15},{8,10},{9,17},{... | collective-permute-start | bytes 2359304 | tf_op jit(solution)/shard_map/ppermute | solution.py:37
  55.9 2.6 %collective-permute-start.16 = (bf16[256,128]{1,0:T(8,128)(2,1)S(1)}, bf16[256,128]{1,0:T(8,128)(2,1)S(1)}, u32[]{:S(2)}, u32[]{:S(2)}) collective-permute-start(bf16[256,128]{1,0:T(8,128)(2,1)S(1)} %choose.5.a_ref), channel_id=1, source_target_pairs={{0,32},{64,96},{1,33},{65,97},{2,34},{66,98},{3,35},{67,99},{4,36}... | collective-permute-start | bytes 196616 | tf_op jit(solution)/shard_map/ppermute | solution.py:404
  58.5 15.0 %copy-start.1 = (s32[256]{0:T(256)S(1)}, s32[256]{0:T(256)}, u32[]{:S(2)}) copy-start(s32[256]{0:T(256)} %piv_ref.3) | copy-start | bytes 3076
  58.5 13.1 %collective-permute-start.17 = (bf16[512,128]{1,0:T(8,128)(2,1)S(1)}, bf16[512,128]{1,0:T(8,128)(2,1)S(1)}, u32[]{:S(2)}, u32[]{:S(2)}) collective-permute-start(bf16[512,128]{1,0:T(8,128)(2,1)S(1)} %join.1.ud_ref), channel_id=1, source_target_pairs={{0,128},{32,160},{64,192},{96,224},{1,129},{33,161},{65,193},{97,2... | collective-permute-start | bytes 393224 | tf_op jit(solution)/shard_map/ppermute | solution.py:404
  59.8 13.7 %collective-permute-start.20 = (bf16[32,24576]{1,0:T(8,128)(2,1)}, bf16[32,24576]{1,0:T(8,128)(2,1)S(1)}, u32[]{:S(2)}, u32[]{:S(2)}) collective-permute-start(bf16[32,24576]{1,0:T(8,128)(2,1)} %collective-permute-done.12.refs_0_.refs_2_), channel_id=1, source_target_pairs={{0,1},{1,0},{2,3},{3,2},{4,5},{5,4},{6,7},{7,6},{8,9},{9,8},{10,11... | collective-permute-start | bytes 4718600 | tf_op jit(solution)/shard_map/ppermute | solution.py:37
  63.7 9.9 %collective-permute-start.21 = (bf16[32,24576]{1,0:T(8,128)(2,1)S(1)}, bf16[32,24576]{1,0:T(8,128)(2,1)S(1)}, u32[]{:S(2)}, u32[]{:S(2)}) collective-permute-start(bf16[32,24576]{1,0:T(8,128)(2,1)S(1)} %collective-permute-done.13.refs_0_.refs_3_), channel_id=1, source_target_pairs={{0,1},{1,0},{2,3},{3,2},{4,5},{5,4},{6,7},{7,6},{8,9},{9,8},{10,11... | collective-permute-start | bytes 4718600 | tf_op jit(solution)/shard_map/ppermute | solution.py:37
  63.9 7.7 %collective-permute-start.23 = (bf16[32,12288]{1,0:T(8,128)(2,1)S(1)}, bf16[32,12288]{1,0:T(8,128)(2,1)S(1)}, u32[]{:S(2)}, u32[]{:S(2)}) collective-permute-start(bf16[32,12288]{1,0:T(8,128)(2,1)S(1)} %collective-permute-done.19.refs_1_.refs_5_), channel_id=1, source_target_pairs={{0,1},{1,0},{2,3},{3,2},{4,5},{5,4},{6,7},{7,6},{8,9},{9,8},{10,11... | collective-permute-start | bytes 2359304 | tf_op jit(solution)/shard_map/ppermute | solution.py:37
  68.2 5.4 %collective-permute-start.22 = (bf16[32,12288]{1,0:T(8,128)(2,1)S(1)}, bf16[32,12288]{1,0:T(8,128)(2,1)S(1)}, u32[]{:S(2)}, u32[]{:S(2)}) collective-permute-start(bf16[32,12288]{1,0:T(8,128)(2,1)S(1)} %collective-permute-done.18.refs_0_.refs_4_), channel_id=1, source_target_pairs={{0,1},{1,0},{2,3},{3,2},{4,5},{5,4},{6,7},{7,6},{8,9},{9,8},{10,11... | collective-permute-start | bytes 2359304 | tf_op jit(solution)/shard_map/ppermute | solution.py:37

commit v12 on v10

--- a/solution.py
+++ b/solution.py
@@ -418,22 +418,23 @@
     own = stack([diag, diag_p, diag_m, diag_q], 0, width, "stack_l")
     top = add(top, more)
     more = zsend(top, [(2, 0), (3, 1)])
+    top = add(top, more)
+    top, disp, own, block2 = barrier((top, disp, own, block))
     other = send(own, CORES)
-    top = add(top, more)
-    top, disp, other, source = barrier((top, disp, other, trailing))
+    other, source = barrier((other, trailing))
     copy = fetch(pltpu.with_memory_space_constraint(source, pltpu.HBM))
     more = zsend(top, [(1, 0)])
     lower = zsend(disp, [(0, 2)])
     top, block2 = barrier((top, block))
     swap = send(block2, CORES)
     more, disp, lower, copy = barrier((more, disp, lower, copy))
-    u = solve(me, own, other, top, more)
     disp = choose(first, rows, (2,), disp, lower)
     disp = choose(first, rows, (1, 3), disp, zsend(disp, [(0, 1), (2, 3)]))
-    ru = zsend(u, [(0, 2)])
-    ru, near, far, swap, disp, copy = barrier((ru, near, far, swap, disp, copy))
+    more, disp, near, far, swap = barrier((more, disp, near, far, swap))
     fa, fb = stack([near], 0, half, "stack_a"), stack([far], half, half, "stack_b")
     qa, qb = send(fa, up), send(fb, down)
+    u = solve(me, own, other, top, more)
+    ru = zsend(u, [(0, 2)])
     u = choose(first, rows, (2,), u, ru)
     u, near, far = barrier((u, near, far))
     other_near, other_far = send(near, CORES), send(far, CORES)

time: 77.7 us -> 81.3 us (1.046)
  starting transfers between devices: 46.1 us -> 37.6 us
  waiting for transfers between devices: 9.46 us -> 16.1 us
  local copies, waits for them, and re-layouts: 0.69 us -> 4.78 us
  Pallas kernels: 20.8 us -> 21.9 us
    ppermute x8, waiting for transfers between devices: 2.01 us -> 7.24 us  [zsend(): return lax.ppermute(x, 'prow', pairs)]
    ppermute x8, starting transfers between devices: 18.5 us -> 13.4 us  [zsend(): return lax.ppermute(x, 'prow', pairs)]
    unnamed x6 -> x24, local copies, waits for them, and re-layouts: 0.69 us -> 4.78 us
    ppermute x16, starting transfers between devices: 27.6 us -> 24.2 us  [send(): return lax.ppermute(block, 'pcol', pairs)]
    pallas_call x6, Pallas kernels: 1.89 us -> 3.78 us  [stack(): pl.pallas_call(functools.partial(stack_kernel, start, min(cols, 1024)), i...]
    ppermute x16, waiting for transfers between devices: 7.46 us -> 8.82 us  [send(): return lax.ppermute(block, 'pcol', pairs)]
  transfers between devices with their start and end apart: 24 -> 24, of which waited for: 8 -> 9; matrix products, arithmetic and copies ran while one was open for 0% -> 0% of each run, Pallas kernels for 17% -> 17%
where the time goes in v12:
time: 81.3 us; the launch traced here: 80.9 us
  starting transfers between devices  37.6 us (46%)
  Pallas kernels  21.9 us (27%)
  waiting for transfers between devices  16.1 us (20%)
  local copies, waits for them, and re-layouts  4.78 us (6%)
    ppermute x16, starting transfers between devices, send(): return lax.ppermute(block, 'pcol', pairs)  24.2 us
    ppermute x8, starting transfers between devices, zsend(): return lax.ppermute(x, 'prow', pairs)  13.4 us
    ppermute x16, waiting for transfers between devices, send(): return lax.ppermute(block, 'pcol', pairs)  8.82 us
    ppermute x8, waiting for transfers between devices, zsend(): return lax.ppermute(x, 'prow', pairs)  7.24 us
    pallas_call x1, Pallas kernels, update(): pl.pallas_call(update_kernel, in_specs=[SMEM] * 5 + [VMEM] * 14, out_spec...  7.14 us
    unnamed x24, local copies, waits for them, and re-layouts  4.78 us
    pallas_call x1, Pallas kernels, solve(): pl.pallas_call(solve_kernel, in_specs=[SMEM] + [VMEM] * 4, out_specs=VMEM...  4.25 us
    pallas_call x1, Pallas kernels, pick(): pl.pallas_call(functools.partial(pick_kernel, blk), in_specs=[SMEM, SMEM,...  3.84 us
  transfers between devices with their start and end apart: 24, of which 9 were waited for; matrix products, arithmetic and copies ran while one was open for 0% of the time, Pallas kernels for 17%

profile of v12, /device:TPU:1, one launch (start us, length us, event | category | flops | bytes accessed | tf_op | source)
XLA Modules:
  0.0 80.9 jit_solution(13413493789381310617)
XLA Ops:
  0.0 3.7 %collective-permute-start.2 = (bf16[8,24576]{1,0:T(8,128)(2,1)}, bf16[8,24576]{1,0:T(8,128)(2,1)S(1)}, u32[]{:S(2)}, u32[]{:S(2)}) collective-permute-start(bf16[8,24576]{1,0:T(8,128)(2,1)} %refs_0_.3), channel_id=1, source_target_pairs={{0,16},{1,5},{2,18},{3,7},{4,20},{5,1},{6,22},{7,3},{8,24},{9,13},... | collective-permute-start | bytes 1179656 | tf_op jit(solution)/shard_map/ppermute | solution.py:37
  3.7 0.8 collective-permute-start.1
  4.5 0.7 collective-permute-start
  5.2 0.7 copy-done.5
  5.9 3.8 %pick.1 = (bf16[256,128]{1,0:T(8,128)(2,1)S(1)}, bf16[256,128]{1,0:T(8,128)(2,1)S(1)}, s32[1]{0:T(128)}, s32[256]{0:T(256)S(1)}) custom-call(s32[256]{0:T(256)S(1)} %copy-done.5, s32[1]{0:T(128)} %bitcast.first_ref, bf16[24576,128]{1,0:T(8,128)(2,1)} %src_ref), custom_call_target="tpu_custom_call" | custom-call | flops 13200000000 | bytes 42000000 | tf_op jit(solution)/shard_map/pick/pallas_call | solution.py:184
  9.7 1.3 %collective-permute-start.6 = (bf16[256,128]{1,0:T(8,128)(2,1)S(1)}, bf16[256,128]{1,0:T(8,128)(2,1)S(1)}, u32[]{:S(2)}, u32[]{:S(2)}) collective-permute-start(bf16[256,128]{1,0:T(8,128)(2,1)S(1)} %get-tuple-element.46.a_ref), channel_id=1, source_target_pairs={{128,0},{160,32},{192,64},{224,96},{129,1},{161,33},{193,65},{225,... | collective-permute-start | bytes 196616 | tf_op jit(solution)/shard_map/ppermute | solution.py:404
  11.1 0.0 copy-start.8
  11.1 3.0 %collective-permute-done.1.refs_2_ = bf16[8,24576]{1,0:T(8,128)(2,1)S(1)} collective-permute-done((bf16[8,24576]{1,0:T(8,128)(2,1)}, bf16[8,24576]{1,0:T(8,128)(2,1)S(1)}, u32[]{:S(2)}, u32[]{:S(2)}) %collective-permute-start.1) | collective-permute-done | bytes 393248 | tf_op jit(solution)/shard_map/ppermute | solution.py:37
  14.1 2.6 %collective-permute-start.5 = (bf16[32,256]{1,0:T(8,128)(2,1)S(1)}, bf16[32,256]{1,0:T(8,128)(2,1)S(1)}, u32[]{:S(2)}, u32[]{:S(2)}) collective-permute-start(bf16[32,256]{1,0:T(8,128)(2,1)S(1)} %stack_d.1.refs_0_), channel_id=1, source_target_pairs={{0,6},{1,25},{2,0},{3,27},{4,2},{5,29},{6,4},{7,31},{8,14},{9,1},{... | collective-permute-start | bytes 49160 | tf_op jit(solution)/shard_map/ppermute | solution.py:37
  16.6 0.0 collective-permute-start.4
  16.7 1.7 %collective-permute-start.3 = (bf16[32,256]{1,0:T(8,128)(2,1)S(1)}, bf16[32,256]{1,0:T(8,128)(2,1)S(1)}, u32[]{:S(2)}, u32[]{:S(2)}) collective-permute-start(bf16[32,256]{1,0:T(8,128)(2,1)S(1)} %stack_d.1.refs_0_), channel_id=1, source_target_pairs={{0,4},{1,17},{2,6},{3,19},{4,0},{5,21},{6,2},{7,23},{8,12},{9,25},... | collective-permute-start | bytes 49160 | tf_op jit(solution)/shard_map/ppermute | solution.py:37
  18.4 1.0 %copy-done.9 = bf16[8,24576]{1,0:T(8,128)(2,1)S(1)} copy-done((bf16[8,24576]{1,0:T(8,128)(2,1)S(1)}, bf16[8,24576]{1,0:T(8,128)(2,1)}, u32[]{:S(2)}) %copy-start.9) | copy-done | bytes 393240
  19.4 0.3 stack_p.1.refs_1_
  19.7 0.0 collective-permute-done.6.b_ref
  19.7 1.0 %collective-permute-done.4.refs_1_ = bf16[32,256]{1,0:T(8,128)(2,1)S(1)} collective-permute-done((bf16[32,256]{1,0:T(8,128)(2,1)S(1)}, bf16[32,256]{1,0:T(8,128)(2,1)S(1)}, u32[]{:S(2)}, u32[]{:S(2)}) %collective-permute-start.4) | collective-permute-done | bytes 16416 | tf_op jit(solution)/shard_map/ppermute | solution.py:37
  20.7 0.3 collective-permute-done.3.refs_3_
  21.0 2.4 %collective-permute-start.13 = (bf16[32,24576]{1,0:T(8,128)(2,1)S(1)}, bf16[32,24576]{1,0:T(8,128)(2,1)S(1)}, u32[]{:S(2)}, u32[]{:S(2)}) collective-permute-start(bf16[32,24576]{1,0:T(8,128)(2,1)S(1)} %stack_p.1.refs_1_), channel_id=1, source_target_pairs={{0,6},{1,25},{2,0},{3,27},{4,2},{5,29},{6,4},{7,31},{8,14},{9,1},{... | collective-permute-start | bytes 4718600 | tf_op jit(solution)/shard_map/ppermute | solution.py:37
  23.4 1.3 %collective-permute-start.7 = (bf16[256,128]{1,0:T(8,128)(2,1)S(1)}, bf16[256,128]{1,0:T(8,128)(2,1)S(1)}, u32[]{:S(2)}, u32[]{:S(2)}) collective-permute-start(bf16[256,128]{1,0:T(8,128)(2,1)S(1)} %add.2.a_ref), channel_id=1, source_target_pairs={{64,0},{96,32},{65,1},{97,33},{66,2},{98,34},{67,3},{99,35},{68,4}... | collective-permute-start | bytes 196616 | tf_op jit(solution)/shard_map/ppermute | solution.py:404
  24.8 4.6 %collective-permute-done.7.b_ref = bf16[256,128]{1,0:T(8,128)(2,1)S(1)} collective-permute-done((bf16[256,128]{1,0:T(8,128)(2,1)S(1)}, bf16[256,128]{1,0:T(8,128)(2,1)S(1)}, u32[]{:S(2)}, u32[]{:S(2)}) %collective-permute-start.7) | collective-permute-done | bytes 65568 | tf_op jit(solution)/shard_map/ppermute | solution.py:404
  29.4 4.7 %collective-permute-start.14 = (bf16[32,24576]{1,0:T(8,128)(2,1)S(1)}, bf16[32,24576]{1,0:T(8,128)(2,1)S(1)}, u32[]{:S(2)}, u32[]{:S(2)}) collective-permute-start(bf16[32,24576]{1,0:T(8,128)(2,1)S(1)} %stack_p.1.refs_1_), channel_id=1, source_target_pairs={{0,1},{1,0},{2,3},{3,2},{4,5},{5,4},{6,7},{7,6},{8,9},{9,8},{10,11... | collective-permute-start | bytes 4718600 | tf_op jit(solution)/shard_map/ppermute | solution.py:37
  34.1 0.1 collective-permute-start.10
  34.2 1.3 %collective-permute-start.8 = (bf16[256,128]{1,0:T(8,128)(2,1)S(1)}, bf16[256,128]{1,0:T(8,128)(2,1)S(1)}, u32[]{:S(2)}, u32[]{:S(2)}) collective-permute-start(bf16[256,128]{1,0:T(8,128)(2,1)S(1)} %add.3.top_ref), channel_id=1, source_target_pairs={{32,0},{33,1},{34,2},{35,3},{36,4},{37,5},{38,6},{39,7},{40,8},{41... | collective-permute-start | bytes 196616 | tf_op jit(solution)/shard_map/ppermute | solution.py:404
  35.5 1.7 %collective-permute-done.10.other_ref = bf16[128,256]{1,0:T(8,128)(2,1)S(1)} collective-permute-done((bf16[128,256]{1,0:T(8,128)(2,1)S(1)}, bf16[128,256]{1,0:T(8,128)(2,1)S(1)}, u32[]{:S(2)}, u32[]{:S(2)}) %collective-permute-start.10) | collective-permute-done | bytes 65568 | tf_op jit(solution)/shard_map/ppermute | solution.py:37
  37.3 1.3 %collective-permute-start.9 = (bf16[256,128]{1,0:T(8,128)(2,1)S(1)}, bf16[256,128]{1,0:T(8,128)(2,1)S(1)}, u32[]{:S(2)}, u32[]{:S(2)}) collective-permute-start(bf16[256,128]{1,0:T(8,128)(2,1)S(1)} %get-tuple-element.61.a_ref), channel_id=1, source_target_pairs={{0,64},{1,65},{2,66},{3,67},{4,68},{5,69},{6,70},{7,71},{8,72},{9,... | collective-permute-start | bytes 196616 | tf_op jit(solution)/shard_map/ppermute | solution.py:404
  38.6 2.9 %fetch.1.tr_ref = bf16[24576,128]{1,0:T(8,128)(2,1)S(1)} custom-call(bf16[24576,128]{1,0:T(8,128)(2,1)} %src_ref), custom_call_target="tpu_custom_call" | custom-call | tf_op jit(solution)/shard_map/fetch/pallas_call | solution.py:303
  41.4 0.0 copy-start
  41.4 2.7 %copy-done = bf16[24576,128]{1,0:T(8,128)(2,1)} copy-done((bf16[24576,128]{1,0:T(8,128)(2,1)}, bf16[24576,128]{1,0:T(8,128)(2,1)S(1)}, u32[]{:S(2)}) %copy-start) | copy-done | bytes 6291480
  44.2 2.9 %collective-permute-start.11 = (bf16[256,128]{1,0:T(8,128)(2,1)S(1)}, bf16[256,128]{1,0:T(8,128)(2,1)S(1)}, u32[]{:S(2)}, u32[]{:S(2)}) collective-permute-start(bf16[256,128]{1,0:T(8,128)(2,1)S(1)} %choose.3.a_ref), channel_id=1, source_target_pairs={{0,32},{64,96},{1,33},{65,97},{2,34},{66,98},{3,35},{67,99},{4,36}... | collective-permute-start | bytes 196616 | tf_op jit(solution)/shard_map/ppermute | solution.py:404
  47.1 1.3 %collective-permute-done.11.b_ref = bf16[256,128]{1,0:T(8,128)(2,1)S(1)} collective-permute-done((bf16[256,128]{1,0:T(8,128)(2,1)S(1)}, bf16[256,128]{1,0:T(8,128)(2,1)S(1)}, u32[]{:S(2)}, u32[]{:S(2)}) %collective-permute-start.11) | collective-permute-done | bytes 65568 | tf_op jit(solution)/shard_map/ppermute | solution.py:404
  48.4 1.1 %stack_b.1 = bf16[32,12288]{1,0:T(8,128)(2,1)} custom-call(bf16[32,24576]{1,0:T(8,128)(2,1)S(1)} %collective-permute-done.13.refs_0_.refs_3_), custom_call_target="tpu_custom_call" | custom-call | flops 1100000000 | bytes 3500000 | tf_op jit(solution)/shard_map/stack_b/pallas_call | solution.py:60
  49.5 0.4 copy-done.3
  49.9 2.3 %collective-permute-start.19 = (bf16[32,12288]{1,0:T(8,128)(2,1)}, bf16[32,12288]{1,0:T(8,128)(2,1)}, u32[]{:S(2)}, u32[]{:S(2)}) collective-permute-start(bf16[32,12288]{1,0:T(8,128)(2,1)} %stack_b.1), channel_id=1, source_target_pairs={{0,6},{1,25},{2,0},{3,27},{4,2},{5,29},{6,4},{7,31},{8,14},{9,1},{... | collective-permute-start | bytes 2359304 | tf_op jit(solution)/shard_map/ppermute | solution.py:37
  52.3 1.0 %stack_a.1 = bf16[32,12288]{1,0:T(8,128)(2,1)} custom-call(bf16[32,24576]{1,0:T(8,128)(2,1)S(1)} %collective-permute-done.12.refs_0_.refs_2_), custom_call_target="tpu_custom_call" | custom-call | flops 1100000000 | bytes 3500000 | tf_op jit(solution)/shard_map/stack_a/pallas_call | solution.py:60
  53.2 4.2 %solve.1.a_ref = bf16[256,128]{1,0:T(8,128)(2,1)S(1)} custom-call(s32[1]{0:T(128)} %bitcast.1.me_ref, bf16[128,256]{1,0:T(8,128)(2,1)S(1)} %stack_l.1.own_ref, bf16[128,256]{1,0:T(8,128)(2,1)S(1)} %collective-permute-done.10.other_ref, bf16[256,128]{1,0:T(8,128)(2,1)S(1)} %add.3.top_ref, bf16[256,128]{1,0:T(8,128)(2,1)S(1)} %collective-permute-done.8.more_ref), custom_call_target="tpu_custom_call" | custom-call | tf_op jit(solution)/shard_map/solve/pallas_call | solution.py:278
  57.5 1.3 %collective-permute-start.15 = (bf16[256,128]{1,0:T(8,128)(2,1)S(1)}, bf16[256,128]{1,0:T(8,128)(2,1)S(1)}, u32[]{:S(2)}, u32[]{:S(2)}) collective-permute-start(bf16[256,128]{1,0:T(8,128)(2,1)S(1)} %solve.1.a_ref), channel_id=1, source_target_pairs={{0,64},{1,65},{2,66},{3,67},{4,68},{5,69},{6,70},{7,71},{8,72},{9,... | collective-permute-start | bytes 196616 | tf_op jit(solution)/shard_map/ppermute | solution.py:404
  58.8 1.3 %collective-permute-done.15.b_ref = bf16[256,128]{1,0:T(8,128)(2,1)S(1)} collective-permute-done((bf16[256,128]{1,0:T(8,128)(2,1)S(1)}, bf16[256,128]{1,0:T(8,128)(2,1)S(1)}, u32[]{:S(2)}, u32[]{:S(2)}) %collective-permute-start.15) | collective-permute-done | bytes 65568 | tf_op jit(solution)/shard_map/ppermute | solution.py:404
  60.1 1.8 %collective-permute-start.16 = (bf16[256,128]{1,0:T(8,128)(2,1)S(1)}, bf16[256,128]{1,0:T(8,128)(2,1)S(1)}, u32[]{:S(2)}, u32[]{:S(2)}) collective-permute-start(bf16[256,128]{1,0:T(8,128)(2,1)S(1)} %choose.5.a_ref), channel_id=1, source_target_pairs={{0,32},{64,96},{1,33},{65,97},{2,34},{66,98},{3,35},{67,99},{4,36}... | collective-permute-start | bytes 196616 | tf_op jit(solution)/shard_map/ppermute | solution.py:404
  61.9 3.9 %collective-permute-start.20 = (bf16[32,24576]{1,0:T(8,128)(2,1)}, bf16[32,24576]{1,0:T(8,128)(2,1)S(1)}, u32[]{:S(2)}, u32[]{:S(2)}) collective-permute-start(bf16[32,24576]{1,0:T(8,128)(2,1)} %copy-done.1), channel_id=1, source_target_pairs={{0,1},{1,0},{2,3},{3,2},{4,5},{5,4},{6,7},{7,6},{8,9},{9,8},{10,11... | collective-permute-start | bytes 4718600 | tf_op jit(solution)/shard_map/ppermute | solution.py:37
  65.8 0.3 collective-permute-start.21
  66.1 0.0 slice-start.1
  66.1 0.0 copy-start.6
  66.1 2.2 %collective-permute-start.17 = (bf16[512,128]{1,0:T(8,128)(2,1)S(1)}, bf16[512,128]{1,0:T(8,128)(2,1)S(1)}, u32[]{:S(2)}, u32[]{:S(2)}) collective-permute-start(bf16[512,128]{1,0:T(8,128)(2,1)S(1)} %join.1.ud_ref), channel_id=1, source_target_pairs={{0,128},{32,160},{64,192},{96,224},{1,129},{33,161},{65,193},{97,2... | collective-permute-start | bytes 393224 | tf_op jit(solution)/shard_map/ppermute | solution.py:404
  68.4 0.9 %collective-permute-start.23 = (bf16[32,12288]{1,0:T(8,128)(2,1)}, bf16[32,12288]{1,0:T(8,128)(2,1)S(1)}, u32[]{:S(2)}, u32[]{:S(2)}) collective-permute-start(bf16[32,12288]{1,0:T(8,128)(2,1)} %collective-permute-done.19.refs_1_.refs_5_), channel_id=1, source_target_pairs={{0,1},{1,0},{2,3},{3,2},{4,5},{5,4},{6,7},{7,6},{8,9},{9,8},{10,11... | collective-permute-start | bytes 2359304 | tf_op jit(solution)/shard_map/ppermute | solution.py:37
  69.3 0.1 collective-permute-start.22
  69.4 1.4 %stack_q.1.refs_0_ = bf16[64,128]{1,0:T(8,128)(2,1)S(1)} custom-call(bf16[32,12288]{1,0:T(8,128)(2,1)} %collective-permute-done.18.refs_0_.refs_4_, bf16[32,12288]{1,0:T(8,128)(2,1)} %collective-permute-done.19.refs_1_.refs_5_), custom_call_target="tpu_custom_call" | custom-call | flops 65999998976 | bytes 210000000 | tf_op jit(solution)/shard_map/stack_q/pallas_call | solution.py:60
  70.8 1.6 %collective-permute-done.23.refs_10_ = bf16[32,12288]{1,0:T(8,128)(2,1)S(1)} collective-permute-done((bf16[32,12288]{1,0:T(8,128)(2,1)}, bf16[32,12288]{1,0:T(8,128)(2,1)S(1)}, u32[]{:S(2)}, u32[]{:S(2)}) %collective-permute-start.23) | collective-permute-done | bytes 786464 | tf_op jit(solution)/shard_map/ppermute | solution.py:37
  72.4 1.1 %collective-permute-done.22.refs_9_ = bf16[32,12288]{1,0:T(8,128)(2,1)S(1)} collective-permute-done((bf16[32,12288]{1,0:T(8,128)(2,1)}, bf16[32,12288]{1,0:T(8,128)(2,1)S(1)}, u32[]{:S(2)}, u32[]{:S(2)}) %collective-permute-start.22) | collective-permute-done | bytes 786464 | tf_op jit(solution)/shard_map/ppermute | solution.py:37
  73.6 7.1 %update.1 = (bf16[24576,128]{1,0:T(8,128)(2,1)}, bf16[24576,128]{1,0:T(8,128)(2,1)S(1)}) custom-call(s32[1]{0:T(128)} %get-tuple-element.39.cnt_ref, s32[256]{0:T(256)S(1)} %get-tuple-element.40.lst_ref, s32[256]{0:T(256)S(1)} %copy-done.6, s32[1]{0:T(128)} %bitcast.first_ref, s32[1]{0:T(128)} %bitcast.1.me_ref, ...), custom_call_target="tpu_custom_call", output_to_operand_aliasing={{1}: (5, {})} | custom-call | tf_op jit(solution)/shard_map/update/pallas_call | solution.py:377
  (41 shorter events, 0.2 us)
Async XLA Ops:
  0.0 11.0 %collective-permute-start.2 = (bf16[8,24576]{1,0:T(8,128)(2,1)}, bf16[8,24576]{1,0:T(8,128)(2,1)S(1)}, u32[]{:S(2)}, u32[]{:S(2)}) collective-permute-start(bf16[8,24576]{1,0:T(8,128)(2,1)} %refs_0_.3), channel_id=1, source_target_pairs={{0,16},{1,5},{2,18},{3,7},{4,20},{5,1},{6,22},{7,3},{8,24},{9,13},... | collective-permute-start | bytes 1179656 | tf_op jit(solution)/shard_map/ppermute | solution.py:37
  3.7 10.3 %collective-permute-start.1 = (bf16[8,24576]{1,0:T(8,128)(2,1)}, bf16[8,24576]{1,0:T(8,128)(2,1)S(1)}, u32[]{:S(2)}, u32[]{:S(2)}) collective-permute-start(bf16[8,24576]{1,0:T(8,128)(2,1)} %refs_0_.3), channel_id=1, source_target_pairs={{0,24},{1,7},{2,26},{3,1},{4,28},{5,3},{6,30},{7,5},{8,0},{9,15},{... | collective-permute-start | bytes 1179656 | tf_op jit(solution)/shard_map/ppermute | solution.py:37
  4.5 9.5 %collective-permute-start = (bf16[8,24576]{1,0:T(8,128)(2,1)}, bf16[8,24576]{1,0:T(8,128)(2,1)S(1)}, u32[]{:S(2)}, u32[]{:S(2)}) collective-permute-start(bf16[8,24576]{1,0:T(8,128)(2,1)} %refs_0_.3), channel_id=1, source_target_pairs={{0,8},{1,3},{2,10},{3,5},{4,12},{5,7},{6,14},{7,1},{8,16},{9,11},{... | collective-permute-start | bytes 1179656 | tf_op jit(solution)/shard_map/ppermute | solution.py:37
  5.2 0.7 copy-start.5
  5.9 8.2 %copy-start.7 = (bf16[8,24576]{1,0:T(8,128)(2,1)S(1)}, bf16[8,24576]{1,0:T(8,128)(2,1)}, u32[]{:S(2)}) copy-start(bf16[8,24576]{1,0:T(8,128)(2,1)} %refs_0_.3) | copy-start | bytes 1179652
  9.7 10.0 %collective-permute-start.6 = (bf16[256,128]{1,0:T(8,128)(2,1)S(1)}, bf16[256,128]{1,0:T(8,128)(2,1)S(1)}, u32[]{:S(2)}, u32[]{:S(2)}) collective-permute-start(bf16[256,128]{1,0:T(8,128)(2,1)S(1)} %get-tuple-element.46.a_ref), channel_id=1, source_target_pairs={{128,0},{160,32},{192,64},{224,96},{129,1},{161,33},{193,65},{225,... | collective-permute-start | bytes 196616 | tf_op jit(solution)/shard_map/ppermute | solution.py:404
  11.1 3.0 %copy-start.8 = (bf16[8,24576]{1,0:T(8,128)(2,1)}, bf16[8,24576]{1,0:T(8,128)(2,1)S(1)}, u32[]{:S(2)}) copy-start(bf16[8,24576]{1,0:T(8,128)(2,1)S(1)} %collective-permute-done.2.refs_3_) | copy-start | bytes 1179652
  14.1 5.6 %collective-permute-start.5 = (bf16[32,256]{1,0:T(8,128)(2,1)S(1)}, bf16[32,256]{1,0:T(8,128)(2,1)S(1)}, u32[]{:S(2)}, u32[]{:S(2)}) collective-permute-start(bf16[32,256]{1,0:T(8,128)(2,1)S(1)} %stack_d.1.refs_0_), channel_id=1, source_target_pairs={{0,6},{1,25},{2,0},{3,27},{4,2},{5,29},{6,4},{7,31},{8,14},{9,1},{... | collective-permute-start | bytes 49160 | tf_op jit(solution)/shard_map/ppermute | solution.py:37
  16.6 4.1 %collective-permute-start.4 = (bf16[32,256]{1,0:T(8,128)(2,1)S(1)}, bf16[32,256]{1,0:T(8,128)(2,1)S(1)}, u32[]{:S(2)}, u32[]{:S(2)}) collective-permute-start(bf16[32,256]{1,0:T(8,128)(2,1)S(1)} %stack_d.1.refs_0_), channel_id=1, source_target_pairs={{0,2},{1,9},{2,4},{3,11},{4,6},{5,13},{6,0},{7,15},{8,10},{9,17},{... | collective-permute-start | bytes 49160 | tf_op jit(solution)/shard_map/ppermute | solution.py:37
  16.7 4.4 %collective-permute-start.3 = (bf16[32,256]{1,0:T(8,128)(2,1)S(1)}, bf16[32,256]{1,0:T(8,128)(2,1)S(1)}, u32[]{:S(2)}, u32[]{:S(2)}) collective-permute-start(bf16[32,256]{1,0:T(8,128)(2,1)S(1)} %stack_d.1.refs_0_), channel_id=1, source_target_pairs={{0,4},{1,17},{2,6},{3,19},{4,0},{5,21},{6,2},{7,23},{8,12},{9,25},... | collective-permute-start | bytes 49160 | tf_op jit(solution)/shard_map/ppermute | solution.py:37
  18.4 1.0 %copy-start.9 = (bf16[8,24576]{1,0:T(8,128)(2,1)S(1)}, bf16[8,24576]{1,0:T(8,128)(2,1)}, u32[]{:S(2)}) copy-start(bf16[8,24576]{1,0:T(8,128)(2,1)} %copy-done.8) | copy-start | bytes 1179652
  21.0 27.4 %collective-permute-start.13 = (bf16[32,24576]{1,0:T(8,128)(2,1)S(1)}, bf16[32,24576]{1,0:T(8,128)(2,1)S(1)}, u32[]{:S(2)}, u32[]{:S(2)}) collective-permute-start(bf16[32,24576]{1,0:T(8,128)(2,1)S(1)} %stack_p.1.refs_1_), channel_id=1, source_target_pairs={{0,6},{1,25},{2,0},{3,27},{4,2},{5,29},{6,4},{7,31},{8,14},{9,1},{... | collective-permute-start | bytes 4718600 | tf_op jit(solution)/shard_map/ppermute | solution.py:37
  23.4 25.0 %collective-permute-start.12 = (bf16[32,24576]{1,0:T(8,128)(2,1)S(1)}, bf16[32,24576]{1,0:T(8,128)(2,1)S(1)}, u32[]{:S(2)}, u32[]{:S(2)}) collective-permute-start(bf16[32,24576]{1,0:T(8,128)(2,1)S(1)} %stack_p.1.refs_1_), channel_id=1, source_target_pairs={{0,2},{1,9},{2,4},{3,11},{4,6},{5,13},{6,0},{7,15},{8,10},{9,17},{... | collective-permute-start | bytes 4718600 | tf_op jit(solution)/shard_map/ppermute | solution.py:37
  23.4 5.9 %collective-permute-start.7 = (bf16[256,128]{1,0:T(8,128)(2,1)S(1)}, bf16[256,128]{1,0:T(8,128)(2,1)S(1)}, u32[]{:S(2)}, u32[]{:S(2)}) collective-permute-start(bf16[256,128]{1,0:T(8,128)(2,1)S(1)} %add.2.a_ref), channel_id=1, source_target_pairs={{64,0},{96,32},{65,1},{97,33},{66,2},{98,34},{67,3},{99,35},{68,4}... | collective-permute-start | bytes 196616 | tf_op jit(solution)/shard_map/ppermute | solution.py:404
  29.4 19.0 %collective-permute-start.14 = (bf16[32,24576]{1,0:T(8,128)(2,1)S(1)}, bf16[32,24576]{1,0:T(8,128)(2,1)S(1)}, u32[]{:S(2)}, u32[]{:S(2)}) collective-permute-start(bf16[32,24576]{1,0:T(8,128)(2,1)S(1)} %stack_p.1.refs_1_), channel_id=1, source_target_pairs={{0,1},{1,0},{2,3},{3,2},{4,5},{5,4},{6,7},{7,6},{8,9},{9,8},{10,11... | collective-permute-start | bytes 4718600 | tf_op jit(solution)/shard_map/ppermute | solution.py:37
  34.1 3.1 %collective-permute-start.10 = (bf16[128,256]{1,0:T(8,128)(2,1)S(1)}, bf16[128,256]{1,0:T(8,128)(2,1)S(1)}, u32[]{:S(2)}, u32[]{:S(2)}) collective-permute-start(bf16[128,256]{1,0:T(8,128)(2,1)S(1)} %stack_l.1.own_ref), channel_id=1, source_target_pairs={{0,1},{1,0},{2,3},{3,2},{4,5},{5,4},{6,7},{7,6},{8,9},{9,8},{10,11... | collective-permute-start | bytes 196616 | tf_op jit(solution)/shard_map/ppermute | solution.py:37
  34.2 9.9 %collective-permute-start.8 = (bf16[256,128]{1,0:T(8,128)(2,1)S(1)}, bf16[256,128]{1,0:T(8,128)(2,1)S(1)}, u32[]{:S(2)}, u32[]{:S(2)}) collective-permute-start(bf16[256,128]{1,0:T(8,128)(2,1)S(1)} %add.3.top_ref), channel_id=1, source_target_pairs={{32,0},{33,1},{34,2},{35,3},{36,4},{37,5},{38,6},{39,7},{40,8},{41... | collective-permute-start | bytes 196616 | tf_op jit(solution)/shard_map/ppermute | solution.py:404
  37.3 6.9 %collective-permute-start.9 = (bf16[256,128]{1,0:T(8,128)(2,1)S(1)}, bf16[256,128]{1,0:T(8,128)(2,1)S(1)}, u32[]{:S(2)}, u32[]{:S(2)}) collective-permute-start(bf16[256,128]{1,0:T(8,128)(2,1)S(1)} %get-tuple-element.61.a_ref), channel_id=1, source_target_pairs={{0,64},{1,65},{2,66},{3,67},{4,68},{5,69},{6,70},{7,71},{8,72},{9,... | collective-permute-start | bytes 196616 | tf_op jit(solution)/shard_map/ppermute | solution.py:404
  41.4 2.7 %copy-start = (bf16[24576,128]{1,0:T(8,128)(2,1)}, bf16[24576,128]{1,0:T(8,128)(2,1)S(1)}, u32[]{:S(2)}) copy-start(bf16[24576,128]{1,0:T(8,128)(2,1)S(1)} %fetch.1.tr_ref) | copy-start | bytes 18874372
  44.2 4.2 %collective-permute-start.11 = (bf16[256,128]{1,0:T(8,128)(2,1)S(1)}, bf16[256,128]{1,0:T(8,128)(2,1)S(1)}, u32[]{:S(2)}, u32[]{:S(2)}) collective-permute-start(bf16[256,128]{1,0:T(8,128)(2,1)S(1)} %choose.3.a_ref), channel_id=1, source_target_pairs={{0,32},{64,96},{1,33},{65,97},{2,34},{66,98},{3,35},{67,99},{4,36}... | collective-permute-start | bytes 196616 | tf_op jit(solution)/shard_map/ppermute | solution.py:404
  48.4 3.9 %copy-start.1 = (bf16[32,24576]{1,0:T(8,128)(2,1)}, bf16[32,24576]{1,0:T(8,128)(2,1)S(1)}, u32[]{:S(2)}) copy-start(bf16[32,24576]{1,0:T(8,128)(2,1)S(1)} %collective-permute-done.12.refs_0_.refs_2_) | copy-start | bytes 4718596
  48.4 1.5 %copy-start.3 = (bf16[32,24576]{1,0:T(8,128)(2,1)}, bf16[32,24576]{1,0:T(8,128)(2,1)S(1)}, u32[]{:S(2)}) copy-start(bf16[32,24576]{1,0:T(8,128)(2,1)S(1)} %collective-permute-done.14.refs_6_) | copy-start | bytes 4718596
  49.9 18.4 %collective-permute-start.19 = (bf16[32,12288]{1,0:T(8,128)(2,1)}, bf16[32,12288]{1,0:T(8,128)(2,1)}, u32[]{:S(2)}, u32[]{:S(2)}) collective-permute-start(bf16[32,12288]{1,0:T(8,128)(2,1)} %stack_b.1), channel_id=1, source_target_pairs={{0,6},{1,25},{2,0},{3,27},{4,2},{5,29},{6,4},{7,31},{8,14},{9,1},{... | collective-permute-start | bytes 2359304 | tf_op jit(solution)/shard_map/ppermute | solution.py:37
  53.2 16.0 %collective-permute-start.18 = (bf16[32,12288]{1,0:T(8,128)(2,1)}, bf16[32,12288]{1,0:T(8,128)(2,1)}, u32[]{:S(2)}, u32[]{:S(2)}) collective-permute-start(bf16[32,12288]{1,0:T(8,128)(2,1)} %stack_a.1), channel_id=1, source_target_pairs={{0,2},{1,9},{2,4},{3,11},{4,6},{5,13},{6,0},{7,15},{8,10},{9,17},{... | collective-permute-start | bytes 2359304 | tf_op jit(solution)/shard_map/ppermute | solution.py:37
  57.5 2.6 %collective-permute-start.15 = (bf16[256,128]{1,0:T(8,128)(2,1)S(1)}, bf16[256,128]{1,0:T(8,128)(2,1)S(1)}, u32[]{:S(2)}, u32[]{:S(2)}) collective-permute-start(bf16[256,128]{1,0:T(8,128)(2,1)S(1)} %solve.1.a_ref), channel_id=1, source_target_pairs={{0,64},{1,65},{2,66},{3,67},{4,68},{5,69},{6,70},{7,71},{8,72},{9,... | collective-permute-start | bytes 196616 | tf_op jit(solution)/shard_map/ppermute | solution.py:404
  60.1 5.9 %collective-permute-start.16 = (bf16[256,128]{1,0:T(8,128)(2,1)S(1)}, bf16[256,128]{1,0:T(8,128)(2,1)S(1)}, u32[]{:S(2)}, u32[]{:S(2)}) collective-permute-start(bf16[256,128]{1,0:T(8,128)(2,1)S(1)} %choose.5.a_ref), channel_id=1, source_target_pairs={{0,32},{64,96},{1,33},{65,97},{2,34},{66,98},{3,35},{67,99},{4,36}... | collective-permute-start | bytes 196616 | tf_op jit(solution)/shard_map/ppermute | solution.py:404
  61.9 11.6 %collective-permute-start.20 = (bf16[32,24576]{1,0:T(8,128)(2,1)}, bf16[32,24576]{1,0:T(8,128)(2,1)S(1)}, u32[]{:S(2)}, u32[]{:S(2)}) collective-permute-start(bf16[32,24576]{1,0:T(8,128)(2,1)} %copy-done.1), channel_id=1, source_target_pairs={{0,1},{1,0},{2,3},{3,2},{4,5},{5,4},{6,7},{7,6},{8,9},{9,8},{10,11... | collective-permute-start | bytes 4718600 | tf_op jit(solution)/shard_map/ppermute | solution.py:37
  65.8 7.8 %collective-permute-start.21 = (bf16[32,24576]{1,0:T(8,128)(2,1)S(1)}, bf16[32,24576]{1,0:T(8,128)(2,1)S(1)}, u32[]{:S(2)}, u32[]{:S(2)}) collective-permute-start(bf16[32,24576]{1,0:T(8,128)(2,1)S(1)} %collective-permute-done.13.refs_0_.refs_3_), channel_id=1, source_target_pairs={{0,1},{1,0},{2,3},{3,2},{4,5},{5,4},{6,7},{7,6},{8,9},{9,8},{10,11... | collective-permute-start | bytes 4718600 | tf_op jit(solution)/shard_map/ppermute | solution.py:37
  66.1 7.5 %slice-start = ((s8[6291456]{0:T(1024)(128)(4,1)}), s8[4194304]{0:T(1024)(128)(4,1)S(1)}, s32[]{:S(2)}) async-start(s8[6291456]{0:T(1024)(128)(4,1)} %bitcast.2), calls=%async_computation | async-start | bytes 8388608
  66.1 7.5 %slice-start.1 = ((s8[6291456]{0:T(1024)(128)(4,1)}), s8[2097152]{0:T(1024)(128)(4,1)S(1)}, s32[]{:S(2)}) async-start(s8[6291456]{0:T(1024)(128)(4,1)} %bitcast.2), calls=%async_computation.1 | async-start | bytes 4194304
  66.1 7.5 %copy-start.2 = (bf16[32,24576]{1,0:T(8,128)(2,1)S(1)}, bf16[32,24576]{1,0:T(8,128)(2,1)}, u32[]{:S(2)}) copy-start(bf16[32,24576]{1,0:T(8,128)(2,1)} %copy-done.1) | copy-start | bytes 4718596
  66.1 7.5 %copy-start.4 = (bf16[32,24576]{1,0:T(8,128)(2,1)S(1)}, bf16[32,24576]{1,0:T(8,128)(2,1)}, u32[]{:S(2)}) copy-start(bf16[32,24576]{1,0:T(8,128)(2,1)} %copy-done.3) | copy-start | bytes 4718596
  66.1 7.5 %copy-start.6 = (s32[256]{0:T(256)S(1)}, s32[256]{0:T(256)}, u32[]{:S(2)}) copy-start(s32[256]{0:T(256)} %piv_ref.3) | copy-start | bytes 3076
  66.1 4.7 %collective-permute-start.17 = (bf16[512,128]{1,0:T(8,128)(2,1)S(1)}, bf16[512,128]{1,0:T(8,128)(2,1)S(1)}, u32[]{:S(2)}, u32[]{:S(2)}) collective-permute-start(bf16[512,128]{1,0:T(8,128)(2,1)S(1)} %join.1.ud_ref), channel_id=1, source_target_pairs={{0,128},{32,160},{64,192},{96,224},{1,129},{33,161},{65,193},{97,2... | collective-permute-start | bytes 393224 | tf_op jit(solution)/shard_map/ppermute | solution.py:404
  68.4 4.0 %collective-permute-start.23 = (bf16[32,12288]{1,0:T(8,128)(2,1)}, bf16[32,12288]{1,0:T(8,128)(2,1)S(1)}, u32[]{:S(2)}, u32[]{:S(2)}) collective-permute-start(bf16[32,12288]{1,0:T(8,128)(2,1)} %collective-permute-done.19.refs_1_.refs_5_), channel_id=1, source_target_pairs={{0,1},{1,0},{2,3},{3,2},{4,5},{5,4},{6,7},{7,6},{8,9},{9,8},{10,11... | collective-permute-start | bytes 2359304 | tf_op jit(solution)/shard_map/ppermute | solution.py:37
  69.3 4.2 %collective-permute-start.22 = (bf16[32,12288]{1,0:T(8,128)(2,1)}, bf16[32,12288]{1,0:T(8,128)(2,1)S(1)}, u32[]{:S(2)}, u32[]{:S(2)}) collective-permute-start(bf16[32,12288]{1,0:T(8,128)(2,1)} %collective-permute-done.18.refs_0_.refs_4_), channel_id=1, source_target_pairs={{0,1},{1,0},{2,3},{3,2},{4,5},{5,4},{6,7},{7,6},{8,9},{9,8},{10,11... | collective-permute-start | bytes 2359304 | tf_op jit(solution)/shard_map/ppermute | solution.py:37

commit v13 on v12

--- a/solution.py
+++ b/solution.py
@@ -421,20 +421,20 @@
     top = add(top, more)
     top, disp, own, block2 = barrier((top, disp, own, block))
     other = send(own, CORES)
-    other, source = barrier((other, trailing))
-    copy = fetch(pltpu.with_memory_space_constraint(source, pltpu.HBM))
     more = zsend(top, [(1, 0)])
     lower = zsend(disp, [(0, 2)])
     top, block2 = barrier((top, block))
     swap = send(block2, CORES)
-    more, disp, lower, copy = barrier((more, disp, lower, copy))
-    disp = choose(first, rows, (2,), disp, lower)
-    disp = choose(first, rows, (1, 3), disp, zsend(disp, [(0, 1), (2, 3)]))
-    more, disp, near, far, swap = barrier((more, disp, near, far, swap))
+    more, disp, lower, other, near, far, swap = barrier((more, disp, lower, other, near, far, swap))
     fa, fb = stack([near], 0, half, "stack_a"), stack([far], half, half, "stack_b")
     qa, qb = send(fa, up), send(fb, down)
     u = solve(me, own, other, top, more)
     ru = zsend(u, [(0, 2)])
+    u, source = barrier((u, trailing))
+    copy = fetch(pltpu.with_memory_space_constraint(source, pltpu.HBM))
+    ru, copy = barrier((ru, copy))
+    disp = choose(first, rows, (2,), disp, lower)
+    disp = choose(first, rows, (1, 3), disp, zsend(disp, [(0, 1), (2, 3)]))
     u = choose(first, rows, (2,), u, ru)
     u, near, far = barrier((u, near, far))
     other_near, other_far = send(near, CORES), send(far, CORES)

time: 81.3 us -> 83.9 us (1.032)
  waiting for transfers between devices: 16.1 us -> 19.5 us
  local copies, waits for them, and re-layouts: 4.78 us -> 1.54 us
  starting transfers between devices: 37.6 us -> 40 us
    ppermute x16, waiting for transfers between devices: 8.82 us -> 12.4 us  [send(): return lax.ppermute(block, 'pcol', pairs)]
    unnamed x24 -> x14, local copies, waits for them, and re-layouts: 4.78 us -> 1.54 us
    ppermute x8, starting transfers between devices: 13.4 us -> 15.9 us  [zsend(): return lax.ppermute(x, 'prow', pairs)]
  transfers between devices with their start and end apart: 24 -> 24, of which waited for: 9 -> 13; matrix products, arithmetic and copies ran while one was open for 0% -> 0% of each run, Pallas kernels for 17% -> 16%
where the time goes in v13:
time: 83.9 us; the launch traced here: 83.5 us
  starting transfers between devices  40 us (48%)
  Pallas kernels  22.1 us (26%)
  waiting for transfers between devices  19.5 us (23%)
  local copies, waits for them, and re-layouts  1.54 us (2%)
    ppermute x16, starting transfers between devices, send(): return lax.ppermute(block, 'pcol', pairs)  24 us
    ppermute x8, starting transfers between devices, zsend(): return lax.ppermute(x, 'prow', pairs)  15.9 us
    ppermute x16, waiting for transfers between devices, send(): return lax.ppermute(block, 'pcol', pairs)  12.4 us
    pallas_call x1, Pallas kernels, update(): pl.pallas_call(update_kernel, in_specs=[SMEM] * 5 + [VMEM] * 14, out_spec...  7.34 us
    ppermute x8, waiting for transfers between devices, zsend(): return lax.ppermute(x, 'prow', pairs)  7.11 us
    pallas_call x1, Pallas kernels, solve(): pl.pallas_call(solve_kernel, in_specs=[SMEM] + [VMEM] * 4, out_specs=VMEM...  4.25 us
    pallas_call x1, Pallas kernels, pick(): pl.pallas_call(functools.partial(pick_kernel, blk), in_specs=[SMEM, SMEM,...  3.84 us
    pallas_call x6, Pallas kernels, stack(): pl.pallas_call(functools.partial(stack_kernel, start, min(cols, 1024)), i...  3.73 us
  transfers between devices with their start and end apart: 24, of which 13 were waited for; matrix products, arithmetic and copies ran while one was open for 0% of the time, Pallas kernels for 16%

profile of v13, /device:TPU:1, one launch (start us, length us, event | category | flops | bytes accessed | tf_op | source)
XLA Modules:
  0.0 83.5 jit_solution(3658262743709098043)
XLA Ops:
  0.0 3.7 %collective-permute-start.2 = (bf16[8,24576]{1,0:T(8,128)(2,1)}, bf16[8,24576]{1,0:T(8,128)(2,1)S(1)}, u32[]{:S(2)}, u32[]{:S(2)}) collective-permute-start(bf16[8,24576]{1,0:T(8,128)(2,1)} %refs_0_.3), channel_id=1, source_target_pairs={{0,16},{1,5},{2,18},{3,7},{4,20},{5,1},{6,22},{7,3},{8,24},{9,13},... | collective-permute-start | bytes 1179656 | tf_op jit(solution)/shard_map/ppermute | solution.py:37
  3.7 0.8 collective-permute-start.1
  4.5 0.7 collective-permute-start
  5.2 0.7 copy-done.4
  5.9 3.8 %pick.1 = (bf16[256,128]{1,0:T(8,128)(2,1)S(1)}, bf16[256,128]{1,0:T(8,128)(2,1)S(1)}, s32[1]{0:T(128)}, s32[256]{0:T(256)S(1)}) custom-call(s32[256]{0:T(256)S(1)} %copy-done.4, s32[1]{0:T(128)} %bitcast.first_ref, bf16[24576,128]{1,0:T(8,128)(2,1)} %src_ref), custom_call_target="tpu_custom_call" | custom-call | flops 13200000000 | bytes 42000000 | tf_op jit(solution)/shard_map/pick/pallas_call | solution.py:184
  9.7 1.3 %collective-permute-start.6 = (bf16[256,128]{1,0:T(8,128)(2,1)S(1)}, bf16[256,128]{1,0:T(8,128)(2,1)S(1)}, u32[]{:S(2)}, u32[]{:S(2)}) collective-permute-start(bf16[256,128]{1,0:T(8,128)(2,1)S(1)} %get-tuple-element.46.a_ref), channel_id=1, source_target_pairs={{128,0},{160,32},{192,64},{224,96},{129,1},{161,33},{193,65},{225,... | collective-permute-start | bytes 196616 | tf_op jit(solution)/shard_map/ppermute | solution.py:404
  11.1 3.0 %collective-permute-done.1.refs_2_ = bf16[8,24576]{1,0:T(8,128)(2,1)S(1)} collective-permute-done((bf16[8,24576]{1,0:T(8,128)(2,1)}, bf16[8,24576]{1,0:T(8,128)(2,1)S(1)}, u32[]{:S(2)}, u32[]{:S(2)}) %collective-permute-start.1) | collective-permute-done | bytes 393248 | tf_op jit(solution)/shard_map/ppermute | solution.py:37
  14.1 2.6 %collective-permute-start.5 = (bf16[32,256]{1,0:T(8,128)(2,1)S(1)}, bf16[32,256]{1,0:T(8,128)(2,1)S(1)}, u32[]{:S(2)}, u32[]{:S(2)}) collective-permute-start(bf16[32,256]{1,0:T(8,128)(2,1)S(1)} %stack_d.1.refs_0_), channel_id=1, source_target_pairs={{0,6},{1,25},{2,0},{3,27},{4,2},{5,29},{6,4},{7,31},{8,14},{9,1},{... | collective-permute-start | bytes 49160 | tf_op jit(solution)/shard_map/ppermute | solution.py:37
  16.6 1.7 %collective-permute-start.3 = (bf16[32,256]{1,0:T(8,128)(2,1)S(1)}, bf16[32,256]{1,0:T(8,128)(2,1)S(1)}, u32[]{:S(2)}, u32[]{:S(2)}) collective-permute-start(bf16[32,256]{1,0:T(8,128)(2,1)S(1)} %stack_d.1.refs_0_), channel_id=1, source_target_pairs={{0,4},{1,17},{2,6},{3,19},{4,0},{5,21},{6,2},{7,23},{8,12},{9,25},... | collective-permute-start | bytes 49160 | tf_op jit(solution)/shard_map/ppermute | solution.py:37
  18.4 0.3 stack_p.1.refs_1_
  18.7 0.6 collective-permute-done.6.b_ref
  19.3 1.4 %collective-permute-done.4.refs_1_ = bf16[32,256]{1,0:T(8,128)(2,1)S(1)} collective-permute-done((bf16[32,256]{1,0:T(8,128)(2,1)S(1)}, bf16[32,256]{1,0:T(8,128)(2,1)S(1)}, u32[]{:S(2)}, u32[]{:S(2)}) %collective-permute-start.4) | collective-permute-done | bytes 16416 | tf_op jit(solution)/shard_map/ppermute | solution.py:37
  20.7 0.3 collective-permute-done.3.refs_3_
  21.0 2.4 %collective-permute-start.12 = (bf16[32,24576]{1,0:T(8,128)(2,1)S(1)}, bf16[32,24576]{1,0:T(8,128)(2,1)S(1)}, u32[]{:S(2)}, u32[]{:S(2)}) collective-permute-start(bf16[32,24576]{1,0:T(8,128)(2,1)S(1)} %stack_p.1.refs_1_), channel_id=1, source_target_pairs={{0,6},{1,25},{2,0},{3,27},{4,2},{5,29},{6,4},{7,31},{8,14},{9,1},{... | collective-permute-start | bytes 4718600 | tf_op jit(solution)/shard_map/ppermute | solution.py:37
  23.4 1.3 %collective-permute-start.7 = (bf16[256,128]{1,0:T(8,128)(2,1)S(1)}, bf16[256,128]{1,0:T(8,128)(2,1)S(1)}, u32[]{:S(2)}, u32[]{:S(2)}) collective-permute-start(bf16[256,128]{1,0:T(8,128)(2,1)S(1)} %add.2.a_ref), channel_id=1, source_target_pairs={{64,0},{96,32},{65,1},{97,33},{66,2},{98,34},{67,3},{99,35},{68,4}... | collective-permute-start | bytes 196616 | tf_op jit(solution)/shard_map/ppermute | solution.py:404
  24.7 4.6 %collective-permute-done.7.b_ref = bf16[256,128]{1,0:T(8,128)(2,1)S(1)} collective-permute-done((bf16[256,128]{1,0:T(8,128)(2,1)S(1)}, bf16[256,128]{1,0:T(8,128)(2,1)S(1)}, u32[]{:S(2)}, u32[]{:S(2)}) %collective-permute-start.7) | collective-permute-done | bytes 65568 | tf_op jit(solution)/shard_map/ppermute | solution.py:404
  29.4 4.7 %collective-permute-start.13 = (bf16[32,24576]{1,0:T(8,128)(2,1)S(1)}, bf16[32,24576]{1,0:T(8,128)(2,1)S(1)}, u32[]{:S(2)}, u32[]{:S(2)}) collective-permute-start(bf16[32,24576]{1,0:T(8,128)(2,1)S(1)} %stack_p.1.refs_1_), channel_id=1, source_target_pairs={{0,1},{1,0},{2,3},{3,2},{4,5},{5,4},{6,7},{7,6},{8,9},{9,8},{10,11... | collective-permute-start | bytes 4718600 | tf_op jit(solution)/shard_map/ppermute | solution.py:37
  34.1 0.1 collective-permute-start.10
  34.2 1.3 %collective-permute-start.8 = (bf16[256,128]{1,0:T(8,128)(2,1)S(1)}, bf16[256,128]{1,0:T(8,128)(2,1)S(1)}, u32[]{:S(2)}, u32[]{:S(2)}) collective-permute-start(bf16[256,128]{1,0:T(8,128)(2,1)S(1)} %add.3.top_ref), channel_id=1, source_target_pairs={{32,0},{33,1},{34,2},{35,3},{36,4},{37,5},{38,6},{39,7},{40,8},{41... | collective-permute-start | bytes 196616 | tf_op jit(solution)/shard_map/ppermute | solution.py:404
  35.5 1.7 %collective-permute-done.10.other_ref = bf16[128,256]{1,0:T(8,128)(2,1)S(1)} collective-permute-done((bf16[128,256]{1,0:T(8,128)(2,1)S(1)}, bf16[128,256]{1,0:T(8,128)(2,1)S(1)}, u32[]{:S(2)}, u32[]{:S(2)}) %collective-permute-start.10) | collective-permute-done | bytes 65568 | tf_op jit(solution)/shard_map/ppermute | solution.py:37
  37.3 1.3 %collective-permute-start.9 = (bf16[256,128]{1,0:T(8,128)(2,1)S(1)}, bf16[256,128]{1,0:T(8,128)(2,1)S(1)}, u32[]{:S(2)}, u32[]{:S(2)}) collective-permute-start(bf16[256,128]{1,0:T(8,128)(2,1)S(1)} %get-tuple-element.67.a_ref), channel_id=1, source_target_pairs={{0,64},{1,65},{2,66},{3,67},{4,68},{5,69},{6,70},{7,71},{8,72},{9,... | collective-permute-start | bytes 196616 | tf_op jit(solution)/shard_map/ppermute | solution.py:404
  38.5 1.0 %collective-permute-done.8.more_ref = bf16[256,128]{1,0:T(8,128)(2,1)S(1)} collective-permute-done((bf16[256,128]{1,0:T(8,128)(2,1)S(1)}, bf16[256,128]{1,0:T(8,128)(2,1)S(1)}, u32[]{:S(2)}, u32[]{:S(2)}) %collective-permute-start.8) | collective-permute-done | bytes 65568 | tf_op jit(solution)/shard_map/ppermute | solution.py:404
  39.5 0.3 collective-permute-done.9.b_ref
  39.9 0.9 %collective-permute-done.12.refs_0_.refs_3_ = bf16[32,24576]{1,0:T(8,128)(2,1)S(1)} collective-permute-done((bf16[32,24576]{1,0:T(8,128)(2,1)S(1)}, bf16[32,24576]{1,0:T(8,128)(2,1)S(1)}, u32[]{:S(2)}, u32[]{:S(2)}) %collective-permute-start.12) | collective-permute-done | bytes 1572896 | tf_op jit(solution)/shard_map/ppermute | solution.py:37
  40.8 3.4 %collective-permute-done.11.refs_0_.refs_2_ = bf16[32,24576]{1,0:T(8,128)(2,1)S(1)} collective-permute-done((bf16[32,24576]{1,0:T(8,128)(2,1)S(1)}, bf16[32,24576]{1,0:T(8,128)(2,1)S(1)}, u32[]{:S(2)}, u32[]{:S(2)}) %collective-permute-start.11) | collective-permute-done | bytes 1572896 | tf_op jit(solution)/shard_map/ppermute | solution.py:37
  44.2 1.1 %stack_b.1 = bf16[32,12288]{1,0:T(8,128)(2,1)} custom-call(bf16[32,24576]{1,0:T(8,128)(2,1)S(1)} %collective-permute-done.12.refs_0_.refs_3_), custom_call_target="tpu_custom_call" | custom-call | flops 1100000000 | bytes 3500000 | tf_op jit(solution)/shard_map/stack_b/pallas_call | solution.py:60
  45.3 0.4 copy-done.2
  45.6 0.0 collective-permute-start.19
  45.6 0.5 copy-done
  46.1 1.0 %stack_a.1 = bf16[32,12288]{1,0:T(8,128)(2,1)} custom-call(bf16[32,24576]{1,0:T(8,128)(2,1)S(1)} %collective-permute-done.11.refs_0_.refs_2_), custom_call_target="tpu_custom_call" | custom-call | flops 1100000000 | bytes 3500000 | tf_op jit(solution)/shard_map/stack_a/pallas_call | solution.py:60
  47.1 1.0 %collective-permute-start.18 = (bf16[32,12288]{1,0:T(8,128)(2,1)}, bf16[32,12288]{1,0:T(8,128)(2,1)}, u32[]{:S(2)}, u32[]{:S(2)}) collective-permute-start(bf16[32,12288]{1,0:T(8,128)(2,1)} %stack_a.1), channel_id=1, source_target_pairs={{0,2},{1,9},{2,4},{3,11},{4,6},{5,13},{6,0},{7,15},{8,10},{9,17},{... | collective-permute-start | bytes 2359304 | tf_op jit(solution)/shard_map/ppermute | solution.py:37
  48.1 4.2 %solve.1.a_ref = bf16[256,128]{1,0:T(8,128)(2,1)S(1)} custom-call(s32[1]{0:T(128)} %bitcast.1.me_ref, bf16[128,256]{1,0:T(8,128)(2,1)S(1)} %stack_l.1.own_ref, bf16[128,256]{1,0:T(8,128)(2,1)S(1)} %collective-permute-done.10.other_ref, bf16[256,128]{1,0:T(8,128)(2,1)S(1)} %add.3.top_ref, bf16[256,128]{1,0:T(8,128)(2,1)S(1)} %collective-permute-done.8.more_ref), custom_call_target="tpu_custom_call" | custom-call | tf_op jit(solution)/shard_map/solve/pallas_call | solution.py:278
  52.3 4.9 %collective-permute-start.14 = (bf16[256,128]{1,0:T(8,128)(2,1)S(1)}, bf16[256,128]{1,0:T(8,128)(2,1)S(1)}, u32[]{:S(2)}, u32[]{:S(2)}) collective-permute-start(bf16[256,128]{1,0:T(8,128)(2,1)S(1)} %solve.1.a_ref), channel_id=1, source_target_pairs={{0,64},{1,65},{2,66},{3,67},{4,68},{5,69},{6,70},{7,71},{8,72},{9,... | collective-permute-start | bytes 196616 | tf_op jit(solution)/shard_map/ppermute | solution.py:404
  57.3 0.0 copy-start.1
  57.3 1.4 %collective-permute-start.16 = (bf16[256,128]{1,0:T(8,128)(2,1)S(1)}, bf16[256,128]{1,0:T(8,128)(2,1)S(1)}, u32[]{:S(2)}, u32[]{:S(2)}) collective-permute-start(bf16[256,128]{1,0:T(8,128)(2,1)S(1)} %choose.4.a_ref), channel_id=1, source_target_pairs={{0,32},{64,96},{1,33},{65,97},{2,34},{66,98},{3,35},{67,99},{4,36}... | collective-permute-start | bytes 196616 | tf_op jit(solution)/shard_map/ppermute | solution.py:404
  58.7 2.9 %fetch.1.tr_ref = bf16[24576,128]{1,0:T(8,128)(2,1)S(1)} custom-call(bf16[24576,128]{1,0:T(8,128)(2,1)} %src_ref), custom_call_target="tpu_custom_call" | custom-call | tf_op jit(solution)/shard_map/fetch/pallas_call | solution.py:303
  61.6 1.3 %collective-permute-start.15 = (bf16[256,128]{1,0:T(8,128)(2,1)S(1)}, bf16[256,128]{1,0:T(8,128)(2,1)S(1)}, u32[]{:S(2)}, u32[]{:S(2)}) collective-permute-start(bf16[256,128]{1,0:T(8,128)(2,1)S(1)} %choose.3.a_ref), channel_id=1, source_target_pairs={{0,32},{64,96},{1,33},{65,97},{2,34},{66,98},{3,35},{67,99},{4,36}... | collective-permute-start | bytes 196616 | tf_op jit(solution)/shard_map/ppermute | solution.py:404
  62.9 5.3 %collective-permute-start.20 = (bf16[32,24576]{1,0:T(8,128)(2,1)S(1)}, bf16[32,24576]{1,0:T(8,128)(2,1)S(1)}, u32[]{:S(2)}, u32[]{:S(2)}) collective-permute-start(bf16[32,24576]{1,0:T(8,128)(2,1)S(1)} %copy-done.1), channel_id=1, source_target_pairs={{0,1},{1,0},{2,3},{3,2},{4,5},{5,4},{6,7},{7,6},{8,9},{9,8},{10,11... | collective-permute-start | bytes 4718600 | tf_op jit(solution)/shard_map/ppermute | solution.py:37
  68.2 0.3 collective-permute-start.21
  68.6 0.0 copy-start.5
  68.6 3.2 %collective-permute-start.17 = (bf16[512,128]{1,0:T(8,128)(2,1)S(1)}, bf16[512,128]{1,0:T(8,128)(2,1)S(1)}, u32[]{:S(2)}, u32[]{:S(2)}) collective-permute-start(bf16[512,128]{1,0:T(8,128)(2,1)S(1)} %join.1.ud_ref), channel_id=1, source_target_pairs={{0,128},{32,160},{64,192},{96,224},{1,129},{33,161},{65,193},{97,2... | collective-permute-start | bytes 393224 | tf_op jit(solution)/shard_map/ppermute | solution.py:404
  71.8 0.6 collective-permute-start.23
  72.4 0.1 collective-permute-start.22
  72.5 1.4 %stack_q.1.refs_0_ = bf16[64,128]{1,0:T(8,128)(2,1)S(1)} custom-call(bf16[32,12288]{1,0:T(8,128)(2,1)} %collective-permute-done.18.refs_0_.refs_4_, bf16[32,12288]{1,0:T(8,128)(2,1)} %collective-permute-done.19.refs_1_.refs_5_), custom_call_target="tpu_custom_call" | custom-call | flops 65999998976 | bytes 210000000 | tf_op jit(solution)/shard_map/stack_q/pallas_call | solution.py:60
  73.9 0.6 collective-permute-done.17.rest_ref
  74.4 0.4 collective-permute-done.23.refs_10_
  74.9 1.1 %collective-permute-done.22.refs_9_ = bf16[32,12288]{1,0:T(8,128)(2,1)S(1)} collective-permute-done((bf16[32,12288]{1,0:T(8,128)(2,1)}, bf16[32,12288]{1,0:T(8,128)(2,1)S(1)}, u32[]{:S(2)}, u32[]{:S(2)}) %collective-permute-start.22) | collective-permute-done | bytes 786464 | tf_op jit(solution)/shard_map/ppermute | solution.py:37
  76.0 7.3 %update.1 = (bf16[24576,128]{1,0:T(8,128)(2,1)}, bf16[24576,128]{1,0:T(8,128)(2,1)S(1)}) custom-call(s32[1]{0:T(128)} %get-tuple-element.39.cnt_ref, s32[256]{0:T(256)S(1)} %get-tuple-element.40.lst_ref, s32[256]{0:T(256)S(1)} %copy-done.5, s32[1]{0:T(128)} %bitcast.first_ref, s32[1]{0:T(128)} %bitcast.1.me_ref, ...), custom_call_target="tpu_custom_call", output_to_operand_aliasing={{1}: (5, {})} | custom-call | tf_op jit(solution)/shard_map/update/pallas_call | solution.py:377
  (30 shorter events, 0.2 us)
Async XLA Ops:
  0.0 11.0 %collective-permute-start.2 = (bf16[8,24576]{1,0:T(8,128)(2,1)}, bf16[8,24576]{1,0:T(8,128)(2,1)S(1)}, u32[]{:S(2)}, u32[]{:S(2)}) collective-permute-start(bf16[8,24576]{1,0:T(8,128)(2,1)} %refs_0_.3), channel_id=1, source_target_pairs={{0,16},{1,5},{2,18},{3,7},{4,20},{5,1},{6,22},{7,3},{8,24},{9,13},... | collective-permute-start | bytes 1179656 | tf_op jit(solution)/shard_map/ppermute | solution.py:37
  3.7 10.3 %collective-permute-start.1 = (bf16[8,24576]{1,0:T(8,128)(2,1)}, bf16[8,24576]{1,0:T(8,128)(2,1)S(1)}, u32[]{:S(2)}, u32[]{:S(2)}) collective-permute-start(bf16[8,24576]{1,0:T(8,128)(2,1)} %refs_0_.3), channel_id=1, source_target_pairs={{0,24},{1,7},{2,26},{3,1},{4,28},{5,3},{6,30},{7,5},{8,0},{9,15},{... | collective-permute-start | bytes 1179656 | tf_op jit(solution)/shard_map/ppermute | solution.py:37
  4.5 9.5 %collective-permute-start = (bf16[8,24576]{1,0:T(8,128)(2,1)}, bf16[8,24576]{1,0:T(8,128)(2,1)S(1)}, u32[]{:S(2)}, u32[]{:S(2)}) collective-permute-start(bf16[8,24576]{1,0:T(8,128)(2,1)} %refs_0_.3), channel_id=1, source_target_pairs={{0,8},{1,3},{2,10},{3,5},{4,12},{5,7},{6,14},{7,1},{8,16},{9,11},{... | collective-permute-start | bytes 1179656 | tf_op jit(solution)/shard_map/ppermute | solution.py:37
  5.2 0.7 copy-start.4
  5.9 8.2 %copy-start.6 = (bf16[8,24576]{1,0:T(8,128)(2,1)S(1)}, bf16[8,24576]{1,0:T(8,128)(2,1)}, u32[]{:S(2)}) copy-start(bf16[8,24576]{1,0:T(8,128)(2,1)} %refs_0_.3) | copy-start | bytes 1179652
  9.7 9.6 %collective-permute-start.6 = (bf16[256,128]{1,0:T(8,128)(2,1)S(1)}, bf16[256,128]{1,0:T(8,128)(2,1)S(1)}, u32[]{:S(2)}, u32[]{:S(2)}) collective-permute-start(bf16[256,128]{1,0:T(8,128)(2,1)S(1)} %get-tuple-element.46.a_ref), channel_id=1, source_target_pairs={{128,0},{160,32},{192,64},{224,96},{129,1},{161,33},{193,65},{225,... | collective-permute-start | bytes 196616 | tf_op jit(solution)/shard_map/ppermute | solution.py:404
  14.1 5.2 %collective-permute-start.5 = (bf16[32,256]{1,0:T(8,128)(2,1)S(1)}, bf16[32,256]{1,0:T(8,128)(2,1)S(1)}, u32[]{:S(2)}, u32[]{:S(2)}) collective-permute-start(bf16[32,256]{1,0:T(8,128)(2,1)S(1)} %stack_d.1.refs_0_), channel_id=1, source_target_pairs={{0,6},{1,25},{2,0},{3,27},{4,2},{5,29},{6,4},{7,31},{8,14},{9,1},{... | collective-permute-start | bytes 49160 | tf_op jit(solution)/shard_map/ppermute | solution.py:37
  16.6 4.1 %collective-permute-start.4 = (bf16[32,256]{1,0:T(8,128)(2,1)S(1)}, bf16[32,256]{1,0:T(8,128)(2,1)S(1)}, u32[]{:S(2)}, u32[]{:S(2)}) collective-permute-start(bf16[32,256]{1,0:T(8,128)(2,1)S(1)} %stack_d.1.refs_0_), channel_id=1, source_target_pairs={{0,2},{1,9},{2,4},{3,11},{4,6},{5,13},{6,0},{7,15},{8,10},{9,17},{... | collective-permute-start | bytes 49160 | tf_op jit(solution)/shard_map/ppermute | solution.py:37
  16.6 4.4 %collective-permute-start.3 = (bf16[32,256]{1,0:T(8,128)(2,1)S(1)}, bf16[32,256]{1,0:T(8,128)(2,1)S(1)}, u32[]{:S(2)}, u32[]{:S(2)}) collective-permute-start(bf16[32,256]{1,0:T(8,128)(2,1)S(1)} %stack_d.1.refs_0_), channel_id=1, source_target_pairs={{0,4},{1,17},{2,6},{3,19},{4,0},{5,21},{6,2},{7,23},{8,12},{9,25},... | collective-permute-start | bytes 49160 | tf_op jit(solution)/shard_map/ppermute | solution.py:37
  21.0 19.7 %collective-permute-start.12 = (bf16[32,24576]{1,0:T(8,128)(2,1)S(1)}, bf16[32,24576]{1,0:T(8,128)(2,1)S(1)}, u32[]{:S(2)}, u32[]{:S(2)}) collective-permute-start(bf16[32,24576]{1,0:T(8,128)(2,1)S(1)} %stack_p.1.refs_1_), channel_id=1, source_target_pairs={{0,6},{1,25},{2,0},{3,27},{4,2},{5,29},{6,4},{7,31},{8,14},{9,1},{... | collective-permute-start | bytes 4718600 | tf_op jit(solution)/shard_map/ppermute | solution.py:37
  23.4 20.8 %collective-permute-start.11 = (bf16[32,24576]{1,0:T(8,128)(2,1)S(1)}, bf16[32,24576]{1,0:T(8,128)(2,1)S(1)}, u32[]{:S(2)}, u32[]{:S(2)}) collective-permute-start(bf16[32,24576]{1,0:T(8,128)(2,1)S(1)} %stack_p.1.refs_1_), channel_id=1, source_target_pairs={{0,2},{1,9},{2,4},{3,11},{4,6},{5,13},{6,0},{7,15},{8,10},{9,17},{... | collective-permute-start | bytes 4718600 | tf_op jit(solution)/shard_map/ppermute | solution.py:37
  23.4 5.9 %collective-permute-start.7 = (bf16[256,128]{1,0:T(8,128)(2,1)S(1)}, bf16[256,128]{1,0:T(8,128)(2,1)S(1)}, u32[]{:S(2)}, u32[]{:S(2)}) collective-permute-start(bf16[256,128]{1,0:T(8,128)(2,1)S(1)} %add.2.a_ref), channel_id=1, source_target_pairs={{64,0},{96,32},{65,1},{97,33},{66,2},{98,34},{67,3},{99,35},{68,4}... | collective-permute-start | bytes 196616 | tf_op jit(solution)/shard_map/ppermute | solution.py:404
  29.4 14.8 %collective-permute-start.13 = (bf16[32,24576]{1,0:T(8,128)(2,1)S(1)}, bf16[32,24576]{1,0:T(8,128)(2,1)S(1)}, u32[]{:S(2)}, u32[]{:S(2)}) collective-permute-start(bf16[32,24576]{1,0:T(8,128)(2,1)S(1)} %stack_p.1.refs_1_), channel_id=1, source_target_pairs={{0,1},{1,0},{2,3},{3,2},{4,5},{5,4},{6,7},{7,6},{8,9},{9,8},{10,11... | collective-permute-start | bytes 4718600 | tf_op jit(solution)/shard_map/ppermute | solution.py:37
  34.1 3.1 %collective-permute-start.10 = (bf16[128,256]{1,0:T(8,128)(2,1)S(1)}, bf16[128,256]{1,0:T(8,128)(2,1)S(1)}, u32[]{:S(2)}, u32[]{:S(2)}) collective-permute-start(bf16[128,256]{1,0:T(8,128)(2,1)S(1)} %stack_l.1.own_ref), channel_id=1, source_target_pairs={{0,1},{1,0},{2,3},{3,2},{4,5},{5,4},{6,7},{7,6},{8,9},{9,8},{10,11... | collective-permute-start | bytes 196616 | tf_op jit(solution)/shard_map/ppermute | solution.py:37
  34.2 5.3 %collective-permute-start.8 = (bf16[256,128]{1,0:T(8,128)(2,1)S(1)}, bf16[256,128]{1,0:T(8,128)(2,1)S(1)}, u32[]{:S(2)}, u32[]{:S(2)}) collective-permute-start(bf16[256,128]{1,0:T(8,128)(2,1)S(1)} %add.3.top_ref), channel_id=1, source_target_pairs={{32,0},{33,1},{34,2},{35,3},{36,4},{37,5},{38,6},{39,7},{40,8},{41... | collective-permute-start | bytes 196616 | tf_op jit(solution)/shard_map/ppermute | solution.py:404
  37.3 2.6 %collective-permute-start.9 = (bf16[256,128]{1,0:T(8,128)(2,1)S(1)}, bf16[256,128]{1,0:T(8,128)(2,1)S(1)}, u32[]{:S(2)}, u32[]{:S(2)}) collective-permute-start(bf16[256,128]{1,0:T(8,128)(2,1)S(1)} %get-tuple-element.67.a_ref), channel_id=1, source_target_pairs={{0,64},{1,65},{2,66},{3,67},{4,68},{5,69},{6,70},{7,71},{8,72},{9,... | collective-permute-start | bytes 196616 | tf_op jit(solution)/shard_map/ppermute | solution.py:404
  44.2 1.9 %copy-start = (bf16[32,24576]{1,0:T(8,128)(2,1)}, bf16[32,24576]{1,0:T(8,128)(2,1)S(1)}, u32[]{:S(2)}) copy-start(bf16[32,24576]{1,0:T(8,128)(2,1)S(1)} %collective-permute-done.11.refs_0_.refs_2_) | copy-start | bytes 4718596
  44.2 1.4 %copy-start.2 = (bf16[32,24576]{1,0:T(8,128)(2,1)}, bf16[32,24576]{1,0:T(8,128)(2,1)S(1)}, u32[]{:S(2)}) copy-start(bf16[32,24576]{1,0:T(8,128)(2,1)S(1)} %collective-permute-done.13.refs_6_) | copy-start | bytes 4718596
  45.6 26.2 %collective-permute-start.19 = (bf16[32,12288]{1,0:T(8,128)(2,1)}, bf16[32,12288]{1,0:T(8,128)(2,1)}, u32[]{:S(2)}, u32[]{:S(2)}) collective-permute-start(bf16[32,12288]{1,0:T(8,128)(2,1)} %stack_b.1), channel_id=1, source_target_pairs={{0,6},{1,25},{2,0},{3,27},{4,2},{5,29},{6,4},{7,31},{8,14},{9,1},{... | collective-permute-start | bytes 2359304 | tf_op jit(solution)/shard_map/ppermute | solution.py:37
  47.1 25.3 %collective-permute-start.18 = (bf16[32,12288]{1,0:T(8,128)(2,1)}, bf16[32,12288]{1,0:T(8,128)(2,1)}, u32[]{:S(2)}, u32[]{:S(2)}) collective-permute-start(bf16[32,12288]{1,0:T(8,128)(2,1)} %stack_a.1), channel_id=1, source_target_pairs={{0,2},{1,9},{2,4},{3,11},{4,6},{5,13},{6,0},{7,15},{8,10},{9,17},{... | collective-permute-start | bytes 2359304 | tf_op jit(solution)/shard_map/ppermute | solution.py:37
  52.3 9.3 %collective-permute-start.14 = (bf16[256,128]{1,0:T(8,128)(2,1)S(1)}, bf16[256,128]{1,0:T(8,128)(2,1)S(1)}, u32[]{:S(2)}, u32[]{:S(2)}) collective-permute-start(bf16[256,128]{1,0:T(8,128)(2,1)S(1)} %solve.1.a_ref), channel_id=1, source_target_pairs={{0,64},{1,65},{2,66},{3,67},{4,68},{5,69},{6,70},{7,71},{8,72},{9,... | collective-permute-start | bytes 196616 | tf_op jit(solution)/shard_map/ppermute | solution.py:404
  57.3 5.7 %copy-start.1 = (bf16[32,24576]{1,0:T(8,128)(2,1)S(1)}, bf16[32,24576]{1,0:T(8,128)(2,1)}, u32[]{:S(2)}) copy-start(bf16[32,24576]{1,0:T(8,128)(2,1)} %copy-done) | copy-start | bytes 4718596
  57.3 11.0 %collective-permute-start.16 = (bf16[256,128]{1,0:T(8,128)(2,1)S(1)}, bf16[256,128]{1,0:T(8,128)(2,1)S(1)}, u32[]{:S(2)}, u32[]{:S(2)}) collective-permute-start(bf16[256,128]{1,0:T(8,128)(2,1)S(1)} %choose.4.a_ref), channel_id=1, source_target_pairs={{0,32},{64,96},{1,33},{65,97},{2,34},{66,98},{3,35},{67,99},{4,36}... | collective-permute-start | bytes 196616 | tf_op jit(solution)/shard_map/ppermute | solution.py:404
  61.6 6.9 %collective-permute-start.15 = (bf16[256,128]{1,0:T(8,128)(2,1)S(1)}, bf16[256,128]{1,0:T(8,128)(2,1)S(1)}, u32[]{:S(2)}, u32[]{:S(2)}) collective-permute-start(bf16[256,128]{1,0:T(8,128)(2,1)S(1)} %choose.3.a_ref), channel_id=1, source_target_pairs={{0,32},{64,96},{1,33},{65,97},{2,34},{66,98},{3,35},{67,99},{4,36}... | collective-permute-start | bytes 196616 | tf_op jit(solution)/shard_map/ppermute | solution.py:404
  62.9 13.1 %collective-permute-start.20 = (bf16[32,24576]{1,0:T(8,128)(2,1)S(1)}, bf16[32,24576]{1,0:T(8,128)(2,1)S(1)}, u32[]{:S(2)}, u32[]{:S(2)}) collective-permute-start(bf16[32,24576]{1,0:T(8,128)(2,1)S(1)} %copy-done.1), channel_id=1, source_target_pairs={{0,1},{1,0},{2,3},{3,2},{4,5},{5,4},{6,7},{7,6},{8,9},{9,8},{10,11... | collective-permute-start | bytes 4718600 | tf_op jit(solution)/shard_map/ppermute | solution.py:37
  68.2 7.7 %collective-permute-start.21 = (bf16[32,24576]{1,0:T(8,128)(2,1)S(1)}, bf16[32,24576]{1,0:T(8,128)(2,1)S(1)}, u32[]{:S(2)}, u32[]{:S(2)}) collective-permute-start(bf16[32,24576]{1,0:T(8,128)(2,1)S(1)} %collective-permute-done.12.refs_0_.refs_3_), channel_id=1, source_target_pairs={{0,1},{1,0},{2,3},{3,2},{4,5},{5,4},{6,7},{7,6},{8,9},{9,8},{10,11... | collective-permute-start | bytes 4718600 | tf_op jit(solution)/shard_map/ppermute | solution.py:37
  68.6 7.4 %copy-start.3 = (bf16[32,24576]{1,0:T(8,128)(2,1)S(1)}, bf16[32,24576]{1,0:T(8,128)(2,1)}, u32[]{:S(2)}) copy-start(bf16[32,24576]{1,0:T(8,128)(2,1)} %copy-done.2) | copy-start | bytes 4718596
  68.6 7.4 %copy-start.5 = (s32[256]{0:T(256)S(1)}, s32[256]{0:T(256)}, u32[]{:S(2)}) copy-start(s32[256]{0:T(256)} %piv_ref.3) | copy-start | bytes 3076
  68.6 5.8 %collective-permute-start.17 = (bf16[512,128]{1,0:T(8,128)(2,1)S(1)}, bf16[512,128]{1,0:T(8,128)(2,1)S(1)}, u32[]{:S(2)}, u32[]{:S(2)}) collective-permute-start(bf16[512,128]{1,0:T(8,128)(2,1)S(1)} %join.1.ud_ref), channel_id=1, source_target_pairs={{0,128},{32,160},{64,192},{96,224},{1,129},{33,161},{65,193},{97,2... | collective-permute-start | bytes 393224 | tf_op jit(solution)/shard_map/ppermute | solution.py:404
  71.8 3.1 %collective-permute-start.23 = (bf16[32,12288]{1,0:T(8,128)(2,1)}, bf16[32,12288]{1,0:T(8,128)(2,1)S(1)}, u32[]{:S(2)}, u32[]{:S(2)}) collective-permute-start(bf16[32,12288]{1,0:T(8,128)(2,1)} %collective-permute-done.19.refs_1_.refs_5_), channel_id=1, source_target_pairs={{0,1},{1,0},{2,3},{3,2},{4,5},{5,4},{6,7},{7,6},{8,9},{9,8},{10,11... | collective-permute-start | bytes 2359304 | tf_op jit(solution)/shard_map/ppermute | solution.py:37
  72.4 3.6 %collective-permute-start.22 = (bf16[32,12288]{1,0:T(8,128)(2,1)}, bf16[32,12288]{1,0:T(8,128)(2,1)S(1)}, u32[]{:S(2)}, u32[]{:S(2)}) collective-permute-start(bf16[32,12288]{1,0:T(8,128)(2,1)} %collective-permute-done.18.refs_0_.refs_4_), channel_id=1, source_target_pairs={{0,1},{1,0},{2,3},{3,2},{4,5},{5,4},{6,7},{7,6},{8,9},{9,8},{10,11... | collective-permute-start | bytes 2359304 | tf_op jit(solution)/shard_map/ppermute | solution.py:37

commit v14 on v11

--- a/solution.py
+++ b/solution.py
@@ -418,10 +418,9 @@
     own = stack([diag, diag_p, diag_m, diag_q], 0, width, "stack_l")
     top = add(top, more)
     more = zsend(top, [(2, 0), (3, 1)])
+    other = send(own, CORES)
     top = add(top, more)
-    top, disp, own = barrier((top, disp, own))
-    other = send(own, CORES)
-    other, source = barrier((other, trailing))
+    top, disp, other, source = barrier((top, disp, other, trailing))
     copy = fetch(pltpu.with_memory_space_constraint(source, pltpu.HBM))
     more = zsend(top, [(1, 0)])
     lower = zsend(disp, [(0, 2)])

time: 81.8 us -> 78.8 us (0.963)
  waiting for transfers between devices: 18 us -> 12.6 us
  starting transfers between devices: 41.8 us -> 44.7 us
    ppermute x8, starting transfers between devices: 12.5 us -> 17.5 us  [zsend(): return lax.ppermute(x, 'prow', pairs)]
    ppermute x8, waiting for transfers between devices: 8.22 us -> 3.47 us  [zsend(): return lax.ppermute(x, 'prow', pairs)]
    ppermute x16, starting transfers between devices: 29.2 us -> 27.2 us  [send(): return lax.ppermute(block, 'pcol', pairs)]
where the time goes in v14:
time: 78.8 us; the launch traced here: 78.5 us
  starting transfers between devices  44.7 us (57%)
  Pallas kernels  20 us (25%)
  waiting for transfers between devices  12.6 us (16%)
    ppermute x16, starting transfers between devices, send(): return lax.ppermute(block, 'pcol', pairs)  27.2 us
    ppermute x8, starting transfers between devices, zsend(): return lax.ppermute(x, 'prow', pairs)  17.5 us
    ppermute x16, waiting for transfers between devices, send(): return lax.ppermute(block, 'pcol', pairs)  9.13 us
    pallas_call x1, Pallas kernels, update(): pl.pallas_call(update_kernel, in_specs=[SMEM] * 5 + [VMEM] * 14, out_spec...  7.52 us
    pallas_call x1, Pallas kernels, solve(): pl.pallas_call(solve_kernel, in_specs=[SMEM] + [VMEM] * 4, out_specs=VMEM...  4.26 us
    ppermute x8, waiting for transfers between devices, zsend(): return lax.ppermute(x, 'prow', pairs)  3.47 us
    pallas_call x1, Pallas kernels, pick(): pl.pallas_call(functools.partial(pick_kernel, blk), in_specs=[SMEM, SMEM,...  3.4 us
    pallas_call x1, Pallas kernels, fetch(): pl.pallas_call(fetch_kernel, in_specs=[pl.BlockSpec(memory_space=pltpu.HB...  2.87 us
  transfers between devices with their start and end apart: 24, of which 10 were waited for; matrix products, arithmetic and copies ran while one was open for 0% of the time, Pallas kernels for 16%

profile of v14, /device:TPU:1, one launch (start us, length us, event | category | flops | bytes accessed | tf_op | source)
XLA Modules:
  0.0 78.5 jit_solution(9151730270036872224)
XLA Ops:
  0.0 3.7 %collective-permute-start.2 = (bf16[8,24576]{1,0:T(8,128)(2,1)}, bf16[8,24576]{1,0:T(8,128)(2,1)S(1)}, u32[]{:S(2)}, u32[]{:S(2)}) collective-permute-start(bf16[8,24576]{1,0:T(8,128)(2,1)} %refs_0_.3), channel_id=1, source_target_pairs={{0,16},{1,5},{2,18},{3,7},{4,20},{5,1},{6,22},{7,3},{8,24},{9,13},... | collective-permute-start | bytes 1179656 | tf_op jit(solution)/shard_map/ppermute | solution.py:37
  3.7 0.8 collective-permute-start.1
  4.5 0.7 collective-permute-start
  5.2 0.7 copy-done
  5.9 3.4 %pick.1 = (bf16[256,128]{1,0:T(8,128)(2,1)S(1)}, bf16[256,128]{1,0:T(8,128)(2,1)S(1)}, s32[1]{0:T(128)}, s32[256]{0:T(256)S(1)}) custom-call(s32[256]{0:T(256)S(1)} %copy-done, s32[1]{0:T(128)} %bitcast.first_ref, bf16[24576,128]{1,0:T(8,128)(2,1)} %src_ref), custom_call_target="tpu_custom_call" | custom-call | flops 13200000000 | bytes 42000000 | tf_op jit(solution)/shard_map/pick/pallas_call | solution.py:184
  9.3 1.3 %collective-permute-start.6 = (bf16[256,128]{1,0:T(8,128)(2,1)S(1)}, bf16[256,128]{1,0:T(8,128)(2,1)S(1)}, u32[]{:S(2)}, u32[]{:S(2)}) collective-permute-start(bf16[256,128]{1,0:T(8,128)(2,1)S(1)} %get-tuple-element.49.a_ref), channel_id=1, source_target_pairs={{128,0},{160,32},{192,64},{224,96},{129,1},{161,33},{193,65},{225,... | collective-permute-start | bytes 196616 | tf_op jit(solution)/shard_map/ppermute | solution.py:404
  10.6 0.0 collective-permute-done.2.refs_3_
  10.6 3.5 %collective-permute-done.1.refs_2_ = bf16[8,24576]{1,0:T(8,128)(2,1)S(1)} collective-permute-done((bf16[8,24576]{1,0:T(8,128)(2,1)}, bf16[8,24576]{1,0:T(8,128)(2,1)S(1)}, u32[]{:S(2)}, u32[]{:S(2)}) %collective-permute-start.1) | collective-permute-done | bytes 393248 | tf_op jit(solution)/shard_map/ppermute | solution.py:37
  14.1 2.6 %collective-permute-start.5 = (bf16[32,256]{1,0:T(8,128)(2,1)S(1)}, bf16[32,256]{1,0:T(8,128)(2,1)S(1)}, u32[]{:S(2)}, u32[]{:S(2)}) collective-permute-start(bf16[32,256]{1,0:T(8,128)(2,1)S(1)} %stack_d.1.refs_0_), channel_id=1, source_target_pairs={{0,6},{1,25},{2,0},{3,27},{4,2},{5,29},{6,4},{7,31},{8,14},{9,1},{... | collective-permute-start | bytes 49160 | tf_op jit(solution)/shard_map/ppermute | solution.py:37
  16.6 0.0 collective-permute-start.4
  16.6 1.7 %collective-permute-start.3 = (bf16[32,256]{1,0:T(8,128)(2,1)S(1)}, bf16[32,256]{1,0:T(8,128)(2,1)S(1)}, u32[]{:S(2)}, u32[]{:S(2)}) collective-permute-start(bf16[32,256]{1,0:T(8,128)(2,1)S(1)} %stack_d.1.refs_0_), channel_id=1, source_target_pairs={{0,4},{1,17},{2,6},{3,19},{4,0},{5,21},{6,2},{7,23},{8,12},{9,25},... | collective-permute-start | bytes 49160 | tf_op jit(solution)/shard_map/ppermute | solution.py:37
  18.4 0.3 stack_p.1.refs_1_
  18.7 0.9 %collective-permute-done.6.b_ref = bf16[256,128]{1,0:T(8,128)(2,1)S(1)} collective-permute-done((bf16[256,128]{1,0:T(8,128)(2,1)S(1)}, bf16[256,128]{1,0:T(8,128)(2,1)S(1)}, u32[]{:S(2)}, u32[]{:S(2)}) %collective-permute-start.6) | collective-permute-done | bytes 65568 | tf_op jit(solution)/shard_map/ppermute | solution.py:404
  19.6 0.0 collective-permute-done.5.refs_2_
  19.6 1.2 %collective-permute-done.4.refs_1_ = bf16[32,256]{1,0:T(8,128)(2,1)S(1)} collective-permute-done((bf16[32,256]{1,0:T(8,128)(2,1)S(1)}, bf16[32,256]{1,0:T(8,128)(2,1)S(1)}, u32[]{:S(2)}, u32[]{:S(2)}) %collective-permute-start.4) | collective-permute-done | bytes 16416 | tf_op jit(solution)/shard_map/ppermute | solution.py:37
  20.7 0.3 collective-permute-done.3.refs_3_
  21.1 1.3 %collective-permute-start.7 = (bf16[256,128]{1,0:T(8,128)(2,1)S(1)}, bf16[256,128]{1,0:T(8,128)(2,1)S(1)}, u32[]{:S(2)}, u32[]{:S(2)}) collective-permute-start(bf16[256,128]{1,0:T(8,128)(2,1)S(1)} %add.2.a_ref), channel_id=1, source_target_pairs={{64,0},{96,32},{65,1},{97,33},{66,2},{98,34},{67,3},{99,35},{68,4}... | collective-permute-start | bytes 196616 | tf_op jit(solution)/shard_map/ppermute | solution.py:404
  22.4 3.4 %collective-permute-start.8 = (bf16[128,256]{1,0:T(8,128)(2,1)S(1)}, bf16[128,256]{1,0:T(8,128)(2,1)S(1)}, u32[]{:S(2)}, u32[]{:S(2)}) collective-permute-start(bf16[128,256]{1,0:T(8,128)(2,1)S(1)} %stack_l.1.own_ref), channel_id=1, source_target_pairs={{0,1},{1,0},{2,3},{3,2},{4,5},{5,4},{6,7},{7,6},{8,9},{9,8},{10,11... | collective-permute-start | bytes 196616 | tf_op jit(solution)/shard_map/ppermute | solution.py:37
  25.7 1.7 %collective-permute-start.13 = (bf16[32,24576]{1,0:T(8,128)(2,1)S(1)}, bf16[32,24576]{1,0:T(8,128)(2,1)S(1)}, u32[]{:S(2)}, u32[]{:S(2)}) collective-permute-start(bf16[32,24576]{1,0:T(8,128)(2,1)S(1)} %stack_p.1.refs_1_), channel_id=1, source_target_pairs={{0,6},{1,25},{2,0},{3,27},{4,2},{5,29},{6,4},{7,31},{8,14},{9,1},{... | collective-permute-start | bytes 4718600 | tf_op jit(solution)/shard_map/ppermute | solution.py:37
  27.5 0.0 collective-permute-start.12
  27.5 0.0 collective-permute-done.7.b_ref
  27.5 0.0 collective-permute-done.8.other_ref
  27.5 4.0 %collective-permute-start.14 = (bf16[32,24576]{1,0:T(8,128)(2,1)S(1)}, bf16[32,24576]{1,0:T(8,128)(2,1)}, u32[]{:S(2)}, u32[]{:S(2)}) collective-permute-start(bf16[32,24576]{1,0:T(8,128)(2,1)S(1)} %stack_p.1.refs_1_), channel_id=1, source_target_pairs={{0,1},{1,0},{2,3},{3,2},{4,5},{5,4},{6,7},{7,6},{8,9},{9,8},{10,11... | collective-permute-start | bytes 4718600 | tf_op jit(solution)/shard_map/ppermute | solution.py:37
  31.5 1.3 %collective-permute-start.9 = (bf16[256,128]{1,0:T(8,128)(2,1)S(1)}, bf16[256,128]{1,0:T(8,128)(2,1)S(1)}, u32[]{:S(2)}, u32[]{:S(2)}) collective-permute-start(bf16[256,128]{1,0:T(8,128)(2,1)S(1)} %add.3.top_ref), channel_id=1, source_target_pairs={{32,0},{33,1},{34,2},{35,3},{36,4},{37,5},{38,6},{39,7},{40,8},{41... | collective-permute-start | bytes 196616 | tf_op jit(solution)/shard_map/ppermute | solution.py:404
  32.8 1.6 %collective-permute-start.10 = (bf16[256,128]{1,0:T(8,128)(2,1)S(1)}, bf16[256,128]{1,0:T(8,128)(2,1)S(1)}, u32[]{:S(2)}, u32[]{:S(2)}) collective-permute-start(bf16[256,128]{1,0:T(8,128)(2,1)S(1)} %get-tuple-element.60.a_ref), channel_id=1, source_target_pairs={{0,64},{1,65},{2,66},{3,67},{4,68},{5,69},{6,70},{7,71},{8,72},{9,... | collective-permute-start | bytes 196616 | tf_op jit(solution)/shard_map/ppermute | solution.py:404
  34.4 2.9 %fetch.1.tr_ref = bf16[24576,128]{1,0:T(8,128)(2,1)S(1)} custom-call(bf16[24576,128]{1,0:T(8,128)(2,1)} %src_ref), custom_call_target="tpu_custom_call" | custom-call | tf_op jit(solution)/shard_map/fetch/pallas_call | solution.py:303
  37.3 0.0 collective-permute-done.10.b_ref
  37.3 3.0 %collective-permute-start.15 = (bf16[256,128]{1,0:T(8,128)(2,1)S(1)}, bf16[256,128]{1,0:T(8,128)(2,1)S(1)}, u32[]{:S(2)}, u32[]{:S(2)}) collective-permute-start(bf16[256,128]{1,0:T(8,128)(2,1)S(1)} %choose.3.a_ref), channel_id=1, source_target_pairs={{0,32},{64,96},{1,33},{65,97},{2,34},{66,98},{3,35},{67,99},{4,36}... | collective-permute-start | bytes 196616 | tf_op jit(solution)/shard_map/ppermute | solution.py:404
  40.4 4.3 %solve.1.a_ref = bf16[256,128]{1,0:T(8,128)(2,1)S(1)} custom-call(s32[1]{0:T(128)} %bitcast.1.me_ref, bf16[128,256]{1,0:T(8,128)(2,1)S(1)} %stack_l.1.own_ref, bf16[128,256]{1,0:T(8,128)(2,1)S(1)} %collective-permute-done.8.other_ref, bf16[256,128]{1,0:T(8,128)(2,1)S(1)} %add.3.top_ref, bf16[256,128]{1,0:T(8,128)(2,1)S(1)} %collective-permute-done.9.more_ref), custom_call_target="tpu_custom_call" | custom-call | tf_op jit(solution)/shard_map/solve/pallas_call | solution.py:278
  44.7 1.9 %collective-permute-start.11 = (bf16[256,128]{1,0:T(8,128)(2,1)S(1)}, bf16[256,128]{1,0:T(8,128)(2,1)S(1)}, u32[]{:S(2)}, u32[]{:S(2)}) collective-permute-start(bf16[256,128]{1,0:T(8,128)(2,1)S(1)} %solve.1.a_ref), channel_id=1, source_target_pairs={{0,64},{1,65},{2,66},{3,67},{4,68},{5,69},{6,70},{7,71},{8,72},{9,... | collective-permute-start | bytes 196616 | tf_op jit(solution)/shard_map/ppermute | solution.py:404
  46.6 1.3 %collective-permute-done.11.b_ref = bf16[256,128]{1,0:T(8,128)(2,1)S(1)} collective-permute-done((bf16[256,128]{1,0:T(8,128)(2,1)S(1)}, bf16[256,128]{1,0:T(8,128)(2,1)S(1)}, u32[]{:S(2)}, u32[]{:S(2)}) %collective-permute-start.11) | collective-permute-done | bytes 65568 | tf_op jit(solution)/shard_map/ppermute | solution.py:404
  47.9 0.5 collective-permute-done.12.refs_0_.refs_2_
  48.3 0.1 stack_b.1
  48.4 2.0 %collective-permute-start.19 = (bf16[32,12288]{1,0:T(8,128)(2,1)S(1)}, bf16[32,12288]{1,0:T(8,128)(2,1)S(1)}, u32[]{:S(2)}, u32[]{:S(2)}) collective-permute-start(bf16[32,12288]{1,0:T(8,128)(2,1)S(1)} %stack_b.1), channel_id=1, source_target_pairs={{0,6},{1,25},{2,0},{3,27},{4,2},{5,29},{6,4},{7,31},{8,14},{9,1},{... | collective-permute-start | bytes 2359304 | tf_op jit(solution)/shard_map/ppermute | solution.py:37
  50.4 1.5 %stack_a.1 = bf16[32,12288]{1,0:T(8,128)(2,1)S(1)} custom-call(bf16[32,24576]{1,0:T(8,128)(2,1)} %collective-permute-done.12.refs_0_.refs_2_), custom_call_target="tpu_custom_call" | custom-call | flops 1100000000 | bytes 3500000 | tf_op jit(solution)/shard_map/stack_a/pallas_call | solution.py:60
  51.9 0.1 collective-permute-start.18
  52.0 3.1 %collective-permute-start.16 = (bf16[256,128]{1,0:T(8,128)(2,1)S(1)}, bf16[256,128]{1,0:T(8,128)(2,1)S(1)}, u32[]{:S(2)}, u32[]{:S(2)}) collective-permute-start(bf16[256,128]{1,0:T(8,128)(2,1)S(1)} %choose.5.a_ref), channel_id=1, source_target_pairs={{0,32},{64,96},{1,33},{65,97},{2,34},{66,98},{3,35},{67,99},{4,36}... | collective-permute-start | bytes 196616 | tf_op jit(solution)/shard_map/ppermute | solution.py:404
  55.1 1.3 %collective-permute-done.16.b_ref = bf16[256,128]{1,0:T(8,128)(2,1)S(1)} collective-permute-done((bf16[256,128]{1,0:T(8,128)(2,1)S(1)}, bf16[256,128]{1,0:T(8,128)(2,1)S(1)}, u32[]{:S(2)}, u32[]{:S(2)}) %collective-permute-start.16) | collective-permute-done | bytes 65568 | tf_op jit(solution)/shard_map/ppermute | solution.py:404
  56.4 0.0 copy-start.1
  56.4 4.0 %collective-permute-start.17 = (bf16[512,128]{1,0:T(8,128)(2,1)S(1)}, bf16[512,128]{1,0:T(8,128)(2,1)S(1)}, u32[]{:S(2)}, u32[]{:S(2)}) collective-permute-start(bf16[512,128]{1,0:T(8,128)(2,1)S(1)} %join.1.ud_ref), channel_id=1, source_target_pairs={{0,128},{32,160},{64,192},{96,224},{1,129},{33,161},{65,193},{97,2... | collective-permute-start | bytes 393224 | tf_op jit(solution)/shard_map/ppermute | solution.py:404
  60.5 2.8 %collective-permute-start.20 = (bf16[32,24576]{1,0:T(8,128)(2,1)}, bf16[32,24576]{1,0:T(8,128)(2,1)S(1)}, u32[]{:S(2)}, u32[]{:S(2)}) collective-permute-start(bf16[32,24576]{1,0:T(8,128)(2,1)} %collective-permute-done.12.refs_0_.refs_2_), channel_id=1, source_target_pairs={{0,1},{1,0},{2,3},{3,2},{4,5},{5,4},{6,7},{7,6},{8,9},{9,8},{10,11... | collective-permute-start | bytes 4718600 | tf_op jit(solution)/shard_map/ppermute | solution.py:37
  63.2 0.3 collective-permute-start.21
  63.5 0.2 collective-permute-start.23
  63.7 0.6 collective-permute-done.18.refs_0_.refs_4_
  64.3 3.3 %collective-permute-start.22 = (bf16[32,12288]{1,0:T(8,128)(2,1)S(1)}, bf16[32,12288]{1,0:T(8,128)(2,1)S(1)}, u32[]{:S(2)}, u32[]{:S(2)}) collective-permute-start(bf16[32,12288]{1,0:T(8,128)(2,1)S(1)} %collective-permute-done.18.refs_0_.refs_4_), channel_id=1, source_target_pairs={{0,1},{1,0},{2,3},{3,2},{4,5},{5,4},{6,7},{7,6},{8,9},{9,8},{10,11... | collective-permute-start | bytes 2359304 | tf_op jit(solution)/shard_map/ppermute | solution.py:37
  67.6 2.0 %collective-permute-done.23.refs_10_ = bf16[32,12288]{1,0:T(8,128)(2,1)S(1)} collective-permute-done((bf16[32,12288]{1,0:T(8,128)(2,1)S(1)}, bf16[32,12288]{1,0:T(8,128)(2,1)S(1)}, u32[]{:S(2)}, u32[]{:S(2)}) %collective-permute-start.23) | collective-permute-done | bytes 786464 | tf_op jit(solution)/shard_map/ppermute | solution.py:37
  69.6 1.1 %collective-permute-done.22.refs_9_ = bf16[32,12288]{1,0:T(8,128)(2,1)S(1)} collective-permute-done((bf16[32,12288]{1,0:T(8,128)(2,1)S(1)}, bf16[32,12288]{1,0:T(8,128)(2,1)S(1)}, u32[]{:S(2)}, u32[]{:S(2)}) %collective-permute-start.22) | collective-permute-done | bytes 786464 | tf_op jit(solution)/shard_map/ppermute | solution.py:37
  70.8 7.5 %update.1 = (bf16[24576,128]{1,0:T(8,128)(2,1)}, bf16[24576,128]{1,0:T(8,128)(2,1)S(1)}) custom-call(s32[1]{0:T(128)} %get-tuple-element.39.cnt_ref, s32[256]{0:T(256)S(1)} %get-tuple-element.40.lst_ref, s32[256]{0:T(256)S(1)} %copy-done.1, s32[1]{0:T(128)} %bitcast.first_ref, s32[1]{0:T(128)} %bitcast.1.me_ref, ...), custom_call_target="tpu_custom_call", output_to_operand_aliasing={{1}: (5, {})} | custom-call | tf_op jit(solution)/shard_map/update/pallas_call | solution.py:377
  (22 shorter events, 0.2 us)
Async XLA Ops:
  0.0 10.6 %collective-permute-start.2 = (bf16[8,24576]{1,0:T(8,128)(2,1)}, bf16[8,24576]{1,0:T(8,128)(2,1)S(1)}, u32[]{:S(2)}, u32[]{:S(2)}) collective-permute-start(bf16[8,24576]{1,0:T(8,128)(2,1)} %refs_0_.3), channel_id=1, source_target_pairs={{0,16},{1,5},{2,18},{3,7},{4,20},{5,1},{6,22},{7,3},{8,24},{9,13},... | collective-permute-start | bytes 1179656 | tf_op jit(solution)/shard_map/ppermute | solution.py:37
  3.7 10.3 %collective-permute-start.1 = (bf16[8,24576]{1,0:T(8,128)(2,1)}, bf16[8,24576]{1,0:T(8,128)(2,1)S(1)}, u32[]{:S(2)}, u32[]{:S(2)}) collective-permute-start(bf16[8,24576]{1,0:T(8,128)(2,1)} %refs_0_.3), channel_id=1, source_target_pairs={{0,24},{1,7},{2,26},{3,1},{4,28},{5,3},{6,30},{7,5},{8,0},{9,15},{... | collective-permute-start | bytes 1179656 | tf_op jit(solution)/shard_map/ppermute | solution.py:37
  4.5 9.5 %collective-permute-start = (bf16[8,24576]{1,0:T(8,128)(2,1)}, bf16[8,24576]{1,0:T(8,128)(2,1)S(1)}, u32[]{:S(2)}, u32[]{:S(2)}) collective-permute-start(bf16[8,24576]{1,0:T(8,128)(2,1)} %refs_0_.3), channel_id=1, source_target_pairs={{0,8},{1,3},{2,10},{3,5},{4,12},{5,7},{6,14},{7,1},{8,16},{9,11},{... | collective-permute-start | bytes 1179656 | tf_op jit(solution)/shard_map/ppermute | solution.py:37
  5.2 0.7 copy-start
  5.9 8.2 %copy-start.2 = (bf16[8,24576]{1,0:T(8,128)(2,1)S(1)}, bf16[8,24576]{1,0:T(8,128)(2,1)}, u32[]{:S(2)}) copy-start(bf16[8,24576]{1,0:T(8,128)(2,1)} %refs_0_.3) | copy-start | bytes 1179652
  9.3 10.3 %collective-permute-start.6 = (bf16[256,128]{1,0:T(8,128)(2,1)S(1)}, bf16[256,128]{1,0:T(8,128)(2,1)S(1)}, u32[]{:S(2)}, u32[]{:S(2)}) collective-permute-start(bf16[256,128]{1,0:T(8,128)(2,1)S(1)} %get-tuple-element.49.a_ref), channel_id=1, source_target_pairs={{128,0},{160,32},{192,64},{224,96},{129,1},{161,33},{193,65},{225,... | collective-permute-start | bytes 196616 | tf_op jit(solution)/shard_map/ppermute | solution.py:404
  14.1 5.5 %collective-permute-start.5 = (bf16[32,256]{1,0:T(8,128)(2,1)S(1)}, bf16[32,256]{1,0:T(8,128)(2,1)S(1)}, u32[]{:S(2)}, u32[]{:S(2)}) collective-permute-start(bf16[32,256]{1,0:T(8,128)(2,1)S(1)} %stack_d.1.refs_0_), channel_id=1, source_target_pairs={{0,6},{1,25},{2,0},{3,27},{4,2},{5,29},{6,4},{7,31},{8,14},{9,1},{... | collective-permute-start | bytes 49160 | tf_op jit(solution)/shard_map/ppermute | solution.py:37
  16.6 4.1 %collective-permute-start.4 = (bf16[32,256]{1,0:T(8,128)(2,1)S(1)}, bf16[32,256]{1,0:T(8,128)(2,1)S(1)}, u32[]{:S(2)}, u32[]{:S(2)}) collective-permute-start(bf16[32,256]{1,0:T(8,128)(2,1)S(1)} %stack_d.1.refs_0_), channel_id=1, source_target_pairs={{0,2},{1,9},{2,4},{3,11},{4,6},{5,13},{6,0},{7,15},{8,10},{9,17},{... | collective-permute-start | bytes 49160 | tf_op jit(solution)/shard_map/ppermute | solution.py:37
  16.6 4.4 %collective-permute-start.3 = (bf16[32,256]{1,0:T(8,128)(2,1)S(1)}, bf16[32,256]{1,0:T(8,128)(2,1)S(1)}, u32[]{:S(2)}, u32[]{:S(2)}) collective-permute-start(bf16[32,256]{1,0:T(8,128)(2,1)S(1)} %stack_d.1.refs_0_), channel_id=1, source_target_pairs={{0,4},{1,17},{2,6},{3,19},{4,0},{5,21},{6,2},{7,23},{8,12},{9,25},... | collective-permute-start | bytes 49160 | tf_op jit(solution)/shard_map/ppermute | solution.py:37
  21.1 6.4 %collective-permute-start.7 = (bf16[256,128]{1,0:T(8,128)(2,1)S(1)}, bf16[256,128]{1,0:T(8,128)(2,1)S(1)}, u32[]{:S(2)}, u32[]{:S(2)}) collective-permute-start(bf16[256,128]{1,0:T(8,128)(2,1)S(1)} %add.2.a_ref), channel_id=1, source_target_pairs={{64,0},{96,32},{65,1},{97,33},{66,2},{98,34},{67,3},{99,35},{68,4}... | collective-permute-start | bytes 196616 | tf_op jit(solution)/shard_map/ppermute | solution.py:404
  22.4 5.1 %collective-permute-start.8 = (bf16[128,256]{1,0:T(8,128)(2,1)S(1)}, bf16[128,256]{1,0:T(8,128)(2,1)S(1)}, u32[]{:S(2)}, u32[]{:S(2)}) collective-permute-start(bf16[128,256]{1,0:T(8,128)(2,1)S(1)} %stack_l.1.own_ref), channel_id=1, source_target_pairs={{0,1},{1,0},{2,3},{3,2},{4,5},{5,4},{6,7},{7,6},{8,9},{9,8},{10,11... | collective-permute-start | bytes 196616 | tf_op jit(solution)/shard_map/ppermute | solution.py:37
  25.7 22.1 %collective-permute-start.13 = (bf16[32,24576]{1,0:T(8,128)(2,1)S(1)}, bf16[32,24576]{1,0:T(8,128)(2,1)S(1)}, u32[]{:S(2)}, u32[]{:S(2)}) collective-permute-start(bf16[32,24576]{1,0:T(8,128)(2,1)S(1)} %stack_p.1.refs_1_), channel_id=1, source_target_pairs={{0,6},{1,25},{2,0},{3,27},{4,2},{5,29},{6,4},{7,31},{8,14},{9,1},{... | collective-permute-start | bytes 4718600 | tf_op jit(solution)/shard_map/ppermute | solution.py:37
  27.5 20.9 %collective-permute-start.12 = (bf16[32,24576]{1,0:T(8,128)(2,1)S(1)}, bf16[32,24576]{1,0:T(8,128)(2,1)}, u32[]{:S(2)}, u32[]{:S(2)}) collective-permute-start(bf16[32,24576]{1,0:T(8,128)(2,1)S(1)} %stack_p.1.refs_1_), channel_id=1, source_target_pairs={{0,2},{1,9},{2,4},{3,11},{4,6},{5,13},{6,0},{7,15},{8,10},{9,17},{... | collective-permute-start | bytes 4718600 | tf_op jit(solution)/shard_map/ppermute | solution.py:37
  27.5 20.8 %collective-permute-start.14 = (bf16[32,24576]{1,0:T(8,128)(2,1)S(1)}, bf16[32,24576]{1,0:T(8,128)(2,1)}, u32[]{:S(2)}, u32[]{:S(2)}) collective-permute-start(bf16[32,24576]{1,0:T(8,128)(2,1)S(1)} %stack_p.1.refs_1_), channel_id=1, source_target_pairs={{0,1},{1,0},{2,3},{3,2},{4,5},{5,4},{6,7},{7,6},{8,9},{9,8},{10,11... | collective-permute-start | bytes 4718600 | tf_op jit(solution)/shard_map/ppermute | solution.py:37
  31.5 5.8 %collective-permute-start.9 = (bf16[256,128]{1,0:T(8,128)(2,1)S(1)}, bf16[256,128]{1,0:T(8,128)(2,1)S(1)}, u32[]{:S(2)}, u32[]{:S(2)}) collective-permute-start(bf16[256,128]{1,0:T(8,128)(2,1)S(1)} %add.3.top_ref), channel_id=1, source_target_pairs={{32,0},{33,1},{34,2},{35,3},{36,4},{37,5},{38,6},{39,7},{40,8},{41... | collective-permute-start | bytes 196616 | tf_op jit(solution)/shard_map/ppermute | solution.py:404
  32.8 4.5 %collective-permute-start.10 = (bf16[256,128]{1,0:T(8,128)(2,1)S(1)}, bf16[256,128]{1,0:T(8,128)(2,1)S(1)}, u32[]{:S(2)}, u32[]{:S(2)}) collective-permute-start(bf16[256,128]{1,0:T(8,128)(2,1)S(1)} %get-tuple-element.60.a_ref), channel_id=1, source_target_pairs={{0,64},{1,65},{2,66},{3,67},{4,68},{5,69},{6,70},{7,71},{8,72},{9,... | collective-permute-start | bytes 196616 | tf_op jit(solution)/shard_map/ppermute | solution.py:404
  37.3 9.2 %collective-permute-start.15 = (bf16[256,128]{1,0:T(8,128)(2,1)S(1)}, bf16[256,128]{1,0:T(8,128)(2,1)S(1)}, u32[]{:S(2)}, u32[]{:S(2)}) collective-permute-start(bf16[256,128]{1,0:T(8,128)(2,1)S(1)} %choose.3.a_ref), channel_id=1, source_target_pairs={{0,32},{64,96},{1,33},{65,97},{2,34},{66,98},{3,35},{67,99},{4,36}... | collective-permute-start | bytes 196616 | tf_op jit(solution)/shard_map/ppermute | solution.py:404
  44.7 3.2 %collective-permute-start.11 = (bf16[256,128]{1,0:T(8,128)(2,1)S(1)}, bf16[256,128]{1,0:T(8,128)(2,1)S(1)}, u32[]{:S(2)}, u32[]{:S(2)}) collective-permute-start(bf16[256,128]{1,0:T(8,128)(2,1)S(1)} %solve.1.a_ref), channel_id=1, source_target_pairs={{0,64},{1,65},{2,66},{3,67},{4,68},{5,69},{6,70},{7,71},{8,72},{9,... | collective-permute-start | bytes 196616 | tf_op jit(solution)/shard_map/ppermute | solution.py:404
  48.4 15.1 %collective-permute-start.19 = (bf16[32,12288]{1,0:T(8,128)(2,1)S(1)}, bf16[32,12288]{1,0:T(8,128)(2,1)S(1)}, u32[]{:S(2)}, u32[]{:S(2)}) collective-permute-start(bf16[32,12288]{1,0:T(8,128)(2,1)S(1)} %stack_b.1), channel_id=1, source_target_pairs={{0,6},{1,25},{2,0},{3,27},{4,2},{5,29},{6,4},{7,31},{8,14},{9,1},{... | collective-permute-start | bytes 2359304 | tf_op jit(solution)/shard_map/ppermute | solution.py:37
  51.9 12.4 %collective-permute-start.18 = (bf16[32,12288]{1,0:T(8,128)(2,1)S(1)}, bf16[32,12288]{1,0:T(8,128)(2,1)S(1)}, u32[]{:S(2)}, u32[]{:S(2)}) collective-permute-start(bf16[32,12288]{1,0:T(8,128)(2,1)S(1)} %stack_a.1), channel_id=1, source_target_pairs={{0,2},{1,9},{2,4},{3,11},{4,6},{5,13},{6,0},{7,15},{8,10},{9,17},{... | collective-permute-start | bytes 2359304 | tf_op jit(solution)/shard_map/ppermute | solution.py:37
  52.0 4.4 %collective-permute-start.16 = (bf16[256,128]{1,0:T(8,128)(2,1)S(1)}, bf16[256,128]{1,0:T(8,128)(2,1)S(1)}, u32[]{:S(2)}, u32[]{:S(2)}) collective-permute-start(bf16[256,128]{1,0:T(8,128)(2,1)S(1)} %choose.5.a_ref), channel_id=1, source_target_pairs={{0,32},{64,96},{1,33},{65,97},{2,34},{66,98},{3,35},{67,99},{4,36}... | collective-permute-start | bytes 196616 | tf_op jit(solution)/shard_map/ppermute | solution.py:404
  56.4 14.4 %copy-start.1 = (s32[256]{0:T(256)S(1)}, s32[256]{0:T(256)}, u32[]{:S(2)}) copy-start(s32[256]{0:T(256)} %piv_ref.3) | copy-start | bytes 3076
  56.4 11.2 %collective-permute-start.17 = (bf16[512,128]{1,0:T(8,128)(2,1)S(1)}, bf16[512,128]{1,0:T(8,128)(2,1)S(1)}, u32[]{:S(2)}, u32[]{:S(2)}) collective-permute-start(bf16[512,128]{1,0:T(8,128)(2,1)S(1)} %join.1.ud_ref), channel_id=1, source_target_pairs={{0,128},{32,160},{64,192},{96,224},{1,129},{33,161},{65,193},{97,2... | collective-permute-start | bytes 393224 | tf_op jit(solution)/shard_map/ppermute | solution.py:404
  60.5 10.3 %collective-permute-start.20 = (bf16[32,24576]{1,0:T(8,128)(2,1)}, bf16[32,24576]{1,0:T(8,128)(2,1)S(1)}, u32[]{:S(2)}, u32[]{:S(2)}) collective-permute-start(bf16[32,24576]{1,0:T(8,128)(2,1)} %collective-permute-done.12.refs_0_.refs_2_), channel_id=1, source_target_pairs={{0,1},{1,0},{2,3},{3,2},{4,5},{5,4},{6,7},{7,6},{8,9},{9,8},{10,11... | collective-permute-start | bytes 4718600 | tf_op jit(solution)/shard_map/ppermute | solution.py:37
  63.2 7.5 %collective-permute-start.21 = (bf16[32,24576]{1,0:T(8,128)(2,1)S(1)}, bf16[32,24576]{1,0:T(8,128)(2,1)S(1)}, u32[]{:S(2)}, u32[]{:S(2)}) collective-permute-start(bf16[32,24576]{1,0:T(8,128)(2,1)S(1)} %collective-permute-done.13.refs_0_.refs_3_), channel_id=1, source_target_pairs={{0,1},{1,0},{2,3},{3,2},{4,5},{5,4},{6,7},{7,6},{8,9},{9,8},{10,11... | collective-permute-start | bytes 4718600 | tf_op jit(solution)/shard_map/ppermute | solution.py:37
  63.5 6.1 %collective-permute-start.23 = (bf16[32,12288]{1,0:T(8,128)(2,1)S(1)}, bf16[32,12288]{1,0:T(8,128)(2,1)S(1)}, u32[]{:S(2)}, u32[]{:S(2)}) collective-permute-start(bf16[32,12288]{1,0:T(8,128)(2,1)S(1)} %collective-permute-done.19.refs_1_.refs_5_), channel_id=1, source_target_pairs={{0,1},{1,0},{2,3},{3,2},{4,5},{5,4},{6,7},{7,6},{8,9},{9,8},{10,11... | collective-permute-start | bytes 2359304 | tf_op jit(solution)/shard_map/ppermute | solution.py:37
  64.3 6.4 %collective-permute-start.22 = (bf16[32,12288]{1,0:T(8,128)(2,1)S(1)}, bf16[32,12288]{1,0:T(8,128)(2,1)S(1)}, u32[]{:S(2)}, u32[]{:S(2)}) collective-permute-start(bf16[32,12288]{1,0:T(8,128)(2,1)S(1)} %collective-permute-done.18.refs_0_.refs_4_), channel_id=1, source_target_pairs={{0,1},{1,0},{2,3},{3,2},{4,5},{5,4},{6,7},{7,6},{8,9},{9,8},{10,11... | collective-permute-start | bytes 2359304 | tf_op jit(solution)/shard_map/ppermute | solution.py:37
